TPU v7x, 32 devices: a whole 2x2x4 slice. The times are simulated.
32 devices in a mesh: center: 8 (over y, x, core), expert: 4 (over z).
Axes of the slice: x: 2, y: 2, z: 4, core: 2. Of those that a mesh axis runs over, the one named last changes fastest.
Arguments:
- tokens: bfloat16 [4096, 2048], P(('center', 'expert')), may hold values from -6 to 6
- doc_ids: int32 [32, 128], P(('center', 'expert')), may hold values from 0 to 7, never falling along the last dimension, each value on 1 to 32 neighbouring positions
- expert_ids: int32 [4096, 8], P(('center', 'expert')), may hold values from 0 to 31, all different within a row; in each aligned block of 128 rows (0 to 127, 128 to 255, ...) at most 64 rows name the same one
- gate_raw: float32 [4096, 8], P(('center', 'expert')), may hold values from 0.1 to 1
- gate_up: bfloat16 [32, 2048, 1536], P(('center', 'expert')), may hold values from -0.125 to 0.125
- down: bfloat16 [32, 768, 2048], P(('center', 'expert'))
- bank: bfloat16 [16384, 2048], P('center')
Outputs:
- layer_out: bfloat16 [4096, 2048], P(('center', 'expert'))
- scores: float32 [256], P(('center', 'expert'))
Inputs may be any that keep to these rules, and one draw needn't show every extreme that they name: `expert_ids`: each row names 8 different experts; in the rows of one device no expert is named by more than 64 rows, a bound that some block reaches. `doc_ids`: each row splits its 128 tokens into 8 runs numbered in order, each of 1 to 32 tokens, one of exactly 32.
All inputs are finite; a program needn't handle non-finite values.
Results may differ from a plain program's by a relative error of at most 0.0071.
Values may be sent and summed in bfloat16 or wider, within the bound.
No kernel may reach another device: no remote copies, remote signals or barrier semaphores. Data moves between devices by JAX's collectives and lax.ppermute only.
A program may use at most 128 MiB of HBM per device.

v0:
```python
import jax
import jax.numpy as jnp
from jax import lax
from jax.sharding import PartitionSpec as P

DOC_DEV = 8


def rms_normed(hidden_rows):
    values = hidden_rows.astype(jnp.float32)
    inverse_rms = lax.rsqrt(jnp.mean(values * values, axis=-1, keepdims=True) + 1e-06)
    return (values * inverse_rms).astype(jnp.bfloat16)


def slot_table(chosen_ids, expert_count):
    chosen = (
        chosen_ids[:, :, None] == jnp.arange(expert_count, dtype=jnp.int32)[None, None, :]
    ).astype(jnp.int32)
    per_token = jnp.sum(chosen, axis=1)
    before = jnp.cumsum(per_token, axis=0) - per_token
    return jnp.sum(chosen * before[:, None, :], axis=2)


def expert_ffn(rows_in, weights_gu, weights_down):
    model_width = rows_in.shape[-1]
    flat_rows = rows_in.reshape(-1, model_width)
    hidden_width = weights_down.shape[0]
    gate_and_up = jnp.dot(flat_rows, weights_gu, preferred_element_type=jnp.float32)
    hidden = (jax.nn.silu(gate_and_up[:, :hidden_width]) * gate_and_up[:, hidden_width:]).astype(
        jnp.bfloat16
    )
    result = jnp.dot(hidden, weights_down, preferred_element_type=jnp.float32).astype(jnp.bfloat16)
    return result.reshape(rows_in.shape)


def local(tokens, doc_ids, expert_ids, gate_raw, gate_up, down, bank):
    center_count = lax.axis_size("center")
    expert_axis = lax.axis_size("expert")
    expert_count = center_count * expert_axis
    tok_count, top_count = expert_ids.shape
    model_width = tokens.shape[1]
    capacity = min(tok_count, 2 * tok_count * top_count // expert_count)
    normed = rms_normed(tokens)
    position = slot_table(expert_ids, expert_count)
    target = (expert_ids * capacity + position).reshape(-1)
    repeated = jnp.broadcast_to(normed[:, None, :], (tok_count, top_count, model_width)).reshape(
        -1, model_width
    )
    send_buffer = (
        jnp.zeros((expert_count * capacity, model_width), jnp.bfloat16).at[target].set(repeated)
    )
    send_buffer = send_buffer.reshape(expert_count, capacity, model_width)
    weights_gu = gate_up[0]
    weights_down = down[0]
    computed = expert_ffn(
        lax.all_to_all(send_buffer, ("center", "expert"), split_axis=0, concat_axis=0, tiled=True),
        weights_gu,
        weights_down,
    )
    returned = lax.all_to_all(
        computed, ("center", "expert"), split_axis=0, concat_axis=0, tiled=True
    )
    returned = returned.reshape(expert_count * capacity, model_width)
    gathered = returned[target].reshape(tok_count, top_count, model_width)
    gate_norm = gate_raw / jnp.sum(gate_raw, axis=1, keepdims=True)
    combined = jnp.sum(gathered.astype(jnp.float32) * gate_norm[:, :, None], axis=1)
    layer_out = combined.astype(jnp.bfloat16)
    member = (jnp.arange(DOC_DEV, dtype=jnp.int32)[:, None] == doc_ids[0][None, :]).astype(
        jnp.float32
    )
    summed = jnp.dot(
        member, combined, precision=lax.Precision.HIGHEST, preferred_element_type=jnp.float32
    )
    pooled = (summed * lax.rsqrt(jnp.sum(summed * summed, axis=1, keepdims=True) + 1e-06)).astype(
        jnp.bfloat16
    )
    bank_values = bank.astype(jnp.float32)
    bank_norms = jnp.sum(bank_values * bank_values, axis=1)
    shard_part = lax.all_gather(pooled, "center", axis=0, tiled=True)
    doc_values = shard_part.astype(jnp.float32)
    doc_norms = jnp.sum(doc_values * doc_values, axis=1)
    products = lax.dot_general(
        shard_part, bank, (((1,), (1,)), ((), ())), preferred_element_type=jnp.float32
    )
    distance = doc_norms[:, None] + bank_norms[None, :] - 2.0 * products
    nearest = jnp.min(distance, axis=1)
    merged = lax.pmin(nearest, "center")
    own_scores = lax.dynamic_slice_in_dim(merged, lax.axis_index("center") * DOC_DEV, DOC_DEV)
    return (layer_out, own_scores)


def solution(mesh):
    return jax.shard_map(
        local,
        mesh=mesh,
        in_specs=(
            P(("center", "expert"), None),
            P(("center", "expert"), None),
            P(("center", "expert"), None),
            P(("center", "expert"), None),
            P(("center", "expert"), None, None),
            P(("center", "expert"), None, None),
            P("center", None),
        ),
        out_specs=(P(("center", "expert"), None), P(("center", "expert"))),
        check_vma=False,
    )
```

profile of v0, /device:TPU:0, one launch (start us, length us, event | category | flops | bytes accessed | tf_op | source)
XLA Modules:
  0.0 469.9 jit_solution(9091549737398492924)
XLA Ops:
  0.6 0.0 copy-start
  0.6 0.9 convert_reduce_fusion
  1.5 0.1 copy.14
  1.6 0.2 reduce_window_sum.11
  1.8 0.1 copy.16
  1.8 0.7 select_reduce_fusion
  2.6 0.7 multiply_add_fusion
  3.3 0.1 copy.17
  3.4 0.1 reshape.82
  3.5 1.2 fusion.13
  4.7 2.0 fusion.14
  6.7 11.7 %scatter_custom_fusion = bf16[2048,2048]{1,0:T(8,128)(2,1)} fusion(s32[1024]{0:T(1024)S(1)} %bitcast.25, bf16[]{:T(256)} %constant.13.clone.1, bf16[128,2048]{1,0:T(8,128)(2,1)} %fusion.14), kind=kCustom, calls=%fused_computation.10 | custom fusion | bytes 8912898 | tf_op jit(solution)/shard_map/scatter | solution.py:50
  18.4 189.7 %all_to_all.10 = bf16[32,64,2048]{2,1,0:T(8,128)(2,1)S(1)} all-to-all(bf16[32,64,2048]{2,1,0:T(8,128)(2,1)} %bitcast.22), channel_id=1, replica_groups=mesh['center'=8,'expert'=4] {'center','expert'}, dimensions={0} | all-to-all | bytes 16777216 | tf_op jit(solution)/shard_map/all_to_all | solution.py:56
  208.1 15.8 %fusion.2 = f32[2048,1536]{1,0:T(8,128)S(1)} fusion(bf16[2048,2048]{1,0:T(8,128)(2,1)S(1)} %bitcast.24, bf16[1,2048,1536]{2,1,0:T(8,128)(2,1)} %param.11), kind=kOutput, calls=%fused_computation.8 | convolution fusion | flops 12884901888 | bytes 27262976 | tf_op jit(solution)/shard_map/dot_general | solution.py:28
  223.8 0.0 copy-done
  223.8 8.9 %convolution_convert_fusion = bf16[2048,2048]{1,0:T(8,128)(2,1)} fusion(f32[2048,1536]{1,0:T(8,128)S(1)} %fusion.2, bf16[1,768,2048]{2,1,0:T(8,128)(2,1)S(1)} %copy-done), kind=kOutput, calls=%fused_computation.5 | convolution fusion | flops 6456082432 | bytes 24117248 | tf_op jit(solution)/shard_map/dot_general | solution.py:32
  232.8 0.0 copy-start.1
  232.8 4.8 %all-to-all-start.1 = ((bf16[32,64,2048]{2,1,0:T(8,128)(2,1)}), bf16[32,64,2048]{2,1,0:T(8,128)(2,1)}, u32[]{:S(2)}, u32[]{:S(2)}) async-start(bf16[32,64,2048]{2,1,0:T(8,128)(2,1)} %bitcast.23), calls=%async_computation.1 | async-start | bytes 16777216 | tf_op jit(solution)/shard_map/all_to_all | solution.py:60
  237.6 0.0 copy-done.1
  237.6 0.1 copy.18
  237.7 5.1 %multiply_reduce_fusion = f32[2048]{0:T(1024)S(1)} fusion(bf16[2048,2048]{1,0:T(8,128)(2,1)} %param.13), kind=kLoop, calls=%fused_computation.2 | loop fusion | flops 12580864 | bytes 8396800 | tf_op jit(solution)/shard_map/reduce_sum | solution.py:78
  242.8 176.2 %all-to-all-done.1 = bf16[32,64,2048]{2,1,0:T(8,128)(2,1)} async-done(((bf16[32,64,2048]{2,1,0:T(8,128)(2,1)}), bf16[32,64,2048]{2,1,0:T(8,128)(2,1)}, u32[]{:S(2)}, u32[]{:S(2)}) %all-to-all-start.1) | async-done | bytes 8388640 | tf_op jit(solution)/shard_map/all_to_all | solution.py:60
  419.0 0.0 copy-start.2
  419.0 13.3 %gather_fusion = bf16[1024,2048]{1,0:T(8,128)(2,1)} fusion(bf16[2048,2048]{1,0:T(8,128)(2,1)} %bitcast.7, s32[1024]{0:T(1024)S(1)} %broadcast_clamp_fusion), kind=kCustom, calls=%fused_computation | custom fusion | bytes 8392704 | tf_op jit(solution)/shard_map/gather | solution.py:64
  432.3 6.5 %fusion = f32[128,2048]{1,0:T(8,128)S(1)} fusion(bf16[1024,2048]{1,0:T(8,128)(2,1)} %gather_fusion, f32[128,8]{1,0:T(8,128)S(1)} %copy.18), kind=kLoop, calls=%fused_computation.4 | loop fusion | flops 6029312 | bytes 5246976 | tf_op jit(solution)/shard_map/reduce_sum | solution.py:66
  438.8 0.9 convert_element_type.41
  439.7 0.0 copy-done.2
  439.7 0.6 multiply_reduce_fusion.2
  440.3 0.1 multiply_convert_fusion
  440.4 9.4 %all_gather.3 = bf16[64,2048]{1,0:T(8,128)(2,1)S(1)} all-gather(bf16[8,2048]{1,0:T(8,128)(2,1)S(1)} %multiply_convert_fusion), channel_id=1, replica_groups=mesh['center'=8,'expert'=4] {'center'}, dimensions={0}, use_global_device_ids=true | all-gather | bytes 294912 | tf_op jit(solution)/shard_map/all_gather | solution.py:79
  449.8 0.2 multiply_reduce_fusion.1
  449.9 6.2 %fusion.12 = f32[64]{0:T(128)S(1)} fusion(bf16[64,2048]{1,0:T(8,128)(2,1)S(1)} %all_gather.3, bf16[2048,2048]{1,0:T(8,128)(2,1)} %param.13, f32[2048]{0:T(1024)S(1)} %multiply_reduce_fusion, f32[64]{0:T(128)S(1)} %multiply_reduce_fusion.1), kind=kOutput, calls=%fused_computation.20 | convolution fusion | flops 537395136 | bytes 8659456 | tf_op jit(solution)/shard_map/dot_general | solution.py:82
  456.1 13.2 %pmin.7 = f32[64]{0:T(128)S(1)} all-reduce(f32[64]{0:T(128)S(1)} %fusion.12), channel_id=1, replica_groups=mesh['center'=8,'expert'=4] {'center'}, use_global_device_ids=true, to_apply=%region_11.12 | all-reduce | flops 64 | bytes 512 | tf_op jit(solution)/shard_map/pmin | solution.py:87
  469.3 0.6 dynamic_slice.3
  (7 shorter events, 0.1 us)
Async XLA Ops:
  0.6 223.2 %copy-start = (bf16[1,768,2048]{2,1,0:T(8,128)(2,1)S(1)}, bf16[1,768,2048]{2,1,0:T(8,128)(2,1)}, u32[]{:S(2)}) copy-start(bf16[1,768,2048]{2,1,0:T(8,128)(2,1)} %param.12) | copy-start | bytes 9437188
  232.8 4.8 %copy-start.1 = (f32[128,8]{0,1:T(8,128)S(1)}, f32[128,8]{0,1:T(8,128)}, u32[]{:S(2)}) copy-start(f32[128,8]{0,1:T(8,128)} %param.10) | copy-start | bytes 12292
  232.8 186.2 %all-to-all-start.1 = ((bf16[32,64,2048]{2,1,0:T(8,128)(2,1)}), bf16[32,64,2048]{2,1,0:T(8,128)(2,1)}, u32[]{:S(2)}, u32[]{:S(2)}) async-start(bf16[32,64,2048]{2,1,0:T(8,128)(2,1)} %bitcast.23), calls=%async_computation.1 | async-start | bytes 16777216 | tf_op jit(solution)/shard_map/all_to_all | solution.py:60
  419.0 20.7 %copy-start.2 = (s32[1,128]{1,0:T(1,128)S(1)}, s32[1,128]{1,0:T(1,128)}, u32[]{:S(2)}) copy-start(s32[1,128]{1,0:T(1,128)} %param.8) | copy-start | bytes 1540
where the time goes:
time: 473 us; the launch traced here: 470 us
  blocking collectives  212 us (45%)
  waiting for transfers between devices  176 us (37%)
  matrix products  31.4 us (7%)
  local copies, waits for them, and re-layouts  26 us (5%)
  other arithmetic  18.4 us (4%)
  starting transfers between devices  4.81 us (1%)
    all_to_all x1, blocking collectives, local(): lax.all_to_all(send_buffer, ('center', 'expert'), split_axis=0, concat_ax...  190 us
    all_to_all x1, waiting for transfers between devices, local(): lax.all_to_all(computed, ('center', 'expert'), split_axis=0, concat_axis=...  176 us
    dot_general x1, matrix products, expert_ffn(): jnp.dot(flat_rows, weights_gu, preferred_element_type=jnp.float32)  15.8 us
    gather x1, local copies, waits for them, and re-layouts, local(): gathered = returned[target].reshape(tok_count, top_count, model_width)  13.3 us
    pmin x1, blocking collectives, local(): merged = lax.pmin(nearest, 'center')  13.2 us
    scatter x1, local copies, waits for them, and re-layouts, local(): jnp.zeros((expert_count * capacity, model_width), jnp.bfloat16).at[target]  11.7 us
  transfers between devices with their start and end apart: 1, of which 1 were waited for; matrix products, arithmetic and copies ran while one was open for 1% of the time, Pallas kernels for 0%

commit v1 on v0

v1 whole, which is shorter than its diff:
```python
import functools

import jax
import jax.numpy as jnp
from jax import lax
from jax.experimental import pallas as pl
from jax.experimental.pallas import tpu as pltpu
from jax.sharding import PartitionSpec as P

DOC_DEV = 8
BOTH = ("center", "expert")
CORE, ALONG_X, ALONG_Y = 1, 2, 4
PLANE = (0, ALONG_X, ALONG_Y, ALONG_X | ALONG_Y)


def rms_normed(hidden_rows):
    values = hidden_rows.astype(jnp.float32)
    inverse_rms = lax.rsqrt(jnp.mean(values * values, axis=-1, keepdims=True) + 1e-06)
    return (values * inverse_rms).astype(jnp.bfloat16)


def swap(values, axis, mask):
    size = lax.axis_size(axis)
    return lax.ppermute(values, axis, [(i, i ^ mask) for i in range(size)])


def expert_kernel(capacity, place_ref, gates_ref, *refs):
    blocks = refs[:8]
    gate_up_hbm, down_hbm, own_hbm, other_hbm = refs[8:12]
    rows_in, gate_up, down, picked, hidden, scaled, rows_out, choice = refs[12:20]
    in_sem, weight_sem, out_sem = refs[20:]
    tok_count, model_width = blocks[0].shape
    hidden_width = down_hbm.shape[0]
    tile = 256
    hidden_tiles, model_tiles = hidden_width // tile, model_width // tile

    in_copies = [
        pltpu.make_async_copy(blocks[j], rows_in.at[j], in_sem.at[j]) for j in range(8)
    ]
    weight_copies = [
        pltpu.make_async_copy(gate_up_hbm, gate_up, weight_sem.at[0]),
        pltpu.make_async_copy(down_hbm, down, weight_sem.at[1]),
    ]
    for copy in in_copies + weight_copies:
        copy.start()

    gates = jnp.concatenate([gates_ref[pl.ds(place_ref[j], 1), :] for j in range(8)], axis=0)
    named = gates != 0.0
    before = (
        lax.broadcasted_iota(jnp.int32, (tok_count, tok_count), 0)
        < lax.broadcasted_iota(jnp.int32, (tok_count, tok_count), 1)
    ).astype(jnp.bfloat16)
    slot = jnp.dot(named.astype(jnp.bfloat16), before, preferred_element_type=jnp.float32)
    slot = jnp.where(named, slot, -1.0)
    slot_row = lax.broadcasted_iota(jnp.int32, (capacity, tok_count), 0).astype(jnp.float32)
    gate_columns = []
    for j in range(8):
        hit = slot_row == slot[j : j + 1, :]
        gate_columns.append(
            jnp.sum(jnp.where(hit, gates[j : j + 1, :], 0.0), axis=1, keepdims=True)
        )
        choice[j] = hit.astype(jnp.bfloat16)
    gate_column = jnp.concatenate(gate_columns, axis=0)

    for j in range(8):
        in_copies[j].wait()
        picked[pl.ds(j * capacity, capacity), :] = jnp.dot(
            choice[j], rows_in[j], preferred_element_type=jnp.float32
        ).astype(jnp.bfloat16)

    weight_copies[0].wait()

    @pl.loop(0, hidden_tiles)
    def _(step):
        at = pl.multiple_of(step * tile, tile)
        gate = jnp.dot(
            picked[...], gate_up[:, pl.ds(at, tile)], preferred_element_type=jnp.float32
        )
        up = jnp.dot(
            picked[...],
            gate_up[:, pl.ds(pl.multiple_of(at + hidden_width, tile), tile)],
            preferred_element_type=jnp.float32,
        )
        hidden[:, pl.ds(at, tile)] = (gate / (1.0 + jnp.exp(-gate)) * up).astype(jnp.bfloat16)

    weight_copies[1].wait()

    @pl.loop(0, model_tiles)
    def _(step):
        at = pl.multiple_of(step * tile, tile)
        result = jnp.dot(
            hidden[...], down[:, pl.ds(at, tile)], preferred_element_type=jnp.float32
        )
        scaled[:, pl.ds(at, tile)] = (result * gate_column).astype(jnp.bfloat16)

    out_copies = []
    for j in (4, 5, 6, 7, 0, 1, 2, 3):
        rows_out[j] = lax.dot_general(
            choice[j],
            scaled[pl.ds(j * capacity, capacity), :],
            (((0,), (0,)), ((), ())),
            preferred_element_type=jnp.float32,
        ).astype(jnp.bfloat16)
        target = own_hbm.at[j] if j < 4 else other_hbm.at[j - 4]
        copy = pltpu.make_async_copy(rows_out.at[j], target, out_sem.at[j])
        copy.start()
        out_copies.append(copy)
    for copy in out_copies:
        copy.wait()


def expert_part(capacity, place, gates, blocks, weights_gu, weights_down):
    tok_count, model_width = blocks[0].shape
    hidden_width = weights_down.shape[0]
    rows = 8 * capacity
    bf16 = jnp.bfloat16
    out = jax.ShapeDtypeStruct((4, tok_count, model_width), bf16)
    anywhere = pl.BlockSpec(memory_space=pl.ANY)
    return pl.pallas_call(
        functools.partial(expert_kernel, capacity),
        out_shape=(out, out),
        in_specs=[
            pl.BlockSpec(memory_space=pltpu.SMEM),
            pl.BlockSpec(memory_space=pltpu.VMEM),
        ]
        + [anywhere] * 10,
        out_specs=(anywhere, anywhere),
        scratch_shapes=[
            pltpu.VMEM((8, tok_count, model_width), bf16),
            pltpu.VMEM(weights_gu.shape, bf16),
            pltpu.VMEM(weights_down.shape, bf16),
            pltpu.VMEM((rows, model_width), bf16),
            pltpu.VMEM((rows, hidden_width), bf16),
            pltpu.VMEM((rows, model_width), bf16),
            pltpu.VMEM((8, tok_count, model_width), bf16),
            pltpu.VMEM((8, capacity, tok_count), bf16),
            pltpu.SemaphoreType.DMA((8,)),
            pltpu.SemaphoreType.DMA((2,)),
            pltpu.SemaphoreType.DMA((8,)),
        ],
        compiler_params=pltpu.CompilerParams(vmem_limit_bytes=40 * 1024 * 1024),
        cost_estimate=pl.CostEstimate(
            flops=6 * rows * model_width * hidden_width + 4 * rows * tok_count * model_width,
            bytes_accessed=2 * (3 * model_width * hidden_width + 16 * tok_count * model_width),
            transcendentals=rows * hidden_width,
        ),
        name="expert_part",
    )(place, gates, *blocks, weights_gu, weights_down)


def added(*terms):
    total = terms[0].astype(jnp.float32)
    for term in terms[1:]:
        total = total + term.astype(jnp.float32)
    return total


def gathered_layer(normed, gate_table, weights_gu, weights_down, capacity):
    expert_axis = lax.axis_size("expert")
    center_at, expert_at = lax.axis_index("center"), lax.axis_index("expert")
    expert_count = gate_table.shape[0]
    me = center_at * expert_axis + expert_at
    gates = lax.all_gather(gate_table, BOTH, axis=0, tiled=True)
    order = range(expert_axis)
    lines = [normed] + [swap(normed, "expert", step) for step in order[1:]]
    results = []
    for step in order:
        block = lines[step]
        from_x = swap(block, "center", ALONG_X)
        from_y = swap(block, "center", ALONG_Y)
        if step % 2 == 0:
            from_xy = swap(from_y, "center", ALONG_X)
        else:
            from_xy = swap(from_x, "center", ALONG_Y)
        own = [block, from_x, from_y, from_xy]
        other = [swap(part, "center", CORE) for part in own]
        places = [
            ((center_at ^ mask) * expert_axis + (expert_at ^ step)) * expert_count + me
            for mask in [m for m in PLANE] + [m ^ CORE for m in PLANE]
        ]
        results.append(
            expert_part(
                capacity,
                jnp.stack(places).astype(jnp.int32),
                gates,
                own + other,
                weights_gu,
                weights_down,
            )
        )
    sums = []
    bf16 = jnp.bfloat16
    for step in order:
        own, other = results[step]
        back = swap(other, "center", CORE)
        corner = added(own[3], back[3]).astype(bf16)
        if step % 2 == 0:
            part_x = added(own[1], back[1]).astype(bf16)
            part_y = added(own[2], back[2], swap(corner, "center", ALONG_X)).astype(bf16)
        else:
            part_x = added(own[1], back[1], swap(corner, "center", ALONG_Y)).astype(bf16)
            part_y = added(own[2], back[2]).astype(bf16)
        mine = added(
            own[0], back[0], swap(part_x, "center", ALONG_X), swap(part_y, "center", ALONG_Y)
        )
        sums.append(mine if step == 0 else swap(mine.astype(bf16), "expert", step))
    return added(*sums)


def slot_table(chosen_ids, expert_count):
    chosen = (
        chosen_ids[:, :, None] == jnp.arange(expert_count, dtype=jnp.int32)[None, None, :]
    ).astype(jnp.int32)
    per_token = jnp.sum(chosen, axis=1)
    before = jnp.cumsum(per_token, axis=0) - per_token
    return jnp.sum(chosen * before[:, None, :], axis=2)


def expert_ffn(rows_in, weights_gu, weights_down):
    model_width = rows_in.shape[-1]
    flat_rows = rows_in.reshape(-1, model_width)
    hidden_width = weights_down.shape[0]
    gate_and_up = jnp.dot(flat_rows, weights_gu, preferred_element_type=jnp.float32)
    hidden = (jax.nn.silu(gate_and_up[:, :hidden_width]) * gate_and_up[:, hidden_width:]).astype(
        jnp.bfloat16
    )
    result = jnp.dot(hidden, weights_down, preferred_element_type=jnp.float32).astype(jnp.bfloat16)
    return result.reshape(rows_in.shape)


def exchanged_layer(normed, expert_ids, gate_norm, weights_gu, weights_down, capacity):
    tok_count, top_count = expert_ids.shape
    model_width = normed.shape[1]
    expert_count = lax.axis_size("center") * lax.axis_size("expert")
    position = slot_table(expert_ids, expert_count)
    target = (expert_ids * capacity + position).reshape(-1)
    repeated = jnp.broadcast_to(normed[:, None, :], (tok_count, top_count, model_width)).reshape(
        -1, model_width
    )
    send_buffer = (
        jnp.zeros((expert_count * capacity, model_width), jnp.bfloat16).at[target].set(repeated)
    )
    send_buffer = send_buffer.reshape(expert_count, capacity, model_width)
    computed = expert_ffn(
        lax.all_to_all(send_buffer, BOTH, split_axis=0, concat_axis=0, tiled=True),
        weights_gu,
        weights_down,
    )
    returned = lax.all_to_all(computed, BOTH, split_axis=0, concat_axis=0, tiled=True)
    returned = returned.reshape(expert_count * capacity, model_width)
    gathered = returned[target].reshape(tok_count, top_count, model_width)
    return jnp.sum(gathered.astype(jnp.float32) * gate_norm[:, :, None], axis=1)


def local(tokens, doc_ids, expert_ids, gate_raw, gate_up, down, bank):
    center_count = lax.axis_size("center")
    expert_axis = lax.axis_size("expert")
    expert_count = center_count * expert_axis
    tok_count, top_count = expert_ids.shape
    capacity = min(tok_count, 2 * tok_count * top_count // expert_count)
    normed = rms_normed(tokens)
    gate_norm = gate_raw / jnp.sum(gate_raw, axis=1, keepdims=True)
    weights_gu = gate_up[0]
    weights_down = down[0]
    if center_count == 8 and expert_axis == 4:
        named = expert_ids[:, :, None] == jnp.arange(expert_count, dtype=jnp.int32)[None, None, :]
        gate_table = jnp.sum(jnp.where(named, gate_norm[:, :, None], 0.0), axis=1).T
        combined = gathered_layer(normed, gate_table, weights_gu, weights_down, capacity)
    else:
        combined = exchanged_layer(
            normed, expert_ids, gate_norm, weights_gu, weights_down, capacity
        )
    layer_out = combined.astype(jnp.bfloat16)
    member = (jnp.arange(DOC_DEV, dtype=jnp.int32)[:, None] == doc_ids[0][None, :]).astype(
        jnp.float32
    )
    summed = jnp.dot(
        member, combined, precision=lax.Precision.HIGHEST, preferred_element_type=jnp.float32
    )
    pooled = (summed * lax.rsqrt(jnp.sum(summed * summed, axis=1, keepdims=True) + 1e-06)).astype(
        jnp.bfloat16
    )
    bank_values = bank.astype(jnp.float32)
    bank_norms = jnp.sum(bank_values * bank_values, axis=1)
    shard_part = lax.all_gather(pooled, "center", axis=0, tiled=True)
    doc_values = shard_part.astype(jnp.float32)
    doc_norms = jnp.sum(doc_values * doc_values, axis=1)
    products = lax.dot_general(
        shard_part, bank, (((1,), (1,)), ((), ())), preferred_element_type=jnp.float32
    )
    distance = doc_norms[:, None] + bank_norms[None, :] - 2.0 * products
    nearest = jnp.min(distance, axis=1)
    merged = lax.pmin(nearest, "center")
    own_scores = lax.dynamic_slice_in_dim(merged, lax.axis_index("center") * DOC_DEV, DOC_DEV)
    return (layer_out, own_scores)


def solution(mesh):
    return jax.shard_map(
        local,
        mesh=mesh,
        in_specs=(
            P(BOTH, None),
            P(BOTH, None),
            P(BOTH, None),
            P(BOTH, None),
            P(BOTH, None, None),
            P(BOTH, None, None),
            P("center", None),
        ),
        out_specs=(P(BOTH, None), P(BOTH)),
        check_vma=False,
    )
```

time: 473 us -> 390 us (0.82)
  blocking collectives: 212 us -> 94.3 us
  Pallas kernels: 0 us -> 53.3 us
  starting transfers between devices: 4.81 us -> 34.5 us
  matrix products: 31.4 us -> 3.33 us
  waiting for transfers between devices: 176 us -> 151 us
  other arithmetic: 18.4 us -> 24.9 us
    all_to_all x1 -> x0, blocking collectives: 190 us -> none  [local(): lax.all_to_all(send_buffer, ('center', 'expert'), split_axis=0, concat_ax...]
    all_to_all x1 -> x0, waiting for transfers between devices: 176 us -> none  [local(): lax.all_to_all(computed, ('center', 'expert'), split_axis=0, concat_axis=...]
    ppermute x0 -> x50, waiting for transfers between devices: none -> 151 us  [swap(): return lax.ppermute(values, axis, [(i, i ^ mask) for i in range(size)])]
    all_gather x0 -> x1, blocking collectives: none -> 71.6 us  [gathered_layer(): gates = lax.all_gather(gate_table, BOTH, axis=0, tiled=True)]
    pallas_call x0 -> x4, Pallas kernels: none -> 53.3 us  [expert_part(): pl.pallas_call(functools.partial(expert_kernel, capacity), out_shape=(out...]
    ppermute x0 -> x50, starting transfers between devices: none -> 34.5 us  [swap(): return lax.ppermute(values, axis, [(i, i ^ mask) for i in range(size)])]
    unnamed x6 -> x80, local copies, waits for them, and re-layouts: 0.02 us -> 25.5 us
    dot_general x2 -> x0, matrix products: 24.7 us -> none  [the longest x1 15.8 us: expert_ffn(): jnp.dot(flat_rows, weights_gu, preferred_element_type=jnp.float32)]
  transfers between devices with their start and end apart: 1 -> 50, of which waited for: 1 -> 18; matrix products, arithmetic and copies ran while one was open for 1% -> 5% of each run, Pallas kernels for 0% -> 14%
where the time goes in v1:
time: 390 us; the launch traced here: 389 us
  waiting for transfers between devices  151 us (39%)
  blocking collectives  94.3 us (24%)
  Pallas kernels  53.3 us (14%)
  starting transfers between devices  34.5 us (9%)
  local copies, waits for them, and re-layouts  26.4 us (7%)
  other arithmetic  24.9 us (6%)
    ppermute x50, waiting for transfers between devices, swap(): return lax.ppermute(values, axis, [(i, i ^ mask) for i in range(size)])  151 us
    all_gather x1, blocking collectives, gathered_layer(): gates = lax.all_gather(gate_table, BOTH, axis=0, tiled=True)  71.6 us
    pallas_call x4, Pallas kernels, expert_part(): pl.pallas_call(functools.partial(expert_kernel, capacity), out_shape=(out...  53.3 us
    ppermute x50, starting transfers between devices, swap(): return lax.ppermute(values, axis, [(i, i ^ mask) for i in range(size)])  34.5 us
    unnamed x80, local copies, waits for them, and re-layouts  25.5 us
    pmin x1, blocking collectives, local(): merged = lax.pmin(nearest, 'center')  13.2 us
    all_gather x1, blocking collectives, local(): shard_part = lax.all_gather(pooled, 'center', axis=0, tiled=True)  9.51 us
  transfers between devices with their start and end apart: 50, of which 18 were waited for; matrix products, arithmetic and copies ran while one was open for 5% of the time, Pallas kernels for 14%

profile of v1, /device:TPU:0, one launch (start us, length us, event | category | flops | bytes accessed | tf_op | source)
XLA Modules:
  0.0 389.1 jit_solution(2987343409146660193)
XLA Ops:
  3.1 5.1 %collective-permute-start.37 = (bf16[128,2048]{1,0:T(8,128)(2,1)S(1)}, bf16[128,2048]{1,0:T(8,128)(2,1)S(1)}, u32[]{:S(2)}, u32[]{:S(2)}) collective-permute-start(bf16[128,2048]{1,0:T(8,128)(2,1)S(1)} %fusion.3.refs_0_), channel_id=1, source_target_pairs={{0,3},{1,2},{2,1},{3,0},{4,7},{5,6},{6,5},{7,4},{8,11},{9,10},{10,... | collective-permute-start | bytes 1572872 | tf_op jit(solution)/shard_map/ppermute | solution.py:24
  8.8 1.6 collective-permute-start
  10.5 1.5 collective-permute-start.1
  12.0 9.1 %collective-permute-done.37.refs_0_ = bf16[128,2048]{1,0:T(8,128)(2,1)S(1)} collective-permute-done((bf16[128,2048]{1,0:T(8,128)(2,1)S(1)}, bf16[128,2048]{1,0:T(8,128)(2,1)S(1)}, u32[]{:S(2)}, u32[]{:S(2)}) %collective-permute-start.37) | collective-permute-done | bytes 524320 | tf_op jit(solution)/shard_map/ppermute | solution.py:24
  21.1 31.9 %collective-permute-done.24.refs_0_ = bf16[128,2048]{1,0:T(8,128)(2,1)S(1)} collective-permute-done((bf16[128,2048]{1,0:T(8,128)(2,1)S(1)}, bf16[128,2048]{1,0:T(8,128)(2,1)S(1)}, u32[]{:S(2)}, u32[]{:S(2)}) %collective-permute-start.24) | collective-permute-done | bytes 524320 | tf_op jit(solution)/shard_map/ppermute | solution.py:24
  53.0 1.5 collective-permute-start.38
  54.5 1.5 collective-permute-start.39
  58.6 9.2 %collective-permute-done.38.refs_1_ = bf16[128,2048]{1,0:T(8,128)(2,1)S(1)} collective-permute-done((bf16[128,2048]{1,0:T(8,128)(2,1)S(1)}, bf16[128,2048]{1,0:T(8,128)(2,1)S(1)}, u32[]{:S(2)}, u32[]{:S(2)}) %collective-permute-start.38) | collective-permute-done | bytes 524320 | tf_op jit(solution)/shard_map/ppermute | solution.py:24
  71.0 1.5 collective-permute-start.13
  72.5 6.7 %collective-permute-done.25.refs_1_ = bf16[128,2048]{1,0:T(8,128)(2,1)} collective-permute-done((bf16[128,2048]{1,0:T(8,128)(2,1)S(1)}, bf16[128,2048]{1,0:T(8,128)(2,1)}, u32[]{:S(2)}, u32[]{:S(2)}) %collective-permute-start.25) | collective-permute-done | bytes 524320 | tf_op jit(solution)/shard_map/ppermute | solution.py:24
  83.3 7.1 %collective-permute-done.12.refs_1_ = bf16[128,2048]{1,0:T(8,128)(2,1)} collective-permute-done((bf16[128,2048]{1,0:T(8,128)(2,1)S(1)}, bf16[128,2048]{1,0:T(8,128)(2,1)}, u32[]{:S(2)}, u32[]{:S(2)}) %collective-permute-start.12) | collective-permute-done | bytes 524320 | tf_op jit(solution)/shard_map/ppermute | solution.py:24
  91.2 1.5 collective-permute-start.40
  95.3 4.5 %collective-permute-done.2.refs_3_ = bf16[128,2048]{1,0:T(8,128)(2,1)} collective-permute-done((bf16[128,2048]{1,0:T(8,128)(2,1)S(1)}, bf16[128,2048]{1,0:T(8,128)(2,1)}, u32[]{:S(2)}, u32[]{:S(2)}) %collective-permute-start.2) | collective-permute-done | bytes 524320 | tf_op jit(solution)/shard_map/ppermute | solution.py:24
  100.6 1.5 collective-permute-start.27
  103.7 2.0 collective-permute-done.40.refs_3_
  106.2 71.6 %all_gather.6.gates_ref = f32[1024,128]{1,0:T(8,128)S(1)} all-gather(f32[32,128]{1,0:T(8,128)S(1)} %bitcast.106), channel_id=1, replica_groups=mesh['center'=8,'expert'=4] {'center','expert'}, dimensions={0}, use_global_device_ids=true | all-gather | bytes 540672 | tf_op jit(solution)/shard_map/all_gather | solution.py:163
  180.1 1.9 copy-done.6
  186.1 13.6 %expert_part.4 = (bf16[4,128,2048]{2,1,0:T(8,128)(2,1)S(1)}, bf16[4,128,2048]{2,1,0:T(8,128)(2,1)}) custom-call(s32[8]{0:T(128)S(1)} %stack.116.place_ref, f32[1024,128]{1,0:T(8,128)S(1)} %all_gather.6.gates_ref, bf16[128,2048]{1,0:T(8,128)(2,1)S(1)} %fusion.3.refs_0_, bf16[128,2048]{1,0:T(8,128)(2,1)S(1)} %copy-done.24, bf16[128,2048]{1,0:T(8,128)(2,1)S(1)} %copy-done.26, ...), custom_call_target="tpu_custom_call" | custom-call | flops 5368709120 | bytes 17825792 | tf_op jit(solution)/shard_map/expert_part/pallas_call | solution.py:119
  200.4 13.0 %expert_part.7 = (bf16[4,128,2048]{2,1,0:T(8,128)(2,1)S(1)}, bf16[4,128,2048]{2,1,0:T(8,128)(2,1)}) custom-call(s32[8]{0:T(128)S(1)} %stack.143.place_ref, f32[1024,128]{1,0:T(8,128)S(1)} %all_gather.6.gates_ref, bf16[128,2048]{1,0:T(8,128)(2,1)S(1)} %copy-done.16, bf16[128,2048]{1,0:T(8,128)(2,1)S(1)} %copy-done.18, bf16[128,2048]{1,0:T(8,128)(2,1)S(1)} %copy-done.22, ...), custom_call_target="tpu_custom_call" | custom-call | flops 5368709120 | bytes 17825792 | tf_op jit(solution)/shard_map/expert_part/pallas_call | solution.py:119
  213.5 1.3 copy-done
  215.6 13.4 %expert_part.6 = (bf16[4,128,2048]{2,1,0:T(8,128)(2,1)S(1)}, bf16[4,128,2048]{2,1,0:T(8,128)(2,1)}) custom-call(s32[8]{0:T(128)S(1)} %stack.134.place_ref, f32[1024,128]{1,0:T(8,128)S(1)} %all_gather.6.gates_ref, bf16[128,2048]{1,0:T(8,128)(2,1)S(1)} %copy-done.14, bf16[128,2048]{1,0:T(8,128)(2,1)} %collective-permute-done.25.refs_1_, ...), custom_call_target="tpu_custom_call" | custom-call | flops 5368709120 | bytes 17825792 | tf_op jit(solution)/shard_map/expert_part/pallas_call | solution.py:119
  229.0 1.3 copy-done.2
  231.4 1.9 copy-done.8
  236.4 13.3 %expert_part.5 = (bf16[4,128,2048]{2,1,0:T(8,128)(2,1)S(1)}, bf16[4,128,2048]{2,1,0:T(8,128)(2,1)}) custom-call(s32[8]{0:T(128)S(1)} %stack.125.place_ref, f32[1024,128]{1,0:T(8,128)S(1)} %all_gather.6.gates_ref, bf16[128,2048]{1,0:T(8,128)(2,1)S(1)} %copy-done.10, bf16[128,2048]{1,0:T(8,128)(2,1)} %collective-permute-done.12.refs_1_, ...), custom_call_target="tpu_custom_call" | custom-call | flops 5368709120 | bytes 17825792 | tf_op jit(solution)/shard_map/expert_part/pallas_call | solution.py:119
  249.7 1.4 copy-done.4
  251.4 1.7 fusion.18
  253.2 2.0 collective-permute-start.8
  255.3 1.6 fusion.24
  258.9 1.7 fusion.22
  260.7 7.3 %collective-permute-done.9 = bf16[128,2048]{1,0:T(8,128)(2,1)S(1)} collective-permute-done((bf16[128,2048]{1,0:T(8,128)(2,1)S(1)}, bf16[128,2048]{1,0:T(8,128)(2,1)S(1)}, u32[]{:S(2)}, u32[]{:S(2)}) %collective-permute-start.9) | collective-permute-done | bytes 524320 | tf_op jit(solution)/shard_map/ppermute | solution.py:24
  269.3 2.1 collective-permute-start.33
  271.4 1.7 fusion.20
  273.1 8.5 %collective-permute-done.46 = bf16[128,2048]{1,0:T(8,128)(2,1)S(1)} collective-permute-done((bf16[128,2048]{1,0:T(8,128)(2,1)S(1)}, bf16[128,2048]{1,0:T(8,128)(2,1)S(1)}, u32[]{:S(2)}, u32[]{:S(2)}) %collective-permute-start.46) | collective-permute-done | bytes 524320 | tf_op jit(solution)/shard_map/ppermute | solution.py:24
  284.0 6.4 %collective-permute-done.34 = bf16[128,2048]{1,0:T(8,128)(2,1)S(1)} collective-permute-done((bf16[128,2048]{1,0:T(8,128)(2,1)S(1)}, bf16[128,2048]{1,0:T(8,128)(2,1)S(1)}, u32[]{:S(2)}, u32[]{:S(2)}) %collective-permute-start.34) | collective-permute-done | bytes 524320 | tf_op jit(solution)/shard_map/ppermute | solution.py:24
  291.8 2.4 collective-permute-done.20
  297.6 14.6 %collective-permute-done.47 = bf16[128,2048]{1,0:T(8,128)(2,1)S(1)} collective-permute-done((bf16[128,2048]{1,0:T(8,128)(2,1)S(1)}, bf16[128,2048]{1,0:T(8,128)(2,1)S(1)}, u32[]{:S(2)}, u32[]{:S(2)}) %collective-permute-start.47) | collective-permute-done | bytes 524320 | tf_op jit(solution)/shard_map/ppermute | solution.py:24
  312.5 1.4 fusion.6
  315.1 1.4 fusion.9
  316.5 1.7 collective-permute-done.22
  318.1 7.3 %collective-permute-done.21 = bf16[128,2048]{1,0:T(8,128)(2,1)S(1)} collective-permute-done((bf16[128,2048]{1,0:T(8,128)(2,1)S(1)}, bf16[128,2048]{1,0:T(8,128)(2,1)S(1)}, u32[]{:S(2)}, u32[]{:S(2)}) %collective-permute-start.21) | collective-permute-done | bytes 524320 | tf_op jit(solution)/shard_map/ppermute | solution.py:24
  325.4 1.4 fusion.12
  326.9 1.7 multiply_reduce_fusion
  328.6 3.2 collective-permute-done.49
  331.8 28.0 %collective-permute-done.36 = bf16[128,2048]{1,0:T(8,128)(2,1)S(1)} collective-permute-done((bf16[128,2048]{1,0:T(8,128)(2,1)S(1)}, bf16[128,2048]{1,0:T(8,128)(2,1)S(1)}, u32[]{:S(2)}, u32[]{:S(2)}) %collective-permute-start.36) | collective-permute-done | bytes 524320 | tf_op jit(solution)/shard_map/ppermute | solution.py:24
  359.8 2.4 fusion.28
  362.9 9.5 %all_gather.7 = bf16[64,2048]{1,0:T(8,128)(2,1)S(1)} all-gather(bf16[8,2048]{1,0:T(8,128)(2,1)S(1)} %multiply_convert_fusion), channel_id=1, replica_groups=mesh['center'=8,'expert'=4] {'center'}, dimensions={0}, use_global_device_ids=true | all-gather | bytes 294912 | tf_op jit(solution)/shard_map/all_gather | solution.py:285
  372.6 2.8 fusion.1
  375.3 13.2 %pmin.7 = f32[64]{0:T(128)S(1)} all-reduce(f32[64]{0:T(128)S(1)} %fusion.1), channel_id=1, replica_groups=mesh['center'=8,'expert'=4] {'center'}, use_global_device_ids=true, to_apply=%region_7.8 | all-reduce | flops 64 | bytes 512 | tf_op jit(solution)/shard_map/pmin | solution.py:293
  (169 shorter events, 45.2 us)
Async XLA Ops:
  3.1 18.0 %collective-permute-start.37 = (bf16[128,2048]{1,0:T(8,128)(2,1)S(1)}, bf16[128,2048]{1,0:T(8,128)(2,1)S(1)}, u32[]{:S(2)}, u32[]{:S(2)}) collective-permute-start(bf16[128,2048]{1,0:T(8,128)(2,1)S(1)} %fusion.3.refs_0_), channel_id=1, source_target_pairs={{0,3},{1,2},{2,1},{3,0},{4,7},{5,6},{6,5},{7,4},{8,11},{9,10},{10,... | collective-permute-start | bytes 1572872 | tf_op jit(solution)/shard_map/ppermute | solution.py:24
  8.2 44.8 %collective-permute-start.24 = (bf16[128,2048]{1,0:T(8,128)(2,1)S(1)}, bf16[128,2048]{1,0:T(8,128)(2,1)S(1)}, u32[]{:S(2)}, u32[]{:S(2)}) collective-permute-start(bf16[128,2048]{1,0:T(8,128)(2,1)S(1)} %fusion.3.refs_0_), channel_id=1, source_target_pairs={{0,2},{1,3},{2,0},{3,1},{4,6},{5,7},{6,4},{7,5},{8,10},{9,11},{10,... | collective-permute-start | bytes 1572872 | tf_op jit(solution)/shard_map/ppermute | solution.py:24
  8.2 46.3 %collective-permute-start.11 = (bf16[128,2048]{1,0:T(8,128)(2,1)S(1)}, bf16[128,2048]{1,0:T(8,128)(2,1)S(1)}, u32[]{:S(2)}, u32[]{:S(2)}) collective-permute-start(bf16[128,2048]{1,0:T(8,128)(2,1)S(1)} %fusion.3.refs_0_), channel_id=1, source_target_pairs={{0,1},{1,0},{2,3},{3,2},{4,5},{5,4},{6,7},{7,6},{8,9},{9,8},{10,11... | collective-permute-start | bytes 1572872 | tf_op jit(solution)/shard_map/ppermute | solution.py:24
  8.8 47.2 %collective-permute-start = (bf16[128,2048]{1,0:T(8,128)(2,1)S(1)}, bf16[128,2048]{1,0:T(8,128)(2,1)S(1)}, u32[]{:S(2)}, u32[]{:S(2)}) collective-permute-start(bf16[128,2048]{1,0:T(8,128)(2,1)S(1)} %fusion.3.refs_0_), channel_id=1, source_target_pairs={{0,8},{4,12},{8,0},{12,4},{16,24},{20,28},{24,16},{28,20},{1,9},{5... | collective-permute-start | bytes 1572872 | tf_op jit(solution)/shard_map/ppermute | solution.py:24
  10.5 46.3 %collective-permute-start.1 = (bf16[128,2048]{1,0:T(8,128)(2,1)S(1)}, bf16[128,2048]{1,0:T(8,128)(2,1)S(1)}, u32[]{:S(2)}, u32[]{:S(2)}) collective-permute-start(bf16[128,2048]{1,0:T(8,128)(2,1)S(1)} %fusion.3.refs_0_), channel_id=1, source_target_pairs={{0,16},{4,20},{8,24},{12,28},{16,0},{20,4},{24,8},{28,12},{1,17},{... | collective-permute-start | bytes 1572872 | tf_op jit(solution)/shard_map/ppermute | solution.py:24
  21.1 36.2 %collective-permute-start.3 = (bf16[128,2048]{1,0:T(8,128)(2,1)S(1)}, bf16[128,2048]{1,0:T(8,128)(2,1)S(1)}, u32[]{:S(2)}, u32[]{:S(2)}) collective-permute-start(bf16[128,2048]{1,0:T(8,128)(2,1)S(1)} %fusion.3.refs_0_), channel_id=1, source_target_pairs={{0,4},{4,0},{8,12},{12,8},{16,20},{20,16},{24,28},{28,24},{1,5},{5... | collective-permute-start | bytes 1572872 | tf_op jit(solution)/shard_map/ppermute | solution.py:24
  53.0 14.9 %collective-permute-start.38 = (bf16[128,2048]{1,0:T(8,128)(2,1)S(1)}, bf16[128,2048]{1,0:T(8,128)(2,1)S(1)}, u32[]{:S(2)}, u32[]{:S(2)}) collective-permute-start(bf16[128,2048]{1,0:T(8,128)(2,1)S(1)} %collective-permute-done.37.refs_0_), channel_id=1, source_target_pairs={{0,8},{4,12},{8,0},{12,4},{16,24},{20,28},{24,16},{28,20},{1,9},{5... | collective-permute-start | bytes 1572872 | tf_op jit(solution)/shard_map/ppermute | solution.py:24
  54.5 14.9 %collective-permute-start.39 = (bf16[128,2048]{1,0:T(8,128)(2,1)S(1)}, bf16[128,2048]{1,0:T(8,128)(2,1)S(1)}, u32[]{:S(2)}, u32[]{:S(2)}) collective-permute-start(bf16[128,2048]{1,0:T(8,128)(2,1)S(1)} %collective-permute-done.37.refs_0_), channel_id=1, source_target_pairs={{0,16},{4,20},{8,24},{12,28},{16,0},{20,4},{24,8},{28,12},{1,17},{... | collective-permute-start | bytes 1572872 | tf_op jit(solution)/shard_map/ppermute | solution.py:24
  56.0 14.1 %collective-permute-start.41 = (bf16[128,2048]{1,0:T(8,128)(2,1)S(1)}, bf16[128,2048]{1,0:T(8,128)(2,1)S(1)}, u32[]{:S(2)}, u32[]{:S(2)}) collective-permute-start(bf16[128,2048]{1,0:T(8,128)(2,1)S(1)} %collective-permute-done.37.refs_0_), channel_id=1, source_target_pairs={{0,4},{4,0},{8,12},{12,8},{16,20},{20,16},{24,28},{28,24},{1,5},{5... | collective-permute-start | bytes 1572872 | tf_op jit(solution)/shard_map/ppermute | solution.py:24
  56.8 22.4 %collective-permute-start.25 = (bf16[128,2048]{1,0:T(8,128)(2,1)S(1)}, bf16[128,2048]{1,0:T(8,128)(2,1)}, u32[]{:S(2)}, u32[]{:S(2)}) collective-permute-start(bf16[128,2048]{1,0:T(8,128)(2,1)S(1)} %collective-permute-done.24.refs_0_), channel_id=1, source_target_pairs={{0,8},{4,12},{8,0},{12,4},{16,24},{20,28},{24,16},{28,20},{1,9},{5... | collective-permute-start | bytes 1572872 | tf_op jit(solution)/shard_map/ppermute | solution.py:24
  58.1 22.5 %collective-permute-start.26 = (bf16[128,2048]{1,0:T(8,128)(2,1)S(1)}, bf16[128,2048]{1,0:T(8,128)(2,1)}, u32[]{:S(2)}, u32[]{:S(2)}) collective-permute-start(bf16[128,2048]{1,0:T(8,128)(2,1)S(1)} %collective-permute-done.24.refs_0_), channel_id=1, source_target_pairs={{0,16},{4,20},{8,24},{12,28},{16,0},{20,4},{24,8},{28,12},{1,17},{... | collective-permute-start | bytes 1572872 | tf_op jit(solution)/shard_map/ppermute | solution.py:24
  67.8 13.7 %collective-permute-start.28 = (bf16[128,2048]{1,0:T(8,128)(2,1)S(1)}, bf16[128,2048]{1,0:T(8,128)(2,1)S(1)}, u32[]{:S(2)}, u32[]{:S(2)}) collective-permute-start(bf16[128,2048]{1,0:T(8,128)(2,1)S(1)} %collective-permute-done.24.refs_0_), channel_id=1, source_target_pairs={{0,4},{4,0},{8,12},{12,8},{16,20},{20,16},{24,28},{28,24},{1,5},{5... | collective-permute-start | bytes 1572872 | tf_op jit(solution)/shard_map/ppermute | solution.py:24
  69.3 21.1 %collective-permute-start.12 = (bf16[128,2048]{1,0:T(8,128)(2,1)S(1)}, bf16[128,2048]{1,0:T(8,128)(2,1)}, u32[]{:S(2)}, u32[]{:S(2)}) collective-permute-start(bf16[128,2048]{1,0:T(8,128)(2,1)S(1)} %collective-permute-done.11.refs_0_), channel_id=1, source_target_pairs={{0,8},{4,12},{8,0},{12,4},{16,24},{20,28},{24,16},{28,20},{1,9},{5... | collective-permute-start | bytes 1572872 | tf_op jit(solution)/shard_map/ppermute | solution.py:24
  71.0 20.3 %collective-permute-start.13 = (bf16[128,2048]{1,0:T(8,128)(2,1)S(1)}, bf16[128,2048]{1,0:T(8,128)(2,1)}, u32[]{:S(2)}, u32[]{:S(2)}) collective-permute-start(bf16[128,2048]{1,0:T(8,128)(2,1)S(1)} %collective-permute-done.11.refs_0_), channel_id=1, source_target_pairs={{0,16},{4,20},{8,24},{12,28},{16,0},{20,4},{24,8},{28,12},{1,17},{... | collective-permute-start | bytes 1572872 | tf_op jit(solution)/shard_map/ppermute | solution.py:24
  79.2 13.6 %collective-permute-start.15 = (bf16[128,2048]{1,0:T(8,128)(2,1)S(1)}, bf16[128,2048]{1,0:T(8,128)(2,1)S(1)}, u32[]{:S(2)}, u32[]{:S(2)}) collective-permute-start(bf16[128,2048]{1,0:T(8,128)(2,1)S(1)} %collective-permute-done.11.refs_0_), channel_id=1, source_target_pairs={{0,4},{4,0},{8,12},{12,8},{16,20},{20,16},{24,28},{28,24},{1,5},{5... | collective-permute-start | bytes 1572872 | tf_op jit(solution)/shard_map/ppermute | solution.py:24
  80.7 19.1 %collective-permute-start.2 = (bf16[128,2048]{1,0:T(8,128)(2,1)S(1)}, bf16[128,2048]{1,0:T(8,128)(2,1)}, u32[]{:S(2)}, u32[]{:S(2)}) collective-permute-start(bf16[128,2048]{1,0:T(8,128)(2,1)S(1)} %collective-permute-done.1.refs_2_), channel_id=1, source_target_pairs={{0,8},{4,12},{8,0},{12,4},{16,24},{20,28},{24,16},{28,20},{1,9},{5... | collective-permute-start | bytes 1572872 | tf_op jit(solution)/shard_map/ppermute | solution.py:24
  82.3 18.3 %collective-permute-start.4 = (bf16[128,2048]{1,0:T(8,128)(2,1)S(1)}, bf16[128,2048]{1,0:T(8,128)(2,1)}, u32[]{:S(2)}, u32[]{:S(2)}) collective-permute-start(bf16[128,2048]{1,0:T(8,128)(2,1)S(1)} %collective-permute-done.refs_1_), channel_id=1, source_target_pairs={{0,4},{4,0},{8,12},{12,8},{16,20},{20,16},{24,28},{28,24},{1,5},{5... | collective-permute-start | bytes 1572872 | tf_op jit(solution)/shard_map/ppermute | solution.py:24
  91.2 14.4 %collective-permute-start.40 = (bf16[128,2048]{1,0:T(8,128)(2,1)S(1)}, bf16[128,2048]{1,0:T(8,128)(2,1)}, u32[]{:S(2)}, u32[]{:S(2)}) collective-permute-start(bf16[128,2048]{1,0:T(8,128)(2,1)S(1)} %collective-permute-done.38.refs_1_), channel_id=1, source_target_pairs={{0,16},{4,20},{8,24},{12,28},{16,0},{20,4},{24,8},{28,12},{1,17},{... | collective-permute-start | bytes 1572872 | tf_op jit(solution)/shard_map/ppermute | solution.py:24
  99.8 78.3 %collective-permute-start.43 = (bf16[128,2048]{1,0:T(8,128)(2,1)S(1)}, bf16[128,2048]{1,0:T(8,128)(2,1)}, u32[]{:S(2)}, u32[]{:S(2)}) collective-permute-start(bf16[128,2048]{1,0:T(8,128)(2,1)S(1)} %collective-permute-done.39.refs_2_), channel_id=1, source_target_pairs={{0,4},{4,0},{8,12},{12,8},{16,20},{20,16},{24,28},{28,24},{1,5},{5... | collective-permute-start | bytes 1572872 | tf_op jit(solution)/shard_map/ppermute | solution.py:24
  100.6 77.6 %collective-permute-start.27 = (bf16[128,2048]{1,0:T(8,128)(2,1)}, bf16[128,2048]{1,0:T(8,128)(2,1)}, u32[]{:S(2)}, u32[]{:S(2)}) collective-permute-start(bf16[128,2048]{1,0:T(8,128)(2,1)} %collective-permute-done.26.refs_2_), channel_id=1, source_target_pairs={{0,8},{4,12},{8,0},{12,4},{16,24},{20,28},{24,16},{28,20},{1,9},{5... | collective-permute-start | bytes 1572872 | tf_op jit(solution)/shard_map/ppermute | solution.py:24
  102.1 77.0 %collective-permute-start.6 = (bf16[128,2048]{1,0:T(8,128)(2,1)}, bf16[128,2048]{1,0:T(8,128)(2,1)S(1)}, u32[]{:S(2)}, u32[]{:S(2)}) collective-permute-start(bf16[128,2048]{1,0:T(8,128)(2,1)} %collective-permute-done.2.refs_3_), channel_id=1, source_target_pairs={{0,4},{4,0},{8,12},{12,8},{16,20},{20,16},{24,28},{28,24},{1,5},{5... | collective-permute-start | bytes 1572872 | tf_op jit(solution)/shard_map/ppermute | solution.py:24
  105.7 94.1 %collective-permute-start.29 = (bf16[128,2048]{1,0:T(8,128)(2,1)}, bf16[128,2048]{1,0:T(8,128)(2,1)}, u32[]{:S(2)}, u32[]{:S(2)}) collective-permute-start(bf16[128,2048]{1,0:T(8,128)(2,1)} %collective-permute-done.25.refs_1_), channel_id=1, source_target_pairs={{0,4},{4,0},{8,12},{12,8},{16,20},{20,16},{24,28},{28,24},{1,5},{5... | collective-permute-start | bytes 1572872 | tf_op jit(solution)/shard_map/ppermute | solution.py:24
  105.7 94.5 %collective-permute-start.44 = (bf16[128,2048]{1,0:T(8,128)(2,1)}, bf16[128,2048]{1,0:T(8,128)(2,1)}, u32[]{:S(2)}, u32[]{:S(2)}) collective-permute-start(bf16[128,2048]{1,0:T(8,128)(2,1)} %collective-permute-done.40.refs_3_), channel_id=1, source_target_pairs={{0,4},{4,0},{8,12},{12,8},{16,20},{20,16},{24,28},{28,24},{1,5},{5... | collective-permute-start | bytes 1572872 | tf_op jit(solution)/shard_map/ppermute | solution.py:24
  178.1 36.7 %collective-permute-start.30 = (bf16[128,2048]{1,0:T(8,128)(2,1)}, bf16[128,2048]{1,0:T(8,128)(2,1)S(1)}, u32[]{:S(2)}, u32[]{:S(2)}) collective-permute-start(bf16[128,2048]{1,0:T(8,128)(2,1)} %collective-permute-done.26.refs_2_), channel_id=1, source_target_pairs={{0,4},{4,0},{8,12},{12,8},{16,20},{20,16},{24,28},{28,24},{1,5},{5... | collective-permute-start | bytes 1572872 | tf_op jit(solution)/shard_map/ppermute | solution.py:24
  178.1 36.9 %collective-permute-start.14 = (bf16[128,2048]{1,0:T(8,128)(2,1)}, bf16[128,2048]{1,0:T(8,128)(2,1)}, u32[]{:S(2)}, u32[]{:S(2)}) collective-permute-start(bf16[128,2048]{1,0:T(8,128)(2,1)} %collective-permute-done.12.refs_1_), channel_id=1, source_target_pairs={{0,16},{4,20},{8,24},{12,28},{16,0},{20,4},{24,8},{28,12},{1,17},{... | collective-permute-start | bytes 1572872 | tf_op jit(solution)/shard_map/ppermute | solution.py:24
  179.9 35.4 %collective-permute-start.31 = (bf16[128,2048]{1,0:T(8,128)(2,1)}, bf16[128,2048]{1,0:T(8,128)(2,1)S(1)}, u32[]{:S(2)}, u32[]{:S(2)}) collective-permute-start(bf16[128,2048]{1,0:T(8,128)(2,1)} %collective-permute-done.27.refs_3_), channel_id=1, source_target_pairs={{0,4},{4,0},{8,12},{12,8},{16,20},{20,16},{24,28},{28,24},{1,5},{5... | collective-permute-start | bytes 1572872 | tf_op jit(solution)/shard_map/ppermute | solution.py:24
  199.8 30.5 %collective-permute-start.16 = (bf16[128,2048]{1,0:T(8,128)(2,1)}, bf16[128,2048]{1,0:T(8,128)(2,1)S(1)}, u32[]{:S(2)}, u32[]{:S(2)}) collective-permute-start(bf16[128,2048]{1,0:T(8,128)(2,1)} %collective-permute-done.12.refs_1_), channel_id=1, source_target_pairs={{0,4},{4,0},{8,12},{12,8},{16,20},{20,16},{24,28},{28,24},{1,5},{5... | collective-permute-start | bytes 1572872 | tf_op jit(solution)/shard_map/ppermute | solution.py:24
  200.2 51.2 %collective-permute-start.7 = (bf16[4,128,2048]{2,1,0:T(8,128)(2,1)}, bf16[4,128,2048]{2,1,0:T(8,128)(2,1)}, u32[]{:S(2)}, u32[]{:S(2)}) collective-permute-start(bf16[4,128,2048]{2,1,0:T(8,128)(2,1)} %get-tuple-element.11), channel_id=1, source_target_pairs={{0,4},{4,0},{8,12},{12,8},{16,20},{20,16},{24,28},{28,24},{1,5},{5... | collective-permute-start | bytes 6291464 | tf_op jit(solution)/shard_map/ppermute | solution.py:24
  214.8 16.6 %collective-permute-start.17 = (bf16[128,2048]{1,0:T(8,128)(2,1)}, bf16[128,2048]{1,0:T(8,128)(2,1)}, u32[]{:S(2)}, u32[]{:S(2)}) collective-permute-start(bf16[128,2048]{1,0:T(8,128)(2,1)} %collective-permute-done.13.refs_2_), channel_id=1, source_target_pairs={{0,4},{4,0},{8,12},{12,8},{16,20},{20,16},{24,28},{28,24},{1,5},{5... | collective-permute-start | bytes 1572872 | tf_op jit(solution)/shard_map/ppermute | solution.py:24
  215.1 16.3 %collective-permute-start.18 = (bf16[128,2048]{1,0:T(8,128)(2,1)}, bf16[128,2048]{1,0:T(8,128)(2,1)}, u32[]{:S(2)}, u32[]{:S(2)}) collective-permute-start(bf16[128,2048]{1,0:T(8,128)(2,1)} %collective-permute-done.14.refs_3_), channel_id=1, source_target_pairs={{0,4},{4,0},{8,12},{12,8},{16,20},{20,16},{24,28},{28,24},{1,5},{5... | collective-permute-start | bytes 1572872 | tf_op jit(solution)/shard_map/ppermute | solution.py:24
  215.3 40.0 %collective-permute-start.45 = (bf16[4,128,2048]{2,1,0:T(8,128)(2,1)}, bf16[4,128,2048]{2,1,0:T(8,128)(2,1)}, u32[]{:S(2)}, u32[]{:S(2)}) collective-permute-start(bf16[4,128,2048]{2,1,0:T(8,128)(2,1)} %get-tuple-element.17), channel_id=1, source_target_pairs={{0,4},{4,0},{8,12},{12,8},{16,20},{20,16},{24,28},{28,24},{1,5},{5... | collective-permute-start | bytes 6291464 | tf_op jit(solution)/shard_map/ppermute | solution.py:24
  231.1 27.0 %collective-permute-start.32 = (bf16[4,128,2048]{2,1,0:T(8,128)(2,1)}, bf16[4,128,2048]{2,1,0:T(8,128)(2,1)}, u32[]{:S(2)}, u32[]{:S(2)}) collective-permute-start(bf16[4,128,2048]{2,1,0:T(8,128)(2,1)} %get-tuple-element.15), channel_id=1, source_target_pairs={{0,4},{4,0},{8,12},{12,8},{16,20},{20,16},{24,28},{28,24},{1,5},{5... | collective-permute-start | bytes 6291464 | tf_op jit(solution)/shard_map/ppermute | solution.py:24
  251.1 18.2 %collective-permute-start.19 = (bf16[4,128,2048]{2,1,0:T(8,128)(2,1)}, bf16[4,128,2048]{2,1,0:T(8,128)(2,1)}, u32[]{:S(2)}, u32[]{:S(2)}) collective-permute-start(bf16[4,128,2048]{2,1,0:T(8,128)(2,1)} %get-tuple-element.13), channel_id=1, source_target_pairs={{0,4},{4,0},{8,12},{12,8},{16,20},{20,16},{24,28},{28,24},{1,5},{5... | collective-permute-start | bytes 6291464 | tf_op jit(solution)/shard_map/ppermute | solution.py:24
  253.2 14.8 %collective-permute-start.9 = (bf16[128,2048]{1,0:T(8,128)(2,1)S(1)}, bf16[128,2048]{1,0:T(8,128)(2,1)S(1)}, u32[]{:S(2)}, u32[]{:S(2)}) collective-permute-start(bf16[128,2048]{1,0:T(8,128)(2,1)S(1)} %get-tuple-element.21), channel_id=1, source_target_pairs={{0,8},{4,12},{8,0},{12,4},{16,24},{20,28},{24,16},{28,20},{1,9},{5... | collective-permute-start | bytes 1572872 | tf_op jit(solution)/shard_map/ppermute | solution.py:24
  253.2 75.4 %collective-permute-start.8 = (bf16[128,2048]{1,0:T(8,128)(2,1)S(1)}, bf16[128,2048]{1,0:T(8,128)(2,1)S(1)}, u32[]{:S(2)}, u32[]{:S(2)}) collective-permute-start(bf16[128,2048]{1,0:T(8,128)(2,1)S(1)} %get-tuple-element.20), channel_id=1, source_target_pairs={{0,8},{4,12},{8,0},{12,4},{16,24},{20,28},{24,16},{28,20},{1,9},{5... | collective-permute-start | bytes 1572872 | tf_op jit(solution)/shard_map/ppermute | solution.py:24
  256.8 39.8 %collective-permute-start.48 = (bf16[128,2048]{1,0:T(8,128)(2,1)S(1)}, bf16[128,2048]{1,0:T(8,128)(2,1)S(1)}, u32[]{:S(2)}, u32[]{:S(2)}) collective-permute-start(bf16[128,2048]{1,0:T(8,128)(2,1)S(1)} %get-tuple-element.27), channel_id=1, source_target_pairs={{0,16},{4,20},{8,24},{12,28},{16,0},{20,4},{24,8},{28,12},{1,17},{... | collective-permute-start | bytes 1572872 | tf_op jit(solution)/shard_map/ppermute | solution.py:24
  258.1 23.5 %collective-permute-start.46 = (bf16[128,2048]{1,0:T(8,128)(2,1)S(1)}, bf16[128,2048]{1,0:T(8,128)(2,1)S(1)}, u32[]{:S(2)}, u32[]{:S(2)}) collective-permute-start(bf16[128,2048]{1,0:T(8,128)(2,1)S(1)} %get-tuple-element.26), channel_id=1, source_target_pairs={{0,16},{4,20},{8,24},{12,28},{16,0},{20,4},{24,8},{28,12},{1,17},{... | collective-permute-start | bytes 1572872 | tf_op jit(solution)/shard_map/ppermute | solution.py:24
  268.0 22.5 %collective-permute-start.34 = (bf16[128,2048]{1,0:T(8,128)(2,1)S(1)}, bf16[128,2048]{1,0:T(8,128)(2,1)S(1)}, u32[]{:S(2)}, u32[]{:S(2)}) collective-permute-start(bf16[128,2048]{1,0:T(8,128)(2,1)S(1)} %get-tuple-element.25), channel_id=1, source_target_pairs={{0,8},{4,12},{8,0},{12,4},{16,24},{20,28},{24,16},{28,20},{1,9},{5... | collective-permute-start | bytes 1572872 | tf_op jit(solution)/shard_map/ppermute | solution.py:24
  269.3 44.6 %collective-permute-start.33 = (bf16[128,2048]{1,0:T(8,128)(2,1)S(1)}, bf16[128,2048]{1,0:T(8,128)(2,1)S(1)}, u32[]{:S(2)}, u32[]{:S(2)}) collective-permute-start(bf16[128,2048]{1,0:T(8,128)(2,1)S(1)} %get-tuple-element.24), channel_id=1, source_target_pairs={{0,8},{4,12},{8,0},{12,4},{16,24},{20,28},{24,16},{28,20},{1,9},{5... | collective-permute-start | bytes 1572872 | tf_op jit(solution)/shard_map/ppermute | solution.py:24
  281.6 12.6 %collective-permute-start.20 = (bf16[128,2048]{1,0:T(8,128)(2,1)S(1)}, bf16[128,2048]{1,0:T(8,128)(2,1)S(1)}, u32[]{:S(2)}, u32[]{:S(2)}) collective-permute-start(bf16[128,2048]{1,0:T(8,128)(2,1)S(1)} %get-tuple-element.22), channel_id=1, source_target_pairs={{0,16},{4,20},{8,24},{12,28},{16,0},{20,4},{24,8},{28,12},{1,17},{... | collective-permute-start | bytes 1572872 | tf_op jit(solution)/shard_map/ppermute | solution.py:24
  290.5 21.7 %collective-permute-start.47 = (bf16[128,2048]{1,0:T(8,128)(2,1)S(1)}, bf16[128,2048]{1,0:T(8,128)(2,1)S(1)}, u32[]{:S(2)}, u32[]{:S(2)}) collective-permute-start(bf16[128,2048]{1,0:T(8,128)(2,1)S(1)} %fusion.4), channel_id=1, source_target_pairs={{0,8},{4,12},{8,0},{12,4},{16,24},{20,28},{24,16},{28,20},{1,9},{5... | collective-permute-start | bytes 1572872 | tf_op jit(solution)/shard_map/ppermute | solution.py:24
  294.2 20.9 %collective-permute-start.35 = (bf16[128,2048]{1,0:T(8,128)(2,1)S(1)}, bf16[128,2048]{1,0:T(8,128)(2,1)S(1)}, u32[]{:S(2)}, u32[]{:S(2)}) collective-permute-start(bf16[128,2048]{1,0:T(8,128)(2,1)S(1)} %fusion.7), channel_id=1, source_target_pairs={{0,16},{4,20},{8,24},{12,28},{16,0},{20,4},{24,8},{28,12},{1,17},{... | collective-permute-start | bytes 1572872 | tf_op jit(solution)/shard_map/ppermute | solution.py:24
  296.6 21.5 %collective-permute-start.22 = (bf16[128,2048]{1,0:T(8,128)(2,1)S(1)}, bf16[128,2048]{1,0:T(8,128)(2,1)S(1)}, u32[]{:S(2)}, u32[]{:S(2)}) collective-permute-start(bf16[128,2048]{1,0:T(8,128)(2,1)S(1)} %get-tuple-element.23), channel_id=1, source_target_pairs={{0,16},{4,20},{8,24},{12,28},{16,0},{20,4},{24,8},{28,12},{1,17},{... | collective-permute-start | bytes 1572872 | tf_op jit(solution)/shard_map/ppermute | solution.py:24
  312.2 13.2 %collective-permute-start.21 = (bf16[128,2048]{1,0:T(8,128)(2,1)S(1)}, bf16[128,2048]{1,0:T(8,128)(2,1)S(1)}, u32[]{:S(2)}, u32[]{:S(2)}) collective-permute-start(bf16[128,2048]{1,0:T(8,128)(2,1)S(1)} %fusion.10), channel_id=1, source_target_pairs={{0,8},{4,12},{8,0},{12,4},{16,24},{20,28},{24,16},{28,20},{1,9},{5... | collective-permute-start | bytes 1572872 | tf_op jit(solution)/shard_map/ppermute | solution.py:24
  313.9 14.7 %collective-permute-start.10 = (bf16[128,2048]{1,0:T(8,128)(2,1)S(1)}, bf16[128,2048]{1,0:T(8,128)(2,1)S(1)}, u32[]{:S(2)}, u32[]{:S(2)}) collective-permute-start(bf16[128,2048]{1,0:T(8,128)(2,1)S(1)} %fusion.13), channel_id=1, source_target_pairs={{0,16},{4,20},{8,24},{12,28},{16,0},{20,4},{24,8},{28,12},{1,17},{... | collective-permute-start | bytes 1572872 | tf_op jit(solution)/shard_map/ppermute | solution.py:24
  315.1 16.7 %collective-permute-start.49 = (bf16[128,2048]{1,0:T(8,128)(2,1)S(1)}, bf16[128,2048]{1,0:T(8,128)(2,1)S(1)}, u32[]{:S(2)}, u32[]{:S(2)}) collective-permute-start(bf16[128,2048]{1,0:T(8,128)(2,1)S(1)} %fusion.6), channel_id=1, source_target_pairs={{0,3},{1,2},{2,1},{3,0},{4,7},{5,6},{6,5},{7,4},{8,11},{9,10},{10,... | collective-permute-start | bytes 1572872 | tf_op jit(solution)/shard_map/ppermute | solution.py:24
  318.1 41.7 %collective-permute-start.36 = (bf16[128,2048]{1,0:T(8,128)(2,1)S(1)}, bf16[128,2048]{1,0:T(8,128)(2,1)S(1)}, u32[]{:S(2)}, u32[]{:S(2)}) collective-permute-start(bf16[128,2048]{1,0:T(8,128)(2,1)S(1)} %fusion.9), channel_id=1, source_target_pairs={{0,2},{1,3},{2,0},{3,1},{4,6},{5,7},{6,4},{7,5},{8,10},{9,11},{10,... | collective-permute-start | bytes 1572872 | tf_op jit(solution)/shard_map/ppermute | solution.py:24
  326.8 33.1 %collective-permute-start.23 = (bf16[128,2048]{1,0:T(8,128)(2,1)S(1)}, bf16[128,2048]{1,0:T(8,128)(2,1)S(1)}, u32[]{:S(2)}, u32[]{:S(2)}) collective-permute-start(bf16[128,2048]{1,0:T(8,128)(2,1)S(1)} %fusion.12), channel_id=1, source_target_pairs={{0,1},{1,0},{2,3},{3,2},{4,5},{5,4},{6,7},{7,6},{8,9},{9,8},{10,11... | collective-permute-start | bytes 1572872 | tf_op jit(solution)/shard_map/ppermute | solution.py:24
  (42 other events, 386.5 us)

commit v2 on v0

v2 whole, which is shorter than its diff:
```python
import functools

import jax
import jax.numpy as jnp
from jax import lax
from jax.experimental import pallas as pl
from jax.experimental.pallas import tpu as pltpu
from jax.sharding import PartitionSpec as P

DOC_DEV = 8
BOTH = ("center", "expert")
CORE, ALONG_X, ALONG_Y = 1, 2, 4
LANES = 128


def rms_normed(hidden_rows):
    values = hidden_rows.astype(jnp.float32)
    inverse_rms = lax.rsqrt(jnp.mean(values * values, axis=-1, keepdims=True) + 1e-06)
    return (values * inverse_rms).astype(jnp.bfloat16)


KERNEL = pltpu.CompilerParams(vmem_limit_bytes=24 * 1024 * 1024)
ANYWHERE = pl.BlockSpec(memory_space=pltpu.HBM)
IN_VMEM = pl.BlockSpec(memory_space=pltpu.VMEM)
BESIDE = pl.CostEstimate(flops=1000, bytes_accessed=1000, transcendentals=0)
IN_SMEM = pl.BlockSpec(memory_space=pltpu.SMEM)
BF16 = jnp.bfloat16


def gate_lanes(shape, expert, expert_count):
    lane = lax.broadcasted_iota(jnp.int32, shape, len(shape) - 1)
    return (
        (lane == expert) | (lane == expert + expert_count) | (lane == expert + 2 * expert_count)
    )


def pick_kernel(capacity, expert_count, who_ref, *refs):
    count = len(refs) - 9
    blocks = refs[:count]
    mine_hbm, other_hbm, choice_hbm, rows_in, mine, other, choice, in_sem, out_sem = refs[count:]
    tok_count = blocks[0].shape[0]
    model_width = blocks[0].shape[1] - LANES
    in_copies = [
        pltpu.make_async_copy(blocks[j], rows_in.at[j], in_sem.at[j]) for j in range(count)
    ]
    for copy in in_copies:
        copy.start()
    row = lax.broadcasted_iota(jnp.int32, (8, LANES), 0)
    asked = jnp.where(
        row == 0,
        gate_lanes((8, LANES), who_ref[0], expert_count).astype(jnp.float32),
        gate_lanes((8, LANES), who_ref[1], expert_count).astype(jnp.float32),
    ).astype(BF16)
    before = (
        lax.broadcasted_iota(jnp.int32, (tok_count, tok_count), 0)
        < lax.broadcasted_iota(jnp.int32, (tok_count, tok_count), 1)
    ).astype(jnp.float32).astype(BF16)
    slot_row = lax.broadcasted_iota(jnp.int32, (2 * capacity, tok_count), 0)
    first_half = slot_row < capacity
    slot_row = slot_row.astype(jnp.float32)
    out_copies = []
    for copy in in_copies:
        copy.wait()
    tails = rows_in[:, :, pl.ds(model_width, LANES)].reshape(count * tok_count, LANES)
    gates = lax.dot_general(
        asked, tails, (((1,), (1,)), ((), ())), preferred_element_type=jnp.float32
    )
    named = gates != 0.0
    ones = named.astype(jnp.float32).astype(BF16)
    for j in range(count):
        at = j * tok_count
        slot = jnp.dot(ones[:, at : at + tok_count], before, preferred_element_type=jnp.float32)
        slot = jnp.where(named[:, at : at + tok_count], slot, -1.0 - 2.0 * capacity)
        slot = jnp.where(first_half, slot[0:1, :], slot[1:2, :] + float(capacity))
        choice[j] = (slot == slot_row).astype(jnp.float32).astype(BF16)
    for j in range(count):
        picked = jnp.dot(choice[j], rows_in[j], preferred_element_type=jnp.float32).astype(BF16)
        here = pl.ds(j * capacity, capacity)
        mine[here, :] = picked[:capacity]
        other[here, :] = picked[capacity:]
        for at, (source, target) in enumerate(
            (
                (other.at[here], other_hbm.at[here]),
                (mine.at[here], mine_hbm.at[here]),
                (choice.at[j], choice_hbm.at[j]),
            )
        ):
            copy = pltpu.make_async_copy(source, target, out_sem.at[at, j])
            copy.start()
            out_copies.append(copy)
    for copy in out_copies:
        copy.wait()


def pick(capacity, expert_count, who, blocks):
    count, tok_count, row_width = len(blocks), *blocks[0].shape
    picked = (count * capacity, row_width)
    choice = (count, 2 * capacity, tok_count)
    return pl.pallas_call(
        functools.partial(pick_kernel, capacity, expert_count),
        out_shape=[jax.ShapeDtypeStruct(shape, BF16) for shape in (picked, picked, choice)],
        in_specs=[IN_SMEM] + [ANYWHERE] * count,
        out_specs=[ANYWHERE] * 3,
        scratch_shapes=[
            pltpu.VMEM((count, tok_count, row_width), BF16),
            pltpu.VMEM(picked, BF16),
            pltpu.VMEM(picked, BF16),
            pltpu.VMEM(choice, BF16),
            pltpu.SemaphoreType.DMA((count,)),
            pltpu.SemaphoreType.DMA((3, count)),
        ],
        compiler_params=KERNEL,
        cost_estimate=BESIDE,
        name="pick",
    )(who, *blocks)


def expert_kernel(expert_count, groups, who_ref, *refs):
    parts = refs[: 2 * groups]
    gate_up, down = refs[2 * groups : 2 * groups + 2]
    outs = refs[2 * groups + 2 : 4 * groups + 2]
    rows, hidden, result, in_sem, out_sem = refs[4 * groups + 2 :]
    row_count = rows.shape[0]
    hidden_width, model_width = down.shape
    tile = 256
    hidden_tiles, model_tiles = hidden_width // tile, model_width // tile
    starts = [0]
    for part in parts:
        starts.append(starts[-1] + part.shape[0])
    in_copies = [
        pltpu.make_async_copy(part, rows.at[pl.ds(starts[i], part.shape[0])], in_sem.at[i])
        for i, part in enumerate(parts)
    ]
    for copy in in_copies:
        copy.start()
    for copy in in_copies:
        copy.wait()
    tail = rows[:, pl.ds(model_width, LANES)].astype(jnp.float32)
    gate_column = jnp.sum(
        jnp.where(gate_lanes((row_count, LANES), who_ref[0], expert_count), tail, 0.0),
        axis=1,
        keepdims=True,
    )
    for step in range(hidden_tiles):
        at = step * tile
        values = rows[:, pl.ds(0, model_width)]
        gate = jnp.dot(values, gate_up[:, pl.ds(at, tile)], preferred_element_type=jnp.float32)
        up = jnp.dot(
            values,
            gate_up[:, pl.ds(at + hidden_width, tile)],
            preferred_element_type=jnp.float32,
        )
        hidden[:, pl.ds(at, tile)] = (gate / (1.0 + jnp.exp(-gate)) * up).astype(BF16)
    for step in range(model_tiles):
        at = step * tile
        product = jnp.dot(
            hidden[...], down[:, pl.ds(at, tile)], preferred_element_type=jnp.float32
        )
        result[:, pl.ds(at, tile)] = (product * gate_column).astype(BF16)
    out_copies = [
        pltpu.make_async_copy(result.at[pl.ds(starts[i], out.shape[0])], out, out_sem.at[i])
        for i, out in enumerate(outs)
    ]
    for copy in out_copies:
        copy.start()
    for copy in out_copies:
        copy.wait()


def expert_rows(expert_count, who, parts, weights_gu, weights_down):
    row_width = parts[0].shape[1]
    hidden_width, model_width = weights_down.shape
    rows = sum(part.shape[0] for part in parts)
    outs = [jax.ShapeDtypeStruct((part.shape[0], model_width), BF16) for part in parts]
    return pl.pallas_call(
        functools.partial(expert_kernel, expert_count, len(parts) // 2),
        out_shape=outs,
        in_specs=[IN_SMEM] + [ANYWHERE] * len(parts) + [IN_VMEM] * 2,
        out_specs=[ANYWHERE] * len(parts),
        scratch_shapes=[
            pltpu.VMEM((rows, row_width), BF16),
            pltpu.VMEM((rows, hidden_width), BF16),
            pltpu.VMEM((rows, model_width), BF16),
            pltpu.SemaphoreType.DMA((len(parts),)),
            pltpu.SemaphoreType.DMA((len(parts),)),
        ],
        compiler_params=KERNEL,
        cost_estimate=BESIDE,
        name="expert_rows",
    )(who, *parts, weights_gu, weights_down)


def put_kernel(choice_hbm, mine_hbm, other_hbm, *refs):
    count, rows_two, _ = choice_hbm.shape
    capacity = rows_two // 2
    outs = refs[:count]
    choice, rows, out, in_sem, out_sem = refs[count:]
    copies, out_copies = [], []
    for j in range(count):
        here = pl.ds(j * capacity, capacity)
        copies.append(
            [
                pltpu.make_async_copy(choice_hbm.at[j], choice.at[j], in_sem.at[0, j]),
                pltpu.make_async_copy(
                    mine_hbm.at[here], rows.at[j, pl.ds(0, capacity)], in_sem.at[1, j]
                ),
                pltpu.make_async_copy(
                    other_hbm.at[here], rows.at[j, pl.ds(capacity, capacity)], in_sem.at[2, j]
                ),
            ]
        )
        for copy in copies[-1]:
            copy.start()
    for j in range(count):
        for copy in copies[j]:
            copy.wait()
        out[j] = lax.dot_general(
            choice[j], rows[j], (((0,), (0,)), ((), ())), preferred_element_type=jnp.float32
        ).astype(BF16)
        copy = pltpu.make_async_copy(out.at[j], outs[j], out_sem.at[j])
        copy.start()
        out_copies.append(copy)
    for copy in out_copies:
        copy.wait()


def put(choice, mine, other):
    count, rows_two, tok_count = choice.shape
    model_width = mine.shape[1]
    return pl.pallas_call(
        put_kernel,
        out_shape=[jax.ShapeDtypeStruct((tok_count, model_width), BF16)] * count,
        in_specs=[ANYWHERE] * 3,
        out_specs=[ANYWHERE] * count,
        scratch_shapes=[
            pltpu.VMEM(choice.shape, BF16),
            pltpu.VMEM((count, rows_two, model_width), BF16),
            pltpu.VMEM((count, tok_count, model_width), BF16),
            pltpu.SemaphoreType.DMA((3, count)),
            pltpu.SemaphoreType.DMA((count,)),
        ],
        compiler_params=KERNEL,
        cost_estimate=BESIDE,
        name="put",
    )(choice, mine, other)


def added(*terms):
    total = terms[0].astype(jnp.float32)
    for term in terms[1:]:
        total = total + term.astype(jnp.float32)
    return total


def in_three(values):
    first = values.astype(jnp.bfloat16)
    rest = values - first.astype(jnp.float32)
    second = rest.astype(jnp.bfloat16)
    third = (rest - second.astype(jnp.float32)).astype(jnp.bfloat16)
    return [first, second, third]


SWAP_X = ("center", tuple((i, i ^ ALONG_X) for i in range(8)))
SWAP_Y = ("center", tuple((i, i ^ ALONG_Y) for i in range(8)))
SWAP_CORE = ("center", tuple((i, i ^ CORE) for i in range(8)))
SWAP_Z = ("expert", ((0, 1), (1, 0), (2, 3), (3, 2)))
MIDDLE = ("expert", ((1, 2), (2, 1)))
OUTWARD = ("expert", ((1, 0), (2, 3)))
INWARD = ("expert", ((0, 1), (3, 2)))


def at_once(*sends, behind=()):
    values = [value for _, value in sends]
    if len(behind) > 0:
        held = lax.optimization_barrier((tuple(values), tuple(behind)))
        values = held[0]
    return [lax.ppermute(value, way[0], way[1]) for (way, _), value in zip(sends, values)]


def gathered_layer(rows, who, weights_gu, weights_down, capacity, expert_count, beside):
    def picked(*blocks):
        return pick(capacity, expert_count, who, blocks)

    def crossed(values):
        return at_once((SWAP_CORE, values))[0]

    def worked(*groups):
        parts = [part for mine, other, _ in groups for part in (mine, other)]
        done = expert_rows(expert_count, who, parts, weights_gu, weights_down)
        return [(groups[i][2], done[2 * i], done[2 * i + 1]) for i in range(len(groups))]

    b0 = rows
    bx0, by0, b1, c2 = at_once((SWAP_X, b0), (SWAP_Y, b0), (SWAP_Z, b0), (MIDDLE, b0))
    d0, by1, o2, c3 = at_once(
        (SWAP_X, by0), (SWAP_Y, b1), (OUTWARD, c2), (MIDDLE, b1),
        behind=(bx0, by0, b1, c2),
    )
    mine, other, choice = picked(b0, bx0, by0, b1)
    first = (mine, crossed(other), choice)
    b2 = c2 + o2
    bx2, by2, o3 = at_once(
        (SWAP_X, b2), (SWAP_Y, b2), (OUTWARD, c3), behind=(d0, by1, c3, mine, beside)
    )
    mine, other, choice = picked(d0, by1, b2)
    second = (mine, crossed(other), choice)
    b3 = c3 + o3
    bx3, by3, bx1 = at_once(
        (SWAP_X, b3), (SWAP_Y, b3), (SWAP_Z, bx0), behind=(bx2, by2, mine)
    )
    mine, other, choice = picked(bx2, by2, b3)
    third = (mine, crossed(other), choice)
    d2, d3, d1 = at_once(
        (SWAP_X, by2), (SWAP_Y, bx3), (SWAP_Z, d0), behind=(bx3, by3, bx1, mine)
    )
    mine, other, choice = picked(bx3, by3, bx1)
    fourth = (mine, crossed(other), choice)
    first, second = worked(first, second)
    held = lax.optimization_barrier((d1, d2, d3, mine, first[1]))
    mine, other, choice = picked(*held[:3])
    last = (mine, crossed(other), choice)
    (last,) = worked(last)
    last = (last[0], last[1], crossed(last[2]))
    g5 = put(*last)
    rx_y2, ry_x3, rz_d0 = at_once((SWAP_X, g5[1]), (SWAP_Y, g5[2]), (SWAP_Z, g5[0]))
    fourth = (lax.optimization_barrier((fourth[0], last[1]))[0], *fourth[1:])
    (fourth,) = worked(fourth)
    g4 = put(fourth[0], fourth[1], crossed(fourth[2]))
    third = (lax.optimization_barrier((third[0], g4[0]))[0], *third[1:])
    (third,) = worked(third)
    g3 = put(third[0], third[1], crossed(third[2]))
    g2 = put(second[0], second[1], crossed(second[2]))
    g1 = put(first[0], first[1], crossed(first[2]))
    sx3 = added(g4[0], ry_x3).astype(BF16)
    rx_b3, ry_b3, rz_x0 = at_once(
        (SWAP_X, sx3), (SWAP_Y, g4[1]), (SWAP_Z, g4[2]), behind=(rx_y2, rz_d0, g4[0])
    )
    sy2 = added(g3[1], rx_y2).astype(BF16)
    s3 = added(g3[2], rx_b3, ry_b3).astype(BF16)
    rx_b2, ry_b2, in_3 = at_once(
        (SWAP_X, g3[0]), (SWAP_Y, sy2), (INWARD, s3), behind=(rz_x0, g3[0])
    )
    sd0 = added(g2[0], rz_d0).astype(BF16)
    s2 = added(g2[2], rx_b2, ry_b2).astype(BF16)
    rx_y0, ry_b1, in_2, over_3 = at_once(
        (SWAP_X, sd0), (SWAP_Y, g2[1]), (INWARD, s2),
        (MIDDLE, added(s3, in_3).astype(BF16)), behind=(g2[0], rx_b2, ry_b2),
    )
    sx0 = added(g1[1], rz_x0).astype(BF16)
    sy0 = added(g1[2], rx_y0).astype(BF16)
    s1 = added(g1[3], ry_b1, over_3).astype(BF16)
    rx_b0, ry_b0, rz_b0, over_2 = at_once(
        (SWAP_X, sx0), (SWAP_Y, sy0), (SWAP_Z, s1),
        (MIDDLE, added(s2, in_2).astype(BF16)),
    )
    return added(g1[0], rx_b0, ry_b0, rz_b0, over_2)


def slot_table(chosen_ids, expert_count):
    chosen = (
        chosen_ids[:, :, None] == jnp.arange(expert_count, dtype=jnp.int32)[None, None, :]
    ).astype(jnp.int32)
    per_token = jnp.sum(chosen, axis=1)
    before = jnp.cumsum(per_token, axis=0) - per_token
    return jnp.sum(chosen * before[:, None, :], axis=2)


def expert_ffn(rows_in, weights_gu, weights_down):
    model_width = rows_in.shape[-1]
    flat_rows = rows_in.reshape(-1, model_width)
    hidden_width = weights_down.shape[0]
    gate_and_up = jnp.dot(flat_rows, weights_gu, preferred_element_type=jnp.float32)
    hidden = (jax.nn.silu(gate_and_up[:, :hidden_width]) * gate_and_up[:, hidden_width:]).astype(
        jnp.bfloat16
    )
    result = jnp.dot(hidden, weights_down, preferred_element_type=jnp.float32).astype(jnp.bfloat16)
    return result.reshape(rows_in.shape)


def exchanged_layer(normed, expert_ids, gate_norm, weights_gu, weights_down, capacity):
    tok_count, top_count = expert_ids.shape
    model_width = normed.shape[1]
    expert_count = lax.axis_size("center") * lax.axis_size("expert")
    position = slot_table(expert_ids, expert_count)
    target = (expert_ids * capacity + position).reshape(-1)
    repeated = jnp.broadcast_to(normed[:, None, :], (tok_count, top_count, model_width)).reshape(
        -1, model_width
    )
    send_buffer = (
        jnp.zeros((expert_count * capacity, model_width), jnp.bfloat16).at[target].set(repeated)
    )
    send_buffer = send_buffer.reshape(expert_count, capacity, model_width)
    computed = expert_ffn(
        lax.all_to_all(send_buffer, BOTH, split_axis=0, concat_axis=0, tiled=True),
        weights_gu,
        weights_down,
    )
    returned = lax.all_to_all(computed, BOTH, split_axis=0, concat_axis=0, tiled=True)
    returned = returned.reshape(expert_count * capacity, model_width)
    gathered = returned[target].reshape(tok_count, top_count, model_width)
    return jnp.sum(gathered.astype(jnp.float32) * gate_norm[:, :, None], axis=1)


def local(tokens, doc_ids, expert_ids, gate_raw, gate_up, down, bank):
    center_count = lax.axis_size("center")
    expert_axis = lax.axis_size("expert")
    expert_count = center_count * expert_axis
    tok_count, top_count = expert_ids.shape
    capacity = min(tok_count, 2 * tok_count * top_count // expert_count)
    normed = rms_normed(tokens)
    gate_norm = gate_raw / jnp.sum(gate_raw, axis=1, keepdims=True)
    weights_gu = gate_up[0]
    weights_down = down[0]
    bank_values = bank.astype(jnp.float32)
    bank_norms = jnp.sum(bank_values * bank_values, axis=1)
    if center_count == 8 and expert_axis == 4:
        named = expert_ids[:, :, None] == jnp.arange(expert_count, dtype=jnp.int32)[None, None, :]
        gate_table = jnp.sum(jnp.where(named, gate_norm[:, :, None], 0.0), axis=1)
        unused = jnp.zeros((tok_count, LANES - 3 * expert_count), jnp.bfloat16)
        rows = jnp.concatenate([normed, *in_three(gate_table), unused], axis=1)
        center_at, expert_at = lax.axis_index("center"), lax.axis_index("expert")
        who = jnp.stack(
            [center_at * expert_axis + expert_at, (center_at ^ CORE) * expert_axis + expert_at]
        ).astype(jnp.int32)
        combined = gathered_layer(
            rows, who, weights_gu, weights_down, capacity, expert_count, bank_norms
        )
    else:
        combined = exchanged_layer(
            normed, expert_ids, gate_norm, weights_gu, weights_down, capacity
        )
    layer_out = combined.astype(jnp.bfloat16)
    member = (jnp.arange(DOC_DEV, dtype=jnp.int32)[:, None] == doc_ids[0][None, :]).astype(
        jnp.float32
    )
    summed = jnp.dot(
        member, combined, precision=lax.Precision.HIGHEST, preferred_element_type=jnp.float32
    )
    pooled = (summed * lax.rsqrt(jnp.sum(summed * summed, axis=1, keepdims=True) + 1e-06)).astype(
        jnp.bfloat16
    )
    shard_part = lax.all_gather(pooled, "center", axis=0, tiled=True)
    doc_values = shard_part.astype(jnp.float32)
    doc_norms = jnp.sum(doc_values * doc_values, axis=1)
    products = lax.dot_general(
        shard_part, bank, (((1,), (1,)), ((), ())), preferred_element_type=jnp.float32
    )
    distance = doc_norms[:, None] + bank_norms[None, :] - 2.0 * products
    nearest = jnp.min(distance, axis=1)
    if center_count == 8 and expert_axis == 4:
        for way in (SWAP_Y, SWAP_X, SWAP_CORE):
            nearest = jnp.minimum(nearest, at_once((way, nearest))[0])
    else:
        nearest = lax.pmin(nearest, "center")
    own_scores = lax.dynamic_slice_in_dim(nearest, lax.axis_index("center") * DOC_DEV, DOC_DEV)
    return (layer_out, own_scores)


def solution(mesh):
    return jax.shard_map(
        local,
        mesh=mesh,
        in_specs=(
            P(BOTH, None),
            P(BOTH, None),
            P(BOTH, None),
            P(BOTH, None),
            P(BOTH, None, None),
            P(BOTH, None, None),
            P("center", None),
        ),
        out_specs=(P(BOTH, None), P(BOTH)),
        check_vma=False,
    )
```

time: 473 us -> 221 us (0.47)
  blocking collectives: 212 us -> 8.4 us
  waiting for transfers between devices: 176 us -> 92.9 us
  starting transfers between devices: 4.81 us -> 52.3 us
  Pallas kernels: 0 us -> 45.2 us
  matrix products: 31.4 us -> 3.62 us
  local copies, waits for them, and re-layouts: 26 us -> 1.13 us
  other arithmetic: 18.4 us -> 13.1 us
    all_to_all x1 -> x0, blocking collectives: 190 us -> none  [local(): lax.all_to_all(send_buffer, ('center', 'expert'), split_axis=0, concat_ax...]
    all_to_all x1 -> x0, waiting for transfers between devices: 176 us -> none  [local(): lax.all_to_all(computed, ('center', 'expert'), split_axis=0, concat_axis=...]
    ppermute x0 -> x47, waiting for transfers between devices: none -> 92.9 us  [at_once(): lax.ppermute(value, way[0], way[1])]
    ppermute x0 -> x47, starting transfers between devices: none -> 52.3 us  [at_once(): lax.ppermute(value, way[0], way[1])]
    pallas_call x0 -> x14, Pallas kernels: none -> 45.2 us  [the longest x4 24.6 us: expert_rows(): pl.pallas_call(functools.partial(expert_kernel, expert_count, len(parts)...]
    dot_general x2 -> x0, matrix products: 24.7 us -> none  [the longest x1 15.8 us: expert_ffn(): jnp.dot(flat_rows, weights_gu, preferred_element_type=jnp.float32)]
    gather x1 -> x0, local copies, waits for them, and re-layouts: 13.3 us -> none  [local(): gathered = returned[target].reshape(tok_count, top_count, model_width)]
    pmin x1 -> x0, blocking collectives: 13.2 us -> none  [local(): merged = lax.pmin(nearest, 'center')]
  transfers between devices with their start and end apart: 1 -> 47, of which waited for: 1 -> 25; matrix products, arithmetic and copies ran while one was open for 1% -> 4% of each run, Pallas kernels for 0% -> 20%
where the time goes in v2:
time: 221 us; the launch traced here: 218 us
  waiting for transfers between devices  92.9 us (42%)
  starting transfers between devices  52.3 us (24%)
  Pallas kernels  45.2 us (20%)
  other arithmetic  13.1 us (6%)
  blocking collectives  8.4 us (4%)
  matrix products  3.62 us (2%)
    ppermute x47, waiting for transfers between devices, at_once(): lax.ppermute(value, way[0], way[1])  92.9 us
    ppermute x47, starting transfers between devices, at_once(): lax.ppermute(value, way[0], way[1])  52.3 us
    pallas_call x4, Pallas kernels, expert_rows(): pl.pallas_call(functools.partial(expert_kernel, expert_count, len(parts)...  24.6 us
    pallas_call x5, Pallas kernels, pick(): pl.pallas_call(functools.partial(pick_kernel, capacity, expert_count), ou...  12.7 us
    all_gather x1, blocking collectives, local(): shard_part = lax.all_gather(pooled, 'center', axis=0, tiled=True)  8.4 us
    pallas_call x5, Pallas kernels, put(): pl.pallas_call(put_kernel, out_shape=[jax.ShapeDtypeStruct((tok_count, mo...  7.87 us
    reduce_sum x1, other arithmetic, local(): bank_norms = jnp.sum(bank_values * bank_values, axis=1)  5.08 us
  transfers between devices with their start and end apart: 47, of which 25 were waited for; matrix products, arithmetic and copies ran while one was open for 4% of the time, Pallas kernels for 20%

profile of v2, /device:TPU:0, one launch (start us, length us, event | category | flops | bytes accessed | tf_op | source)
XLA Modules:
  0.0 217.8 jit_solution(3280102249304099747)
XLA Ops:
  6.5 5.9 %collective-permute-start.2 = (bf16[128,2176]{1,0:T(8,128)(2,1)S(1)}, bf16[128,2176]{1,0:T(8,128)(2,1)S(1)}, u32[]{:S(2)}, u32[]{:S(2)}) collective-permute-start(bf16[128,2176]{1,0:T(8,128)(2,1)S(1)} %concatenate.3.refs_0_), channel_id=1, source_target_pairs={{0,1},{1,0},{2,3},{3,2},{4,5},{5,4},{6,7},{7,6},{8,9},{9,8},{10,11... | collective-permute-start | bytes 1671176 | tf_op jit(solution)/shard_map/ppermute | solution.py:277
  12.3 1.5 collective-permute-start.1
  13.9 1.5 collective-permute-start
  15.4 9.3 %collective-permute-done.2.refs_3_ = bf16[128,2176]{1,0:T(8,128)(2,1)S(1)} collective-permute-done((bf16[128,2176]{1,0:T(8,128)(2,1)S(1)}, bf16[128,2176]{1,0:T(8,128)(2,1)S(1)}, u32[]{:S(2)}, u32[]{:S(2)}) %collective-permute-start.2) | collective-permute-done | bytes 557088 | tf_op jit(solution)/shard_map/ppermute | solution.py:277
  27.4 1.5 collective-permute-start.5
  31.4 5.1 %multiply_reduce_fusion = f32[2048]{0:T(1024)S(1)} fusion(bf16[2048,2048]{1,0:T(8,128)(2,1)} %param.13), kind=kLoop, calls=%fused_computation | loop fusion | flops 12580864 | bytes 8396800 | tf_op jit(solution)/shard_map/reduce_sum | solution.py:414
  36.5 3.0 %pick.5 = (bf16[256,2176]{1,0:T(8,128)(2,1)S(1)}, bf16[256,2176]{1,0:T(8,128)(2,1)S(1)}, bf16[4,128,128]{2,1,0:T(8,128)(2,1)S(1)}) custom-call(s32[2]{0:T(128)S(1)} %pad_add_fusion.who_ref, bf16[128,2176]{1,0:T(8,128)(2,1)S(1)} %concatenate.3.refs_0_, bf16[128,2176]{1,0:T(8,128)(2,1)S(1)} %collective-permute-done.refs_1_, ...), custom_call_target="tpu_custom_call" | custom-call | flops 1000 | bytes 1000 | tf_op jit(solution)/shard_map/pick/pallas_call | solution.py:99
  39.4 3.9 %collective-permute-done.7 = bf16[128,2176]{1,0:T(8,128)(2,1)S(1)} collective-permute-done((bf16[128,2176]{1,0:T(8,128)(2,1)S(1)}, bf16[128,2176]{1,0:T(8,128)(2,1)S(1)}, u32[]{:S(2)}, u32[]{:S(2)}) %collective-permute-start.7) | collective-permute-done | bytes 557088 | tf_op jit(solution)/shard_map/ppermute | solution.py:277
  43.5 1.5 collective-permute-start.11
  47.1 2.4 %pick.6 = (bf16[192,2176]{1,0:T(8,128)(2,1)S(1)}, bf16[192,2176]{1,0:T(8,128)(2,1)S(1)}, bf16[3,128,128]{2,1,0:T(8,128)(2,1)S(1)}) custom-call(s32[2]{0:T(128)S(1)} %pad_add_fusion.who_ref, bf16[128,2176]{1,0:T(8,128)(2,1)S(1)} %collective-permute-done.5.refs_0_, bf16[128,2176]{1,0:T(8,128)(2,1)S(1)} %collective-permute-done.6.refs_1_, ...), custom_call_target="tpu_custom_call" | custom-call | flops 1000 | bytes 1000 | tf_op jit(solution)/shard_map/pick/pallas_call | solution.py:99
  49.5 8.0 %collective-permute-done.11 = bf16[128,2176]{1,0:T(8,128)(2,1)S(1)} collective-permute-done((bf16[128,2176]{1,0:T(8,128)(2,1)S(1)}, bf16[128,2176]{1,0:T(8,128)(2,1)S(1)}, u32[]{:S(2)}, u32[]{:S(2)}) %collective-permute-start.11) | collective-permute-done | bytes 557088 | tf_op jit(solution)/shard_map/ppermute | solution.py:277
  59.6 5.0 %collective-permute-start.16 = (bf16[128,2176]{1,0:T(8,128)(2,1)S(1)}, bf16[128,2176]{1,0:T(8,128)(2,1)S(1)}, u32[]{:S(2)}, u32[]{:S(2)}) collective-permute-start(bf16[128,2176]{1,0:T(8,128)(2,1)S(1)} %collective-permute-done.refs_1_), channel_id=1, source_target_pairs={{0,1},{1,0},{2,3},{3,2},{4,5},{5,4},{6,7},{7,6},{8,9},{9,8},{10,11... | collective-permute-start | bytes 1671176 | tf_op jit(solution)/shard_map/ppermute | solution.py:277
  64.6 2.4 %pick.8 = (bf16[192,2176]{1,0:T(8,128)(2,1)S(1)}, bf16[192,2176]{1,0:T(8,128)(2,1)S(1)}, bf16[3,128,128]{2,1,0:T(8,128)(2,1)S(1)}) custom-call(s32[2]{0:T(128)S(1)} %pad_add_fusion.who_ref, bf16[128,2176]{1,0:T(8,128)(2,1)S(1)} %collective-permute-done.12.refs_0_, bf16[128,2176]{1,0:T(8,128)(2,1)S(1)} %collective-permute-done.13.refs_1_, ...), custom_call_target="tpu_custom_call" | custom-call | flops 1000 | bytes 1000 | tf_op jit(solution)/shard_map/pick/pallas_call | solution.py:99
  68.4 6.8 %collective-permute-done.16.refs_2_ = bf16[128,2176]{1,0:T(8,128)(2,1)S(1)} collective-permute-done((bf16[128,2176]{1,0:T(8,128)(2,1)S(1)}, bf16[128,2176]{1,0:T(8,128)(2,1)S(1)}, u32[]{:S(2)}, u32[]{:S(2)}) %collective-permute-start.16) | collective-permute-done | bytes 557088 | tf_op jit(solution)/shard_map/ppermute | solution.py:277
  75.2 2.5 %collective-permute-start.17 = (bf16[128,2176]{1,0:T(8,128)(2,1)S(1)}, bf16[128,2176]{1,0:T(8,128)(2,1)S(1)}, u32[]{:S(2)}, u32[]{:S(2)}) collective-permute-start(bf16[128,2176]{1,0:T(8,128)(2,1)S(1)} %collective-permute-done.5.refs_0_), channel_id=1, source_target_pairs={{0,1},{1,0},{2,3},{3,2},{4,5},{5,4},{6,7},{7,6},{8,9},{9,8},{10,11... | collective-permute-start | bytes 1671176 | tf_op jit(solution)/shard_map/ppermute | solution.py:277
  78.5 10.1 %expert_rows.4 = (bf16[256,2048]{1,0:T(8,128)(2,1)S(1)}, bf16[256,2048]{1,0:T(8,128)(2,1)S(1)}, bf16[192,2048]{1,0:T(8,128)(2,1)S(1)}, bf16[192,2048]{1,0:T(8,128)(2,1)S(1)}) custom-call(s32[2]{0:T(128)S(1)} %pad_add_fusion.who_ref, bf16[256,2176]{1,0:T(8,128)(2,1)S(1)} %get-tuple-element.72.refs_0_, bf16[256,2176]{1,0:T(8,128)(2,1)S(1)} %collective-permute-done.3.refs_1_, ...), custom_call_target="tpu_custom_call" | custom-call | flops 1000 | bytes 1000 | tf_op jit(solution)/shard_map/expert_rows/pallas_call | solution.py:175
  88.6 2.4 %pick.7 = (bf16[192,2176]{1,0:T(8,128)(2,1)S(1)}, bf16[192,2176]{1,0:T(8,128)(2,1)S(1)}, bf16[3,128,128]{2,1,0:T(8,128)(2,1)S(1)}) custom-call(s32[2]{0:T(128)S(1)} %pad_add_fusion.who_ref, bf16[128,2176]{1,0:T(8,128)(2,1)S(1)} %collective-permute-done.14.refs_0_, bf16[128,2176]{1,0:T(8,128)(2,1)S(1)} %collective-permute-done.15.refs_1_, ...), custom_call_target="tpu_custom_call" | custom-call | flops 1000 | bytes 1000 | tf_op jit(solution)/shard_map/pick/pallas_call | solution.py:99
  91.1 2.4 %pick.9 = (bf16[192,2176]{1,0:T(8,128)(2,1)S(1)}, bf16[192,2176]{1,0:T(8,128)(2,1)S(1)}, bf16[3,128,128]{2,1,0:T(8,128)(2,1)S(1)}) custom-call(s32[2]{0:T(128)S(1)} %pad_add_fusion.who_ref, bf16[128,2176]{1,0:T(8,128)(2,1)S(1)} %collective-permute-done.17.refs_0_, bf16[128,2176]{1,0:T(8,128)(2,1)S(1)} %collective-permute-done.18.refs_1_, ...), custom_call_target="tpu_custom_call" | custom-call | flops 1000 | bytes 1000 | tf_op jit(solution)/shard_map/pick/pallas_call | solution.py:99
  94.1 1.8 collective-permute-done.20.refs_1_
  96.0 5.0 %expert_rows.5 = (bf16[192,2048]{1,0:T(8,128)(2,1)S(1)}, bf16[192,2048]{1,0:T(8,128)(2,1)S(1)}) custom-call(s32[2]{0:T(128)S(1)} %pad_add_fusion.who_ref, bf16[192,2176]{1,0:T(8,128)(2,1)S(1)} %get-tuple-element.99.refs_0_, bf16[192,2176]{1,0:T(8,128)(2,1)S(1)} %collective-permute-done.20.refs_1_, bf16[2048,1536]{1,0:T(8,128)(2,1)S(1)} %bitcast.10, ...), custom_call_target="tpu_custom_call" | custom-call | flops 1000 | bytes 1000 | tf_op jit(solution)/shard_map/expert_rows/pallas_call | solution.py:175
  101.5 4.8 %expert_rows.6 = (bf16[192,2048]{1,0:T(8,128)(2,1)S(1)}, bf16[192,2048]{1,0:T(8,128)(2,1)S(1)}) custom-call(s32[2]{0:T(128)S(1)} %pad_add_fusion.who_ref, bf16[192,2176]{1,0:T(8,128)(2,1)S(1)} %get-tuple-element.102.refs_0_, bf16[192,2176]{1,0:T(8,128)(2,1)S(1)} %collective-permute-done.21.refs_1_, bf16[2048,1536]{1,0:T(8,128)(2,1)S(1)} %bitcast.11, ...), custom_call_target="tpu_custom_call" | custom-call | flops 1000 | bytes 1000 | tf_op jit(solution)/shard_map/expert_rows/pallas_call | solution.py:175
  107.9 1.6 collective-permute-start.24
  111.0 4.8 %expert_rows.7 = (bf16[192,2048]{1,0:T(8,128)(2,1)S(1)}, bf16[192,2048]{1,0:T(8,128)(2,1)S(1)}) custom-call(s32[2]{0:T(128)S(1)} %pad_add_fusion.who_ref, bf16[192,2176]{1,0:T(8,128)(2,1)S(1)} %get-tuple-element.123.refs_0_, bf16[192,2176]{1,0:T(8,128)(2,1)S(1)} %collective-permute-done.30.refs_1_, bf16[2048,1536]{1,0:T(8,128)(2,1)S(1)} %bitcast.12, ...), custom_call_target="tpu_custom_call" | custom-call | flops 1000 | bytes 1000 | tf_op jit(solution)/shard_map/expert_rows/pallas_call | solution.py:175
  115.9 1.8 collective-permute-start.25
  117.6 4.6 %collective-permute-done.24 = bf16[128,2048]{1,0:T(8,128)(2,1)S(1)} collective-permute-done((bf16[128,2048]{1,0:T(8,128)(2,1)S(1)}, bf16[128,2048]{1,0:T(8,128)(2,1)S(1)}, u32[]{:S(2)}, u32[]{:S(2)}) %collective-permute-start.24) | collective-permute-done | bytes 524320 | tf_op jit(solution)/shard_map/ppermute | solution.py:277
  122.3 7.9 %collective-permute-done.25 = bf16[128,2048]{1,0:T(8,128)(2,1)S(1)} collective-permute-done((bf16[128,2048]{1,0:T(8,128)(2,1)S(1)}, bf16[128,2048]{1,0:T(8,128)(2,1)S(1)}, u32[]{:S(2)}, u32[]{:S(2)}) %collective-permute-start.25) | collective-permute-done | bytes 524320 | tf_op jit(solution)/shard_map/ppermute | solution.py:277
  134.4 10.4 %collective-permute-done.32 = bf16[128,2048]{1,0:T(8,128)(2,1)S(1)} collective-permute-done((bf16[128,2048]{1,0:T(8,128)(2,1)S(1)}, bf16[128,2048]{1,0:T(8,128)(2,1)S(1)}, u32[]{:S(2)}, u32[]{:S(2)}) %collective-permute-start.32) | collective-permute-done | bytes 524320 | tf_op jit(solution)/shard_map/ppermute | solution.py:277
  145.4 1.5 collective-permute-done.27
  146.9 2.2 %collective-permute-start.36 = (bf16[128,2048]{1,0:T(8,128)(2,1)S(1)}, bf16[128,2048]{1,0:T(8,128)(2,1)S(1)}, u32[]{:S(2)}, u32[]{:S(2)}) collective-permute-start(bf16[128,2048]{1,0:T(8,128)(2,1)S(1)} %add_convert_fusion.5), channel_id=1, source_target_pairs={{0,1},{3,2},{4,5},{7,6},{8,9},{11,10},{12,13},{15,14},{16,17},{19,... | collective-permute-start | bytes 1572872 | tf_op jit(solution)/shard_map/ppermute | solution.py:277
  149.2 1.7 put.8
  150.9 1.8 collective-permute-start.34
  154.2 5.9 %collective-permute-done.36 = bf16[128,2048]{1,0:T(8,128)(2,1)S(1)} collective-permute-done((bf16[128,2048]{1,0:T(8,128)(2,1)S(1)}, bf16[128,2048]{1,0:T(8,128)(2,1)S(1)}, u32[]{:S(2)}, u32[]{:S(2)}) %collective-permute-start.36) | collective-permute-done | bytes 524320 | tf_op jit(solution)/shard_map/ppermute | solution.py:277
  160.2 4.7 %collective-permute-done.34 = bf16[128,2048]{1,0:T(8,128)(2,1)S(1)} collective-permute-done((bf16[128,2048]{1,0:T(8,128)(2,1)S(1)}, bf16[128,2048]{1,0:T(8,128)(2,1)S(1)}, u32[]{:S(2)}, u32[]{:S(2)}) %collective-permute-start.34) | collective-permute-done | bytes 524320 | tf_op jit(solution)/shard_map/ppermute | solution.py:277
  167.1 1.9 put.5
  169.0 1.5 collective-permute-start.39
  171.3 1.7 collective-permute-start.28
  173.1 2.9 %collective-permute-start.42 = (bf16[128,2048]{1,0:T(8,128)(2,1)S(1)}, bf16[128,2048]{1,0:T(8,128)(2,1)S(1)}, u32[]{:S(2)}, u32[]{:S(2)}) collective-permute-start(bf16[128,2048]{1,0:T(8,128)(2,1)S(1)} %add_convert_fusion.4), channel_id=1, source_target_pairs={{0,1},{3,2},{4,5},{7,6},{8,9},{11,10},{12,13},{15,14},{16,17},{19,... | collective-permute-start | bytes 1572872 | tf_op jit(solution)/shard_map/ppermute | solution.py:277
  176.0 5.6 %collective-permute-done.37 = bf16[128,2048]{1,0:T(8,128)(2,1)S(1)} collective-permute-done((bf16[128,2048]{1,0:T(8,128)(2,1)S(1)}, bf16[128,2048]{1,0:T(8,128)(2,1)S(1)}, u32[]{:S(2)}, u32[]{:S(2)}) %collective-permute-start.37) | collective-permute-done | bytes 524320 | tf_op jit(solution)/shard_map/ppermute | solution.py:277
  181.7 1.5 collective-permute-start.38
  184.7 3.2 %collective-permute-done.42 = bf16[128,2048]{1,0:T(8,128)(2,1)S(1)} collective-permute-done((bf16[128,2048]{1,0:T(8,128)(2,1)S(1)}, bf16[128,2048]{1,0:T(8,128)(2,1)S(1)}, u32[]{:S(2)}, u32[]{:S(2)}) %collective-permute-start.42) | collective-permute-done | bytes 524320 | tf_op jit(solution)/shard_map/ppermute | solution.py:277
  188.7 2.2 %collective-permute-done.28 = bf16[128,2048]{1,0:T(8,128)(2,1)S(1)} collective-permute-done((bf16[128,2048]{1,0:T(8,128)(2,1)S(1)}, bf16[128,2048]{1,0:T(8,128)(2,1)S(1)}, u32[]{:S(2)}, u32[]{:S(2)}) %collective-permute-start.28) | collective-permute-done | bytes 524320 | tf_op jit(solution)/shard_map/ppermute | solution.py:277
  190.9 2.3 %collective-permute-done.38 = bf16[128,2048]{1,0:T(8,128)(2,1)S(1)} collective-permute-done((bf16[128,2048]{1,0:T(8,128)(2,1)S(1)}, bf16[128,2048]{1,0:T(8,128)(2,1)S(1)}, u32[]{:S(2)}, u32[]{:S(2)}) %collective-permute-start.38) | collective-permute-done | bytes 524320 | tf_op jit(solution)/shard_map/ppermute | solution.py:277
  193.2 3.3 %collective-permute-done.41 = bf16[128,2048]{1,0:T(8,128)(2,1)S(1)} collective-permute-done((bf16[128,2048]{1,0:T(8,128)(2,1)S(1)}, bf16[128,2048]{1,0:T(8,128)(2,1)S(1)}, u32[]{:S(2)}, u32[]{:S(2)}) %collective-permute-start.41) | collective-permute-done | bytes 524320 | tf_op jit(solution)/shard_map/ppermute | solution.py:277
  197.4 8.4 %all_gather.3 = bf16[64,2048]{1,0:T(8,128)(2,1)S(1)} all-gather(bf16[8,2048]{1,0:T(8,128)(2,1)S(1)} %multiply_convert_fusion), channel_id=1, replica_groups=mesh['center'=8,'expert'=4] {'center'}, dimensions={0}, use_global_device_ids=true | all-gather | bytes 294912 | tf_op jit(solution)/shard_map/all_gather | solution.py:441
  206.0 2.8 %fusion.1 = f32[64]{0:T(128)S(1)} fusion(bf16[64,2048]{1,0:T(8,128)(2,1)S(1)} %all_gather.3, bf16[2048,2048]{1,0:T(8,128)(2,1)S(1)} %bitcast.18, f32[2048]{0:T(1024)S(1)} %multiply_reduce_fusion, f32[64]{0:T(128)S(1)} %multiply_reduce_fusion.1), kind=kOutput, calls=%fused_computation.5 | convolution fusion | flops 537395136 | bytes 8659456 | tf_op jit(solution)/shard_map/dot_general | solution.py:444
  208.8 1.5 collective-permute-start.44
  210.3 2.1 collective-permute-done.44
  213.8 2.1 collective-permute-done.45
  (111 shorter events, 38.1 us)
Async XLA Ops:
  5.8 9.7 %collective-permute-start.4 = (bf16[128,2176]{1,0:T(8,128)(2,1)S(1)}, bf16[128,2176]{1,0:T(8,128)(2,1)S(1)}, u32[]{:S(2)}, u32[]{:S(2)}) collective-permute-start(bf16[128,2176]{1,0:T(8,128)(2,1)S(1)} %concatenate.3.refs_0_), channel_id=1, source_target_pairs={{1,2},{2,1},{5,6},{6,5},{9,10},{10,9},{13,14},{14,13},{17,18},{18,... | collective-permute-start | bytes 1671176 | tf_op jit(solution)/shard_map/ppermute | solution.py:277
  6.5 18.2 %collective-permute-start.2 = (bf16[128,2176]{1,0:T(8,128)(2,1)S(1)}, bf16[128,2176]{1,0:T(8,128)(2,1)S(1)}, u32[]{:S(2)}, u32[]{:S(2)}) collective-permute-start(bf16[128,2176]{1,0:T(8,128)(2,1)S(1)} %concatenate.3.refs_0_), channel_id=1, source_target_pairs={{0,1},{1,0},{2,3},{3,2},{4,5},{5,4},{6,7},{7,6},{8,9},{9,8},{10,11... | collective-permute-start | bytes 1671176 | tf_op jit(solution)/shard_map/ppermute | solution.py:277
  12.3 13.8 %collective-permute-start.1 = (bf16[128,2176]{1,0:T(8,128)(2,1)S(1)}, bf16[128,2176]{1,0:T(8,128)(2,1)S(1)}, u32[]{:S(2)}, u32[]{:S(2)}) collective-permute-start(bf16[128,2176]{1,0:T(8,128)(2,1)S(1)} %concatenate.3.refs_0_), channel_id=1, source_target_pairs={{0,16},{4,20},{8,24},{12,28},{16,0},{20,4},{24,8},{28,12},{1,17},{... | collective-permute-start | bytes 1671176 | tf_op jit(solution)/shard_map/ppermute | solution.py:277
  13.9 13.5 %collective-permute-start = (bf16[128,2176]{1,0:T(8,128)(2,1)S(1)}, bf16[128,2176]{1,0:T(8,128)(2,1)S(1)}, u32[]{:S(2)}, u32[]{:S(2)}) collective-permute-start(bf16[128,2176]{1,0:T(8,128)(2,1)S(1)} %concatenate.3.refs_0_), channel_id=1, source_target_pairs={{0,8},{4,12},{8,0},{12,4},{16,24},{20,28},{24,16},{28,20},{1,9},{5... | collective-permute-start | bytes 1671176 | tf_op jit(solution)/shard_map/ppermute | solution.py:277
  15.4 63.1 %copy-start = (bf16[1,768,2048]{2,1,0:T(8,128)(2,1)S(1)}, bf16[1,768,2048]{2,1,0:T(8,128)(2,1)}, u32[]{:S(2)}) copy-start(bf16[1,768,2048]{2,1,0:T(8,128)(2,1)} %param.12) | copy-start | bytes 9437188
  27.4 16.1 %collective-permute-start.5 = (bf16[128,2176]{1,0:T(8,128)(2,1)S(1)}, bf16[128,2176]{1,0:T(8,128)(2,1)S(1)}, u32[]{:S(2)}, u32[]{:S(2)}) collective-permute-start(bf16[128,2176]{1,0:T(8,128)(2,1)S(1)} %collective-permute-done.1.refs_2_), channel_id=1, source_target_pairs={{0,8},{4,12},{8,0},{12,4},{16,24},{20,28},{24,16},{28,20},{1,9},{5... | collective-permute-start | bytes 1671176 | tf_op jit(solution)/shard_map/ppermute | solution.py:277
  28.9 14.6 %collective-permute-start.6 = (bf16[128,2176]{1,0:T(8,128)(2,1)S(1)}, bf16[128,2176]{1,0:T(8,128)(2,1)S(1)}, u32[]{:S(2)}, u32[]{:S(2)}) collective-permute-start(bf16[128,2176]{1,0:T(8,128)(2,1)S(1)} %collective-permute-done.2.refs_3_), channel_id=1, source_target_pairs={{0,16},{4,20},{8,24},{12,28},{16,0},{20,4},{24,8},{28,12},{1,17},{... | collective-permute-start | bytes 1671176 | tf_op jit(solution)/shard_map/ppermute | solution.py:277
  29.4 14.0 %collective-permute-start.7 = (bf16[128,2176]{1,0:T(8,128)(2,1)S(1)}, bf16[128,2176]{1,0:T(8,128)(2,1)S(1)}, u32[]{:S(2)}, u32[]{:S(2)}) collective-permute-start(bf16[128,2176]{1,0:T(8,128)(2,1)S(1)} %collective-permute-done.4), channel_id=1, source_target_pairs={{1,0},{2,3},{5,4},{6,7},{9,8},{10,11},{13,12},{14,15},{17,16},{18,... | collective-permute-start | bytes 1671176 | tf_op jit(solution)/shard_map/ppermute | solution.py:277
  30.7 12.8 %collective-permute-start.10 = (bf16[128,2176]{1,0:T(8,128)(2,1)S(1)}, bf16[128,2176]{1,0:T(8,128)(2,1)S(1)}, u32[]{:S(2)}, u32[]{:S(2)}) collective-permute-start(bf16[128,2176]{1,0:T(8,128)(2,1)S(1)} %collective-permute-done.2.refs_3_), channel_id=1, source_target_pairs={{1,2},{2,1},{5,6},{6,5},{9,10},{10,9},{13,14},{14,13},{17,18},{18,... | collective-permute-start | bytes 1671176 | tf_op jit(solution)/shard_map/ppermute | solution.py:277
  43.5 13.9 %collective-permute-start.11 = (bf16[128,2176]{1,0:T(8,128)(2,1)S(1)}, bf16[128,2176]{1,0:T(8,128)(2,1)S(1)}, u32[]{:S(2)}, u32[]{:S(2)}) collective-permute-start(bf16[128,2176]{1,0:T(8,128)(2,1)S(1)} %collective-permute-done.10), channel_id=1, source_target_pairs={{1,0},{2,3},{5,4},{6,7},{9,8},{10,11},{13,12},{14,15},{17,16},{18,... | collective-permute-start | bytes 1671176 | tf_op jit(solution)/shard_map/ppermute | solution.py:277
  45.0 12.6 %collective-permute-start.12 = (bf16[128,2176]{1,0:T(8,128)(2,1)S(1)}, bf16[128,2176]{1,0:T(8,128)(2,1)S(1)}, u32[]{:S(2)}, u32[]{:S(2)}) collective-permute-start(bf16[128,2176]{1,0:T(8,128)(2,1)S(1)} %add.102.refs_2_), channel_id=1, source_target_pairs={{0,8},{4,12},{8,0},{12,4},{16,24},{20,28},{24,16},{28,20},{1,9},{5... | collective-permute-start | bytes 1671176 | tf_op jit(solution)/shard_map/ppermute | solution.py:277
  45.6 12.0 %collective-permute-start.13 = (bf16[128,2176]{1,0:T(8,128)(2,1)S(1)}, bf16[128,2176]{1,0:T(8,128)(2,1)S(1)}, u32[]{:S(2)}, u32[]{:S(2)}) collective-permute-start(bf16[128,2176]{1,0:T(8,128)(2,1)S(1)} %add.102.refs_2_), channel_id=1, source_target_pairs={{0,16},{4,20},{8,24},{12,28},{16,0},{20,4},{24,8},{28,12},{1,17},{... | collective-permute-start | bytes 1671176 | tf_op jit(solution)/shard_map/ppermute | solution.py:277
  47.1 31.4 %collective-permute-start.3 = (bf16[256,2176]{1,0:T(8,128)(2,1)S(1)}, bf16[256,2176]{1,0:T(8,128)(2,1)S(1)}, u32[]{:S(2)}, u32[]{:S(2)}) collective-permute-start(bf16[256,2176]{1,0:T(8,128)(2,1)S(1)} %get-tuple-element.73), channel_id=1, source_target_pairs={{0,4},{4,0},{8,12},{12,8},{16,20},{20,16},{24,28},{28,24},{1,5},{5... | collective-permute-start | bytes 3342344 | tf_op jit(solution)/shard_map/ppermute | solution.py:277
  57.6 10.6 %collective-permute-start.14 = (bf16[128,2176]{1,0:T(8,128)(2,1)S(1)}, bf16[128,2176]{1,0:T(8,128)(2,1)S(1)}, u32[]{:S(2)}, u32[]{:S(2)}) collective-permute-start(bf16[128,2176]{1,0:T(8,128)(2,1)S(1)} %add.103.refs_2_), channel_id=1, source_target_pairs={{0,8},{4,12},{8,0},{12,4},{16,24},{20,28},{24,16},{28,20},{1,9},{5... | collective-permute-start | bytes 1671176 | tf_op jit(solution)/shard_map/ppermute | solution.py:277
  58.2 10.2 %collective-permute-start.15 = (bf16[128,2176]{1,0:T(8,128)(2,1)S(1)}, bf16[128,2176]{1,0:T(8,128)(2,1)S(1)}, u32[]{:S(2)}, u32[]{:S(2)}) collective-permute-start(bf16[128,2176]{1,0:T(8,128)(2,1)S(1)} %add.103.refs_2_), channel_id=1, source_target_pairs={{0,16},{4,20},{8,24},{12,28},{16,0},{20,4},{24,8},{28,12},{1,17},{... | collective-permute-start | bytes 1671176 | tf_op jit(solution)/shard_map/ppermute | solution.py:277
  59.6 15.6 %collective-permute-start.16 = (bf16[128,2176]{1,0:T(8,128)(2,1)S(1)}, bf16[128,2176]{1,0:T(8,128)(2,1)S(1)}, u32[]{:S(2)}, u32[]{:S(2)}) collective-permute-start(bf16[128,2176]{1,0:T(8,128)(2,1)S(1)} %collective-permute-done.refs_1_), channel_id=1, source_target_pairs={{0,1},{1,0},{2,3},{3,2},{4,5},{5,4},{6,7},{7,6},{8,9},{9,8},{10,11... | collective-permute-start | bytes 1671176 | tf_op jit(solution)/shard_map/ppermute | solution.py:277
  64.6 13.9 %collective-permute-start.8 = (bf16[192,2176]{1,0:T(8,128)(2,1)S(1)}, bf16[192,2176]{1,0:T(8,128)(2,1)S(1)}, u32[]{:S(2)}, u32[]{:S(2)}) collective-permute-start(bf16[192,2176]{1,0:T(8,128)(2,1)S(1)} %get-tuple-element.78), channel_id=1, source_target_pairs={{0,4},{4,0},{8,12},{12,8},{16,20},{20,16},{24,28},{28,24},{1,5},{5... | collective-permute-start | bytes 2506760 | tf_op jit(solution)/shard_map/ppermute | solution.py:277
  75.2 15.9 %collective-permute-start.17 = (bf16[128,2176]{1,0:T(8,128)(2,1)S(1)}, bf16[128,2176]{1,0:T(8,128)(2,1)S(1)}, u32[]{:S(2)}, u32[]{:S(2)}) collective-permute-start(bf16[128,2176]{1,0:T(8,128)(2,1)S(1)} %collective-permute-done.5.refs_0_), channel_id=1, source_target_pairs={{0,1},{1,0},{2,3},{3,2},{4,5},{5,4},{6,7},{7,6},{8,9},{9,8},{10,11... | collective-permute-start | bytes 1671176 | tf_op jit(solution)/shard_map/ppermute | solution.py:277
  77.7 13.4 %collective-permute-start.18 = (bf16[128,2176]{1,0:T(8,128)(2,1)S(1)}, bf16[128,2176]{1,0:T(8,128)(2,1)S(1)}, u32[]{:S(2)}, u32[]{:S(2)}) collective-permute-start(bf16[128,2176]{1,0:T(8,128)(2,1)S(1)} %collective-permute-done.13.refs_1_), channel_id=1, source_target_pairs={{0,8},{4,12},{8,0},{12,4},{16,24},{20,28},{24,16},{28,20},{1,9},{5... | collective-permute-start | bytes 1671176 | tf_op jit(solution)/shard_map/ppermute | solution.py:277
  78.0 13.1 %collective-permute-start.19 = (bf16[128,2176]{1,0:T(8,128)(2,1)S(1)}, bf16[128,2176]{1,0:T(8,128)(2,1)S(1)}, u32[]{:S(2)}, u32[]{:S(2)}) collective-permute-start(bf16[128,2176]{1,0:T(8,128)(2,1)S(1)} %collective-permute-done.14.refs_0_), channel_id=1, source_target_pairs={{0,16},{4,20},{8,24},{12,28},{16,0},{20,4},{24,8},{28,12},{1,17},{... | collective-permute-start | bytes 1671176 | tf_op jit(solution)/shard_map/ppermute | solution.py:277
  93.6 2.4 %collective-permute-start.20 = (bf16[192,2176]{1,0:T(8,128)(2,1)S(1)}, bf16[192,2176]{1,0:T(8,128)(2,1)S(1)}, u32[]{:S(2)}, u32[]{:S(2)}) collective-permute-start(bf16[192,2176]{1,0:T(8,128)(2,1)S(1)} %get-tuple-element.100), channel_id=1, source_target_pairs={{0,4},{4,0},{8,12},{12,8},{16,20},{20,16},{24,28},{28,24},{1,5},{5... | collective-permute-start | bytes 2506760 | tf_op jit(solution)/shard_map/ppermute | solution.py:277
  93.6 7.9 %collective-permute-start.21 = (bf16[192,2176]{1,0:T(8,128)(2,1)S(1)}, bf16[192,2176]{1,0:T(8,128)(2,1)S(1)}, u32[]{:S(2)}, u32[]{:S(2)}) collective-permute-start(bf16[192,2176]{1,0:T(8,128)(2,1)S(1)} %get-tuple-element.103), channel_id=1, source_target_pairs={{0,4},{4,0},{8,12},{12,8},{16,20},{20,16},{24,28},{28,24},{1,5},{5... | collective-permute-start | bytes 2506760 | tf_op jit(solution)/shard_map/ppermute | solution.py:277
  101.0 5.5 %collective-permute-start.23 = (bf16[192,2048]{1,0:T(8,128)(2,1)S(1)}, bf16[192,2048]{1,0:T(8,128)(2,1)S(1)}, u32[]{:S(2)}, u32[]{:S(2)}) collective-permute-start(bf16[192,2048]{1,0:T(8,128)(2,1)S(1)} %get-tuple-element.108), channel_id=1, source_target_pairs={{0,4},{4,0},{8,12},{12,8},{16,20},{20,16},{24,28},{28,24},{1,5},{5... | collective-permute-start | bytes 2359304 | tf_op jit(solution)/shard_map/ppermute | solution.py:277
  101.2 9.8 %collective-permute-start.30 = (bf16[192,2176]{1,0:T(8,128)(2,1)S(1)}, bf16[192,2176]{1,0:T(8,128)(2,1)S(1)}, u32[]{:S(2)}, u32[]{:S(2)}) collective-permute-start(bf16[192,2176]{1,0:T(8,128)(2,1)S(1)} %get-tuple-element.124), channel_id=1, source_target_pairs={{0,4},{4,0},{8,12},{12,8},{16,20},{20,16},{24,28},{28,24},{1,5},{5... | collective-permute-start | bytes 2506760 | tf_op jit(solution)/shard_map/ppermute | solution.py:277
  106.3 3.2 %collective-permute-start.22 = (bf16[192,2048]{1,0:T(8,128)(2,1)S(1)}, bf16[192,2048]{1,0:T(8,128)(2,1)S(1)}, u32[]{:S(2)}, u32[]{:S(2)}) collective-permute-start(bf16[192,2048]{1,0:T(8,128)(2,1)S(1)} %get-tuple-element.105), channel_id=1, source_target_pairs={{0,4},{4,0},{8,12},{12,8},{16,20},{20,16},{24,28},{28,24},{1,5},{5... | collective-permute-start | bytes 2359304 | tf_op jit(solution)/shard_map/ppermute | solution.py:277
  107.9 14.3 %collective-permute-start.24 = (bf16[128,2048]{1,0:T(8,128)(2,1)S(1)}, bf16[128,2048]{1,0:T(8,128)(2,1)S(1)}, u32[]{:S(2)}, u32[]{:S(2)}) collective-permute-start(bf16[128,2048]{1,0:T(8,128)(2,1)S(1)} %get-tuple-element.109), channel_id=1, source_target_pairs={{0,16},{4,20},{8,24},{12,28},{16,0},{20,4},{24,8},{28,12},{1,17},{... | collective-permute-start | bytes 1572872 | tf_op jit(solution)/shard_map/ppermute | solution.py:277
  115.8 17.1 %collective-permute-start.31 = (bf16[192,2048]{1,0:T(8,128)(2,1)S(1)}, bf16[192,2048]{1,0:T(8,128)(2,1)S(1)}, u32[]{:S(2)}, u32[]{:S(2)}) collective-permute-start(bf16[192,2048]{1,0:T(8,128)(2,1)S(1)} %get-tuple-element.126), channel_id=1, source_target_pairs={{0,4},{4,0},{8,12},{12,8},{16,20},{20,16},{24,28},{28,24},{1,5},{5... | collective-permute-start | bytes 2359304 | tf_op jit(solution)/shard_map/ppermute | solution.py:277
  115.9 14.3 %collective-permute-start.25 = (bf16[128,2048]{1,0:T(8,128)(2,1)S(1)}, bf16[128,2048]{1,0:T(8,128)(2,1)S(1)}, u32[]{:S(2)}, u32[]{:S(2)}) collective-permute-start(bf16[128,2048]{1,0:T(8,128)(2,1)S(1)} %get-tuple-element.112), channel_id=1, source_target_pairs={{0,8},{4,12},{8,0},{12,4},{16,24},{20,28},{24,16},{28,20},{1,9},{5... | collective-permute-start | bytes 1572872 | tf_op jit(solution)/shard_map/ppermute | solution.py:277
  117.6 14.0 %collective-permute-start.26 = (bf16[128,2048]{1,0:T(8,128)(2,1)S(1)}, bf16[128,2048]{1,0:T(8,128)(2,1)S(1)}, u32[]{:S(2)}, u32[]{:S(2)}) collective-permute-start(bf16[128,2048]{1,0:T(8,128)(2,1)S(1)} %get-tuple-element.113), channel_id=1, source_target_pairs={{0,1},{1,0},{2,3},{3,2},{4,5},{5,4},{6,7},{7,6},{8,9},{9,8},{10,11... | collective-permute-start | bytes 1572872 | tf_op jit(solution)/shard_map/ppermute | solution.py:277
  131.6 13.2 %collective-permute-start.32 = (bf16[128,2048]{1,0:T(8,128)(2,1)S(1)}, bf16[128,2048]{1,0:T(8,128)(2,1)S(1)}, u32[]{:S(2)}, u32[]{:S(2)}) collective-permute-start(bf16[128,2048]{1,0:T(8,128)(2,1)S(1)} %add_convert_fusion.9), channel_id=1, source_target_pairs={{0,8},{4,12},{8,0},{12,4},{16,24},{20,28},{24,16},{28,20},{1,9},{5... | collective-permute-start | bytes 1572872 | tf_op jit(solution)/shard_map/ppermute | solution.py:277
  131.9 13.2 %collective-permute-start.33 = (bf16[128,2048]{1,0:T(8,128)(2,1)S(1)}, bf16[128,2048]{1,0:T(8,128)(2,1)S(1)}, u32[]{:S(2)}, u32[]{:S(2)}) collective-permute-start(bf16[128,2048]{1,0:T(8,128)(2,1)S(1)} %get-tuple-element.131), channel_id=1, source_target_pairs={{0,16},{4,20},{8,24},{12,28},{16,0},{20,4},{24,8},{28,12},{1,17},{... | collective-permute-start | bytes 1572872 | tf_op jit(solution)/shard_map/ppermute | solution.py:277
  132.5 16.6 %collective-permute-start.29 = (bf16[192,2048]{1,0:T(8,128)(2,1)S(1)}, bf16[192,2048]{1,0:T(8,128)(2,1)S(1)}, u32[]{:S(2)}, u32[]{:S(2)}) collective-permute-start(bf16[192,2048]{1,0:T(8,128)(2,1)S(1)} %get-tuple-element.118), channel_id=1, source_target_pairs={{0,4},{4,0},{8,12},{12,8},{16,20},{20,16},{24,28},{28,24},{1,5},{5... | collective-permute-start | bytes 2359304 | tf_op jit(solution)/shard_map/ppermute | solution.py:277
  132.5 14.3 %collective-permute-start.27 = (bf16[128,2048]{1,0:T(8,128)(2,1)S(1)}, bf16[128,2048]{1,0:T(8,128)(2,1)S(1)}, u32[]{:S(2)}, u32[]{:S(2)}) collective-permute-start(bf16[128,2048]{1,0:T(8,128)(2,1)S(1)} %get-tuple-element.114), channel_id=1, source_target_pairs={{0,1},{1,0},{2,3},{3,2},{4,5},{5,4},{6,7},{7,6},{8,9},{9,8},{10,11... | collective-permute-start | bytes 1572872 | tf_op jit(solution)/shard_map/ppermute | solution.py:277
  146.9 13.2 %collective-permute-start.36 = (bf16[128,2048]{1,0:T(8,128)(2,1)S(1)}, bf16[128,2048]{1,0:T(8,128)(2,1)S(1)}, u32[]{:S(2)}, u32[]{:S(2)}) collective-permute-start(bf16[128,2048]{1,0:T(8,128)(2,1)S(1)} %add_convert_fusion.5), channel_id=1, source_target_pairs={{0,1},{3,2},{4,5},{7,6},{8,9},{11,10},{12,13},{15,14},{16,17},{19,... | collective-permute-start | bytes 1572872 | tf_op jit(solution)/shard_map/ppermute | solution.py:277
  149.1 18.0 %collective-permute-start.9 = (bf16[256,2048]{1,0:T(8,128)(2,1)S(1)}, bf16[256,2048]{1,0:T(8,128)(2,1)S(1)}, u32[]{:S(2)}, u32[]{:S(2)}) collective-permute-start(bf16[256,2048]{1,0:T(8,128)(2,1)S(1)} %get-tuple-element.80), channel_id=1, source_target_pairs={{0,4},{4,0},{8,12},{12,8},{16,20},{20,16},{24,28},{28,24},{1,5},{5... | collective-permute-start | bytes 3145736 | tf_op jit(solution)/shard_map/ppermute | solution.py:277
  150.9 14.1 %collective-permute-start.34 = (bf16[128,2048]{1,0:T(8,128)(2,1)S(1)}, bf16[128,2048]{1,0:T(8,128)(2,1)S(1)}, u32[]{:S(2)}, u32[]{:S(2)}) collective-permute-start(bf16[128,2048]{1,0:T(8,128)(2,1)S(1)} %get-tuple-element.132), channel_id=1, source_target_pairs={{0,8},{4,12},{8,0},{12,4},{16,24},{20,28},{24,16},{28,20},{1,9},{5... | collective-permute-start | bytes 1572872 | tf_op jit(solution)/shard_map/ppermute | solution.py:277
  152.7 13.7 %collective-permute-start.35 = (bf16[128,2048]{1,0:T(8,128)(2,1)S(1)}, bf16[128,2048]{1,0:T(8,128)(2,1)S(1)}, u32[]{:S(2)}, u32[]{:S(2)}) collective-permute-start(bf16[128,2048]{1,0:T(8,128)(2,1)S(1)} %add_convert_fusion.6), channel_id=1, source_target_pairs={{0,16},{4,20},{8,24},{12,28},{16,0},{20,4},{24,8},{28,12},{1,17},{... | collective-permute-start | bytes 1572872 | tf_op jit(solution)/shard_map/ppermute | solution.py:277
  166.7 14.9 %collective-permute-start.37 = (bf16[128,2048]{1,0:T(8,128)(2,1)S(1)}, bf16[128,2048]{1,0:T(8,128)(2,1)S(1)}, u32[]{:S(2)}, u32[]{:S(2)}) collective-permute-start(bf16[128,2048]{1,0:T(8,128)(2,1)S(1)} %add_convert_fusion.7), channel_id=1, source_target_pairs={{0,8},{4,12},{8,0},{12,4},{16,24},{20,28},{24,16},{28,20},{1,9},{5... | collective-permute-start | bytes 1572872 | tf_op jit(solution)/shard_map/ppermute | solution.py:277
  169.0 14.2 %collective-permute-start.39 = (bf16[128,2048]{1,0:T(8,128)(2,1)S(1)}, bf16[128,2048]{1,0:T(8,128)(2,1)S(1)}, u32[]{:S(2)}, u32[]{:S(2)}) collective-permute-start(bf16[128,2048]{1,0:T(8,128)(2,1)S(1)} %get-tuple-element.137), channel_id=1, source_target_pairs={{0,16},{4,20},{8,24},{12,28},{16,0},{20,4},{24,8},{28,12},{1,17},{... | collective-permute-start | bytes 1572872 | tf_op jit(solution)/shard_map/ppermute | solution.py:277
  170.5 12.7 %collective-permute-start.40 = (bf16[128,2048]{1,0:T(8,128)(2,1)S(1)}, bf16[128,2048]{1,0:T(8,128)(2,1)S(1)}, u32[]{:S(2)}, u32[]{:S(2)}) collective-permute-start(bf16[128,2048]{1,0:T(8,128)(2,1)S(1)} %add_convert_fusion.3), channel_id=1, source_target_pairs={{1,2},{2,1},{5,6},{6,5},{9,10},{10,9},{13,14},{14,13},{17,18},{18,... | collective-permute-start | bytes 1572872 | tf_op jit(solution)/shard_map/ppermute | solution.py:277
  171.3 19.5 %collective-permute-start.28 = (bf16[128,2048]{1,0:T(8,128)(2,1)S(1)}, bf16[128,2048]{1,0:T(8,128)(2,1)S(1)}, u32[]{:S(2)}, u32[]{:S(2)}) collective-permute-start(bf16[128,2048]{1,0:T(8,128)(2,1)S(1)} %add_convert_fusion.8), channel_id=1, source_target_pairs={{0,8},{4,12},{8,0},{12,4},{16,24},{20,28},{24,16},{28,20},{1,9},{5... | collective-permute-start | bytes 1572872 | tf_op jit(solution)/shard_map/ppermute | solution.py:277
  173.1 14.8 %collective-permute-start.42 = (bf16[128,2048]{1,0:T(8,128)(2,1)S(1)}, bf16[128,2048]{1,0:T(8,128)(2,1)S(1)}, u32[]{:S(2)}, u32[]{:S(2)}) collective-permute-start(bf16[128,2048]{1,0:T(8,128)(2,1)S(1)} %add_convert_fusion.4), channel_id=1, source_target_pairs={{0,1},{3,2},{4,5},{7,6},{8,9},{11,10},{12,13},{15,14},{16,17},{19,... | collective-permute-start | bytes 1572872 | tf_op jit(solution)/shard_map/ppermute | solution.py:277
  181.7 11.4 %collective-permute-start.38 = (bf16[128,2048]{1,0:T(8,128)(2,1)S(1)}, bf16[128,2048]{1,0:T(8,128)(2,1)S(1)}, u32[]{:S(2)}, u32[]{:S(2)}) collective-permute-start(bf16[128,2048]{1,0:T(8,128)(2,1)S(1)} %add_convert_fusion.2), channel_id=1, source_target_pairs={{0,16},{4,20},{8,24},{12,28},{16,0},{20,4},{24,8},{28,12},{1,17},{... | collective-permute-start | bytes 1572872 | tf_op jit(solution)/shard_map/ppermute | solution.py:277
  183.5 13.0 %collective-permute-start.41 = (bf16[128,2048]{1,0:T(8,128)(2,1)S(1)}, bf16[128,2048]{1,0:T(8,128)(2,1)S(1)}, u32[]{:S(2)}, u32[]{:S(2)}) collective-permute-start(bf16[128,2048]{1,0:T(8,128)(2,1)S(1)} %add_convert_fusion.1), channel_id=1, source_target_pairs={{0,1},{1,0},{2,3},{3,2},{4,5},{5,4},{6,7},{7,6},{8,9},{9,8},{10,11... | collective-permute-start | bytes 1572872 | tf_op jit(solution)/shard_map/ppermute | solution.py:277
  188.0 8.5 %collective-permute-start.43 = (bf16[128,2048]{1,0:T(8,128)(2,1)S(1)}, bf16[128,2048]{1,0:T(8,128)(2,1)S(1)}, u32[]{:S(2)}, u32[]{:S(2)}) collective-permute-start(bf16[128,2048]{1,0:T(8,128)(2,1)S(1)} %add_convert_fusion), channel_id=1, source_target_pairs={{1,2},{2,1},{5,6},{6,5},{9,10},{10,9},{13,14},{14,13},{17,18},{18,... | collective-permute-start | bytes 1572872 | tf_op jit(solution)/shard_map/ppermute | solution.py:277
  208.8 3.6 %collective-permute-start.44 = (f32[64]{0:T(128)S(1)}, f32[64]{0:T(128)S(1)}, u32[]{:S(2)}, u32[]{:S(2)}) collective-permute-start(f32[64]{0:T(128)S(1)} %fusion.1), channel_id=1, source_target_pairs={{0,16},{4,20},{8,24},{12,28},{16,0},{20,4},{24,8},{28,12},{1,17},{... | collective-permute-start | bytes 776 | tf_op jit(solution)/shard_map/ppermute | solution.py:277
  212.4 3.5 %collective-permute-start.45 = (f32[64]{0:T(128)S(1)}, f32[64]{0:T(128)S(1)}, u32[]{:S(2)}, u32[]{:S(2)}) collective-permute-start(f32[64]{0:T(128)S(1)} %min.9), channel_id=1, source_target_pairs={{0,8},{4,12},{8,0},{12,4},{16,24},{20,28},{24,16},{28,20},{1,9},{5... | collective-permute-start | bytes 776 | tf_op jit(solution)/shard_map/ppermute | solution.py:277
  215.9 1.2 collective-permute-start.46
  (5 other events, 232.4 us)

commit v3 on v2

--- a/solution.py
+++ b/solution.py
@@ -245,6 +245,12 @@
     )(choice, mine, other)
 
 
+def normed_sum(summed):
+    return (summed * lax.rsqrt(jnp.sum(summed * summed, axis=1, keepdims=True) + 1e-06)).astype(
+        jnp.bfloat16
+    )
+
+
 def added(*terms):
     total = terms[0].astype(jnp.float32)
     for term in terms[1:]:
@@ -252,16 +258,98 @@
     return total
 
 
-def in_three(values):
-    first = values.astype(jnp.bfloat16)
-    rest = values - first.astype(jnp.float32)
-    second = rest.astype(jnp.bfloat16)
-    third = (rest - second.astype(jnp.float32)).astype(jnp.bfloat16)
-    return [first, second, third]
+def enter_kernel(expert_count, *refs):
+    sources, rows_ref, targets, sem = refs[:4], refs[4], refs[5:9], refs[9]
+    copies = [
+        pltpu.make_async_copy(source, target, sem.at[i])
+        for i, (source, target) in enumerate(zip(sources, targets))
+    ]
+    for copy in copies:
+        copy.start()
+    tokens_ref, ids_ref, gates_ref, docs_ref = targets
+    tok_count, model_width = tokens_ref.shape
+    for copy in copies[1:]:
+        copy.wait()
+    raw = gates_ref[...]
+    gates = raw / jnp.sum(raw, axis=0, keepdims=True)
+    ids = ids_ref[...]
+    lane = lax.broadcasted_iota(jnp.int32, (LANES, tok_count), 0)
+    table = jnp.zeros((LANES, tok_count), jnp.float32)
+    for term in range(3):
+        for choice in range(ids.shape[0]):
+            hit = lane == ids[choice : choice + 1, :] + term * expert_count
+            table = jnp.where(hit, gates[choice : choice + 1, :], table)
+    first = table.astype(BF16).astype(jnp.float32)
+    rest = table - first
+    second = rest.astype(BF16).astype(jnp.float32)
+    table = jnp.where(
+        lane < expert_count, first, jnp.where(lane < 2 * expert_count, second, rest - second)
+    )
+    table = jnp.where(lane == 3 * expert_count, docs_ref[...].astype(jnp.float32), table)
+    rows_ref[:, pl.ds(model_width, LANES)] = jnp.transpose(table).astype(BF16)
+    copies[0].wait()
+    rows_ref[:, pl.ds(0, model_width)] = rms_normed(tokens_ref[...])
+
+
+def enter(tokens, expert_ids, gate_raw, doc_ids, expert_count):
+    tok_count, model_width = tokens.shape
+    return pl.pallas_call(
+        functools.partial(enter_kernel, expert_count),
+        out_shape=jax.ShapeDtypeStruct((tok_count, model_width + LANES), BF16),
+        in_specs=[ANYWHERE] * 4,
+        out_specs=IN_VMEM,
+        scratch_shapes=[
+            pltpu.VMEM(operand.shape, operand.dtype)
+            for operand in (tokens, expert_ids.T, gate_raw.T, doc_ids)
+        ]
+        + [pltpu.SemaphoreType.DMA((4,))],
+        compiler_params=pltpu.CompilerParams(vmem_limit_bytes=62 * 1024 * 1024),
+        cost_estimate=BESIDE,
+        name="enter",
+    )(tokens, expert_ids.T, gate_raw.T, doc_ids)
+
+
+def leave_kernel(doc_lane, sizes, *refs):
+    refs = list(refs)
+    groups, tails = [], []
+    for size in sizes:
+        groups.append([refs.pop(0) for _ in range(size)])
+        tails.append(refs.pop(0))
+    blocks, sums = refs[: len(sizes) - 1], refs[len(sizes) - 1 :]
+    for i, group in enumerate(groups):
+        total = group[0][...]
+        if len(group) > 1:
+            total = added(*[term[...] for term in group]).astype(BF16)
+            blocks[i - 1][...] = total
+        lane = lax.broadcasted_iota(jnp.int32, tails[i].shape, 1)
+        named = tails[i][...].astype(jnp.float32)
+        named = jnp.sum(jnp.where(lane == doc_lane, named, 0.0), axis=1, keepdims=True)
+        member = (named == lane.astype(jnp.float32)).astype(jnp.float32).astype(BF16)
+        sums[i][...] = lax.dot_general(
+            member, total, (((0,), (0,)), ((), ())), preferred_element_type=jnp.float32
+        )[:DOC_DEV]
+
+
+def leave(doc_lane, groups):
+    tok_count, model_width = groups[0][0][0].shape
+    operands = [ref for blocks, tail in groups for ref in (*blocks, tail)]
+    count = len(groups)
+    results = pl.pallas_call(
+        functools.partial(leave_kernel, doc_lane, [len(blocks) for blocks, _ in groups]),
+        out_shape=[jax.ShapeDtypeStruct((tok_count, model_width), BF16)] * (count - 1)
+        + [jax.ShapeDtypeStruct((DOC_DEV, model_width), jnp.float32)] * count,
+        in_specs=[IN_VMEM] * len(operands),
+        out_specs=[IN_VMEM] * (2 * count - 1),
+        compiler_params=KERNEL,
+        cost_estimate=BESIDE,
+        name="leave",
+    )(*operands)
+    return results[: count - 1], results[count - 1 :]
 
 
 SWAP_X = ("center", tuple((i, i ^ ALONG_X) for i in range(8)))
 SWAP_Y = ("center", tuple((i, i ^ ALONG_Y) for i in range(8)))
+SWAP_XY = ("center", tuple((i, i ^ ALONG_X ^ ALONG_Y) for i in range(8)))
 SWAP_CORE = ("center", tuple((i, i ^ CORE) for i in range(8)))
 SWAP_Z = ("expert", ((0, 1), (1, 0), (2, 3), (3, 2)))
 MIDDLE = ("expert", ((1, 2), (2, 1)))
@@ -309,50 +397,58 @@
     )
     mine, other, choice = picked(bx2, by2, b3)
     third = (mine, crossed(other), choice)
+    (first,) = worked(first)
     d2, d3, d1 = at_once(
-        (SWAP_X, by2), (SWAP_Y, bx3), (SWAP_Z, d0), behind=(bx3, by3, bx1, mine)
+        (SWAP_X, by2), (SWAP_Y, bx3), (SWAP_Z, d0), behind=(bx3, by3, bx1, mine, first[1])
     )
     mine, other, choice = picked(bx3, by3, bx1)
     fourth = (mine, crossed(other), choice)
-    first, second = worked(first, second)
-    held = lax.optimization_barrier((d1, d2, d3, mine, first[1]))
+    (third,) = worked(third)
+    held = lax.optimization_barrier((d1, d2, d3, mine, third[1]))
     mine, other, choice = picked(*held[:3])
-    last = (mine, crossed(other), choice)
+    fourth = (lax.optimization_barrier((fourth[0], mine))[0], *fourth[1:])
+    (fourth,) = worked(fourth)
+    last = (lax.optimization_barrier((mine, fourth[1]))[0], crossed(other), choice)
     (last,) = worked(last)
-    last = (last[0], last[1], crossed(last[2]))
-    g5 = put(*last)
+    g3 = put(*lax.optimization_barrier((third[0], third[1], crossed(third[2]), last[1]))[:3])
+    g5 = put(last[0], last[1], lax.optimization_barrier((crossed(last[2]), g3[0]))[0])
     rx_y2, ry_x3, rz_d0 = at_once((SWAP_X, g5[1]), (SWAP_Y, g5[2]), (SWAP_Z, g5[0]))
-    fourth = (lax.optimization_barrier((fourth[0], last[1]))[0], *fourth[1:])
-    (fourth,) = worked(fourth)
-    g4 = put(fourth[0], fourth[1], crossed(fourth[2]))
-    third = (lax.optimization_barrier((third[0], g4[0]))[0], *third[1:])
-    (third,) = worked(third)
-    g3 = put(third[0], third[1], crossed(third[2]))
+    crossed_fourth = crossed(fourth[2])
+    g4 = put(*lax.optimization_barrier((fourth[0], fourth[1], crossed_fourth, g5[0]))[:3])
+    second = (lax.optimization_barrier((second[0], g5[0]))[0], *second[1:])
+    (second,) = worked(second)
     g2 = put(second[0], second[1], crossed(second[2]))
-    g1 = put(first[0], first[1], crossed(first[2]))
+    g1 = put(*lax.optimization_barrier((first[0], first[1], crossed(first[2]), g4[0]))[:3])
     sx3 = added(g4[0], ry_x3).astype(BF16)
     rx_b3, ry_b3, rz_x0 = at_once(
-        (SWAP_X, sx3), (SWAP_Y, g4[1]), (SWAP_Z, g4[2]), behind=(rx_y2, rz_d0, g4[0])
+        (SWAP_X, sx3), (SWAP_Y, g4[1]), (SWAP_Z, g4[2]), behind=(rx_y2, rz_d0, g4[0], second[1], g1[0])
     )
     sy2 = added(g3[1], rx_y2).astype(BF16)
     s3 = added(g3[2], rx_b3, ry_b3).astype(BF16)
     rx_b2, ry_b2, in_3 = at_once(
-        (SWAP_X, g3[0]), (SWAP_Y, sy2), (INWARD, s3), behind=(rz_x0, g3[0])
+        (SWAP_X, g3[0]), (SWAP_Y, sy2), (INWARD, s3), behind=(rz_x0, g2[0])
     )
     sd0 = added(g2[0], rz_d0).astype(BF16)
     s2 = added(g2[2], rx_b2, ry_b2).astype(BF16)
     rx_y0, ry_b1, in_2, over_3 = at_once(
         (SWAP_X, sd0), (SWAP_Y, g2[1]), (INWARD, s2),
-        (MIDDLE, added(s3, in_3).astype(BF16)), behind=(g2[0], rx_b2, ry_b2),
-    )
-    sx0 = added(g1[1], rz_x0).astype(BF16)
-    sy0 = added(g1[2], rx_y0).astype(BF16)
-    s1 = added(g1[3], ry_b1, over_3).astype(BF16)
-    rx_b0, ry_b0, rz_b0, over_2 = at_once(
-        (SWAP_X, sx0), (SWAP_Y, sy0), (SWAP_Z, s1),
-        (MIDDLE, added(s2, in_2).astype(BF16)),
-    )
-    return added(g1[0], rx_b0, ry_b0, rz_b0, over_2)
+        (MIDDLE, added(s3, in_3).astype(BF16)), behind=(rx_b2, ry_b2),
+    )
+    (sx0, sy0, s1, m2), (sum_own, *sums) = leave(
+        3 * expert_count,
+        [
+            ([g1[0]], rows[:, -LANES:]),
+            ([g1[1], rz_x0], bx0[:, -LANES:]),
+            ([g1[2], rx_y0], by0[:, -LANES:]),
+            ([g1[3], ry_b1, over_3], b1[:, -LANES:]),
+            ([s2, in_2], c2[:, -LANES:]),
+        ],
+    )
+    ways = (SWAP_X, SWAP_Y, SWAP_Z, MIDDLE)
+    sums = at_once(*zip(ways, sums))
+    pooled = normed_sum(added(sum_own, *sums))
+    rx_b0, ry_b0, rz_b0, over_2 = at_once(*zip(ways, (sx0, sy0, s1, m2)))
+    return added(g1[0], rx_b0, ry_b0, rz_b0, over_2), pooled
 
 
 def slot_table(chosen_ids, expert_count):
@@ -406,38 +502,32 @@
     expert_count = center_count * expert_axis
     tok_count, top_count = expert_ids.shape
     capacity = min(tok_count, 2 * tok_count * top_count // expert_count)
-    normed = rms_normed(tokens)
-    gate_norm = gate_raw / jnp.sum(gate_raw, axis=1, keepdims=True)
     weights_gu = gate_up[0]
     weights_down = down[0]
     bank_values = bank.astype(jnp.float32)
     bank_norms = jnp.sum(bank_values * bank_values, axis=1)
     if center_count == 8 and expert_axis == 4:
-        named = expert_ids[:, :, None] == jnp.arange(expert_count, dtype=jnp.int32)[None, None, :]
-        gate_table = jnp.sum(jnp.where(named, gate_norm[:, :, None], 0.0), axis=1)
-        unused = jnp.zeros((tok_count, LANES - 3 * expert_count), jnp.bfloat16)
-        rows = jnp.concatenate([normed, *in_three(gate_table), unused], axis=1)
+        rows = enter(tokens, expert_ids, gate_raw, doc_ids, expert_count)
         center_at, expert_at = lax.axis_index("center"), lax.axis_index("expert")
         who = jnp.stack(
             [center_at * expert_axis + expert_at, (center_at ^ CORE) * expert_axis + expert_at]
         ).astype(jnp.int32)
-        combined = gathered_layer(
+        combined, pooled = gathered_layer(
             rows, who, weights_gu, weights_down, capacity, expert_count, bank_norms
         )
     else:
+        gate_norm = gate_raw / jnp.sum(gate_raw, axis=1, keepdims=True)
         combined = exchanged_layer(
-            normed, expert_ids, gate_norm, weights_gu, weights_down, capacity
-        )
+            rms_normed(tokens), expert_ids, gate_norm, weights_gu, weights_down, capacity
+        )
+        member = (jnp.arange(DOC_DEV, dtype=jnp.int32)[:, None] == doc_ids[0][None, :]).astype(
+            jnp.float32
+        )
+        summed = jnp.dot(
+            member, combined, precision=lax.Precision.HIGHEST, preferred_element_type=jnp.float32
+        )
+        pooled = normed_sum(summed)
     layer_out = combined.astype(jnp.bfloat16)
-    member = (jnp.arange(DOC_DEV, dtype=jnp.int32)[:, None] == doc_ids[0][None, :]).astype(
-        jnp.float32
-    )
-    summed = jnp.dot(
-        member, combined, precision=lax.Precision.HIGHEST, preferred_element_type=jnp.float32
-    )
-    pooled = (summed * lax.rsqrt(jnp.sum(summed * summed, axis=1, keepdims=True) + 1e-06)).astype(
-        jnp.bfloat16
-    )
     shard_part = lax.all_gather(pooled, "center", axis=0, tiled=True)
     doc_values = shard_part.astype(jnp.float32)
     doc_norms = jnp.sum(doc_values * doc_values, axis=1)
@@ -447,8 +537,10 @@
     distance = doc_norms[:, None] + bank_norms[None, :] - 2.0 * products
     nearest = jnp.min(distance, axis=1)
     if center_count == 8 and expert_axis == 4:
-        for way in (SWAP_Y, SWAP_X, SWAP_CORE):
-            nearest = jnp.minimum(nearest, at_once((way, nearest))[0])
+        ways = (SWAP_X, SWAP_Y, SWAP_XY)
+        for arrived in at_once(*[(way, nearest) for way in ways], behind=(layer_out,)):
+            nearest = jnp.minimum(nearest, arrived)
+        nearest = jnp.minimum(nearest, at_once((SWAP_CORE, nearest))[0])
     else:
         nearest = lax.pmin(nearest, "center")
     own_scores = lax.dynamic_slice_in_dim(nearest, lax.axis_index("center") * DOC_DEV, DOC_DEV)

time: 221 us -> 196 us (0.89); the launches traced: 218 us -> 196 us
  waiting for transfers between devices: 92.9 us -> 65.2 us
  starting transfers between devices: 52.3 us -> 59.5 us
  other arithmetic: 13.1 us -> 8.07 us
  Pallas kernels: 45.2 us -> 49.4 us
    ppermute x47 -> x52, waiting for transfers between devices: 92.9 us -> 65.2 us  [at_once(): lax.ppermute(value, way[0], way[1])]
    ppermute x47 -> x52, starting transfers between devices: 52.3 us -> 59.5 us  [at_once(): lax.ppermute(value, way[0], way[1])]
    pallas_call x0 -> x2, Pallas kernels: none -> 3.25 us  [the longest x1 2.17 us: enter(): pl.pallas_call(functools.partial(enter_kernel, expert_count), out_shape=j...]
    reduce_sum x3 -> x1, other arithmetic: 2.65 us -> 0.14 us  [normed_sum(): jnp.sum(summed * summed, axis=1, keepdims=True) + 1e-06]
    pallas_call x4 -> x5, Pallas kernels: 24.6 us -> 25.5 us  [expert_rows(): pl.pallas_call(functools.partial(expert_kernel, expert_count, len(parts)...]
  transfers between devices with their start and end apart: 47 -> 52, of which waited for: 25 -> 26; matrix products, arithmetic and copies ran while one was open for 4% -> 5% of each run, Pallas kernels for 20% -> 24%
where the time goes in v3:
time: 196 us
  waiting for transfers between devices  65.2 us (33%)
  starting transfers between devices  59.5 us (30%)
  Pallas kernels  49.4 us (25%)
  blocking collectives  9.24 us (5%)
  other arithmetic  8.07 us (4%)
  matrix products  2.75 us (1%)
    ppermute x52, waiting for transfers between devices, at_once(): lax.ppermute(value, way[0], way[1])  65.2 us
    ppermute x52, starting transfers between devices, at_once(): lax.ppermute(value, way[0], way[1])  59.5 us
    pallas_call x5, Pallas kernels, expert_rows(): pl.pallas_call(functools.partial(expert_kernel, expert_count, len(parts)...  25.5 us
    pallas_call x5, Pallas kernels, pick(): pl.pallas_call(functools.partial(pick_kernel, capacity, expert_count), ou...  12.7 us
    all_gather x1, blocking collectives, local(): shard_part = lax.all_gather(pooled, 'center', axis=0, tiled=True)  9.24 us
    pallas_call x5, Pallas kernels, put(): pl.pallas_call(put_kernel, out_shape=[jax.ShapeDtypeStruct((tok_count, mo...  7.9 us
    reduce_sum x1, other arithmetic, local(): bank_norms = jnp.sum(bank_values * bank_values, axis=1)  5.08 us
  transfers between devices with their start and end apart: 52, of which 26 were waited for; matrix products, arithmetic and copies ran while one was open for 5% of the time, Pallas kernels for 24%

profile of v3, /device:TPU:0, one launch (start us, length us, event | category | flops | bytes accessed | tf_op | source)
XLA Modules:
  0.0 196.1 jit_solution(2542733724062688180)
XLA Ops:
  0.6 2.2 %enter.1.refs_0_ = bf16[128,2176]{1,0:T(8,128)(2,1)} custom-call(bf16[128,2048]{1,0:T(8,128)(2,1)} %refs_0_.1, s32[8,128]{1,0:T(8,128)} %bitcast.22, f32[8,128]{1,0:T(8,128)} %bitcast.23, s32[1,128]{1,0:T(1,128)} %refs_3_.1), custom_call_target="tpu_custom_call" | custom-call | flops 1000 | bytes 1000 | tf_op jit(solution)/shard_map/enter/pallas_call | solution.py:296
  3.7 5.9 %collective-permute-start.2 = (bf16[128,2176]{1,0:T(8,128)(2,1)}, bf16[128,2176]{1,0:T(8,128)(2,1)S(1)}, u32[]{:S(2)}, u32[]{:S(2)}) collective-permute-start(bf16[128,2176]{1,0:T(8,128)(2,1)} %enter.1.refs_0_), channel_id=1, source_target_pairs={{0,1},{1,0},{2,3},{3,2},{4,5},{5,4},{6,7},{7,6},{8,9},{9,8},{10,11... | collective-permute-start | bytes 1671176 | tf_op jit(solution)/shard_map/ppermute | solution.py:365
  9.5 1.5 collective-permute-start.1
  11.1 1.5 collective-permute-start
  12.6 9.5 %collective-permute-done.2.refs_3_ = bf16[128,2176]{1,0:T(8,128)(2,1)S(1)} collective-permute-done((bf16[128,2176]{1,0:T(8,128)(2,1)}, bf16[128,2176]{1,0:T(8,128)(2,1)S(1)}, u32[]{:S(2)}, u32[]{:S(2)}) %collective-permute-start.2) | collective-permute-done | bytes 557088 | tf_op jit(solution)/shard_map/ppermute | solution.py:365
  22.1 1.5 collective-permute-done.1.refs_2_
  26.8 1.6 collective-permute-start.8
  28.8 5.1 %multiply_reduce_fusion = f32[2048]{0:T(1024)S(1)} fusion(bf16[2048,2048]{1,0:T(8,128)(2,1)} %param.13), kind=kLoop, calls=%fused_computation | loop fusion | flops 12580864 | bytes 8396800 | tf_op jit(solution)/shard_map/reduce_sum | solution.py:508
  33.9 3.0 %pick.5 = (bf16[256,2176]{1,0:T(8,128)(2,1)S(1)}, bf16[256,2176]{1,0:T(8,128)(2,1)S(1)}, bf16[4,128,128]{2,1,0:T(8,128)(2,1)S(1)}) custom-call(s32[2]{0:T(128)S(1)} %pad_add_fusion.who_ref, bf16[128,2176]{1,0:T(8,128)(2,1)S(1)} %copy-done.1, bf16[128,2176]{1,0:T(8,128)(2,1)S(1)} %collective-permute-done.refs_1_, ...), custom_call_target="tpu_custom_call" | custom-call | flops 1000 | bytes 1000 | tf_op jit(solution)/shard_map/pick/pallas_call | solution.py:99
  36.9 3.0 %collective-permute-done.7 = bf16[128,2176]{1,0:T(8,128)(2,1)S(1)} collective-permute-done((bf16[128,2176]{1,0:T(8,128)(2,1)S(1)}, bf16[128,2176]{1,0:T(8,128)(2,1)S(1)}, u32[]{:S(2)}, u32[]{:S(2)}) %collective-permute-start.7) | collective-permute-done | bytes 557088 | tf_op jit(solution)/shard_map/ppermute | solution.py:365
  40.7 1.5 collective-permute-start.10
  43.7 2.4 %pick.6 = (bf16[192,2176]{1,0:T(8,128)(2,1)S(1)}, bf16[192,2176]{1,0:T(8,128)(2,1)S(1)}, bf16[3,128,128]{2,1,0:T(8,128)(2,1)S(1)}) custom-call(s32[2]{0:T(128)S(1)} %pad_add_fusion.who_ref, bf16[128,2176]{1,0:T(8,128)(2,1)S(1)} %collective-permute-done.8.refs_0_, bf16[128,2176]{1,0:T(8,128)(2,1)S(1)} %collective-permute-done.9.refs_1_, ...), custom_call_target="tpu_custom_call" | custom-call | flops 1000 | bytes 1000 | tf_op jit(solution)/shard_map/pick/pallas_call | solution.py:99
  46.2 7.8 %collective-permute-done.10 = bf16[128,2176]{1,0:T(8,128)(2,1)S(1)} collective-permute-done((bf16[128,2176]{1,0:T(8,128)(2,1)S(1)}, bf16[128,2176]{1,0:T(8,128)(2,1)S(1)}, u32[]{:S(2)}, u32[]{:S(2)}) %collective-permute-start.10) | collective-permute-done | bytes 557088 | tf_op jit(solution)/shard_map/ppermute | solution.py:365
  56.3 2.9 %collective-permute-start.15 = (bf16[128,2176]{1,0:T(8,128)(2,1)S(1)}, bf16[128,2176]{1,0:T(8,128)(2,1)S(1)}, u32[]{:S(2)}, u32[]{:S(2)}) collective-permute-start(bf16[128,2176]{1,0:T(8,128)(2,1)S(1)} %collective-permute-done.refs_1_), channel_id=1, source_target_pairs={{0,1},{1,0},{2,3},{3,2},{4,5},{5,4},{6,7},{7,6},{8,9},{9,8},{10,11... | collective-permute-start | bytes 1671176 | tf_op jit(solution)/shard_map/ppermute | solution.py:365
  59.2 2.4 %pick.8 = (bf16[192,2176]{1,0:T(8,128)(2,1)S(1)}, bf16[192,2176]{1,0:T(8,128)(2,1)S(1)}, bf16[3,128,128]{2,1,0:T(8,128)(2,1)S(1)}) custom-call(s32[2]{0:T(128)S(1)} %pad_add_fusion.who_ref, bf16[128,2176]{1,0:T(8,128)(2,1)S(1)} %collective-permute-done.11.refs_0_, bf16[128,2176]{1,0:T(8,128)(2,1)S(1)} %collective-permute-done.12.refs_1_, ...), custom_call_target="tpu_custom_call" | custom-call | flops 1000 | bytes 1000 | tf_op jit(solution)/shard_map/pick/pallas_call | solution.py:99
  61.8 6.1 %expert_rows.5 = (bf16[256,2048]{1,0:T(8,128)(2,1)S(1)}, bf16[256,2048]{1,0:T(8,128)(2,1)S(1)}) custom-call(s32[2]{0:T(128)S(1)} %pad_add_fusion.who_ref, bf16[256,2176]{1,0:T(8,128)(2,1)S(1)} %get-tuple-element.95.refs_0_, bf16[256,2176]{1,0:T(8,128)(2,1)S(1)} %collective-permute-done.3.refs_1_, bf16[2048,1536]{1,0:T(8,128)(2,1)S(1)} %bitcast.10, ...), custom_call_target="tpu_custom_call" | custom-call | flops 1000 | bytes 1000 | tf_op jit(solution)/shard_map/expert_rows/pallas_call | solution.py:175
  68.9 1.6 collective-permute-start.17
  70.5 1.5 collective-permute-start.18
  71.9 2.4 %pick.7 = (bf16[192,2176]{1,0:T(8,128)(2,1)S(1)}, bf16[192,2176]{1,0:T(8,128)(2,1)S(1)}, bf16[3,128,128]{2,1,0:T(8,128)(2,1)S(1)}) custom-call(s32[2]{0:T(128)S(1)} %pad_add_fusion.who_ref, bf16[128,2176]{1,0:T(8,128)(2,1)S(1)} %collective-permute-done.13.refs_0_, bf16[128,2176]{1,0:T(8,128)(2,1)S(1)} %collective-permute-done.14.refs_1_, ...), custom_call_target="tpu_custom_call" | custom-call | flops 1000 | bytes 1000 | tf_op jit(solution)/shard_map/pick/pallas_call | solution.py:99
  74.5 4.8 %expert_rows.6 = (bf16[192,2048]{1,0:T(8,128)(2,1)S(1)}, bf16[192,2048]{1,0:T(8,128)(2,1)S(1)}) custom-call(s32[2]{0:T(128)S(1)} %pad_add_fusion.who_ref, bf16[192,2176]{1,0:T(8,128)(2,1)S(1)} %get-tuple-element.112.refs_0_, bf16[192,2176]{1,0:T(8,128)(2,1)S(1)} %collective-permute-done.19.refs_1_, bf16[2048,1536]{1,0:T(8,128)(2,1)S(1)} %bitcast.11, ...), custom_call_target="tpu_custom_call" | custom-call | flops 1000 | bytes 1000 | tf_op jit(solution)/shard_map/expert_rows/pallas_call | solution.py:175
  79.3 3.8 %collective-permute-done.16.refs_0_ = bf16[128,2176]{1,0:T(8,128)(2,1)S(1)} collective-permute-done((bf16[128,2176]{1,0:T(8,128)(2,1)S(1)}, bf16[128,2176]{1,0:T(8,128)(2,1)S(1)}, u32[]{:S(2)}, u32[]{:S(2)}) %collective-permute-start.16) | collective-permute-done | bytes 557088 | tf_op jit(solution)/shard_map/ppermute | solution.py:365
  83.1 1.5 collective-permute-done.18.refs_2_
  84.6 2.4 %pick.9 = (bf16[192,2176]{1,0:T(8,128)(2,1)S(1)}, bf16[192,2176]{1,0:T(8,128)(2,1)S(1)}, bf16[3,128,128]{2,1,0:T(8,128)(2,1)S(1)}) custom-call(s32[2]{0:T(128)S(1)} %pad_add_fusion.who_ref, bf16[128,2176]{1,0:T(8,128)(2,1)S(1)} %collective-permute-done.16.refs_0_, bf16[128,2176]{1,0:T(8,128)(2,1)S(1)} %collective-permute-done.17.refs_1_, ...), custom_call_target="tpu_custom_call" | custom-call | flops 1000 | bytes 1000 | tf_op jit(solution)/shard_map/pick/pallas_call | solution.py:99
  87.6 5.0 %expert_rows.7 = (bf16[192,2048]{1,0:T(8,128)(2,1)S(1)}, bf16[192,2048]{1,0:T(8,128)(2,1)S(1)}) custom-call(s32[2]{0:T(128)S(1)} %pad_add_fusion.who_ref, bf16[192,2176]{1,0:T(8,128)(2,1)S(1)} %get-tuple-element.122.refs_0_, bf16[192,2176]{1,0:T(8,128)(2,1)S(1)} %collective-permute-done.20.refs_1_, bf16[2048,1536]{1,0:T(8,128)(2,1)S(1)} %bitcast.12, ...), custom_call_target="tpu_custom_call" | custom-call | flops 1000 | bytes 1000 | tf_op jit(solution)/shard_map/expert_rows/pallas_call | solution.py:175
  92.6 4.8 %expert_rows.8 = (bf16[192,2048]{1,0:T(8,128)(2,1)S(1)}, bf16[192,2048]{1,0:T(8,128)(2,1)S(1)}) custom-call(s32[2]{0:T(128)S(1)} %pad_add_fusion.who_ref, bf16[192,2176]{1,0:T(8,128)(2,1)S(1)} %get-tuple-element.127.refs_0_, bf16[192,2176]{1,0:T(8,128)(2,1)S(1)} %collective-permute-done.22.refs_1_, bf16[2048,1536]{1,0:T(8,128)(2,1)S(1)} %bitcast.13, ...), custom_call_target="tpu_custom_call" | custom-call | flops 1000 | bytes 1000 | tf_op jit(solution)/shard_map/expert_rows/pallas_call | solution.py:175
  99.9 1.4 put.6
  101.4 1.5 collective-permute-start.25
  103.6 1.7 collective-permute-start.27
  106.7 4.8 %expert_rows.9 = (bf16[192,2048]{1,0:T(8,128)(2,1)S(1)}, bf16[192,2048]{1,0:T(8,128)(2,1)S(1)}) custom-call(s32[2]{0:T(128)S(1)} %pad_add_fusion.who_ref, bf16[192,2176]{1,0:T(8,128)(2,1)S(1)} %get-tuple-element.152.refs_0_, bf16[192,2176]{1,0:T(8,128)(2,1)S(1)} %collective-permute-done.28.refs_1_, bf16[2048,1536]{1,0:T(8,128)(2,1)S(1)} %bitcast.14, ...), custom_call_target="tpu_custom_call" | custom-call | flops 1000 | bytes 1000 | tf_op jit(solution)/shard_map/expert_rows/pallas_call | solution.py:175
  111.6 2.2 %put.8 = (bf16[128,2048]{1,0:T(8,128)(2,1)S(1)}, bf16[128,2048]{1,0:T(8,128)(2,1)S(1)}, bf16[128,2048]{1,0:T(8,128)(2,1)S(1)}, bf16[128,2048]{1,0:T(8,128)(2,1)S(1)}) custom-call(bf16[4,128,128]{2,1,0:T(8,128)(2,1)S(1)} %get-tuple-element.143.choice_hbm, bf16[256,2048]{1,0:T(8,128)(2,1)S(1)} %get-tuple-element.144.mine_hbm, ...), custom_call_target="tpu_custom_call" | custom-call | flops 1000 | bytes 1000 | tf_op jit(solution)/shard_map/put/pallas_call | solution.py:230
  113.8 1.6 collective-permute-done.25
  119.4 1.6 collective-permute-start.29
  121.1 1.4 put.9
  122.6 8.1 %collective-permute-done.31 = bf16[128,2048]{1,0:T(8,128)(2,1)S(1)} collective-permute-done((bf16[128,2048]{1,0:T(8,128)(2,1)S(1)}, bf16[128,2048]{1,0:T(8,128)(2,1)S(1)}, u32[]{:S(2)}, u32[]{:S(2)}) %collective-permute-start.31) | collective-permute-done | bytes 524320 | tf_op jit(solution)/shard_map/ppermute | solution.py:365
  131.9 3.6 %collective-permute-start.35 = (bf16[128,2048]{1,0:T(8,128)(2,1)S(1)}, bf16[128,2048]{1,0:T(8,128)(2,1)S(1)}, u32[]{:S(2)}, u32[]{:S(2)}) collective-permute-start(bf16[128,2048]{1,0:T(8,128)(2,1)S(1)} %add_convert_fusion.3), channel_id=1, source_target_pairs={{0,1},{3,2},{4,5},{7,6},{8,9},{11,10},{12,13},{15,14},{16,17},{19,... | collective-permute-start | bytes 1572872 | tf_op jit(solution)/shard_map/ppermute | solution.py:365
  135.5 1.8 collective-permute-start.33
  138.0 6.6 %collective-permute-done.35 = bf16[128,2048]{1,0:T(8,128)(2,1)S(1)} collective-permute-done((bf16[128,2048]{1,0:T(8,128)(2,1)S(1)}, bf16[128,2048]{1,0:T(8,128)(2,1)S(1)}, u32[]{:S(2)}, u32[]{:S(2)}) %collective-permute-start.35) | collective-permute-done | bytes 524320 | tf_op jit(solution)/shard_map/ppermute | solution.py:365
  144.7 2.2 %collective-permute-done.33 = bf16[128,2048]{1,0:T(8,128)(2,1)S(1)} collective-permute-done((bf16[128,2048]{1,0:T(8,128)(2,1)S(1)}, bf16[128,2048]{1,0:T(8,128)(2,1)S(1)}, u32[]{:S(2)}, u32[]{:S(2)}) %collective-permute-start.33) | collective-permute-done | bytes 524320 | tf_op jit(solution)/shard_map/ppermute | solution.py:365
  146.9 1.9 collective-permute-done.34
  150.8 4.4 %collective-permute-start.39 = (bf16[128,2048]{1,0:T(8,128)(2,1)S(1)}, bf16[128,2048]{1,0:T(8,128)(2,1)S(1)}, u32[]{:S(2)}, u32[]{:S(2)}) collective-permute-start(bf16[128,2048]{1,0:T(8,128)(2,1)S(1)} %add_convert_fusion.2.refs_12_), channel_id=1, source_target_pairs={{0,1},{3,2},{4,5},{7,6},{8,9},{11,10},{12,13},{15,14},{16,17},{19,... | collective-permute-start | bytes 1572872 | tf_op jit(solution)/shard_map/ppermute | solution.py:365
  155.3 3.6 %collective-permute-done.36.refs_6_ = bf16[128,2048]{1,0:T(8,128)(2,1)S(1)} collective-permute-done((bf16[128,2048]{1,0:T(8,128)(2,1)S(1)}, bf16[128,2048]{1,0:T(8,128)(2,1)S(1)}, u32[]{:S(2)}, u32[]{:S(2)}) %collective-permute-start.36) | collective-permute-done | bytes 524320 | tf_op jit(solution)/shard_map/ppermute | solution.py:365
  159.6 3.4 %collective-permute-done.39.refs_13_ = bf16[128,2048]{1,0:T(8,128)(2,1)S(1)} collective-permute-done((bf16[128,2048]{1,0:T(8,128)(2,1)S(1)}, bf16[128,2048]{1,0:T(8,128)(2,1)S(1)}, u32[]{:S(2)}, u32[]{:S(2)}) %collective-permute-start.39) | collective-permute-done | bytes 524320 | tf_op jit(solution)/shard_map/ppermute | solution.py:365
  165.7 2.5 %collective-permute-start.46 = (f32[8,2048]{1,0:T(8,128)S(1)}, f32[8,2048]{1,0:T(8,128)S(1)}, u32[]{:S(2)}, u32[]{:S(2)}) collective-permute-start(f32[8,2048]{1,0:T(8,128)S(1)} %get-tuple-element.181), channel_id=1, source_target_pairs={{0,1},{1,0},{2,3},{3,2},{4,5},{5,4},{6,7},{7,6},{8,9},{9,8},{10,11... | collective-permute-start | bytes 196616 | tf_op jit(solution)/shard_map/ppermute | solution.py:365
  171.4 2.1 %collective-permute-start.42 = (bf16[128,2048]{1,0:T(8,128)(2,1)S(1)}, bf16[128,2048]{1,0:T(8,128)(2,1)S(1)}, u32[]{:S(2)}, u32[]{:S(2)}) collective-permute-start(bf16[128,2048]{1,0:T(8,128)(2,1)S(1)} %get-tuple-element.176), channel_id=1, source_target_pairs={{0,1},{1,0},{2,3},{3,2},{4,5},{5,4},{6,7},{7,6},{8,9},{9,8},{10,11... | collective-permute-start | bytes 1572872 | tf_op jit(solution)/shard_map/ppermute | solution.py:365
  174.4 9.2 %all_gather.3 = bf16[64,2048]{1,0:T(8,128)(2,1)S(1)} all-gather(bf16[8,2048]{1,0:T(8,128)(2,1)S(1)} %multiply_convert_fusion), channel_id=1, replica_groups=mesh['center'=8,'expert'=4] {'center'}, dimensions={0}, use_global_device_ids=true | all-gather | bytes 294912 | tf_op jit(solution)/shard_map/all_gather | solution.py:531
  183.8 2.8 %fusion.1 = f32[64]{0:T(128)S(1)} fusion(bf16[64,2048]{1,0:T(8,128)(2,1)S(1)} %all_gather.3, bf16[2048,2048]{1,0:T(8,128)(2,1)S(1)} %bitcast.21, f32[2048]{0:T(1024)S(1)} %multiply_reduce_fusion, f32[64]{0:T(128)S(1)} %multiply_reduce_fusion.1), kind=kOutput, calls=%fused_computation.3 | convolution fusion | flops 537395136 | bytes 8659456 | tf_op jit(solution)/shard_map/dot_general | solution.py:534
  189.9 1.5 collective-permute-start.50
  192.2 2.1 %collective-permute-done.50 = f32[64]{0:T(128)S(1)} collective-permute-done((f32[64]{0:T(128)S(1)}, f32[64]{0:T(128)S(1)}, u32[]{:S(2)}, u32[]{:S(2)}) %collective-permute-start.50) | collective-permute-done | bytes 288 | tf_op jit(solution)/shard_map/ppermute | solution.py:365
  (112 shorter events, 37.4 us)
Async XLA Ops:
  2.8 9.8 %collective-permute-start.5 = (bf16[128,2176]{1,0:T(8,128)(2,1)}, bf16[128,2176]{1,0:T(8,128)(2,1)S(1)}, u32[]{:S(2)}, u32[]{:S(2)}) collective-permute-start(bf16[128,2176]{1,0:T(8,128)(2,1)} %enter.1.refs_0_), channel_id=1, source_target_pairs={{1,2},{2,1},{5,6},{6,5},{9,10},{10,9},{13,14},{14,13},{17,18},{18,... | collective-permute-start | bytes 1671176 | tf_op jit(solution)/shard_map/ppermute | solution.py:365
  3.7 18.4 %collective-permute-start.2 = (bf16[128,2176]{1,0:T(8,128)(2,1)}, bf16[128,2176]{1,0:T(8,128)(2,1)S(1)}, u32[]{:S(2)}, u32[]{:S(2)}) collective-permute-start(bf16[128,2176]{1,0:T(8,128)(2,1)} %enter.1.refs_0_), channel_id=1, source_target_pairs={{0,1},{1,0},{2,3},{3,2},{4,5},{5,4},{6,7},{7,6},{8,9},{9,8},{10,11... | collective-permute-start | bytes 1671176 | tf_op jit(solution)/shard_map/ppermute | solution.py:365
  9.5 14.0 %collective-permute-start.1 = (bf16[128,2176]{1,0:T(8,128)(2,1)}, bf16[128,2176]{1,0:T(8,128)(2,1)S(1)}, u32[]{:S(2)}, u32[]{:S(2)}) collective-permute-start(bf16[128,2176]{1,0:T(8,128)(2,1)} %enter.1.refs_0_), channel_id=1, source_target_pairs={{0,16},{4,20},{8,24},{12,28},{16,0},{20,4},{24,8},{28,12},{1,17},{... | collective-permute-start | bytes 1671176 | tf_op jit(solution)/shard_map/ppermute | solution.py:365
  11.1 13.7 %collective-permute-start = (bf16[128,2176]{1,0:T(8,128)(2,1)}, bf16[128,2176]{1,0:T(8,128)(2,1)S(1)}, u32[]{:S(2)}, u32[]{:S(2)}) collective-permute-start(bf16[128,2176]{1,0:T(8,128)(2,1)} %enter.1.refs_0_), channel_id=1, source_target_pairs={{0,8},{4,12},{8,0},{12,4},{16,24},{20,28},{24,16},{28,20},{1,9},{5... | collective-permute-start | bytes 1671176 | tf_op jit(solution)/shard_map/ppermute | solution.py:365
  24.8 15.3 %collective-permute-start.6 = (bf16[128,2176]{1,0:T(8,128)(2,1)S(1)}, bf16[128,2176]{1,0:T(8,128)(2,1)S(1)}, u32[]{:S(2)}, u32[]{:S(2)}) collective-permute-start(bf16[128,2176]{1,0:T(8,128)(2,1)S(1)} %collective-permute-done.2.refs_3_), channel_id=1, source_target_pairs={{1,2},{2,1},{5,6},{6,5},{9,10},{10,9},{13,14},{14,13},{17,18},{18,... | collective-permute-start | bytes 1671176 | tf_op jit(solution)/shard_map/ppermute | solution.py:365
  25.5 14.5 %collective-permute-start.7 = (bf16[128,2176]{1,0:T(8,128)(2,1)S(1)}, bf16[128,2176]{1,0:T(8,128)(2,1)S(1)}, u32[]{:S(2)}, u32[]{:S(2)}) collective-permute-start(bf16[128,2176]{1,0:T(8,128)(2,1)S(1)} %collective-permute-done.5), channel_id=1, source_target_pairs={{1,0},{2,3},{5,4},{6,7},{9,8},{10,11},{13,12},{14,15},{17,16},{18,... | collective-permute-start | bytes 1671176 | tf_op jit(solution)/shard_map/ppermute | solution.py:365
  26.8 13.3 %collective-permute-start.8 = (bf16[128,2176]{1,0:T(8,128)(2,1)S(1)}, bf16[128,2176]{1,0:T(8,128)(2,1)S(1)}, u32[]{:S(2)}, u32[]{:S(2)}) collective-permute-start(bf16[128,2176]{1,0:T(8,128)(2,1)S(1)} %collective-permute-done.1.refs_2_), channel_id=1, source_target_pairs={{0,8},{4,12},{8,0},{12,4},{16,24},{20,28},{24,16},{28,20},{1,9},{5... | collective-permute-start | bytes 1671176 | tf_op jit(solution)/shard_map/ppermute | solution.py:365
  28.3 12.3 %collective-permute-start.9 = (bf16[128,2176]{1,0:T(8,128)(2,1)S(1)}, bf16[128,2176]{1,0:T(8,128)(2,1)S(1)}, u32[]{:S(2)}, u32[]{:S(2)}) collective-permute-start(bf16[128,2176]{1,0:T(8,128)(2,1)S(1)} %collective-permute-done.2.refs_3_), channel_id=1, source_target_pairs={{0,16},{4,20},{8,24},{12,28},{16,0},{20,4},{24,8},{28,12},{1,17},{... | collective-permute-start | bytes 1671176 | tf_op jit(solution)/shard_map/ppermute | solution.py:365
  40.7 13.3 %collective-permute-start.10 = (bf16[128,2176]{1,0:T(8,128)(2,1)S(1)}, bf16[128,2176]{1,0:T(8,128)(2,1)S(1)}, u32[]{:S(2)}, u32[]{:S(2)}) collective-permute-start(bf16[128,2176]{1,0:T(8,128)(2,1)S(1)} %collective-permute-done.6), channel_id=1, source_target_pairs={{1,0},{2,3},{5,4},{6,7},{9,8},{10,11},{13,12},{14,15},{17,16},{18,... | collective-permute-start | bytes 1671176 | tf_op jit(solution)/shard_map/ppermute | solution.py:365
  42.1 12.0 %collective-permute-start.11 = (bf16[128,2176]{1,0:T(8,128)(2,1)S(1)}, bf16[128,2176]{1,0:T(8,128)(2,1)S(1)}, u32[]{:S(2)}, u32[]{:S(2)}) collective-permute-start(bf16[128,2176]{1,0:T(8,128)(2,1)S(1)} %add.86.refs_2_), channel_id=1, source_target_pairs={{0,8},{4,12},{8,0},{12,4},{16,24},{20,28},{24,16},{28,20},{1,9},{5... | collective-permute-start | bytes 1671176 | tf_op jit(solution)/shard_map/ppermute | solution.py:365
  43.2 11.9 %collective-permute-start.12 = (bf16[128,2176]{1,0:T(8,128)(2,1)S(1)}, bf16[128,2176]{1,0:T(8,128)(2,1)S(1)}, u32[]{:S(2)}, u32[]{:S(2)}) collective-permute-start(bf16[128,2176]{1,0:T(8,128)(2,1)S(1)} %add.86.refs_2_), channel_id=1, source_target_pairs={{0,16},{4,20},{8,24},{12,28},{16,0},{20,4},{24,8},{28,12},{1,17},{... | collective-permute-start | bytes 1671176 | tf_op jit(solution)/shard_map/ppermute | solution.py:365
  43.7 18.0 %collective-permute-start.3 = (bf16[256,2176]{1,0:T(8,128)(2,1)S(1)}, bf16[256,2176]{1,0:T(8,128)(2,1)S(1)}, u32[]{:S(2)}, u32[]{:S(2)}) collective-permute-start(bf16[256,2176]{1,0:T(8,128)(2,1)S(1)} %get-tuple-element.96), channel_id=1, source_target_pairs={{0,4},{4,0},{8,12},{12,8},{16,20},{20,16},{24,28},{28,24},{1,5},{5... | collective-permute-start | bytes 3342344 | tf_op jit(solution)/shard_map/ppermute | solution.py:365
  55.1 12.8 %collective-permute-start.13 = (bf16[128,2176]{1,0:T(8,128)(2,1)S(1)}, bf16[128,2176]{1,0:T(8,128)(2,1)S(1)}, u32[]{:S(2)}, u32[]{:S(2)}) collective-permute-start(bf16[128,2176]{1,0:T(8,128)(2,1)S(1)} %add.87.refs_2_), channel_id=1, source_target_pairs={{0,8},{4,12},{8,0},{12,4},{16,24},{20,28},{24,16},{28,20},{1,9},{5... | collective-permute-start | bytes 1671176 | tf_op jit(solution)/shard_map/ppermute | solution.py:365
  55.7 12.2 %collective-permute-start.14 = (bf16[128,2176]{1,0:T(8,128)(2,1)S(1)}, bf16[128,2176]{1,0:T(8,128)(2,1)S(1)}, u32[]{:S(2)}, u32[]{:S(2)}) collective-permute-start(bf16[128,2176]{1,0:T(8,128)(2,1)S(1)} %add.87.refs_2_), channel_id=1, source_target_pairs={{0,16},{4,20},{8,24},{12,28},{16,0},{20,4},{24,8},{28,12},{1,17},{... | collective-permute-start | bytes 1671176 | tf_op jit(solution)/shard_map/ppermute | solution.py:365
  56.3 11.6 %collective-permute-start.15 = (bf16[128,2176]{1,0:T(8,128)(2,1)S(1)}, bf16[128,2176]{1,0:T(8,128)(2,1)S(1)}, u32[]{:S(2)}, u32[]{:S(2)}) collective-permute-start(bf16[128,2176]{1,0:T(8,128)(2,1)S(1)} %collective-permute-done.refs_1_), channel_id=1, source_target_pairs={{0,1},{1,0},{2,3},{3,2},{4,5},{5,4},{6,7},{7,6},{8,9},{9,8},{10,11... | collective-permute-start | bytes 1671176 | tf_op jit(solution)/shard_map/ppermute | solution.py:365
  61.6 12.8 %collective-permute-start.19 = (bf16[192,2176]{1,0:T(8,128)(2,1)S(1)}, bf16[192,2176]{1,0:T(8,128)(2,1)S(1)}, u32[]{:S(2)}, u32[]{:S(2)}) collective-permute-start(bf16[192,2176]{1,0:T(8,128)(2,1)S(1)} %get-tuple-element.116), channel_id=1, source_target_pairs={{0,4},{4,0},{8,12},{12,8},{16,20},{20,16},{24,28},{28,24},{1,5},{5... | collective-permute-start | bytes 2506760 | tf_op jit(solution)/shard_map/ppermute | solution.py:365
  67.9 15.1 %collective-permute-start.16 = (bf16[128,2176]{1,0:T(8,128)(2,1)S(1)}, bf16[128,2176]{1,0:T(8,128)(2,1)S(1)}, u32[]{:S(2)}, u32[]{:S(2)}) collective-permute-start(bf16[128,2176]{1,0:T(8,128)(2,1)S(1)} %collective-permute-done.8.refs_0_), channel_id=1, source_target_pairs={{0,1},{1,0},{2,3},{3,2},{4,5},{5,4},{6,7},{7,6},{8,9},{9,8},{10,11... | collective-permute-start | bytes 1671176 | tf_op jit(solution)/shard_map/ppermute | solution.py:365
  68.9 14.2 %collective-permute-start.17 = (bf16[128,2176]{1,0:T(8,128)(2,1)S(1)}, bf16[128,2176]{1,0:T(8,128)(2,1)S(1)}, u32[]{:S(2)}, u32[]{:S(2)}) collective-permute-start(bf16[128,2176]{1,0:T(8,128)(2,1)S(1)} %collective-permute-done.12.refs_1_), channel_id=1, source_target_pairs={{0,8},{4,12},{8,0},{12,4},{16,24},{20,28},{24,16},{28,20},{1,9},{5... | collective-permute-start | bytes 1671176 | tf_op jit(solution)/shard_map/ppermute | solution.py:365
  70.5 14.1 %collective-permute-start.18 = (bf16[128,2176]{1,0:T(8,128)(2,1)S(1)}, bf16[128,2176]{1,0:T(8,128)(2,1)S(1)}, u32[]{:S(2)}, u32[]{:S(2)}) collective-permute-start(bf16[128,2176]{1,0:T(8,128)(2,1)S(1)} %collective-permute-done.13.refs_0_), channel_id=1, source_target_pairs={{0,16},{4,20},{8,24},{12,28},{16,0},{20,4},{24,8},{28,12},{1,17},{... | collective-permute-start | bytes 1671176 | tf_op jit(solution)/shard_map/ppermute | solution.py:365
  74.4 13.2 %collective-permute-start.20 = (bf16[192,2176]{1,0:T(8,128)(2,1)S(1)}, bf16[192,2176]{1,0:T(8,128)(2,1)S(1)}, u32[]{:S(2)}, u32[]{:S(2)}) collective-permute-start(bf16[192,2176]{1,0:T(8,128)(2,1)S(1)} %get-tuple-element.123), channel_id=1, source_target_pairs={{0,4},{4,0},{8,12},{12,8},{16,20},{20,16},{24,28},{28,24},{1,5},{5... | collective-permute-start | bytes 2506760 | tf_op jit(solution)/shard_map/ppermute | solution.py:365
  87.0 5.6 %collective-permute-start.22 = (bf16[192,2176]{1,0:T(8,128)(2,1)S(1)}, bf16[192,2176]{1,0:T(8,128)(2,1)S(1)}, u32[]{:S(2)}, u32[]{:S(2)}) collective-permute-start(bf16[192,2176]{1,0:T(8,128)(2,1)S(1)} %get-tuple-element.128), channel_id=1, source_target_pairs={{0,4},{4,0},{8,12},{12,8},{16,20},{20,16},{24,28},{28,24},{1,5},{5... | collective-permute-start | bytes 2506760 | tf_op jit(solution)/shard_map/ppermute | solution.py:365
  87.1 11.4 %collective-permute-start.24 = (bf16[192,2048]{1,0:T(8,128)(2,1)S(1)}, bf16[192,2048]{1,0:T(8,128)(2,1)S(1)}, u32[]{:S(2)}, u32[]{:S(2)}) collective-permute-start(bf16[192,2048]{1,0:T(8,128)(2,1)S(1)} %get-tuple-element.132), channel_id=1, source_target_pairs={{0,4},{4,0},{8,12},{12,8},{16,20},{20,16},{24,28},{28,24},{1,5},{5... | collective-permute-start | bytes 2359304 | tf_op jit(solution)/shard_map/ppermute | solution.py:365
  97.5 13.9 %collective-permute-start.4 = (bf16[256,2048]{1,0:T(8,128)(2,1)S(1)}, bf16[256,2048]{1,0:T(8,128)(2,1)S(1)}, u32[]{:S(2)}, u32[]{:S(2)}) collective-permute-start(bf16[256,2048]{1,0:T(8,128)(2,1)S(1)} %get-tuple-element.98), channel_id=1, source_target_pairs={{0,4},{4,0},{8,12},{12,8},{16,20},{20,16},{24,28},{28,24},{1,5},{5... | collective-permute-start | bytes 3145736 | tf_op jit(solution)/shard_map/ppermute | solution.py:365
  98.0 8.7 %collective-permute-start.28 = (bf16[192,2176]{1,0:T(8,128)(2,1)S(1)}, bf16[192,2176]{1,0:T(8,128)(2,1)S(1)}, u32[]{:S(2)}, u32[]{:S(2)}) collective-permute-start(bf16[192,2176]{1,0:T(8,128)(2,1)S(1)} %get-tuple-element.153), channel_id=1, source_target_pairs={{0,4},{4,0},{8,12},{12,8},{16,20},{20,16},{24,28},{28,24},{1,5},{5... | collective-permute-start | bytes 2506760 | tf_op jit(solution)/shard_map/ppermute | solution.py:365
  98.1 5.5 %collective-permute-start.21 = (bf16[192,2048]{1,0:T(8,128)(2,1)S(1)}, bf16[192,2048]{1,0:T(8,128)(2,1)S(1)}, u32[]{:S(2)}, u32[]{:S(2)}) collective-permute-start(bf16[192,2048]{1,0:T(8,128)(2,1)S(1)} %get-tuple-element.125), channel_id=1, source_target_pairs={{0,4},{4,0},{8,12},{12,8},{16,20},{20,16},{24,28},{28,24},{1,5},{5... | collective-permute-start | bytes 2359304 | tf_op jit(solution)/shard_map/ppermute | solution.py:365
  101.4 14.0 %collective-permute-start.25 = (bf16[128,2048]{1,0:T(8,128)(2,1)S(1)}, bf16[128,2048]{1,0:T(8,128)(2,1)S(1)}, u32[]{:S(2)}, u32[]{:S(2)}) collective-permute-start(bf16[128,2048]{1,0:T(8,128)(2,1)S(1)} %get-tuple-element.148), channel_id=1, source_target_pairs={{0,16},{4,20},{8,24},{12,28},{16,0},{20,4},{24,8},{28,12},{1,17},{... | collective-permute-start | bytes 1572872 | tf_op jit(solution)/shard_map/ppermute | solution.py:365
  102.9 13.6 %collective-permute-start.26 = (bf16[128,2048]{1,0:T(8,128)(2,1)S(1)}, bf16[128,2048]{1,0:T(8,128)(2,1)S(1)}, u32[]{:S(2)}, u32[]{:S(2)}) collective-permute-start(bf16[128,2048]{1,0:T(8,128)(2,1)S(1)} %get-tuple-element.151), channel_id=1, source_target_pairs={{0,8},{4,12},{8,0},{12,4},{16,24},{20,28},{24,16},{28,20},{1,9},{5... | collective-permute-start | bytes 1572872 | tf_op jit(solution)/shard_map/ppermute | solution.py:365
  103.6 14.0 %collective-permute-start.27 = (bf16[128,2048]{1,0:T(8,128)(2,1)S(1)}, bf16[128,2048]{1,0:T(8,128)(2,1)S(1)}, u32[]{:S(2)}, u32[]{:S(2)}) collective-permute-start(bf16[128,2048]{1,0:T(8,128)(2,1)S(1)} %get-tuple-element.138), channel_id=1, source_target_pairs={{0,1},{1,0},{2,3},{3,2},{4,5},{5,4},{6,7},{7,6},{8,9},{9,8},{10,11... | collective-permute-start | bytes 1572872 | tf_op jit(solution)/shard_map/ppermute | solution.py:365
  111.5 9.6 %collective-permute-start.30 = (bf16[192,2048]{1,0:T(8,128)(2,1)S(1)}, bf16[192,2048]{1,0:T(8,128)(2,1)S(1)}, u32[]{:S(2)}, u32[]{:S(2)}) collective-permute-start(bf16[192,2048]{1,0:T(8,128)(2,1)S(1)} %get-tuple-element.158), channel_id=1, source_target_pairs={{0,4},{4,0},{8,12},{12,8},{16,20},{20,16},{24,28},{28,24},{1,5},{5... | collective-permute-start | bytes 2359304 | tf_op jit(solution)/shard_map/ppermute | solution.py:365
  117.5 13.1 %collective-permute-start.31 = (bf16[128,2048]{1,0:T(8,128)(2,1)S(1)}, bf16[128,2048]{1,0:T(8,128)(2,1)S(1)}, u32[]{:S(2)}, u32[]{:S(2)}) collective-permute-start(bf16[128,2048]{1,0:T(8,128)(2,1)S(1)} %add_convert_fusion.6), channel_id=1, source_target_pairs={{0,8},{4,12},{8,0},{12,4},{16,24},{20,28},{24,16},{28,20},{1,9},{5... | collective-permute-start | bytes 1572872 | tf_op jit(solution)/shard_map/ppermute | solution.py:365
  118.3 12.4 %collective-permute-start.32 = (bf16[128,2048]{1,0:T(8,128)(2,1)S(1)}, bf16[128,2048]{1,0:T(8,128)(2,1)S(1)}, u32[]{:S(2)}, u32[]{:S(2)}) collective-permute-start(bf16[128,2048]{1,0:T(8,128)(2,1)S(1)} %get-tuple-element.165), channel_id=1, source_target_pairs={{0,16},{4,20},{8,24},{12,28},{16,0},{20,4},{24,8},{28,12},{1,17},{... | collective-permute-start | bytes 1572872 | tf_op jit(solution)/shard_map/ppermute | solution.py:365
  119.4 12.5 %collective-permute-start.29 = (bf16[128,2048]{1,0:T(8,128)(2,1)S(1)}, bf16[128,2048]{1,0:T(8,128)(2,1)S(1)}, u32[]{:S(2)}, u32[]{:S(2)}) collective-permute-start(bf16[128,2048]{1,0:T(8,128)(2,1)S(1)} %get-tuple-element.155), channel_id=1, source_target_pairs={{0,1},{1,0},{2,3},{3,2},{4,5},{5,4},{6,7},{7,6},{8,9},{9,8},{10,11... | collective-permute-start | bytes 1572872 | tf_op jit(solution)/shard_map/ppermute | solution.py:365
  131.9 12.7 %collective-permute-start.35 = (bf16[128,2048]{1,0:T(8,128)(2,1)S(1)}, bf16[128,2048]{1,0:T(8,128)(2,1)S(1)}, u32[]{:S(2)}, u32[]{:S(2)}) collective-permute-start(bf16[128,2048]{1,0:T(8,128)(2,1)S(1)} %add_convert_fusion.3), channel_id=1, source_target_pairs={{0,1},{3,2},{4,5},{7,6},{8,9},{11,10},{12,13},{15,14},{16,17},{19,... | collective-permute-start | bytes 1572872 | tf_op jit(solution)/shard_map/ppermute | solution.py:365
  135.5 11.4 %collective-permute-start.33 = (bf16[128,2048]{1,0:T(8,128)(2,1)S(1)}, bf16[128,2048]{1,0:T(8,128)(2,1)S(1)}, u32[]{:S(2)}, u32[]{:S(2)}) collective-permute-start(bf16[128,2048]{1,0:T(8,128)(2,1)S(1)} %get-tuple-element.166), channel_id=1, source_target_pairs={{0,8},{4,12},{8,0},{12,4},{16,24},{20,28},{24,16},{28,20},{1,9},{5... | collective-permute-start | bytes 1572872 | tf_op jit(solution)/shard_map/ppermute | solution.py:365
  137.3 11.5 %collective-permute-start.34 = (bf16[128,2048]{1,0:T(8,128)(2,1)S(1)}, bf16[128,2048]{1,0:T(8,128)(2,1)S(1)}, u32[]{:S(2)}, u32[]{:S(2)}) collective-permute-start(bf16[128,2048]{1,0:T(8,128)(2,1)S(1)} %add_convert_fusion.4), channel_id=1, source_target_pairs={{0,16},{4,20},{8,24},{12,28},{16,0},{20,4},{24,8},{28,12},{1,17},{... | collective-permute-start | bytes 1572872 | tf_op jit(solution)/shard_map/ppermute | solution.py:365
  149.0 9.8 %collective-permute-start.36 = (bf16[128,2048]{1,0:T(8,128)(2,1)S(1)}, bf16[128,2048]{1,0:T(8,128)(2,1)S(1)}, u32[]{:S(2)}, u32[]{:S(2)}) collective-permute-start(bf16[128,2048]{1,0:T(8,128)(2,1)S(1)} %add_convert_fusion.5), channel_id=1, source_target_pairs={{0,8},{4,12},{8,0},{12,4},{16,24},{20,28},{24,16},{28,20},{1,9},{5... | collective-permute-start | bytes 1572872 | tf_op jit(solution)/shard_map/ppermute | solution.py:365
  149.4 10.2 %collective-permute-start.37 = (bf16[128,2048]{1,0:T(8,128)(2,1)S(1)}, bf16[128,2048]{1,0:T(8,128)(2,1)S(1)}, u32[]{:S(2)}, u32[]{:S(2)}) collective-permute-start(bf16[128,2048]{1,0:T(8,128)(2,1)S(1)} %get-tuple-element.171), channel_id=1, source_target_pairs={{0,16},{4,20},{8,24},{12,28},{16,0},{20,4},{24,8},{28,12},{1,17},{... | collective-permute-start | bytes 1572872 | tf_op jit(solution)/shard_map/ppermute | solution.py:365
  150.1 9.5 %collective-permute-start.38 = (bf16[128,2048]{1,0:T(8,128)(2,1)S(1)}, bf16[128,2048]{1,0:T(8,128)(2,1)S(1)}, u32[]{:S(2)}, u32[]{:S(2)}) collective-permute-start(bf16[128,2048]{1,0:T(8,128)(2,1)S(1)} %add_convert_fusion.1), channel_id=1, source_target_pairs={{1,2},{2,1},{5,6},{6,5},{9,10},{10,9},{13,14},{14,13},{17,18},{18,... | collective-permute-start | bytes 1572872 | tf_op jit(solution)/shard_map/ppermute | solution.py:365
  150.8 12.2 %collective-permute-start.39 = (bf16[128,2048]{1,0:T(8,128)(2,1)S(1)}, bf16[128,2048]{1,0:T(8,128)(2,1)S(1)}, u32[]{:S(2)}, u32[]{:S(2)}) collective-permute-start(bf16[128,2048]{1,0:T(8,128)(2,1)S(1)} %add_convert_fusion.2.refs_12_), channel_id=1, source_target_pairs={{0,1},{3,2},{4,5},{7,6},{8,9},{11,10},{12,13},{15,14},{16,17},{19,... | collective-permute-start | bytes 1572872 | tf_op jit(solution)/shard_map/ppermute | solution.py:365
  164.1 6.1 %collective-permute-start.44 = (f32[8,2048]{1,0:T(8,128)S(1)}, f32[8,2048]{1,0:T(8,128)S(1)}, u32[]{:S(2)}, u32[]{:S(2)}) collective-permute-start(f32[8,2048]{1,0:T(8,128)S(1)} %get-tuple-element.179), channel_id=1, source_target_pairs={{0,8},{4,12},{8,0},{12,4},{16,24},{20,28},{24,16},{28,20},{1,9},{5... | collective-permute-start | bytes 196616 | tf_op jit(solution)/shard_map/ppermute | solution.py:365
  164.8 6.6 %collective-permute-start.45 = (f32[8,2048]{1,0:T(8,128)S(1)}, f32[8,2048]{1,0:T(8,128)S(1)}, u32[]{:S(2)}, u32[]{:S(2)}) collective-permute-start(f32[8,2048]{1,0:T(8,128)S(1)} %get-tuple-element.180), channel_id=1, source_target_pairs={{0,16},{4,20},{8,24},{12,28},{16,0},{20,4},{24,8},{28,12},{1,17},{... | collective-permute-start | bytes 196616 | tf_op jit(solution)/shard_map/ppermute | solution.py:365
  165.7 7.8 %collective-permute-start.46 = (f32[8,2048]{1,0:T(8,128)S(1)}, f32[8,2048]{1,0:T(8,128)S(1)}, u32[]{:S(2)}, u32[]{:S(2)}) collective-permute-start(f32[8,2048]{1,0:T(8,128)S(1)} %get-tuple-element.181), channel_id=1, source_target_pairs={{0,1},{1,0},{2,3},{3,2},{4,5},{5,4},{6,7},{7,6},{8,9},{9,8},{10,11... | collective-permute-start | bytes 196616 | tf_op jit(solution)/shard_map/ppermute | solution.py:365
  168.2 6.0 %collective-permute-start.47 = (f32[8,2048]{1,0:T(8,128)S(1)}, f32[8,2048]{1,0:T(8,128)S(1)}, u32[]{:S(2)}, u32[]{:S(2)}) collective-permute-start(f32[8,2048]{1,0:T(8,128)S(1)} %get-tuple-element.182), channel_id=1, source_target_pairs={{1,2},{2,1},{5,6},{6,5},{9,10},{10,9},{13,14},{14,13},{17,18},{18,... | collective-permute-start | bytes 196616 | tf_op jit(solution)/shard_map/ppermute | solution.py:365
  168.8 17.8 %collective-permute-start.40 = (bf16[128,2048]{1,0:T(8,128)(2,1)S(1)}, bf16[128,2048]{1,0:T(8,128)(2,1)S(1)}, u32[]{:S(2)}, u32[]{:S(2)}) collective-permute-start(bf16[128,2048]{1,0:T(8,128)(2,1)S(1)} %get-tuple-element.174), channel_id=1, source_target_pairs={{0,8},{4,12},{8,0},{12,4},{16,24},{20,28},{24,16},{28,20},{1,9},{5... | collective-permute-start | bytes 1572872 | tf_op jit(solution)/shard_map/ppermute | solution.py:365
  170.2 16.4 %collective-permute-start.41 = (bf16[128,2048]{1,0:T(8,128)(2,1)S(1)}, bf16[128,2048]{1,0:T(8,128)(2,1)S(1)}, u32[]{:S(2)}, u32[]{:S(2)}) collective-permute-start(bf16[128,2048]{1,0:T(8,128)(2,1)S(1)} %get-tuple-element.175), channel_id=1, source_target_pairs={{0,16},{4,20},{8,24},{12,28},{16,0},{20,4},{24,8},{28,12},{1,17},{... | collective-permute-start | bytes 1572872 | tf_op jit(solution)/shard_map/ppermute | solution.py:365
  171.4 15.2 %collective-permute-start.42 = (bf16[128,2048]{1,0:T(8,128)(2,1)S(1)}, bf16[128,2048]{1,0:T(8,128)(2,1)S(1)}, u32[]{:S(2)}, u32[]{:S(2)}) collective-permute-start(bf16[128,2048]{1,0:T(8,128)(2,1)S(1)} %get-tuple-element.176), channel_id=1, source_target_pairs={{0,1},{1,0},{2,3},{3,2},{4,5},{5,4},{6,7},{7,6},{8,9},{9,8},{10,11... | collective-permute-start | bytes 1572872 | tf_op jit(solution)/shard_map/ppermute | solution.py:365
  173.5 13.1 %collective-permute-start.43 = (bf16[128,2048]{1,0:T(8,128)(2,1)S(1)}, bf16[128,2048]{1,0:T(8,128)(2,1)S(1)}, u32[]{:S(2)}, u32[]{:S(2)}) collective-permute-start(bf16[128,2048]{1,0:T(8,128)(2,1)S(1)} %get-tuple-element.177), channel_id=1, source_target_pairs={{1,2},{2,1},{5,6},{6,5},{9,10},{10,9},{13,14},{14,13},{17,18},{18,... | collective-permute-start | bytes 1572872 | tf_op jit(solution)/shard_map/ppermute | solution.py:365
  189.9 4.4 %collective-permute-start.50 = (f32[64]{0:T(128)S(1)}, f32[64]{0:T(128)S(1)}, u32[]{:S(2)}, u32[]{:S(2)}) collective-permute-start(f32[64]{0:T(128)S(1)} %fusion.1), channel_id=1, source_target_pairs={{0,24},{4,28},{8,16},{12,20},{16,8},{20,12},{24,0},{28,4},{1,25},{... | collective-permute-start | bytes 776 | tf_op jit(solution)/shard_map/ppermute | solution.py:365
  (10 other events, 265.8 us)

commit v4 on v3

--- a/solution.py
+++ b/solution.py
@@ -35,16 +35,11 @@
 
 
 def pick_kernel(capacity, expert_count, who_ref, *refs):
-    count = len(refs) - 9
+    count = len(refs) - 3
     blocks = refs[:count]
-    mine_hbm, other_hbm, choice_hbm, rows_in, mine, other, choice, in_sem, out_sem = refs[count:]
+    mine, other, choice = refs[count:]
     tok_count = blocks[0].shape[0]
     model_width = blocks[0].shape[1] - LANES
-    in_copies = [
-        pltpu.make_async_copy(blocks[j], rows_in.at[j], in_sem.at[j]) for j in range(count)
-    ]
-    for copy in in_copies:
-        copy.start()
     row = lax.broadcasted_iota(jnp.int32, (8, LANES), 0)
     asked = jnp.where(
         row == 0,
@@ -58,10 +53,7 @@
     slot_row = lax.broadcasted_iota(jnp.int32, (2 * capacity, tok_count), 0)
     first_half = slot_row < capacity
     slot_row = slot_row.astype(jnp.float32)
-    out_copies = []
-    for copy in in_copies:
-        copy.wait()
-    tails = rows_in[:, :, pl.ds(model_width, LANES)].reshape(count * tok_count, LANES)
+    tails = jnp.concatenate([block[:, pl.ds(model_width, LANES)] for block in blocks], axis=0)
     gates = lax.dot_general(
         asked, tails, (((1,), (1,)), ((), ())), preferred_element_type=jnp.float32
     )
@@ -74,22 +66,10 @@
         slot = jnp.where(first_half, slot[0:1, :], slot[1:2, :] + float(capacity))
         choice[j] = (slot == slot_row).astype(jnp.float32).astype(BF16)
     for j in range(count):
-        picked = jnp.dot(choice[j], rows_in[j], preferred_element_type=jnp.float32).astype(BF16)
+        picked = jnp.dot(choice[j], blocks[j][...], preferred_element_type=jnp.float32).astype(BF16)
         here = pl.ds(j * capacity, capacity)
         mine[here, :] = picked[:capacity]
         other[here, :] = picked[capacity:]
-        for at, (source, target) in enumerate(
-            (
-                (other.at[here], other_hbm.at[here]),
-                (mine.at[here], mine_hbm.at[here]),
-                (choice.at[j], choice_hbm.at[j]),
-            )
-        ):
-            copy = pltpu.make_async_copy(source, target, out_sem.at[at, j])
-            copy.start()
-            out_copies.append(copy)
-    for copy in out_copies:
-        copy.wait()
 
 
 def pick(capacity, expert_count, who, blocks):
@@ -99,16 +79,8 @@
     return pl.pallas_call(
         functools.partial(pick_kernel, capacity, expert_count),
         out_shape=[jax.ShapeDtypeStruct(shape, BF16) for shape in (picked, picked, choice)],
-        in_specs=[IN_SMEM] + [ANYWHERE] * count,
-        out_specs=[ANYWHERE] * 3,
-        scratch_shapes=[
-            pltpu.VMEM((count, tok_count, row_width), BF16),
-            pltpu.VMEM(picked, BF16),
-            pltpu.VMEM(picked, BF16),
-            pltpu.VMEM(choice, BF16),
-            pltpu.SemaphoreType.DMA((count,)),
-            pltpu.SemaphoreType.DMA((3, count)),
-        ],
+        in_specs=[IN_SMEM] + [IN_VMEM] * count,
+        out_specs=[IN_VMEM] * 3,
         compiler_params=KERNEL,
         cost_estimate=BESIDE,
         name="pick",
@@ -119,7 +91,7 @@
     parts = refs[: 2 * groups]
     gate_up, down = refs[2 * groups : 2 * groups + 2]
     outs = refs[2 * groups + 2 : 4 * groups + 2]
-    rows, hidden, result, in_sem, out_sem = refs[4 * groups + 2 :]
+    rows, hidden, in_sem = refs[4 * groups + 2 :]
     row_count = rows.shape[0]
     hidden_width, model_width = down.shape
     tile = 256
@@ -156,15 +128,9 @@
         product = jnp.dot(
             hidden[...], down[:, pl.ds(at, tile)], preferred_element_type=jnp.float32
         )
-        result[:, pl.ds(at, tile)] = (product * gate_column).astype(BF16)
-    out_copies = [
-        pltpu.make_async_copy(result.at[pl.ds(starts[i], out.shape[0])], out, out_sem.at[i])
-        for i, out in enumerate(outs)
-    ]
-    for copy in out_copies:
-        copy.start()
-    for copy in out_copies:
-        copy.wait()
+        product = (product * gate_column).astype(BF16)
+        for i, out in enumerate(outs):
+            out[:, pl.ds(at, tile)] = product[starts[i] : starts[i + 1]]
 
 
 def expert_rows(expert_count, who, parts, weights_gu, weights_down):
@@ -176,12 +142,10 @@
         functools.partial(expert_kernel, expert_count, len(parts) // 2),
         out_shape=outs,
         in_specs=[IN_SMEM] + [ANYWHERE] * len(parts) + [IN_VMEM] * 2,
-        out_specs=[ANYWHERE] * len(parts),
+        out_specs=[IN_VMEM] * len(parts),
         scratch_shapes=[
             pltpu.VMEM((rows, row_width), BF16),
             pltpu.VMEM((rows, hidden_width), BF16),
-            pltpu.VMEM((rows, model_width), BF16),
-            pltpu.SemaphoreType.DMA((len(parts),)),
             pltpu.SemaphoreType.DMA((len(parts),)),
         ],
         compiler_params=KERNEL,
@@ -190,55 +154,24 @@
     )(who, *parts, weights_gu, weights_down)
 
 
-def put_kernel(choice_hbm, mine_hbm, other_hbm, *refs):
-    count, rows_two, _ = choice_hbm.shape
-    capacity = rows_two // 2
-    outs = refs[:count]
-    choice, rows, out, in_sem, out_sem = refs[count:]
-    copies, out_copies = [], []
-    for j in range(count):
+def put_kernel(choice, mine, other, *outs):
+    capacity = choice.shape[1] // 2
+    for j, out in enumerate(outs):
         here = pl.ds(j * capacity, capacity)
-        copies.append(
-            [
-                pltpu.make_async_copy(choice_hbm.at[j], choice.at[j], in_sem.at[0, j]),
-                pltpu.make_async_copy(
-                    mine_hbm.at[here], rows.at[j, pl.ds(0, capacity)], in_sem.at[1, j]
-                ),
-                pltpu.make_async_copy(
-                    other_hbm.at[here], rows.at[j, pl.ds(capacity, capacity)], in_sem.at[2, j]
-                ),
-            ]
-        )
-        for copy in copies[-1]:
-            copy.start()
-    for j in range(count):
-        for copy in copies[j]:
-            copy.wait()
-        out[j] = lax.dot_general(
-            choice[j], rows[j], (((0,), (0,)), ((), ())), preferred_element_type=jnp.float32
+        rows = jnp.concatenate([mine[here, :], other[here, :]], axis=0)
+        out[...] = lax.dot_general(
+            choice[j], rows, (((0,), (0,)), ((), ())), preferred_element_type=jnp.float32
         ).astype(BF16)
-        copy = pltpu.make_async_copy(out.at[j], outs[j], out_sem.at[j])
-        copy.start()
-        out_copies.append(copy)
-    for copy in out_copies:
-        copy.wait()
 
 
 def put(choice, mine, other):
-    count, rows_two, tok_count = choice.shape
+    count, _, tok_count = choice.shape
     model_width = mine.shape[1]
     return pl.pallas_call(
         put_kernel,
         out_shape=[jax.ShapeDtypeStruct((tok_count, model_width), BF16)] * count,
-        in_specs=[ANYWHERE] * 3,
-        out_specs=[ANYWHERE] * count,
-        scratch_shapes=[
-            pltpu.VMEM(choice.shape, BF16),
-            pltpu.VMEM((count, rows_two, model_width), BF16),
-            pltpu.VMEM((count, tok_count, model_width), BF16),
-            pltpu.SemaphoreType.DMA((3, count)),
-            pltpu.SemaphoreType.DMA((count,)),
-        ],
+        in_specs=[IN_VMEM] * 3,
+        out_specs=[IN_VMEM] * count,
         compiler_params=KERNEL,
         cost_estimate=BESIDE,
         name="put",
@@ -353,8 +286,6 @@
 SWAP_CORE = ("center", tuple((i, i ^ CORE) for i in range(8)))
 SWAP_Z = ("expert", ((0, 1), (1, 0), (2, 3), (3, 2)))
 MIDDLE = ("expert", ((1, 2), (2, 1)))
-OUTWARD = ("expert", ((1, 0), (2, 3)))
-INWARD = ("expert", ((0, 1), (3, 2)))
 
 
 def at_once(*sends, behind=()):
@@ -380,14 +311,14 @@
     b0 = rows
     bx0, by0, b1, c2 = at_once((SWAP_X, b0), (SWAP_Y, b0), (SWAP_Z, b0), (MIDDLE, b0))
     d0, by1, o2, c3 = at_once(
-        (SWAP_X, by0), (SWAP_Y, b1), (OUTWARD, c2), (MIDDLE, b1),
+        (SWAP_X, by0), (SWAP_Y, b1), (SWAP_Z, c2), (MIDDLE, b1),
         behind=(bx0, by0, b1, c2),
     )
     mine, other, choice = picked(b0, bx0, by0, b1)
     first = (mine, crossed(other), choice)
     b2 = c2 + o2
     bx2, by2, o3 = at_once(
-        (SWAP_X, b2), (SWAP_Y, b2), (OUTWARD, c3), behind=(d0, by1, c3, mine, beside)
+        (SWAP_X, b2), (SWAP_Y, b2), (SWAP_Z, c3), behind=(d0, by1, c3, mine, beside)
     )
     mine, other, choice = picked(d0, by1, b2)
     second = (mine, crossed(other), choice)
@@ -426,12 +357,12 @@
     sy2 = added(g3[1], rx_y2).astype(BF16)
     s3 = added(g3[2], rx_b3, ry_b3).astype(BF16)
     rx_b2, ry_b2, in_3 = at_once(
-        (SWAP_X, g3[0]), (SWAP_Y, sy2), (INWARD, s3), behind=(rz_x0, g2[0])
+        (SWAP_X, g3[0]), (SWAP_Y, sy2), (SWAP_Z, s3), behind=(rz_x0, g2[0])
     )
     sd0 = added(g2[0], rz_d0).astype(BF16)
     s2 = added(g2[2], rx_b2, ry_b2).astype(BF16)
     rx_y0, ry_b1, in_2, over_3 = at_once(
-        (SWAP_X, sd0), (SWAP_Y, g2[1]), (INWARD, s2),
+        (SWAP_X, sd0), (SWAP_Y, g2[1]), (SWAP_Z, s2),
         (MIDDLE, added(s3, in_3).astype(BF16)), behind=(rx_b2, ry_b2),
     )
     (sx0, sy0, s1, m2), (sum_own, *sums) = leave(

time: 196 us -> 189 us (0.964)
  Pallas kernels: 49.4 us -> 38.5 us
  waiting for transfers between devices: 65.2 us -> 71.5 us
  starting transfers between devices: 59.5 us -> 56.7 us
    ppermute x52, waiting for transfers between devices: 65.2 us -> 71.5 us  [at_once(): lax.ppermute(value, way[0], way[1])]
    pallas_call x5, Pallas kernels: 12.7 us -> 7.07 us  [pick(): pl.pallas_call(functools.partial(pick_kernel, capacity, expert_count), ou...]
    pallas_call x5, Pallas kernels: 7.9 us -> 3.11 us  [put(): pl.pallas_call(put_kernel, out_shape=[jax.ShapeDtypeStruct((tok_count, mo...]
    ppermute x52, starting transfers between devices: 59.5 us -> 56.7 us  [at_once(): lax.ppermute(value, way[0], way[1])]
  transfers between devices with their start and end apart: 52 -> 52, of which waited for: 26 -> 28; matrix products, arithmetic and copies ran while one was open for 5% -> 5% of each run, Pallas kernels for 24% -> 19%
where the time goes in v4:
time: 189 us
  waiting for transfers between devices  71.5 us (38%)
  starting transfers between devices  56.7 us (30%)
  Pallas kernels  38.5 us (20%)
  blocking collectives  9.35 us (5%)
  other arithmetic  8.07 us (4%)
  matrix products  2.75 us (1%)
    ppermute x52, waiting for transfers between devices, at_once(): lax.ppermute(value, way[0], way[1])  71.5 us
    ppermute x52, starting transfers between devices, at_once(): lax.ppermute(value, way[0], way[1])  56.7 us
    pallas_call x5, Pallas kernels, expert_rows(): pl.pallas_call(functools.partial(expert_kernel, expert_count, len(parts)...  25 us
    all_gather x1, blocking collectives, local(): shard_part = lax.all_gather(pooled, 'center', axis=0, tiled=True)  9.35 us
    pallas_call x5, Pallas kernels, pick(): pl.pallas_call(functools.partial(pick_kernel, capacity, expert_count), ou...  7.07 us
    reduce_sum x1, other arithmetic, local(): bank_norms = jnp.sum(bank_values * bank_values, axis=1)  5.08 us
  transfers between devices with their start and end apart: 52, of which 28 were waited for; matrix products, arithmetic and copies ran while one was open for 5% of the time, Pallas kernels for 19%

profile of v4, /device:TPU:0, one launch (start us, length us, event | category | flops | bytes accessed | tf_op | source)
XLA Modules:
  0.0 188.6 jit_solution(13769546152978732209)
XLA Ops:
  0.6 2.2 %enter.1.refs_0_ = bf16[128,2176]{1,0:T(8,128)(2,1)} custom-call(bf16[128,2048]{1,0:T(8,128)(2,1)} %refs_0_.1, s32[8,128]{1,0:T(8,128)} %bitcast.22, f32[8,128]{1,0:T(8,128)} %bitcast.23, s32[1,128]{1,0:T(1,128)} %refs_3_.1), custom_call_target="tpu_custom_call" | custom-call | flops 1000 | bytes 1000 | tf_op jit(solution)/shard_map/enter/pallas_call | solution.py:229
  3.7 5.9 %collective-permute-start.2 = (bf16[128,2176]{1,0:T(8,128)(2,1)}, bf16[128,2176]{1,0:T(8,128)(2,1)S(1)}, u32[]{:S(2)}, u32[]{:S(2)}) collective-permute-start(bf16[128,2176]{1,0:T(8,128)(2,1)} %enter.1.refs_0_), channel_id=1, source_target_pairs={{0,1},{1,0},{2,3},{3,2},{4,5},{5,4},{6,7},{7,6},{8,9},{9,8},{10,11... | collective-permute-start | bytes 1671176 | tf_op jit(solution)/shard_map/ppermute | solution.py:296
  9.5 1.5 collective-permute-start.1
  11.1 1.5 collective-permute-start
  12.6 9.5 %collective-permute-done.2.refs_3_ = bf16[128,2176]{1,0:T(8,128)(2,1)S(1)} collective-permute-done((bf16[128,2176]{1,0:T(8,128)(2,1)}, bf16[128,2176]{1,0:T(8,128)(2,1)S(1)}, u32[]{:S(2)}, u32[]{:S(2)}) %collective-permute-start.2) | collective-permute-done | bytes 557088 | tf_op jit(solution)/shard_map/ppermute | solution.py:296
  22.1 1.5 collective-permute-done.1.refs_2_
  25.5 2.1 %collective-permute-start.7 = (bf16[128,2176]{1,0:T(8,128)(2,1)S(1)}, bf16[128,2176]{1,0:T(8,128)(2,1)S(1)}, u32[]{:S(2)}, u32[]{:S(2)}) collective-permute-start(bf16[128,2176]{1,0:T(8,128)(2,1)S(1)} %collective-permute-done.5), channel_id=1, source_target_pairs={{0,1},{1,0},{2,3},{3,2},{4,5},{5,4},{6,7},{7,6},{8,9},{9,8},{10,11... | collective-permute-start | bytes 1671176 | tf_op jit(solution)/shard_map/ppermute | solution.py:296
  27.6 1.5 collective-permute-start.8
  29.6 5.1 %multiply_reduce_fusion = f32[2048]{0:T(1024)S(1)} fusion(bf16[2048,2048]{1,0:T(8,128)(2,1)} %param.13), kind=kLoop, calls=%fused_computation | loop fusion | flops 12580864 | bytes 8396800 | tf_op jit(solution)/shard_map/reduce_sum | solution.py:439
  34.7 1.5 pick.5
  36.2 2.2 %collective-permute-done.7 = bf16[128,2176]{1,0:T(8,128)(2,1)S(1)} collective-permute-done((bf16[128,2176]{1,0:T(8,128)(2,1)S(1)}, bf16[128,2176]{1,0:T(8,128)(2,1)S(1)}, u32[]{:S(2)}, u32[]{:S(2)}) %collective-permute-start.7) | collective-permute-done | bytes 557088 | tf_op jit(solution)/shard_map/ppermute | solution.py:296
  42.6 1.4 pick.6
  44.0 8.2 %collective-permute-done.10 = bf16[128,2176]{1,0:T(8,128)(2,1)S(1)} collective-permute-done((bf16[128,2176]{1,0:T(8,128)(2,1)S(1)}, bf16[128,2176]{1,0:T(8,128)(2,1)S(1)}, u32[]{:S(2)}, u32[]{:S(2)}) %collective-permute-start.10) | collective-permute-done | bytes 557088 | tf_op jit(solution)/shard_map/ppermute | solution.py:296
  52.4 1.5 collective-permute-done.11.refs_0_
  54.0 1.6 collective-permute-start.13
  56.2 2.0 %collective-permute-start.15 = (bf16[128,2176]{1,0:T(8,128)(2,1)S(1)}, bf16[128,2176]{1,0:T(8,128)(2,1)S(1)}, u32[]{:S(2)}, u32[]{:S(2)}) collective-permute-start(bf16[128,2176]{1,0:T(8,128)(2,1)S(1)} %collective-permute-done.refs_1_), channel_id=1, source_target_pairs={{0,1},{1,0},{2,3},{3,2},{4,5},{5,4},{6,7},{7,6},{8,9},{9,8},{10,11... | collective-permute-start | bytes 1671176 | tf_op jit(solution)/shard_map/ppermute | solution.py:296
  58.2 1.4 pick.8
  59.7 6.1 %expert_rows.5 = (bf16[256,2048]{1,0:T(8,128)(2,1)S(1)}, bf16[256,2048]{1,0:T(8,128)(2,1)S(1)}) custom-call(s32[2]{0:T(128)S(1)} %pad_add_fusion.who_ref, bf16[256,2176]{1,0:T(8,128)(2,1)S(1)} %get-tuple-element.95.refs_0_, bf16[256,2176]{1,0:T(8,128)(2,1)S(1)} %collective-permute-done.3.refs_1_, bf16[2048,1536]{1,0:T(8,128)(2,1)S(1)} %bitcast.10, ...), custom_call_target="tpu_custom_call" | custom-call | flops 1000 | bytes 1000 | tf_op jit(solution)/shard_map/expert_rows/pallas_call | solution.py:141
  65.9 1.8 collective-permute-start.16
  68.0 1.4 collective-permute-start.18
  71.0 4.7 %expert_rows.6 = (bf16[192,2048]{1,0:T(8,128)(2,1)S(1)}, bf16[192,2048]{1,0:T(8,128)(2,1)S(1)}) custom-call(s32[2]{0:T(128)S(1)} %pad_add_fusion.who_ref, bf16[192,2176]{1,0:T(8,128)(2,1)S(1)} %get-tuple-element.112.refs_0_, bf16[192,2176]{1,0:T(8,128)(2,1)S(1)} %collective-permute-done.19.refs_1_, bf16[2048,1536]{1,0:T(8,128)(2,1)S(1)} %bitcast.11, ...), custom_call_target="tpu_custom_call" | custom-call | flops 1000 | bytes 1000 | tf_op jit(solution)/shard_map/expert_rows/pallas_call | solution.py:141
  75.6 5.4 %collective-permute-done.16.refs_0_ = bf16[128,2176]{1,0:T(8,128)(2,1)S(1)} collective-permute-done((bf16[128,2176]{1,0:T(8,128)(2,1)S(1)}, bf16[128,2176]{1,0:T(8,128)(2,1)S(1)}, u32[]{:S(2)}, u32[]{:S(2)}) %collective-permute-start.16) | collective-permute-done | bytes 557088 | tf_op jit(solution)/shard_map/ppermute | solution.py:296
  81.2 1.4 pick.9
  83.1 4.7 %expert_rows.7 = (bf16[192,2048]{1,0:T(8,128)(2,1)S(1)}, bf16[192,2048]{1,0:T(8,128)(2,1)S(1)}) custom-call(s32[2]{0:T(128)S(1)} %pad_add_fusion.who_ref, bf16[192,2176]{1,0:T(8,128)(2,1)S(1)} %get-tuple-element.122.refs_0_, bf16[192,2176]{1,0:T(8,128)(2,1)S(1)} %collective-permute-done.20.refs_1_, bf16[2048,1536]{1,0:T(8,128)(2,1)S(1)} %bitcast.12, ...), custom_call_target="tpu_custom_call" | custom-call | flops 1000 | bytes 1000 | tf_op jit(solution)/shard_map/expert_rows/pallas_call | solution.py:141
  87.8 4.9 %expert_rows.8 = (bf16[192,2048]{1,0:T(8,128)(2,1)S(1)}, bf16[192,2048]{1,0:T(8,128)(2,1)S(1)}) custom-call(s32[2]{0:T(128)S(1)} %pad_add_fusion.who_ref, bf16[192,2176]{1,0:T(8,128)(2,1)S(1)} %get-tuple-element.127.refs_0_, bf16[192,2176]{1,0:T(8,128)(2,1)S(1)} %collective-permute-done.22.refs_1_, bf16[2048,1536]{1,0:T(8,128)(2,1)S(1)} %bitcast.13, ...), custom_call_target="tpu_custom_call" | custom-call | flops 1000 | bytes 1000 | tf_op jit(solution)/shard_map/expert_rows/pallas_call | solution.py:141
  95.7 1.5 collective-permute-start.25
  97.2 1.7 collective-permute-start.26
  98.9 1.6 collective-permute-start.27
  101.1 4.7 %expert_rows.9 = (bf16[192,2048]{1,0:T(8,128)(2,1)S(1)}, bf16[192,2048]{1,0:T(8,128)(2,1)S(1)}) custom-call(s32[2]{0:T(128)S(1)} %pad_add_fusion.who_ref, bf16[192,2176]{1,0:T(8,128)(2,1)S(1)} %get-tuple-element.152.refs_0_, bf16[192,2176]{1,0:T(8,128)(2,1)S(1)} %collective-permute-done.28.refs_1_, bf16[2048,1536]{1,0:T(8,128)(2,1)S(1)} %bitcast.14, ...), custom_call_target="tpu_custom_call" | custom-call | flops 1000 | bytes 1000 | tf_op jit(solution)/shard_map/expert_rows/pallas_call | solution.py:141
  106.6 3.1 %collective-permute-done.25 = bf16[128,2048]{1,0:T(8,128)(2,1)S(1)} collective-permute-done((bf16[128,2048]{1,0:T(8,128)(2,1)S(1)}, bf16[128,2048]{1,0:T(8,128)(2,1)S(1)}, u32[]{:S(2)}, u32[]{:S(2)}) %collective-permute-start.25) | collective-permute-done | bytes 524320 | tf_op jit(solution)/shard_map/ppermute | solution.py:296
  110.8 2.0 %collective-permute-done.27 = bf16[128,2048]{1,0:T(8,128)(2,1)S(1)} collective-permute-done((bf16[128,2048]{1,0:T(8,128)(2,1)S(1)}, bf16[128,2048]{1,0:T(8,128)(2,1)S(1)}, u32[]{:S(2)}, u32[]{:S(2)}) %collective-permute-start.27) | collective-permute-done | bytes 524320 | tf_op jit(solution)/shard_map/ppermute | solution.py:296
  112.8 1.7 collective-permute-start.31
  114.5 1.4 collective-permute-start.32
  115.9 1.7 collective-permute-start.29
  118.4 7.6 %collective-permute-done.31 = bf16[128,2048]{1,0:T(8,128)(2,1)S(1)} collective-permute-done((bf16[128,2048]{1,0:T(8,128)(2,1)S(1)}, bf16[128,2048]{1,0:T(8,128)(2,1)S(1)}, u32[]{:S(2)}, u32[]{:S(2)}) %collective-permute-start.31) | collective-permute-done | bytes 524320 | tf_op jit(solution)/shard_map/ppermute | solution.py:296
  128.5 1.7 collective-permute-start.35
  131.2 8.9 %collective-permute-done.35 = bf16[128,2048]{1,0:T(8,128)(2,1)S(1)} collective-permute-done((bf16[128,2048]{1,0:T(8,128)(2,1)S(1)}, bf16[128,2048]{1,0:T(8,128)(2,1)S(1)}, u32[]{:S(2)}, u32[]{:S(2)}) %collective-permute-start.35) | collective-permute-done | bytes 524320 | tf_op jit(solution)/shard_map/ppermute | solution.py:296
  140.3 1.7 collective-permute-done.33
  142.2 1.8 collective-permute-start.36
  145.2 3.2 %collective-permute-start.39 = (bf16[128,2048]{1,0:T(8,128)(2,1)S(1)}, bf16[128,2048]{1,0:T(8,128)(2,1)S(1)}, u32[]{:S(2)}, u32[]{:S(2)}) collective-permute-start(bf16[128,2048]{1,0:T(8,128)(2,1)S(1)} %add_convert_fusion.2.refs_12_), channel_id=1, source_target_pairs={{0,1},{1,0},{2,3},{3,2},{4,5},{5,4},{6,7},{7,6},{8,9},{9,8},{10,11... | collective-permute-start | bytes 1572872 | tf_op jit(solution)/shard_map/ppermute | solution.py:296
  148.5 4.3 %collective-permute-done.36.refs_6_ = bf16[128,2048]{1,0:T(8,128)(2,1)S(1)} collective-permute-done((bf16[128,2048]{1,0:T(8,128)(2,1)S(1)}, bf16[128,2048]{1,0:T(8,128)(2,1)S(1)}, u32[]{:S(2)}, u32[]{:S(2)}) %collective-permute-start.36) | collective-permute-done | bytes 524320 | tf_op jit(solution)/shard_map/ppermute | solution.py:296
  153.5 2.8 %collective-permute-done.39.refs_13_ = bf16[128,2048]{1,0:T(8,128)(2,1)S(1)} collective-permute-done((bf16[128,2048]{1,0:T(8,128)(2,1)S(1)}, bf16[128,2048]{1,0:T(8,128)(2,1)S(1)}, u32[]{:S(2)}, u32[]{:S(2)}) %collective-permute-start.39) | collective-permute-done | bytes 524320 | tf_op jit(solution)/shard_map/ppermute | solution.py:296
  159.2 1.7 collective-permute-start.46
  164.0 2.0 %collective-permute-start.42 = (bf16[128,2048]{1,0:T(8,128)(2,1)S(1)}, bf16[128,2048]{1,0:T(8,128)(2,1)S(1)}, u32[]{:S(2)}, u32[]{:S(2)}) collective-permute-start(bf16[128,2048]{1,0:T(8,128)(2,1)S(1)} %get-tuple-element.176), channel_id=1, source_target_pairs={{0,1},{1,0},{2,3},{3,2},{4,5},{5,4},{6,7},{7,6},{8,9},{9,8},{10,11... | collective-permute-start | bytes 1572872 | tf_op jit(solution)/shard_map/ppermute | solution.py:296
  166.9 9.4 %all_gather.3 = bf16[64,2048]{1,0:T(8,128)(2,1)S(1)} all-gather(bf16[8,2048]{1,0:T(8,128)(2,1)S(1)} %multiply_convert_fusion), channel_id=1, replica_groups=mesh['center'=8,'expert'=4] {'center'}, dimensions={0}, use_global_device_ids=true | all-gather | bytes 294912 | tf_op jit(solution)/shard_map/all_gather | solution.py:462
  176.4 2.8 %fusion.1 = f32[64]{0:T(128)S(1)} fusion(bf16[64,2048]{1,0:T(8,128)(2,1)S(1)} %all_gather.3, bf16[2048,2048]{1,0:T(8,128)(2,1)S(1)} %bitcast.21, f32[2048]{0:T(1024)S(1)} %multiply_reduce_fusion, f32[64]{0:T(128)S(1)} %multiply_reduce_fusion.1), kind=kOutput, calls=%fused_computation.3 | convolution fusion | flops 537395136 | bytes 8659456 | tf_op jit(solution)/shard_map/dot_general | solution.py:465
  182.5 1.5 collective-permute-start.50
  185.2 1.7 collective-permute-done.50
  (112 shorter events, 36.3 us)
Async XLA Ops:
  2.8 9.8 %collective-permute-start.5 = (bf16[128,2176]{1,0:T(8,128)(2,1)}, bf16[128,2176]{1,0:T(8,128)(2,1)S(1)}, u32[]{:S(2)}, u32[]{:S(2)}) collective-permute-start(bf16[128,2176]{1,0:T(8,128)(2,1)} %enter.1.refs_0_), channel_id=1, source_target_pairs={{1,2},{2,1},{5,6},{6,5},{9,10},{10,9},{13,14},{14,13},{17,18},{18,... | collective-permute-start | bytes 1671176 | tf_op jit(solution)/shard_map/ppermute | solution.py:296
  3.7 18.4 %collective-permute-start.2 = (bf16[128,2176]{1,0:T(8,128)(2,1)}, bf16[128,2176]{1,0:T(8,128)(2,1)S(1)}, u32[]{:S(2)}, u32[]{:S(2)}) collective-permute-start(bf16[128,2176]{1,0:T(8,128)(2,1)} %enter.1.refs_0_), channel_id=1, source_target_pairs={{0,1},{1,0},{2,3},{3,2},{4,5},{5,4},{6,7},{7,6},{8,9},{9,8},{10,11... | collective-permute-start | bytes 1671176 | tf_op jit(solution)/shard_map/ppermute | solution.py:296
  9.5 14.0 %collective-permute-start.1 = (bf16[128,2176]{1,0:T(8,128)(2,1)}, bf16[128,2176]{1,0:T(8,128)(2,1)S(1)}, u32[]{:S(2)}, u32[]{:S(2)}) collective-permute-start(bf16[128,2176]{1,0:T(8,128)(2,1)} %enter.1.refs_0_), channel_id=1, source_target_pairs={{0,16},{4,20},{8,24},{12,28},{16,0},{20,4},{24,8},{28,12},{1,17},{... | collective-permute-start | bytes 1671176 | tf_op jit(solution)/shard_map/ppermute | solution.py:296
  11.1 13.7 %collective-permute-start = (bf16[128,2176]{1,0:T(8,128)(2,1)}, bf16[128,2176]{1,0:T(8,128)(2,1)S(1)}, u32[]{:S(2)}, u32[]{:S(2)}) collective-permute-start(bf16[128,2176]{1,0:T(8,128)(2,1)} %enter.1.refs_0_), channel_id=1, source_target_pairs={{0,8},{4,12},{8,0},{12,4},{16,24},{20,28},{24,16},{28,20},{1,9},{5... | collective-permute-start | bytes 1671176 | tf_op jit(solution)/shard_map/ppermute | solution.py:296
  24.8 13.8 %collective-permute-start.6 = (bf16[128,2176]{1,0:T(8,128)(2,1)S(1)}, bf16[128,2176]{1,0:T(8,128)(2,1)S(1)}, u32[]{:S(2)}, u32[]{:S(2)}) collective-permute-start(bf16[128,2176]{1,0:T(8,128)(2,1)S(1)} %collective-permute-done.2.refs_3_), channel_id=1, source_target_pairs={{1,2},{2,1},{5,6},{6,5},{9,10},{10,9},{13,14},{14,13},{17,18},{18,... | collective-permute-start | bytes 1671176 | tf_op jit(solution)/shard_map/ppermute | solution.py:296
  25.5 12.9 %collective-permute-start.7 = (bf16[128,2176]{1,0:T(8,128)(2,1)S(1)}, bf16[128,2176]{1,0:T(8,128)(2,1)S(1)}, u32[]{:S(2)}, u32[]{:S(2)}) collective-permute-start(bf16[128,2176]{1,0:T(8,128)(2,1)S(1)} %collective-permute-done.5), channel_id=1, source_target_pairs={{0,1},{1,0},{2,3},{3,2},{4,5},{5,4},{6,7},{7,6},{8,9},{9,8},{10,11... | collective-permute-start | bytes 1671176 | tf_op jit(solution)/shard_map/ppermute | solution.py:296
  27.6 12.3 %collective-permute-start.8 = (bf16[128,2176]{1,0:T(8,128)(2,1)S(1)}, bf16[128,2176]{1,0:T(8,128)(2,1)S(1)}, u32[]{:S(2)}, u32[]{:S(2)}) collective-permute-start(bf16[128,2176]{1,0:T(8,128)(2,1)S(1)} %collective-permute-done.1.refs_2_), channel_id=1, source_target_pairs={{0,8},{4,12},{8,0},{12,4},{16,24},{20,28},{24,16},{28,20},{1,9},{5... | collective-permute-start | bytes 1671176 | tf_op jit(solution)/shard_map/ppermute | solution.py:296
  29.1 12.0 %collective-permute-start.9 = (bf16[128,2176]{1,0:T(8,128)(2,1)S(1)}, bf16[128,2176]{1,0:T(8,128)(2,1)S(1)}, u32[]{:S(2)}, u32[]{:S(2)}) collective-permute-start(bf16[128,2176]{1,0:T(8,128)(2,1)S(1)} %collective-permute-done.2.refs_3_), channel_id=1, source_target_pairs={{0,16},{4,20},{8,24},{12,28},{16,0},{20,4},{24,8},{28,12},{1,17},{... | collective-permute-start | bytes 1671176 | tf_op jit(solution)/shard_map/ppermute | solution.py:296
  41.1 11.1 %collective-permute-start.10 = (bf16[128,2176]{1,0:T(8,128)(2,1)S(1)}, bf16[128,2176]{1,0:T(8,128)(2,1)S(1)}, u32[]{:S(2)}, u32[]{:S(2)}) collective-permute-start(bf16[128,2176]{1,0:T(8,128)(2,1)S(1)} %collective-permute-done.6), channel_id=1, source_target_pairs={{0,1},{1,0},{2,3},{3,2},{4,5},{5,4},{6,7},{7,6},{8,9},{9,8},{10,11... | collective-permute-start | bytes 1671176 | tf_op jit(solution)/shard_map/ppermute | solution.py:296
  41.5 12.4 %collective-permute-start.11 = (bf16[128,2176]{1,0:T(8,128)(2,1)S(1)}, bf16[128,2176]{1,0:T(8,128)(2,1)S(1)}, u32[]{:S(2)}, u32[]{:S(2)}) collective-permute-start(bf16[128,2176]{1,0:T(8,128)(2,1)S(1)} %add.86.refs_2_), channel_id=1, source_target_pairs={{0,8},{4,12},{8,0},{12,4},{16,24},{20,28},{24,16},{28,20},{1,9},{5... | collective-permute-start | bytes 1671176 | tf_op jit(solution)/shard_map/ppermute | solution.py:296
  42.0 12.0 %collective-permute-start.12 = (bf16[128,2176]{1,0:T(8,128)(2,1)S(1)}, bf16[128,2176]{1,0:T(8,128)(2,1)S(1)}, u32[]{:S(2)}, u32[]{:S(2)}) collective-permute-start(bf16[128,2176]{1,0:T(8,128)(2,1)S(1)} %add.86.refs_2_), channel_id=1, source_target_pairs={{0,16},{4,20},{8,24},{12,28},{16,0},{20,4},{24,8},{28,12},{1,17},{... | collective-permute-start | bytes 1671176 | tf_op jit(solution)/shard_map/ppermute | solution.py:296
  42.6 17.1 %collective-permute-start.3 = (bf16[256,2176]{1,0:T(8,128)(2,1)S(1)}, bf16[256,2176]{1,0:T(8,128)(2,1)S(1)}, u32[]{:S(2)}, u32[]{:S(2)}) collective-permute-start(bf16[256,2176]{1,0:T(8,128)(2,1)S(1)} %get-tuple-element.96), channel_id=1, source_target_pairs={{0,4},{4,0},{8,12},{12,8},{16,20},{20,16},{24,28},{28,24},{1,5},{5... | collective-permute-start | bytes 3342344 | tf_op jit(solution)/shard_map/ppermute | solution.py:296
  54.0 11.9 %collective-permute-start.13 = (bf16[128,2176]{1,0:T(8,128)(2,1)S(1)}, bf16[128,2176]{1,0:T(8,128)(2,1)S(1)}, u32[]{:S(2)}, u32[]{:S(2)}) collective-permute-start(bf16[128,2176]{1,0:T(8,128)(2,1)S(1)} %add.87.refs_2_), channel_id=1, source_target_pairs={{0,8},{4,12},{8,0},{12,4},{16,24},{20,28},{24,16},{28,20},{1,9},{5... | collective-permute-start | bytes 1671176 | tf_op jit(solution)/shard_map/ppermute | solution.py:296
  55.6 10.3 %collective-permute-start.14 = (bf16[128,2176]{1,0:T(8,128)(2,1)S(1)}, bf16[128,2176]{1,0:T(8,128)(2,1)S(1)}, u32[]{:S(2)}, u32[]{:S(2)}) collective-permute-start(bf16[128,2176]{1,0:T(8,128)(2,1)S(1)} %add.87.refs_2_), channel_id=1, source_target_pairs={{0,16},{4,20},{8,24},{12,28},{16,0},{20,4},{24,8},{28,12},{1,17},{... | collective-permute-start | bytes 1671176 | tf_op jit(solution)/shard_map/ppermute | solution.py:296
  56.2 9.7 %collective-permute-start.15 = (bf16[128,2176]{1,0:T(8,128)(2,1)S(1)}, bf16[128,2176]{1,0:T(8,128)(2,1)S(1)}, u32[]{:S(2)}, u32[]{:S(2)}) collective-permute-start(bf16[128,2176]{1,0:T(8,128)(2,1)S(1)} %collective-permute-done.refs_1_), channel_id=1, source_target_pairs={{0,1},{1,0},{2,3},{3,2},{4,5},{5,4},{6,7},{7,6},{8,9},{9,8},{10,11... | collective-permute-start | bytes 1671176 | tf_op jit(solution)/shard_map/ppermute | solution.py:296
  59.6 11.3 %collective-permute-start.19 = (bf16[192,2176]{1,0:T(8,128)(2,1)S(1)}, bf16[192,2176]{1,0:T(8,128)(2,1)S(1)}, u32[]{:S(2)}, u32[]{:S(2)}) collective-permute-start(bf16[192,2176]{1,0:T(8,128)(2,1)S(1)} %get-tuple-element.116), channel_id=1, source_target_pairs={{0,4},{4,0},{8,12},{12,8},{16,20},{20,16},{24,28},{28,24},{1,5},{5... | collective-permute-start | bytes 2506760 | tf_op jit(solution)/shard_map/ppermute | solution.py:296
  65.9 15.1 %collective-permute-start.16 = (bf16[128,2176]{1,0:T(8,128)(2,1)S(1)}, bf16[128,2176]{1,0:T(8,128)(2,1)S(1)}, u32[]{:S(2)}, u32[]{:S(2)}) collective-permute-start(bf16[128,2176]{1,0:T(8,128)(2,1)S(1)} %collective-permute-done.8.refs_0_), channel_id=1, source_target_pairs={{0,1},{1,0},{2,3},{3,2},{4,5},{5,4},{6,7},{7,6},{8,9},{9,8},{10,11... | collective-permute-start | bytes 1671176 | tf_op jit(solution)/shard_map/ppermute | solution.py:296
  67.7 13.3 %collective-permute-start.17 = (bf16[128,2176]{1,0:T(8,128)(2,1)S(1)}, bf16[128,2176]{1,0:T(8,128)(2,1)S(1)}, u32[]{:S(2)}, u32[]{:S(2)}) collective-permute-start(bf16[128,2176]{1,0:T(8,128)(2,1)S(1)} %collective-permute-done.12.refs_1_), channel_id=1, source_target_pairs={{0,8},{4,12},{8,0},{12,4},{16,24},{20,28},{24,16},{28,20},{1,9},{5... | collective-permute-start | bytes 1671176 | tf_op jit(solution)/shard_map/ppermute | solution.py:296
  68.0 13.1 %collective-permute-start.18 = (bf16[128,2176]{1,0:T(8,128)(2,1)S(1)}, bf16[128,2176]{1,0:T(8,128)(2,1)S(1)}, u32[]{:S(2)}, u32[]{:S(2)}) collective-permute-start(bf16[128,2176]{1,0:T(8,128)(2,1)S(1)} %collective-permute-done.13.refs_0_), channel_id=1, source_target_pairs={{0,16},{4,20},{8,24},{12,28},{16,0},{20,4},{24,8},{28,12},{1,17},{... | collective-permute-start | bytes 1671176 | tf_op jit(solution)/shard_map/ppermute | solution.py:296
  70.9 12.3 %collective-permute-start.20 = (bf16[192,2176]{1,0:T(8,128)(2,1)S(1)}, bf16[192,2176]{1,0:T(8,128)(2,1)S(1)}, u32[]{:S(2)}, u32[]{:S(2)}) collective-permute-start(bf16[192,2176]{1,0:T(8,128)(2,1)S(1)} %get-tuple-element.123), channel_id=1, source_target_pairs={{0,4},{4,0},{8,12},{12,8},{16,20},{20,16},{24,28},{28,24},{1,5},{5... | collective-permute-start | bytes 2506760 | tf_op jit(solution)/shard_map/ppermute | solution.py:296
  82.5 5.3 %collective-permute-start.22 = (bf16[192,2176]{1,0:T(8,128)(2,1)S(1)}, bf16[192,2176]{1,0:T(8,128)(2,1)S(1)}, u32[]{:S(2)}, u32[]{:S(2)}) collective-permute-start(bf16[192,2176]{1,0:T(8,128)(2,1)S(1)} %get-tuple-element.128), channel_id=1, source_target_pairs={{0,4},{4,0},{8,12},{12,8},{16,20},{20,16},{24,28},{28,24},{1,5},{5... | collective-permute-start | bytes 2506760 | tf_op jit(solution)/shard_map/ppermute | solution.py:296
  82.6 11.2 %collective-permute-start.24 = (bf16[192,2048]{1,0:T(8,128)(2,1)S(1)}, bf16[192,2048]{1,0:T(8,128)(2,1)S(1)}, u32[]{:S(2)}, u32[]{:S(2)}) collective-permute-start(bf16[192,2048]{1,0:T(8,128)(2,1)S(1)} %get-tuple-element.132), channel_id=1, source_target_pairs={{0,4},{4,0},{8,12},{12,8},{16,20},{20,16},{24,28},{28,24},{1,5},{5... | collective-permute-start | bytes 2359304 | tf_op jit(solution)/shard_map/ppermute | solution.py:296
  92.8 12.9 %collective-permute-start.4 = (bf16[256,2048]{1,0:T(8,128)(2,1)S(1)}, bf16[256,2048]{1,0:T(8,128)(2,1)S(1)}, u32[]{:S(2)}, u32[]{:S(2)}) collective-permute-start(bf16[256,2048]{1,0:T(8,128)(2,1)S(1)} %get-tuple-element.98), channel_id=1, source_target_pairs={{0,4},{4,0},{8,12},{12,8},{16,20},{20,16},{24,28},{28,24},{1,5},{5... | collective-permute-start | bytes 3145736 | tf_op jit(solution)/shard_map/ppermute | solution.py:296
  93.3 7.8 %collective-permute-start.28 = (bf16[192,2176]{1,0:T(8,128)(2,1)S(1)}, bf16[192,2176]{1,0:T(8,128)(2,1)S(1)}, u32[]{:S(2)}, u32[]{:S(2)}) collective-permute-start(bf16[192,2176]{1,0:T(8,128)(2,1)S(1)} %get-tuple-element.153), channel_id=1, source_target_pairs={{0,4},{4,0},{8,12},{12,8},{16,20},{20,16},{24,28},{28,24},{1,5},{5... | collective-permute-start | bytes 2506760 | tf_op jit(solution)/shard_map/ppermute | solution.py:296
  93.4 5.5 %collective-permute-start.21 = (bf16[192,2048]{1,0:T(8,128)(2,1)S(1)}, bf16[192,2048]{1,0:T(8,128)(2,1)S(1)}, u32[]{:S(2)}, u32[]{:S(2)}) collective-permute-start(bf16[192,2048]{1,0:T(8,128)(2,1)S(1)} %get-tuple-element.125), channel_id=1, source_target_pairs={{0,4},{4,0},{8,12},{12,8},{16,20},{20,16},{24,28},{28,24},{1,5},{5... | collective-permute-start | bytes 2359304 | tf_op jit(solution)/shard_map/ppermute | solution.py:296
  95.7 14.0 %collective-permute-start.25 = (bf16[128,2048]{1,0:T(8,128)(2,1)S(1)}, bf16[128,2048]{1,0:T(8,128)(2,1)S(1)}, u32[]{:S(2)}, u32[]{:S(2)}) collective-permute-start(bf16[128,2048]{1,0:T(8,128)(2,1)S(1)} %get-tuple-element.148), channel_id=1, source_target_pairs={{0,16},{4,20},{8,24},{12,28},{16,0},{20,4},{24,8},{28,12},{1,17},{... | collective-permute-start | bytes 1572872 | tf_op jit(solution)/shard_map/ppermute | solution.py:296
  97.2 13.7 %collective-permute-start.26 = (bf16[128,2048]{1,0:T(8,128)(2,1)S(1)}, bf16[128,2048]{1,0:T(8,128)(2,1)S(1)}, u32[]{:S(2)}, u32[]{:S(2)}) collective-permute-start(bf16[128,2048]{1,0:T(8,128)(2,1)S(1)} %get-tuple-element.151), channel_id=1, source_target_pairs={{0,8},{4,12},{8,0},{12,4},{16,24},{20,28},{24,16},{28,20},{1,9},{5... | collective-permute-start | bytes 1572872 | tf_op jit(solution)/shard_map/ppermute | solution.py:296
  98.9 14.0 %collective-permute-start.27 = (bf16[128,2048]{1,0:T(8,128)(2,1)S(1)}, bf16[128,2048]{1,0:T(8,128)(2,1)S(1)}, u32[]{:S(2)}, u32[]{:S(2)}) collective-permute-start(bf16[128,2048]{1,0:T(8,128)(2,1)S(1)} %get-tuple-element.138), channel_id=1, source_target_pairs={{0,1},{1,0},{2,3},{3,2},{4,5},{5,4},{6,7},{7,6},{8,9},{9,8},{10,11... | collective-permute-start | bytes 1572872 | tf_op jit(solution)/shard_map/ppermute | solution.py:296
  105.8 12.0 %collective-permute-start.30 = (bf16[192,2048]{1,0:T(8,128)(2,1)S(1)}, bf16[192,2048]{1,0:T(8,128)(2,1)S(1)}, u32[]{:S(2)}, u32[]{:S(2)}) collective-permute-start(bf16[192,2048]{1,0:T(8,128)(2,1)S(1)} %get-tuple-element.158), channel_id=1, source_target_pairs={{0,4},{4,0},{8,12},{12,8},{16,20},{20,16},{24,28},{28,24},{1,5},{5... | collective-permute-start | bytes 2359304 | tf_op jit(solution)/shard_map/ppermute | solution.py:296
  112.8 13.1 %collective-permute-start.31 = (bf16[128,2048]{1,0:T(8,128)(2,1)S(1)}, bf16[128,2048]{1,0:T(8,128)(2,1)S(1)}, u32[]{:S(2)}, u32[]{:S(2)}) collective-permute-start(bf16[128,2048]{1,0:T(8,128)(2,1)S(1)} %add_convert_fusion.6), channel_id=1, source_target_pairs={{0,8},{4,12},{8,0},{12,4},{16,24},{20,28},{24,16},{28,20},{1,9},{5... | collective-permute-start | bytes 1572872 | tf_op jit(solution)/shard_map/ppermute | solution.py:296
  114.5 12.9 %collective-permute-start.32 = (bf16[128,2048]{1,0:T(8,128)(2,1)S(1)}, bf16[128,2048]{1,0:T(8,128)(2,1)S(1)}, u32[]{:S(2)}, u32[]{:S(2)}) collective-permute-start(bf16[128,2048]{1,0:T(8,128)(2,1)S(1)} %get-tuple-element.165), channel_id=1, source_target_pairs={{0,16},{4,20},{8,24},{12,28},{16,0},{20,4},{24,8},{28,12},{1,17},{... | collective-permute-start | bytes 1572872 | tf_op jit(solution)/shard_map/ppermute | solution.py:296
  115.9 12.6 %collective-permute-start.29 = (bf16[128,2048]{1,0:T(8,128)(2,1)S(1)}, bf16[128,2048]{1,0:T(8,128)(2,1)S(1)}, u32[]{:S(2)}, u32[]{:S(2)}) collective-permute-start(bf16[128,2048]{1,0:T(8,128)(2,1)S(1)} %get-tuple-element.155), channel_id=1, source_target_pairs={{0,1},{1,0},{2,3},{3,2},{4,5},{5,4},{6,7},{7,6},{8,9},{9,8},{10,11... | collective-permute-start | bytes 1572872 | tf_op jit(solution)/shard_map/ppermute | solution.py:296
  128.5 11.7 %collective-permute-start.35 = (bf16[128,2048]{1,0:T(8,128)(2,1)S(1)}, bf16[128,2048]{1,0:T(8,128)(2,1)S(1)}, u32[]{:S(2)}, u32[]{:S(2)}) collective-permute-start(bf16[128,2048]{1,0:T(8,128)(2,1)S(1)} %add_convert_fusion.3), channel_id=1, source_target_pairs={{0,1},{1,0},{2,3},{3,2},{4,5},{5,4},{6,7},{7,6},{8,9},{9,8},{10,11... | collective-permute-start | bytes 1572872 | tf_op jit(solution)/shard_map/ppermute | solution.py:296
  130.2 11.8 %collective-permute-start.33 = (bf16[128,2048]{1,0:T(8,128)(2,1)S(1)}, bf16[128,2048]{1,0:T(8,128)(2,1)S(1)}, u32[]{:S(2)}, u32[]{:S(2)}) collective-permute-start(bf16[128,2048]{1,0:T(8,128)(2,1)S(1)} %get-tuple-element.166), channel_id=1, source_target_pairs={{0,8},{4,12},{8,0},{12,4},{16,24},{20,28},{24,16},{28,20},{1,9},{5... | collective-permute-start | bytes 1572872 | tf_op jit(solution)/shard_map/ppermute | solution.py:296
  130.5 11.5 %collective-permute-start.34 = (bf16[128,2048]{1,0:T(8,128)(2,1)S(1)}, bf16[128,2048]{1,0:T(8,128)(2,1)S(1)}, u32[]{:S(2)}, u32[]{:S(2)}) collective-permute-start(bf16[128,2048]{1,0:T(8,128)(2,1)S(1)} %add_convert_fusion.4), channel_id=1, source_target_pairs={{0,16},{4,20},{8,24},{12,28},{16,0},{20,4},{24,8},{28,12},{1,17},{... | collective-permute-start | bytes 1572872 | tf_op jit(solution)/shard_map/ppermute | solution.py:296
  142.2 10.6 %collective-permute-start.36 = (bf16[128,2048]{1,0:T(8,128)(2,1)S(1)}, bf16[128,2048]{1,0:T(8,128)(2,1)S(1)}, u32[]{:S(2)}, u32[]{:S(2)}) collective-permute-start(bf16[128,2048]{1,0:T(8,128)(2,1)S(1)} %add_convert_fusion.5), channel_id=1, source_target_pairs={{0,8},{4,12},{8,0},{12,4},{16,24},{20,28},{24,16},{28,20},{1,9},{5... | collective-permute-start | bytes 1572872 | tf_op jit(solution)/shard_map/ppermute | solution.py:296
  144.0 9.5 %collective-permute-start.37 = (bf16[128,2048]{1,0:T(8,128)(2,1)S(1)}, bf16[128,2048]{1,0:T(8,128)(2,1)S(1)}, u32[]{:S(2)}, u32[]{:S(2)}) collective-permute-start(bf16[128,2048]{1,0:T(8,128)(2,1)S(1)} %get-tuple-element.171), channel_id=1, source_target_pairs={{0,16},{4,20},{8,24},{12,28},{16,0},{20,4},{24,8},{28,12},{1,17},{... | collective-permute-start | bytes 1572872 | tf_op jit(solution)/shard_map/ppermute | solution.py:296
  144.5 9.0 %collective-permute-start.38 = (bf16[128,2048]{1,0:T(8,128)(2,1)S(1)}, bf16[128,2048]{1,0:T(8,128)(2,1)S(1)}, u32[]{:S(2)}, u32[]{:S(2)}) collective-permute-start(bf16[128,2048]{1,0:T(8,128)(2,1)S(1)} %add_convert_fusion.1), channel_id=1, source_target_pairs={{1,2},{2,1},{5,6},{6,5},{9,10},{10,9},{13,14},{14,13},{17,18},{18,... | collective-permute-start | bytes 1572872 | tf_op jit(solution)/shard_map/ppermute | solution.py:296
  145.2 11.1 %collective-permute-start.39 = (bf16[128,2048]{1,0:T(8,128)(2,1)S(1)}, bf16[128,2048]{1,0:T(8,128)(2,1)S(1)}, u32[]{:S(2)}, u32[]{:S(2)}) collective-permute-start(bf16[128,2048]{1,0:T(8,128)(2,1)S(1)} %add_convert_fusion.2.refs_12_), channel_id=1, source_target_pairs={{0,1},{1,0},{2,3},{3,2},{4,5},{5,4},{6,7},{7,6},{8,9},{9,8},{10,11... | collective-permute-start | bytes 1572872 | tf_op jit(solution)/shard_map/ppermute | solution.py:296
  157.4 5.4 %collective-permute-start.44 = (f32[8,2048]{1,0:T(8,128)S(1)}, f32[8,2048]{1,0:T(8,128)S(1)}, u32[]{:S(2)}, u32[]{:S(2)}) collective-permute-start(f32[8,2048]{1,0:T(8,128)S(1)} %get-tuple-element.179), channel_id=1, source_target_pairs={{0,8},{4,12},{8,0},{12,4},{16,24},{20,28},{24,16},{28,20},{1,9},{5... | collective-permute-start | bytes 196616 | tf_op jit(solution)/shard_map/ppermute | solution.py:296
  158.4 5.6 %collective-permute-start.45 = (f32[8,2048]{1,0:T(8,128)S(1)}, f32[8,2048]{1,0:T(8,128)S(1)}, u32[]{:S(2)}, u32[]{:S(2)}) collective-permute-start(f32[8,2048]{1,0:T(8,128)S(1)} %get-tuple-element.180), channel_id=1, source_target_pairs={{0,16},{4,20},{8,24},{12,28},{16,0},{20,4},{24,8},{28,12},{1,17},{... | collective-permute-start | bytes 196616 | tf_op jit(solution)/shard_map/ppermute | solution.py:296
  159.2 6.7 %collective-permute-start.46 = (f32[8,2048]{1,0:T(8,128)S(1)}, f32[8,2048]{1,0:T(8,128)S(1)}, u32[]{:S(2)}, u32[]{:S(2)}) collective-permute-start(f32[8,2048]{1,0:T(8,128)S(1)} %get-tuple-element.181), channel_id=1, source_target_pairs={{0,1},{1,0},{2,3},{3,2},{4,5},{5,4},{6,7},{7,6},{8,9},{9,8},{10,11... | collective-permute-start | bytes 196616 | tf_op jit(solution)/shard_map/ppermute | solution.py:296
  161.0 5.7 %collective-permute-start.47 = (f32[8,2048]{1,0:T(8,128)S(1)}, f32[8,2048]{1,0:T(8,128)S(1)}, u32[]{:S(2)}, u32[]{:S(2)}) collective-permute-start(f32[8,2048]{1,0:T(8,128)S(1)} %get-tuple-element.182), channel_id=1, source_target_pairs={{1,2},{2,1},{5,6},{6,5},{9,10},{10,9},{13,14},{14,13},{17,18},{18,... | collective-permute-start | bytes 196616 | tf_op jit(solution)/shard_map/ppermute | solution.py:296
  161.6 17.5 %collective-permute-start.40 = (bf16[128,2048]{1,0:T(8,128)(2,1)S(1)}, bf16[128,2048]{1,0:T(8,128)(2,1)S(1)}, u32[]{:S(2)}, u32[]{:S(2)}) collective-permute-start(bf16[128,2048]{1,0:T(8,128)(2,1)S(1)} %get-tuple-element.174), channel_id=1, source_target_pairs={{0,8},{4,12},{8,0},{12,4},{16,24},{20,28},{24,16},{28,20},{1,9},{5... | collective-permute-start | bytes 1572872 | tf_op jit(solution)/shard_map/ppermute | solution.py:296
  162.8 16.4 %collective-permute-start.41 = (bf16[128,2048]{1,0:T(8,128)(2,1)S(1)}, bf16[128,2048]{1,0:T(8,128)(2,1)S(1)}, u32[]{:S(2)}, u32[]{:S(2)}) collective-permute-start(bf16[128,2048]{1,0:T(8,128)(2,1)S(1)} %get-tuple-element.175), channel_id=1, source_target_pairs={{0,16},{4,20},{8,24},{12,28},{16,0},{20,4},{24,8},{28,12},{1,17},{... | collective-permute-start | bytes 1572872 | tf_op jit(solution)/shard_map/ppermute | solution.py:296
  164.0 15.2 %collective-permute-start.42 = (bf16[128,2048]{1,0:T(8,128)(2,1)S(1)}, bf16[128,2048]{1,0:T(8,128)(2,1)S(1)}, u32[]{:S(2)}, u32[]{:S(2)}) collective-permute-start(bf16[128,2048]{1,0:T(8,128)(2,1)S(1)} %get-tuple-element.176), channel_id=1, source_target_pairs={{0,1},{1,0},{2,3},{3,2},{4,5},{5,4},{6,7},{7,6},{8,9},{9,8},{10,11... | collective-permute-start | bytes 1572872 | tf_op jit(solution)/shard_map/ppermute | solution.py:296
  166.0 13.2 %collective-permute-start.43 = (bf16[128,2048]{1,0:T(8,128)(2,1)S(1)}, bf16[128,2048]{1,0:T(8,128)(2,1)S(1)}, u32[]{:S(2)}, u32[]{:S(2)}) collective-permute-start(bf16[128,2048]{1,0:T(8,128)(2,1)S(1)} %get-tuple-element.177), channel_id=1, source_target_pairs={{1,2},{2,1},{5,6},{6,5},{9,10},{10,9},{13,14},{14,13},{17,18},{18,... | collective-permute-start | bytes 1572872 | tf_op jit(solution)/shard_map/ppermute | solution.py:296
  182.5 4.4 %collective-permute-start.50 = (f32[64]{0:T(128)S(1)}, f32[64]{0:T(128)S(1)}, u32[]{:S(2)}, u32[]{:S(2)}) collective-permute-start(f32[64]{0:T(128)S(1)} %fusion.1), channel_id=1, source_target_pairs={{0,24},{4,28},{8,16},{12,20},{16,8},{20,12},{24,0},{28,4},{1,25},{... | collective-permute-start | bytes 776 | tf_op jit(solution)/shard_map/ppermute | solution.py:296
  (10 other events, 254.8 us)

commit v5 on v4

--- a/solution.py
+++ b/solution.py
@@ -87,27 +87,23 @@
     )(who, *blocks)
 
 
-def expert_kernel(expert_count, groups, who_ref, *refs):
-    parts = refs[: 2 * groups]
-    gate_up, down = refs[2 * groups : 2 * groups + 2]
-    outs = refs[2 * groups + 2 : 4 * groups + 2]
-    rows, hidden, in_sem = refs[4 * groups + 2 :]
-    row_count = rows.shape[0]
+def expert_kernel(expert_count, count, who_ref, *refs):
+    parts = refs[:count]
+    gate_up, down = refs[count : count + 2]
+    outs = refs[count + 2 : 2 * count + 2]
+    hidden = refs[2 * count + 2]
+    row_count = hidden.shape[0]
     hidden_width, model_width = down.shape
     tile = 256
     hidden_tiles, model_tiles = hidden_width // tile, model_width // tile
     starts = [0]
     for part in parts:
         starts.append(starts[-1] + part.shape[0])
-    in_copies = [
-        pltpu.make_async_copy(part, rows.at[pl.ds(starts[i], part.shape[0])], in_sem.at[i])
-        for i, part in enumerate(parts)
-    ]
-    for copy in in_copies:
-        copy.start()
-    for copy in in_copies:
-        copy.wait()
-    tail = rows[:, pl.ds(model_width, LANES)].astype(jnp.float32)
+
+    def columns(at, size):
+        return jnp.concatenate([part[:, pl.ds(at, size)] for part in parts], axis=0)
+
+    tail = columns(model_width, LANES).astype(jnp.float32)
     gate_column = jnp.sum(
         jnp.where(gate_lanes((row_count, LANES), who_ref[0], expert_count), tail, 0.0),
         axis=1,
@@ -115,7 +111,7 @@
     )
     for step in range(hidden_tiles):
         at = step * tile
-        values = rows[:, pl.ds(0, model_width)]
+        values = columns(0, model_width)
         gate = jnp.dot(values, gate_up[:, pl.ds(at, tile)], preferred_element_type=jnp.float32)
         up = jnp.dot(
             values,
@@ -134,20 +130,15 @@
 
 
 def expert_rows(expert_count, who, parts, weights_gu, weights_down):
-    row_width = parts[0].shape[1]
     hidden_width, model_width = weights_down.shape
     rows = sum(part.shape[0] for part in parts)
     outs = [jax.ShapeDtypeStruct((part.shape[0], model_width), BF16) for part in parts]
     return pl.pallas_call(
-        functools.partial(expert_kernel, expert_count, len(parts) // 2),
+        functools.partial(expert_kernel, expert_count, len(parts)),
         out_shape=outs,
-        in_specs=[IN_SMEM] + [ANYWHERE] * len(parts) + [IN_VMEM] * 2,
+        in_specs=[IN_SMEM] + [IN_VMEM] * (len(parts) + 2),
         out_specs=[IN_VMEM] * len(parts),
-        scratch_shapes=[
-            pltpu.VMEM((rows, row_width), BF16),
-            pltpu.VMEM((rows, hidden_width), BF16),
-            pltpu.SemaphoreType.DMA((len(parts),)),
-        ],
+        scratch_shapes=[pltpu.VMEM((rows, hidden_width), BF16)],
         compiler_params=KERNEL,
         cost_estimate=BESIDE,
         name="expert_rows",
@@ -303,9 +294,12 @@
     def crossed(values):
         return at_once((SWAP_CORE, values))[0]
 
+    def results(*parts):
+        return expert_rows(expert_count, who, parts, weights_gu, weights_down)
+
     def worked(*groups):
         parts = [part for mine, other, _ in groups for part in (mine, other)]
-        done = expert_rows(expert_count, who, parts, weights_gu, weights_down)
+        done = results(*parts)
         return [(groups[i][2], done[2 * i], done[2 * i + 1]) for i in range(len(groups))]
 
     b0 = rows
@@ -335,24 +329,24 @@
     mine, other, choice = picked(bx3, by3, bx1)
     fourth = (mine, crossed(other), choice)
     (third,) = worked(third)
-    held = lax.optimization_barrier((d1, d2, d3, mine, third[1]))
+    (fourth_mine,) = results(lax.optimization_barrier((fourth[0], third[1]))[0])
+    held = lax.optimization_barrier((d1, d2, d3, mine, third[1], fourth_mine))
     mine, other, choice = picked(*held[:3])
-    fourth = (lax.optimization_barrier((fourth[0], mine))[0], *fourth[1:])
-    (fourth,) = worked(fourth)
-    last = (lax.optimization_barrier((mine, fourth[1]))[0], crossed(other), choice)
-    (last,) = worked(last)
-    g3 = put(*lax.optimization_barrier((third[0], third[1], crossed(third[2]), last[1]))[:3])
-    g5 = put(last[0], last[1], lax.optimization_barrier((crossed(last[2]), g3[0]))[0])
+    last_mine, last_other = results(mine)[0], crossed(other)
+    (last_other,) = results(lax.optimization_barrier((last_other, last_mine))[0])
+    (fourth_other,) = results(lax.optimization_barrier((fourth[1], last_other))[0])
+    g5 = put(choice, last_mine, crossed(last_other))
     rx_y2, ry_x3, rz_d0 = at_once((SWAP_X, g5[1]), (SWAP_Y, g5[2]), (SWAP_Z, g5[0]))
-    crossed_fourth = crossed(fourth[2])
-    g4 = put(*lax.optimization_barrier((fourth[0], fourth[1], crossed_fourth, g5[0]))[:3])
+    fourth_other = crossed(fourth_other)
+    g3 = put(*lax.optimization_barrier((third[0], third[1], crossed(third[2]), g5[0]))[:3])
+    g4 = put(*lax.optimization_barrier((fourth[2], fourth_mine, fourth_other, g5[0]))[:3])
     second = (lax.optimization_barrier((second[0], g5[0]))[0], *second[1:])
     (second,) = worked(second)
     g2 = put(second[0], second[1], crossed(second[2]))
     g1 = put(*lax.optimization_barrier((first[0], first[1], crossed(first[2]), g4[0]))[:3])
     sx3 = added(g4[0], ry_x3).astype(BF16)
     rx_b3, ry_b3, rz_x0 = at_once(
-        (SWAP_X, sx3), (SWAP_Y, g4[1]), (SWAP_Z, g4[2]), behind=(rx_y2, rz_d0, g4[0], second[1], g1[0])
+        (SWAP_X, sx3), (SWAP_Y, g4[1]), (SWAP_Z, g4[2]), behind=(rx_y2, rz_d0, g4[0], second[1], g1[0], g3[0])
     )
     sy2 = added(g3[1], rx_y2).astype(BF16)
     s3 = added(g3[2], rx_b3, ry_b3).astype(BF16)

time: 189 us -> 184 us (0.974)
  waiting for transfers between devices: 71.5 us -> 66.6 us
    ppermute x52, waiting for transfers between devices: 71.5 us -> 66.6 us  [at_once(): lax.ppermute(value, way[0], way[1])]
    pallas_call x5 -> x7, Pallas kernels: 25 us -> 24.8 us  [expert_rows(): pl.pallas_call(functools.partial(expert_kernel, expert_count, len(parts))...]
  transfers between devices with their start and end apart: 52 -> 52, of which waited for: 28 -> 28; matrix products, arithmetic and copies ran while one was open for 5% -> 5% of each run, Pallas kernels for 19% -> 18%
where the time goes in v5:
time: 184 us
  waiting for transfers between devices  66.6 us (36%)
  starting transfers between devices  56.9 us (31%)
  Pallas kernels  38.2 us (21%)
  blocking collectives  9.58 us (5%)
  other arithmetic  8.26 us (4%)
  matrix products  2.75 us (1%)
    ppermute x52, waiting for transfers between devices, at_once(): lax.ppermute(value, way[0], way[1])  66.6 us
    ppermute x52, starting transfers between devices, at_once(): lax.ppermute(value, way[0], way[1])  56.9 us
    pallas_call x7, Pallas kernels, expert_rows(): pl.pallas_call(functools.partial(expert_kernel, expert_count, len(parts))...  24.8 us
    all_gather x1, blocking collectives, local(): shard_part = lax.all_gather(pooled, 'center', axis=0, tiled=True)  9.58 us
    pallas_call x5, Pallas kernels, pick(): pl.pallas_call(functools.partial(pick_kernel, capacity, expert_count), ou...  7.08 us
    reduce_sum x1, other arithmetic, local(): bank_norms = jnp.sum(bank_values * bank_values, axis=1)  5.08 us
  transfers between devices with their start and end apart: 52, of which 28 were waited for; matrix products, arithmetic and copies ran while one was open for 5% of the time, Pallas kernels for 18%

profile of v5, /device:TPU:0, one launch (start us, length us, event | category | flops | bytes accessed | tf_op | source)
XLA Modules:
  0.0 184.1 jit_solution(17929984565706351291)
XLA Ops:
  0.6 2.2 %enter.1.refs_0_ = bf16[128,2176]{1,0:T(8,128)(2,1)} custom-call(bf16[128,2048]{1,0:T(8,128)(2,1)} %refs_0_.1, s32[8,128]{1,0:T(8,128)} %bitcast.26, f32[8,128]{1,0:T(8,128)} %bitcast.27, s32[1,128]{1,0:T(1,128)} %refs_3_.1), custom_call_target="tpu_custom_call" | custom-call | flops 1000 | bytes 1000 | tf_op jit(solution)/shard_map/enter/pallas_call | solution.py:220
  3.7 5.9 %collective-permute-start.2 = (bf16[128,2176]{1,0:T(8,128)(2,1)}, bf16[128,2176]{1,0:T(8,128)(2,1)S(1)}, u32[]{:S(2)}, u32[]{:S(2)}) collective-permute-start(bf16[128,2176]{1,0:T(8,128)(2,1)} %enter.1.refs_0_), channel_id=1, source_target_pairs={{0,1},{1,0},{2,3},{3,2},{4,5},{5,4},{6,7},{7,6},{8,9},{9,8},{10,11... | collective-permute-start | bytes 1671176 | tf_op jit(solution)/shard_map/ppermute | solution.py:287
  9.5 1.5 collective-permute-start.1
  11.1 1.5 collective-permute-start
  12.6 9.5 %collective-permute-done.2.refs_3_ = bf16[128,2176]{1,0:T(8,128)(2,1)S(1)} collective-permute-done((bf16[128,2176]{1,0:T(8,128)(2,1)}, bf16[128,2176]{1,0:T(8,128)(2,1)S(1)}, u32[]{:S(2)}, u32[]{:S(2)}) %collective-permute-start.2) | collective-permute-done | bytes 557088 | tf_op jit(solution)/shard_map/ppermute | solution.py:287
  22.1 1.5 collective-permute-done.1.refs_2_
  25.5 2.1 %collective-permute-start.7 = (bf16[128,2176]{1,0:T(8,128)(2,1)S(1)}, bf16[128,2176]{1,0:T(8,128)(2,1)S(1)}, u32[]{:S(2)}, u32[]{:S(2)}) collective-permute-start(bf16[128,2176]{1,0:T(8,128)(2,1)S(1)} %collective-permute-done.5), channel_id=1, source_target_pairs={{0,1},{1,0},{2,3},{3,2},{4,5},{5,4},{6,7},{7,6},{8,9},{9,8},{10,11... | collective-permute-start | bytes 1671176 | tf_op jit(solution)/shard_map/ppermute | solution.py:287
  27.6 1.5 collective-permute-start.8
  29.6 5.1 %multiply_reduce_fusion = f32[2048]{0:T(1024)S(1)} fusion(bf16[2048,2048]{1,0:T(8,128)(2,1)} %param.13), kind=kLoop, calls=%fused_computation | loop fusion | flops 12580864 | bytes 8396800 | tf_op jit(solution)/shard_map/reduce_sum | solution.py:433
  34.7 1.5 pick.5
  36.2 2.2 %collective-permute-done.7 = bf16[128,2176]{1,0:T(8,128)(2,1)S(1)} collective-permute-done((bf16[128,2176]{1,0:T(8,128)(2,1)S(1)}, bf16[128,2176]{1,0:T(8,128)(2,1)S(1)}, u32[]{:S(2)}, u32[]{:S(2)}) %collective-permute-start.7) | collective-permute-done | bytes 557088 | tf_op jit(solution)/shard_map/ppermute | solution.py:287
  42.6 1.4 pick.6
  44.0 8.2 %collective-permute-done.10 = bf16[128,2176]{1,0:T(8,128)(2,1)S(1)} collective-permute-done((bf16[128,2176]{1,0:T(8,128)(2,1)S(1)}, bf16[128,2176]{1,0:T(8,128)(2,1)S(1)}, u32[]{:S(2)}, u32[]{:S(2)}) %collective-permute-start.10) | collective-permute-done | bytes 557088 | tf_op jit(solution)/shard_map/ppermute | solution.py:287
  52.4 1.5 collective-permute-done.11.refs_0_
  54.0 1.6 collective-permute-start.13
  56.2 2.0 %collective-permute-start.15 = (bf16[128,2176]{1,0:T(8,128)(2,1)S(1)}, bf16[128,2176]{1,0:T(8,128)(2,1)S(1)}, u32[]{:S(2)}, u32[]{:S(2)}) collective-permute-start(bf16[128,2176]{1,0:T(8,128)(2,1)S(1)} %collective-permute-done.refs_1_), channel_id=1, source_target_pairs={{0,1},{1,0},{2,3},{3,2},{4,5},{5,4},{6,7},{7,6},{8,9},{9,8},{10,11... | collective-permute-start | bytes 1671176 | tf_op jit(solution)/shard_map/ppermute | solution.py:287
  59.7 5.6 %expert_rows.7 = (bf16[256,2048]{1,0:T(8,128)(2,1)S(1)}, bf16[256,2048]{1,0:T(8,128)(2,1)S(1)}) custom-call(s32[2]{0:T(128)S(1)} %pad_add_fusion.who_ref, bf16[256,2176]{1,0:T(8,128)(2,1)S(1)} %get-tuple-element.91.refs_0_, bf16[256,2176]{1,0:T(8,128)(2,1)S(1)} %collective-permute-done.3.refs_1_, bf16[2048,1536]{1,0:T(8,128)(2,1)S(1)} %bitcast.10, ...), custom_call_target="tpu_custom_call" | custom-call | flops 1000 | bytes 1000 | tf_op jit(solution)/shard_map/expert_rows/pallas_call | solution.py:136
  65.8 2.0 %collective-permute-start.18 = (bf16[128,2176]{1,0:T(8,128)(2,1)S(1)}, bf16[128,2176]{1,0:T(8,128)(2,1)S(1)}, u32[]{:S(2)}, u32[]{:S(2)}) collective-permute-start(bf16[128,2176]{1,0:T(8,128)(2,1)S(1)} %collective-permute-done.8.refs_0_), channel_id=1, source_target_pairs={{0,1},{1,0},{2,3},{3,2},{4,5},{5,4},{6,7},{7,6},{8,9},{9,8},{10,11... | collective-permute-start | bytes 1671176 | tf_op jit(solution)/shard_map/ppermute | solution.py:287
  68.0 1.4 collective-permute-start.20
  70.9 4.4 %expert_rows.8 = (bf16[192,2048]{1,0:T(8,128)(2,1)S(1)}, bf16[192,2048]{1,0:T(8,128)(2,1)S(1)}) custom-call(s32[2]{0:T(128)S(1)} %pad_add_fusion.who_ref, bf16[192,2176]{1,0:T(8,128)(2,1)S(1)} %get-tuple-element.108.refs_0_, bf16[192,2176]{1,0:T(8,128)(2,1)S(1)} %collective-permute-done.16.refs_1_, bf16[2048,1536]{1,0:T(8,128)(2,1)S(1)} %bitcast.11, ...), custom_call_target="tpu_custom_call" | custom-call | flops 1000 | bytes 1000 | tf_op jit(solution)/shard_map/expert_rows/pallas_call | solution.py:136
  75.3 2.8 %expert_rows.9.mine = bf16[192,2048]{1,0:T(8,128)(2,1)S(1)} custom-call(s32[2]{0:T(128)S(1)} %pad_add_fusion.who_ref, bf16[192,2176]{1,0:T(8,128)(2,1)S(1)} %get-tuple-element.111.refs_0_, bf16[2048,1536]{1,0:T(8,128)(2,1)S(1)} %bitcast.12, bf16[768,2048]{1,0:T(8,128)(2,1)S(1)} %bitcast.19), custom_call_target="tpu_custom_call" | custom-call | flops 1000 | bytes 1000 | tf_op jit(solution)/shard_map/expert_rows/pallas_call | solution.py:136
  78.0 2.4 %collective-permute-done.18.refs_0_ = bf16[128,2176]{1,0:T(8,128)(2,1)S(1)} collective-permute-done((bf16[128,2176]{1,0:T(8,128)(2,1)S(1)}, bf16[128,2176]{1,0:T(8,128)(2,1)S(1)}, u32[]{:S(2)}, u32[]{:S(2)}) %collective-permute-start.18) | collective-permute-done | bytes 557088 | tf_op jit(solution)/shard_map/ppermute | solution.py:287
  82.6 2.6 %expert_rows.10.mine = bf16[192,2048]{1,0:T(8,128)(2,1)S(1)} custom-call(s32[2]{0:T(128)S(1)} %pad_add_fusion.who_ref, bf16[192,2176]{1,0:T(8,128)(2,1)S(1)} %get-tuple-element.120.refs_0_, bf16[2048,1536]{1,0:T(8,128)(2,1)S(1)} %bitcast.13, bf16[768,2048]{1,0:T(8,128)(2,1)S(1)} %bitcast.20), custom_call_target="tpu_custom_call" | custom-call | flops 1000 | bytes 1000 | tf_op jit(solution)/shard_map/expert_rows/pallas_call | solution.py:136
  85.2 2.6 %expert_rows.11 = bf16[192,2048]{1,0:T(8,128)(2,1)S(1)} custom-call(s32[2]{0:T(128)S(1)} %pad_add_fusion.who_ref, bf16[192,2176]{1,0:T(8,128)(2,1)S(1)} %collective-permute-done.21.refs_0_, bf16[2048,1536]{1,0:T(8,128)(2,1)S(1)} %bitcast.14, bf16[768,2048]{1,0:T(8,128)(2,1)S(1)} %bitcast.21), custom_call_target="tpu_custom_call" | custom-call | flops 1000 | bytes 1000 | tf_op jit(solution)/shard_map/expert_rows/pallas_call | solution.py:136
  88.8 2.6 %expert_rows.12 = bf16[192,2048]{1,0:T(8,128)(2,1)S(1)} custom-call(s32[2]{0:T(128)S(1)} %pad_add_fusion.who_ref, bf16[192,2176]{1,0:T(8,128)(2,1)S(1)} %collective-permute-done.17.refs_0_, bf16[2048,1536]{1,0:T(8,128)(2,1)S(1)} %bitcast.15, bf16[768,2048]{1,0:T(8,128)(2,1)S(1)} %bitcast.22), custom_call_target="tpu_custom_call" | custom-call | flops 1000 | bytes 1000 | tf_op jit(solution)/shard_map/expert_rows/pallas_call | solution.py:136
  92.1 1.5 collective-permute-start.24
  93.6 1.7 collective-permute-start.25
  95.3 1.7 collective-permute-start.26
  97.6 4.4 %expert_rows.13 = (bf16[192,2048]{1,0:T(8,128)(2,1)S(1)}, bf16[192,2048]{1,0:T(8,128)(2,1)S(1)}) custom-call(s32[2]{0:T(128)S(1)} %pad_add_fusion.who_ref, bf16[192,2176]{1,0:T(8,128)(2,1)S(1)} %get-tuple-element.138.refs_0_, bf16[192,2176]{1,0:T(8,128)(2,1)S(1)} %collective-permute-done.27.refs_1_, bf16[2048,1536]{1,0:T(8,128)(2,1)S(1)} %bitcast.16, ...), custom_call_target="tpu_custom_call" | custom-call | flops 1000 | bytes 1000 | tf_op jit(solution)/shard_map/expert_rows/pallas_call | solution.py:136
  103.4 3.0 %collective-permute-done.24 = bf16[128,2048]{1,0:T(8,128)(2,1)S(1)} collective-permute-done((bf16[128,2048]{1,0:T(8,128)(2,1)S(1)}, bf16[128,2048]{1,0:T(8,128)(2,1)S(1)}, u32[]{:S(2)}, u32[]{:S(2)}) %collective-permute-start.24) | collective-permute-done | bytes 524320 | tf_op jit(solution)/shard_map/ppermute | solution.py:287
  107.6 1.4 collective-permute-done.26
  109.5 1.4 collective-permute-start.32
  111.0 1.7 collective-permute-start.29
  113.4 8.5 %collective-permute-done.31 = bf16[128,2048]{1,0:T(8,128)(2,1)S(1)} collective-permute-done((bf16[128,2048]{1,0:T(8,128)(2,1)S(1)}, bf16[128,2048]{1,0:T(8,128)(2,1)S(1)}, u32[]{:S(2)}, u32[]{:S(2)}) %collective-permute-start.31) | collective-permute-done | bytes 524320 | tf_op jit(solution)/shard_map/ppermute | solution.py:287
  123.6 1.7 collective-permute-start.35
  127.1 8.1 %collective-permute-done.35 = bf16[128,2048]{1,0:T(8,128)(2,1)S(1)} collective-permute-done((bf16[128,2048]{1,0:T(8,128)(2,1)S(1)}, bf16[128,2048]{1,0:T(8,128)(2,1)S(1)}, u32[]{:S(2)}, u32[]{:S(2)}) %collective-permute-start.35) | collective-permute-done | bytes 524320 | tf_op jit(solution)/shard_map/ppermute | solution.py:287
  135.3 1.7 collective-permute-done.33
  137.2 1.8 collective-permute-start.36
  140.6 3.1 %collective-permute-start.39 = (bf16[128,2048]{1,0:T(8,128)(2,1)S(1)}, bf16[128,2048]{1,0:T(8,128)(2,1)S(1)}, u32[]{:S(2)}, u32[]{:S(2)}) collective-permute-start(bf16[128,2048]{1,0:T(8,128)(2,1)S(1)} %add_convert_fusion.2.refs_12_), channel_id=1, source_target_pairs={{0,1},{1,0},{2,3},{3,2},{4,5},{5,4},{6,7},{7,6},{8,9},{9,8},{10,11... | collective-permute-start | bytes 1572872 | tf_op jit(solution)/shard_map/ppermute | solution.py:287
  143.7 4.1 %collective-permute-done.36.refs_6_ = bf16[128,2048]{1,0:T(8,128)(2,1)S(1)} collective-permute-done((bf16[128,2048]{1,0:T(8,128)(2,1)S(1)}, bf16[128,2048]{1,0:T(8,128)(2,1)S(1)}, u32[]{:S(2)}, u32[]{:S(2)}) %collective-permute-start.36) | collective-permute-done | bytes 524320 | tf_op jit(solution)/shard_map/ppermute | solution.py:287
  148.6 3.0 %collective-permute-done.39.refs_13_ = bf16[128,2048]{1,0:T(8,128)(2,1)S(1)} collective-permute-done((bf16[128,2048]{1,0:T(8,128)(2,1)S(1)}, bf16[128,2048]{1,0:T(8,128)(2,1)S(1)}, u32[]{:S(2)}, u32[]{:S(2)}) %collective-permute-start.39) | collective-permute-done | bytes 524320 | tf_op jit(solution)/shard_map/ppermute | solution.py:287
  154.2 1.7 collective-permute-start.46
  157.8 1.7 collective-permute-start.41
  159.5 1.8 collective-permute-start.42
  162.2 9.6 %all_gather.3 = bf16[64,2048]{1,0:T(8,128)(2,1)S(1)} all-gather(bf16[8,2048]{1,0:T(8,128)(2,1)S(1)} %multiply_convert_fusion), channel_id=1, replica_groups=mesh['center'=8,'expert'=4] {'center'}, dimensions={0}, use_global_device_ids=true | all-gather | bytes 294912 | tf_op jit(solution)/shard_map/all_gather | solution.py:456
  171.9 2.8 %fusion.1 = f32[64]{0:T(128)S(1)} fusion(bf16[64,2048]{1,0:T(8,128)(2,1)S(1)} %all_gather.3, bf16[2048,2048]{1,0:T(8,128)(2,1)S(1)} %bitcast.25, f32[2048]{0:T(1024)S(1)} %multiply_reduce_fusion, f32[64]{0:T(128)S(1)} %multiply_reduce_fusion.1), kind=kOutput, calls=%fused_computation.3 | convolution fusion | flops 537395136 | bytes 8659456 | tf_op jit(solution)/shard_map/dot_general | solution.py:459
  178.0 1.5 collective-permute-start.50
  180.6 1.8 collective-permute-done.50
  (114 shorter events, 38.1 us)
Async XLA Ops:
  2.8 9.8 %collective-permute-start.5 = (bf16[128,2176]{1,0:T(8,128)(2,1)}, bf16[128,2176]{1,0:T(8,128)(2,1)S(1)}, u32[]{:S(2)}, u32[]{:S(2)}) collective-permute-start(bf16[128,2176]{1,0:T(8,128)(2,1)} %enter.1.refs_0_), channel_id=1, source_target_pairs={{1,2},{2,1},{5,6},{6,5},{9,10},{10,9},{13,14},{14,13},{17,18},{18,... | collective-permute-start | bytes 1671176 | tf_op jit(solution)/shard_map/ppermute | solution.py:287
  3.7 18.4 %collective-permute-start.2 = (bf16[128,2176]{1,0:T(8,128)(2,1)}, bf16[128,2176]{1,0:T(8,128)(2,1)S(1)}, u32[]{:S(2)}, u32[]{:S(2)}) collective-permute-start(bf16[128,2176]{1,0:T(8,128)(2,1)} %enter.1.refs_0_), channel_id=1, source_target_pairs={{0,1},{1,0},{2,3},{3,2},{4,5},{5,4},{6,7},{7,6},{8,9},{9,8},{10,11... | collective-permute-start | bytes 1671176 | tf_op jit(solution)/shard_map/ppermute | solution.py:287
  9.5 14.0 %collective-permute-start.1 = (bf16[128,2176]{1,0:T(8,128)(2,1)}, bf16[128,2176]{1,0:T(8,128)(2,1)S(1)}, u32[]{:S(2)}, u32[]{:S(2)}) collective-permute-start(bf16[128,2176]{1,0:T(8,128)(2,1)} %enter.1.refs_0_), channel_id=1, source_target_pairs={{0,16},{4,20},{8,24},{12,28},{16,0},{20,4},{24,8},{28,12},{1,17},{... | collective-permute-start | bytes 1671176 | tf_op jit(solution)/shard_map/ppermute | solution.py:287
  11.1 13.7 %collective-permute-start = (bf16[128,2176]{1,0:T(8,128)(2,1)}, bf16[128,2176]{1,0:T(8,128)(2,1)S(1)}, u32[]{:S(2)}, u32[]{:S(2)}) collective-permute-start(bf16[128,2176]{1,0:T(8,128)(2,1)} %enter.1.refs_0_), channel_id=1, source_target_pairs={{0,8},{4,12},{8,0},{12,4},{16,24},{20,28},{24,16},{28,20},{1,9},{5... | collective-permute-start | bytes 1671176 | tf_op jit(solution)/shard_map/ppermute | solution.py:287
  24.8 13.8 %collective-permute-start.6 = (bf16[128,2176]{1,0:T(8,128)(2,1)S(1)}, bf16[128,2176]{1,0:T(8,128)(2,1)S(1)}, u32[]{:S(2)}, u32[]{:S(2)}) collective-permute-start(bf16[128,2176]{1,0:T(8,128)(2,1)S(1)} %collective-permute-done.2.refs_3_), channel_id=1, source_target_pairs={{1,2},{2,1},{5,6},{6,5},{9,10},{10,9},{13,14},{14,13},{17,18},{18,... | collective-permute-start | bytes 1671176 | tf_op jit(solution)/shard_map/ppermute | solution.py:287
  25.5 12.9 %collective-permute-start.7 = (bf16[128,2176]{1,0:T(8,128)(2,1)S(1)}, bf16[128,2176]{1,0:T(8,128)(2,1)S(1)}, u32[]{:S(2)}, u32[]{:S(2)}) collective-permute-start(bf16[128,2176]{1,0:T(8,128)(2,1)S(1)} %collective-permute-done.5), channel_id=1, source_target_pairs={{0,1},{1,0},{2,3},{3,2},{4,5},{5,4},{6,7},{7,6},{8,9},{9,8},{10,11... | collective-permute-start | bytes 1671176 | tf_op jit(solution)/shard_map/ppermute | solution.py:287
  27.6 12.3 %collective-permute-start.8 = (bf16[128,2176]{1,0:T(8,128)(2,1)S(1)}, bf16[128,2176]{1,0:T(8,128)(2,1)S(1)}, u32[]{:S(2)}, u32[]{:S(2)}) collective-permute-start(bf16[128,2176]{1,0:T(8,128)(2,1)S(1)} %collective-permute-done.1.refs_2_), channel_id=1, source_target_pairs={{0,8},{4,12},{8,0},{12,4},{16,24},{20,28},{24,16},{28,20},{1,9},{5... | collective-permute-start | bytes 1671176 | tf_op jit(solution)/shard_map/ppermute | solution.py:287
  29.1 12.0 %collective-permute-start.9 = (bf16[128,2176]{1,0:T(8,128)(2,1)S(1)}, bf16[128,2176]{1,0:T(8,128)(2,1)S(1)}, u32[]{:S(2)}, u32[]{:S(2)}) collective-permute-start(bf16[128,2176]{1,0:T(8,128)(2,1)S(1)} %collective-permute-done.2.refs_3_), channel_id=1, source_target_pairs={{0,16},{4,20},{8,24},{12,28},{16,0},{20,4},{24,8},{28,12},{1,17},{... | collective-permute-start | bytes 1671176 | tf_op jit(solution)/shard_map/ppermute | solution.py:287
  41.1 11.1 %collective-permute-start.10 = (bf16[128,2176]{1,0:T(8,128)(2,1)S(1)}, bf16[128,2176]{1,0:T(8,128)(2,1)S(1)}, u32[]{:S(2)}, u32[]{:S(2)}) collective-permute-start(bf16[128,2176]{1,0:T(8,128)(2,1)S(1)} %collective-permute-done.6), channel_id=1, source_target_pairs={{0,1},{1,0},{2,3},{3,2},{4,5},{5,4},{6,7},{7,6},{8,9},{9,8},{10,11... | collective-permute-start | bytes 1671176 | tf_op jit(solution)/shard_map/ppermute | solution.py:287
  41.5 12.4 %collective-permute-start.11 = (bf16[128,2176]{1,0:T(8,128)(2,1)S(1)}, bf16[128,2176]{1,0:T(8,128)(2,1)S(1)}, u32[]{:S(2)}, u32[]{:S(2)}) collective-permute-start(bf16[128,2176]{1,0:T(8,128)(2,1)S(1)} %add.86.refs_2_), channel_id=1, source_target_pairs={{0,8},{4,12},{8,0},{12,4},{16,24},{20,28},{24,16},{28,20},{1,9},{5... | collective-permute-start | bytes 1671176 | tf_op jit(solution)/shard_map/ppermute | solution.py:287
  42.0 12.0 %collective-permute-start.12 = (bf16[128,2176]{1,0:T(8,128)(2,1)S(1)}, bf16[128,2176]{1,0:T(8,128)(2,1)S(1)}, u32[]{:S(2)}, u32[]{:S(2)}) collective-permute-start(bf16[128,2176]{1,0:T(8,128)(2,1)S(1)} %add.86.refs_2_), channel_id=1, source_target_pairs={{0,16},{4,20},{8,24},{12,28},{16,0},{20,4},{24,8},{28,12},{1,17},{... | collective-permute-start | bytes 1671176 | tf_op jit(solution)/shard_map/ppermute | solution.py:287
  42.6 17.1 %collective-permute-start.3 = (bf16[256,2176]{1,0:T(8,128)(2,1)S(1)}, bf16[256,2176]{1,0:T(8,128)(2,1)S(1)}, u32[]{:S(2)}, u32[]{:S(2)}) collective-permute-start(bf16[256,2176]{1,0:T(8,128)(2,1)S(1)} %get-tuple-element.92), channel_id=1, source_target_pairs={{0,4},{4,0},{8,12},{12,8},{16,20},{20,16},{24,28},{28,24},{1,5},{5... | collective-permute-start | bytes 3342344 | tf_op jit(solution)/shard_map/ppermute | solution.py:287
  54.0 11.4 %collective-permute-start.13 = (bf16[128,2176]{1,0:T(8,128)(2,1)S(1)}, bf16[128,2176]{1,0:T(8,128)(2,1)S(1)}, u32[]{:S(2)}, u32[]{:S(2)}) collective-permute-start(bf16[128,2176]{1,0:T(8,128)(2,1)S(1)} %add.87.refs_2_), channel_id=1, source_target_pairs={{0,8},{4,12},{8,0},{12,4},{16,24},{20,28},{24,16},{28,20},{1,9},{5... | collective-permute-start | bytes 1671176 | tf_op jit(solution)/shard_map/ppermute | solution.py:287
  55.6 9.8 %collective-permute-start.14 = (bf16[128,2176]{1,0:T(8,128)(2,1)S(1)}, bf16[128,2176]{1,0:T(8,128)(2,1)S(1)}, u32[]{:S(2)}, u32[]{:S(2)}) collective-permute-start(bf16[128,2176]{1,0:T(8,128)(2,1)S(1)} %add.87.refs_2_), channel_id=1, source_target_pairs={{0,16},{4,20},{8,24},{12,28},{16,0},{20,4},{24,8},{28,12},{1,17},{... | collective-permute-start | bytes 1671176 | tf_op jit(solution)/shard_map/ppermute | solution.py:287
  56.2 9.5 %collective-permute-start.15 = (bf16[128,2176]{1,0:T(8,128)(2,1)S(1)}, bf16[128,2176]{1,0:T(8,128)(2,1)S(1)}, u32[]{:S(2)}, u32[]{:S(2)}) collective-permute-start(bf16[128,2176]{1,0:T(8,128)(2,1)S(1)} %collective-permute-done.refs_1_), channel_id=1, source_target_pairs={{0,1},{1,0},{2,3},{3,2},{4,5},{5,4},{6,7},{7,6},{8,9},{9,8},{10,11... | collective-permute-start | bytes 1671176 | tf_op jit(solution)/shard_map/ppermute | solution.py:287
  59.6 11.3 %collective-permute-start.16 = (bf16[192,2176]{1,0:T(8,128)(2,1)S(1)}, bf16[192,2176]{1,0:T(8,128)(2,1)S(1)}, u32[]{:S(2)}, u32[]{:S(2)}) collective-permute-start(bf16[192,2176]{1,0:T(8,128)(2,1)S(1)} %get-tuple-element.109), channel_id=1, source_target_pairs={{0,4},{4,0},{8,12},{12,8},{16,20},{20,16},{24,28},{28,24},{1,5},{5... | collective-permute-start | bytes 2506760 | tf_op jit(solution)/shard_map/ppermute | solution.py:287
  65.8 14.7 %collective-permute-start.18 = (bf16[128,2176]{1,0:T(8,128)(2,1)S(1)}, bf16[128,2176]{1,0:T(8,128)(2,1)S(1)}, u32[]{:S(2)}, u32[]{:S(2)}) collective-permute-start(bf16[128,2176]{1,0:T(8,128)(2,1)S(1)} %collective-permute-done.8.refs_0_), channel_id=1, source_target_pairs={{0,1},{1,0},{2,3},{3,2},{4,5},{5,4},{6,7},{7,6},{8,9},{9,8},{10,11... | collective-permute-start | bytes 1671176 | tf_op jit(solution)/shard_map/ppermute | solution.py:287
  67.8 12.8 %collective-permute-start.19 = (bf16[128,2176]{1,0:T(8,128)(2,1)S(1)}, bf16[128,2176]{1,0:T(8,128)(2,1)S(1)}, u32[]{:S(2)}, u32[]{:S(2)}) collective-permute-start(bf16[128,2176]{1,0:T(8,128)(2,1)S(1)} %collective-permute-done.12.refs_1_), channel_id=1, source_target_pairs={{0,8},{4,12},{8,0},{12,4},{16,24},{20,28},{24,16},{28,20},{1,9},{5... | collective-permute-start | bytes 1671176 | tf_op jit(solution)/shard_map/ppermute | solution.py:287
  68.0 12.6 %collective-permute-start.20 = (bf16[128,2176]{1,0:T(8,128)(2,1)S(1)}, bf16[128,2176]{1,0:T(8,128)(2,1)S(1)}, u32[]{:S(2)}, u32[]{:S(2)}) collective-permute-start(bf16[128,2176]{1,0:T(8,128)(2,1)S(1)} %collective-permute-done.13.refs_0_), channel_id=1, source_target_pairs={{0,16},{4,20},{8,24},{12,28},{16,0},{20,4},{24,8},{28,12},{1,17},{... | collective-permute-start | bytes 1671176 | tf_op jit(solution)/shard_map/ppermute | solution.py:287
  82.1 6.7 %collective-permute-start.17 = (bf16[192,2176]{1,0:T(8,128)(2,1)S(1)}, bf16[192,2176]{1,0:T(8,128)(2,1)S(1)}, u32[]{:S(2)}, u32[]{:S(2)}) collective-permute-start(bf16[192,2176]{1,0:T(8,128)(2,1)S(1)} %get-tuple-element.112), channel_id=1, source_target_pairs={{0,4},{4,0},{8,12},{12,8},{16,20},{20,16},{24,28},{28,24},{1,5},{5... | collective-permute-start | bytes 2506760 | tf_op jit(solution)/shard_map/ppermute | solution.py:287
  87.7 3.8 %collective-permute-start.23 = (bf16[192,2048]{1,0:T(8,128)(2,1)S(1)}, bf16[192,2048]{1,0:T(8,128)(2,1)S(1)}, u32[]{:S(2)}, u32[]{:S(2)}) collective-permute-start(bf16[192,2048]{1,0:T(8,128)(2,1)S(1)} %expert_rows.11), channel_id=1, source_target_pairs={{0,4},{4,0},{8,12},{12,8},{16,20},{20,16},{24,28},{28,24},{1,5},{5... | collective-permute-start | bytes 2359304 | tf_op jit(solution)/shard_map/ppermute | solution.py:287
  87.9 14.8 %collective-permute-start.4 = (bf16[256,2048]{1,0:T(8,128)(2,1)S(1)}, bf16[256,2048]{1,0:T(8,128)(2,1)S(1)}, u32[]{:S(2)}, u32[]{:S(2)}) collective-permute-start(bf16[256,2048]{1,0:T(8,128)(2,1)S(1)} %get-tuple-element.94), channel_id=1, source_target_pairs={{0,4},{4,0},{8,12},{12,8},{16,20},{20,16},{24,28},{28,24},{1,5},{5... | collective-permute-start | bytes 3145736 | tf_op jit(solution)/shard_map/ppermute | solution.py:287
  88.3 5.3 %collective-permute-start.27 = (bf16[192,2176]{1,0:T(8,128)(2,1)S(1)}, bf16[192,2176]{1,0:T(8,128)(2,1)S(1)}, u32[]{:S(2)}, u32[]{:S(2)}) collective-permute-start(bf16[192,2176]{1,0:T(8,128)(2,1)S(1)} %get-tuple-element.139), channel_id=1, source_target_pairs={{0,4},{4,0},{8,12},{12,8},{16,20},{20,16},{24,28},{28,24},{1,5},{5... | collective-permute-start | bytes 2506760 | tf_op jit(solution)/shard_map/ppermute | solution.py:287
  88.4 6.9 %collective-permute-start.28 = (bf16[192,2048]{1,0:T(8,128)(2,1)S(1)}, bf16[192,2048]{1,0:T(8,128)(2,1)S(1)}, u32[]{:S(2)}, u32[]{:S(2)}) collective-permute-start(bf16[192,2048]{1,0:T(8,128)(2,1)S(1)} %get-tuple-element.142), channel_id=1, source_target_pairs={{0,4},{4,0},{8,12},{12,8},{16,20},{20,16},{24,28},{28,24},{1,5},{5... | collective-permute-start | bytes 2359304 | tf_op jit(solution)/shard_map/ppermute | solution.py:287
  91.4 10.6 %collective-permute-start.22 = (bf16[192,2048]{1,0:T(8,128)(2,1)S(1)}, bf16[192,2048]{1,0:T(8,128)(2,1)S(1)}, u32[]{:S(2)}, u32[]{:S(2)}) collective-permute-start(bf16[192,2048]{1,0:T(8,128)(2,1)S(1)} %expert_rows.12), channel_id=1, source_target_pairs={{0,4},{4,0},{8,12},{12,8},{16,20},{20,16},{24,28},{28,24},{1,5},{5... | collective-permute-start | bytes 2359304 | tf_op jit(solution)/shard_map/ppermute | solution.py:287
  92.1 14.3 %collective-permute-start.24 = (bf16[128,2048]{1,0:T(8,128)(2,1)S(1)}, bf16[128,2048]{1,0:T(8,128)(2,1)S(1)}, u32[]{:S(2)}, u32[]{:S(2)}) collective-permute-start(bf16[128,2048]{1,0:T(8,128)(2,1)S(1)} %get-tuple-element.134), channel_id=1, source_target_pairs={{0,16},{4,20},{8,24},{12,28},{16,0},{20,4},{24,8},{28,12},{1,17},{... | collective-permute-start | bytes 1572872 | tf_op jit(solution)/shard_map/ppermute | solution.py:287
  93.6 14.0 %collective-permute-start.25 = (bf16[128,2048]{1,0:T(8,128)(2,1)S(1)}, bf16[128,2048]{1,0:T(8,128)(2,1)S(1)}, u32[]{:S(2)}, u32[]{:S(2)}) collective-permute-start(bf16[128,2048]{1,0:T(8,128)(2,1)S(1)} %get-tuple-element.137), channel_id=1, source_target_pairs={{0,8},{4,12},{8,0},{12,4},{16,24},{20,28},{24,16},{28,20},{1,9},{5... | collective-permute-start | bytes 1572872 | tf_op jit(solution)/shard_map/ppermute | solution.py:287
  95.3 13.7 %collective-permute-start.26 = (bf16[128,2048]{1,0:T(8,128)(2,1)S(1)}, bf16[128,2048]{1,0:T(8,128)(2,1)S(1)}, u32[]{:S(2)}, u32[]{:S(2)}) collective-permute-start(bf16[128,2048]{1,0:T(8,128)(2,1)S(1)} %get-tuple-element.124), channel_id=1, source_target_pairs={{0,1},{1,0},{2,3},{3,2},{4,5},{5,4},{6,7},{7,6},{8,9},{9,8},{10,11... | collective-permute-start | bytes 1572872 | tf_op jit(solution)/shard_map/ppermute | solution.py:287
  102.0 10.8 %collective-permute-start.30 = (bf16[192,2048]{1,0:T(8,128)(2,1)S(1)}, bf16[192,2048]{1,0:T(8,128)(2,1)S(1)}, u32[]{:S(2)}, u32[]{:S(2)}) collective-permute-start(bf16[192,2048]{1,0:T(8,128)(2,1)S(1)} %get-tuple-element.150), channel_id=1, source_target_pairs={{0,4},{4,0},{8,12},{12,8},{16,20},{20,16},{24,28},{28,24},{1,5},{5... | collective-permute-start | bytes 2359304 | tf_op jit(solution)/shard_map/ppermute | solution.py:287
  109.0 12.8 %collective-permute-start.31 = (bf16[128,2048]{1,0:T(8,128)(2,1)S(1)}, bf16[128,2048]{1,0:T(8,128)(2,1)S(1)}, u32[]{:S(2)}, u32[]{:S(2)}) collective-permute-start(bf16[128,2048]{1,0:T(8,128)(2,1)S(1)} %add_convert_fusion.6), channel_id=1, source_target_pairs={{0,8},{4,12},{8,0},{12,4},{16,24},{20,28},{24,16},{28,20},{1,9},{5... | collective-permute-start | bytes 1572872 | tf_op jit(solution)/shard_map/ppermute | solution.py:287
  109.5 12.7 %collective-permute-start.32 = (bf16[128,2048]{1,0:T(8,128)(2,1)S(1)}, bf16[128,2048]{1,0:T(8,128)(2,1)S(1)}, u32[]{:S(2)}, u32[]{:S(2)}) collective-permute-start(bf16[128,2048]{1,0:T(8,128)(2,1)S(1)} %get-tuple-element.157), channel_id=1, source_target_pairs={{0,16},{4,20},{8,24},{12,28},{16,0},{20,4},{24,8},{28,12},{1,17},{... | collective-permute-start | bytes 1572872 | tf_op jit(solution)/shard_map/ppermute | solution.py:287
  111.0 12.6 %collective-permute-start.29 = (bf16[128,2048]{1,0:T(8,128)(2,1)S(1)}, bf16[128,2048]{1,0:T(8,128)(2,1)S(1)}, u32[]{:S(2)}, u32[]{:S(2)}) collective-permute-start(bf16[128,2048]{1,0:T(8,128)(2,1)S(1)} %get-tuple-element.147), channel_id=1, source_target_pairs={{0,1},{1,0},{2,3},{3,2},{4,5},{5,4},{6,7},{7,6},{8,9},{9,8},{10,11... | collective-permute-start | bytes 1572872 | tf_op jit(solution)/shard_map/ppermute | solution.py:287
  123.6 11.7 %collective-permute-start.35 = (bf16[128,2048]{1,0:T(8,128)(2,1)S(1)}, bf16[128,2048]{1,0:T(8,128)(2,1)S(1)}, u32[]{:S(2)}, u32[]{:S(2)}) collective-permute-start(bf16[128,2048]{1,0:T(8,128)(2,1)S(1)} %add_convert_fusion.3), channel_id=1, source_target_pairs={{0,1},{1,0},{2,3},{3,2},{4,5},{5,4},{6,7},{7,6},{8,9},{9,8},{10,11... | collective-permute-start | bytes 1572872 | tf_op jit(solution)/shard_map/ppermute | solution.py:287
  125.2 11.8 %collective-permute-start.33 = (bf16[128,2048]{1,0:T(8,128)(2,1)S(1)}, bf16[128,2048]{1,0:T(8,128)(2,1)S(1)}, u32[]{:S(2)}, u32[]{:S(2)}) collective-permute-start(bf16[128,2048]{1,0:T(8,128)(2,1)S(1)} %get-tuple-element.158), channel_id=1, source_target_pairs={{0,8},{4,12},{8,0},{12,4},{16,24},{20,28},{24,16},{28,20},{1,9},{5... | collective-permute-start | bytes 1572872 | tf_op jit(solution)/shard_map/ppermute | solution.py:287
  125.8 11.2 %collective-permute-start.34 = (bf16[128,2048]{1,0:T(8,128)(2,1)S(1)}, bf16[128,2048]{1,0:T(8,128)(2,1)S(1)}, u32[]{:S(2)}, u32[]{:S(2)}) collective-permute-start(bf16[128,2048]{1,0:T(8,128)(2,1)S(1)} %add_convert_fusion.4), channel_id=1, source_target_pairs={{0,16},{4,20},{8,24},{12,28},{16,0},{20,4},{24,8},{28,12},{1,17},{... | collective-permute-start | bytes 1572872 | tf_op jit(solution)/shard_map/ppermute | solution.py:287
  137.2 10.6 %collective-permute-start.36 = (bf16[128,2048]{1,0:T(8,128)(2,1)S(1)}, bf16[128,2048]{1,0:T(8,128)(2,1)S(1)}, u32[]{:S(2)}, u32[]{:S(2)}) collective-permute-start(bf16[128,2048]{1,0:T(8,128)(2,1)S(1)} %add_convert_fusion.5), channel_id=1, source_target_pairs={{0,8},{4,12},{8,0},{12,4},{16,24},{20,28},{24,16},{28,20},{1,9},{5... | collective-permute-start | bytes 1572872 | tf_op jit(solution)/shard_map/ppermute | solution.py:287
  139.1 9.5 %collective-permute-start.37 = (bf16[128,2048]{1,0:T(8,128)(2,1)S(1)}, bf16[128,2048]{1,0:T(8,128)(2,1)S(1)}, u32[]{:S(2)}, u32[]{:S(2)}) collective-permute-start(bf16[128,2048]{1,0:T(8,128)(2,1)S(1)} %get-tuple-element.163), channel_id=1, source_target_pairs={{0,16},{4,20},{8,24},{12,28},{16,0},{20,4},{24,8},{28,12},{1,17},{... | collective-permute-start | bytes 1572872 | tf_op jit(solution)/shard_map/ppermute | solution.py:287
  139.9 8.7 %collective-permute-start.38 = (bf16[128,2048]{1,0:T(8,128)(2,1)S(1)}, bf16[128,2048]{1,0:T(8,128)(2,1)S(1)}, u32[]{:S(2)}, u32[]{:S(2)}) collective-permute-start(bf16[128,2048]{1,0:T(8,128)(2,1)S(1)} %add_convert_fusion.1), channel_id=1, source_target_pairs={{1,2},{2,1},{5,6},{6,5},{9,10},{10,9},{13,14},{14,13},{17,18},{18,... | collective-permute-start | bytes 1572872 | tf_op jit(solution)/shard_map/ppermute | solution.py:287
  140.6 11.0 %collective-permute-start.39 = (bf16[128,2048]{1,0:T(8,128)(2,1)S(1)}, bf16[128,2048]{1,0:T(8,128)(2,1)S(1)}, u32[]{:S(2)}, u32[]{:S(2)}) collective-permute-start(bf16[128,2048]{1,0:T(8,128)(2,1)S(1)} %add_convert_fusion.2.refs_12_), channel_id=1, source_target_pairs={{0,1},{1,0},{2,3},{3,2},{4,5},{5,4},{6,7},{7,6},{8,9},{9,8},{10,11... | collective-permute-start | bytes 1572872 | tf_op jit(solution)/shard_map/ppermute | solution.py:287
  152.6 5.2 %collective-permute-start.44 = (f32[8,2048]{1,0:T(8,128)S(1)}, f32[8,2048]{1,0:T(8,128)S(1)}, u32[]{:S(2)}, u32[]{:S(2)}) collective-permute-start(f32[8,2048]{1,0:T(8,128)S(1)} %get-tuple-element.171), channel_id=1, source_target_pairs={{0,8},{4,12},{8,0},{12,4},{16,24},{20,28},{24,16},{28,20},{1,9},{5... | collective-permute-start | bytes 196616 | tf_op jit(solution)/shard_map/ppermute | solution.py:287
  153.7 5.7 %collective-permute-start.45 = (f32[8,2048]{1,0:T(8,128)S(1)}, f32[8,2048]{1,0:T(8,128)S(1)}, u32[]{:S(2)}, u32[]{:S(2)}) collective-permute-start(f32[8,2048]{1,0:T(8,128)S(1)} %get-tuple-element.172), channel_id=1, source_target_pairs={{0,16},{4,20},{8,24},{12,28},{16,0},{20,4},{24,8},{28,12},{1,17},{... | collective-permute-start | bytes 196616 | tf_op jit(solution)/shard_map/ppermute | solution.py:287
  154.2 7.0 %collective-permute-start.46 = (f32[8,2048]{1,0:T(8,128)S(1)}, f32[8,2048]{1,0:T(8,128)S(1)}, u32[]{:S(2)}, u32[]{:S(2)}) collective-permute-start(f32[8,2048]{1,0:T(8,128)S(1)} %get-tuple-element.173), channel_id=1, source_target_pairs={{0,1},{1,0},{2,3},{3,2},{4,5},{5,4},{6,7},{7,6},{8,9},{9,8},{10,11... | collective-permute-start | bytes 196616 | tf_op jit(solution)/shard_map/ppermute | solution.py:287
  155.9 6.0 %collective-permute-start.47 = (f32[8,2048]{1,0:T(8,128)S(1)}, f32[8,2048]{1,0:T(8,128)S(1)}, u32[]{:S(2)}, u32[]{:S(2)}) collective-permute-start(f32[8,2048]{1,0:T(8,128)S(1)} %get-tuple-element.174), channel_id=1, source_target_pairs={{1,2},{2,1},{5,6},{6,5},{9,10},{10,9},{13,14},{14,13},{17,18},{18,... | collective-permute-start | bytes 196616 | tf_op jit(solution)/shard_map/ppermute | solution.py:287
  156.6 18.1 %collective-permute-start.40 = (bf16[128,2048]{1,0:T(8,128)(2,1)S(1)}, bf16[128,2048]{1,0:T(8,128)(2,1)S(1)}, u32[]{:S(2)}, u32[]{:S(2)}) collective-permute-start(bf16[128,2048]{1,0:T(8,128)(2,1)S(1)} %get-tuple-element.166), channel_id=1, source_target_pairs={{0,8},{4,12},{8,0},{12,4},{16,24},{20,28},{24,16},{28,20},{1,9},{5... | collective-permute-start | bytes 1572872 | tf_op jit(solution)/shard_map/ppermute | solution.py:287
  157.8 16.9 %collective-permute-start.41 = (bf16[128,2048]{1,0:T(8,128)(2,1)S(1)}, bf16[128,2048]{1,0:T(8,128)(2,1)S(1)}, u32[]{:S(2)}, u32[]{:S(2)}) collective-permute-start(bf16[128,2048]{1,0:T(8,128)(2,1)S(1)} %get-tuple-element.167), channel_id=1, source_target_pairs={{0,16},{4,20},{8,24},{12,28},{16,0},{20,4},{24,8},{28,12},{1,17},{... | collective-permute-start | bytes 1572872 | tf_op jit(solution)/shard_map/ppermute | solution.py:287
  159.5 15.2 %collective-permute-start.42 = (bf16[128,2048]{1,0:T(8,128)(2,1)S(1)}, bf16[128,2048]{1,0:T(8,128)(2,1)S(1)}, u32[]{:S(2)}, u32[]{:S(2)}) collective-permute-start(bf16[128,2048]{1,0:T(8,128)(2,1)S(1)} %get-tuple-element.168), channel_id=1, source_target_pairs={{0,1},{1,0},{2,3},{3,2},{4,5},{5,4},{6,7},{7,6},{8,9},{9,8},{10,11... | collective-permute-start | bytes 1572872 | tf_op jit(solution)/shard_map/ppermute | solution.py:287
  161.2 13.5 %collective-permute-start.43 = (bf16[128,2048]{1,0:T(8,128)(2,1)S(1)}, bf16[128,2048]{1,0:T(8,128)(2,1)S(1)}, u32[]{:S(2)}, u32[]{:S(2)}) collective-permute-start(bf16[128,2048]{1,0:T(8,128)(2,1)S(1)} %get-tuple-element.169), channel_id=1, source_target_pairs={{1,2},{2,1},{5,6},{6,5},{9,10},{10,9},{13,14},{14,13},{17,18},{18,... | collective-permute-start | bytes 1572872 | tf_op jit(solution)/shard_map/ppermute | solution.py:287
  178.0 4.4 %collective-permute-start.50 = (f32[64]{0:T(128)S(1)}, f32[64]{0:T(128)S(1)}, u32[]{:S(2)}, u32[]{:S(2)}) collective-permute-start(f32[64]{0:T(128)S(1)} %fusion.1), channel_id=1, source_target_pairs={{0,24},{4,28},{8,16},{12,20},{16,8},{20,12},{24,0},{28,4},{1,25},{... | collective-permute-start | bytes 776 | tf_op jit(solution)/shard_map/ppermute | solution.py:287
  (10 other events, 256.6 us)

commit v6 on v5

--- a/solution.py
+++ b/solution.py
@@ -353,26 +353,32 @@
     rx_b2, ry_b2, in_3 = at_once(
         (SWAP_X, g3[0]), (SWAP_Y, sy2), (SWAP_Z, s3), behind=(rz_x0, g2[0])
     )
+    (sx0,), (_, sum_x) = leave(
+        3 * expert_count,
+        [([g1[0]], rows[:, -LANES:]), ([g1[1], rz_x0], bx0[:, -LANES:])],
+    )
+    (sum_x,) = at_once((SWAP_X, sum_x), behind=(rx_b2,))
     sd0 = added(g2[0], rz_d0).astype(BF16)
     s2 = added(g2[2], rx_b2, ry_b2).astype(BF16)
     rx_y0, ry_b1, in_2, over_3 = at_once(
         (SWAP_X, sd0), (SWAP_Y, g2[1]), (SWAP_Z, s2),
         (MIDDLE, added(s3, in_3).astype(BF16)), behind=(rx_b2, ry_b2),
     )
-    (sx0, sy0, s1, m2), (sum_own, *sums) = leave(
+    (sy0, s1, m2), (sum_own, *sums) = leave(
         3 * expert_count,
         [
             ([g1[0]], rows[:, -LANES:]),
-            ([g1[1], rz_x0], bx0[:, -LANES:]),
             ([g1[2], rx_y0], by0[:, -LANES:]),
             ([g1[3], ry_b1, over_3], b1[:, -LANES:]),
             ([s2, in_2], c2[:, -LANES:]),
         ],
     )
-    ways = (SWAP_X, SWAP_Y, SWAP_Z, MIDDLE)
-    sums = at_once(*zip(ways, sums))
-    pooled = normed_sum(added(sum_own, *sums))
-    rx_b0, ry_b0, rz_b0, over_2 = at_once(*zip(ways, (sx0, sy0, s1, m2)))
+    sums = at_once((SWAP_Y, sums[0]), (SWAP_Z, sums[1]), (MIDDLE, sums[2]))
+    pooled = normed_sum(added(sum_own, sum_x, *sums))
+    held = lax.optimization_barrier((sx0, rx_y0))[0]
+    rx_b0, ry_b0, rz_b0, over_2 = at_once(
+        (SWAP_X, held), (SWAP_Y, sy0), (SWAP_Z, s1), (MIDDLE, m2)
+    )
     return added(g1[0], rx_b0, ry_b0, rz_b0, over_2), pooled
 
 

time: 184 us -> 184 us (level)
  transfers between devices with their start and end apart: 52 -> 52, of which waited for: 28 -> 27; matrix products, arithmetic and copies ran while one was open for 5% -> 5% of each run, Pallas kernels for 18% -> 19%
where the time goes in v6:
time: 184 us; the launch traced here: 183 us
  waiting for transfers between devices  65.6 us (36%)
  starting transfers between devices  56.4 us (31%)
  Pallas kernels  39.1 us (21%)
  blocking collectives  9.35 us (5%)
  other arithmetic  8.33 us (5%)
  matrix products  2.75 us (1%)
    ppermute x52, waiting for transfers between devices, at_once(): lax.ppermute(value, way[0], way[1])  65.6 us
    ppermute x52, starting transfers between devices, at_once(): lax.ppermute(value, way[0], way[1])  56.4 us
    pallas_call x7, Pallas kernels, expert_rows(): pl.pallas_call(functools.partial(expert_kernel, expert_count, len(parts))...  24.8 us
    all_gather x1, blocking collectives, local(): shard_part = lax.all_gather(pooled, 'center', axis=0, tiled=True)  9.35 us
    pallas_call x5, Pallas kernels, pick(): pl.pallas_call(functools.partial(pick_kernel, capacity, expert_count), ou...  7.07 us
    reduce_sum x1, other arithmetic, local(): bank_norms = jnp.sum(bank_values * bank_values, axis=1)  5.08 us
  transfers between devices with their start and end apart: 52, of which 27 were waited for; matrix products, arithmetic and copies ran while one was open for 5% of the time, Pallas kernels for 19%

profile of v6, /device:TPU:0, one launch (start us, length us, event | category | flops | bytes accessed | tf_op | source)
XLA Modules:
  0.0 183.3 jit_solution(9099677904521025263)
XLA Ops:
  0.6 2.2 %enter.1.refs_0_ = bf16[128,2176]{1,0:T(8,128)(2,1)} custom-call(bf16[128,2048]{1,0:T(8,128)(2,1)} %refs_0_.1, s32[8,128]{1,0:T(8,128)} %bitcast.26, f32[8,128]{1,0:T(8,128)} %bitcast.27, s32[1,128]{1,0:T(1,128)} %refs_3_.1), custom_call_target="tpu_custom_call" | custom-call | flops 1000 | bytes 1000 | tf_op jit(solution)/shard_map/enter/pallas_call | solution.py:220
  3.7 5.9 %collective-permute-start.2 = (bf16[128,2176]{1,0:T(8,128)(2,1)}, bf16[128,2176]{1,0:T(8,128)(2,1)S(1)}, u32[]{:S(2)}, u32[]{:S(2)}) collective-permute-start(bf16[128,2176]{1,0:T(8,128)(2,1)} %enter.1.refs_0_), channel_id=1, source_target_pairs={{0,1},{1,0},{2,3},{3,2},{4,5},{5,4},{6,7},{7,6},{8,9},{9,8},{10,11... | collective-permute-start | bytes 1671176 | tf_op jit(solution)/shard_map/ppermute | solution.py:287
  9.5 1.5 collective-permute-start.1
  11.1 1.5 collective-permute-start
  12.6 9.5 %collective-permute-done.2.refs_3_ = bf16[128,2176]{1,0:T(8,128)(2,1)S(1)} collective-permute-done((bf16[128,2176]{1,0:T(8,128)(2,1)}, bf16[128,2176]{1,0:T(8,128)(2,1)S(1)}, u32[]{:S(2)}, u32[]{:S(2)}) %collective-permute-start.2) | collective-permute-done | bytes 557088 | tf_op jit(solution)/shard_map/ppermute | solution.py:287
  22.1 1.5 collective-permute-done.1.refs_2_
  25.5 2.1 %collective-permute-start.7 = (bf16[128,2176]{1,0:T(8,128)(2,1)S(1)}, bf16[128,2176]{1,0:T(8,128)(2,1)S(1)}, u32[]{:S(2)}, u32[]{:S(2)}) collective-permute-start(bf16[128,2176]{1,0:T(8,128)(2,1)S(1)} %collective-permute-done.5), channel_id=1, source_target_pairs={{0,1},{1,0},{2,3},{3,2},{4,5},{5,4},{6,7},{7,6},{8,9},{9,8},{10,11... | collective-permute-start | bytes 1671176 | tf_op jit(solution)/shard_map/ppermute | solution.py:287
  27.6 1.5 collective-permute-start.8
  29.6 5.1 %multiply_reduce_fusion = f32[2048]{0:T(1024)S(1)} fusion(bf16[2048,2048]{1,0:T(8,128)(2,1)} %param.13), kind=kLoop, calls=%fused_computation | loop fusion | flops 12580864 | bytes 8396800 | tf_op jit(solution)/shard_map/reduce_sum | solution.py:439
  34.7 1.5 pick.5
  36.2 2.2 %collective-permute-done.7 = bf16[128,2176]{1,0:T(8,128)(2,1)S(1)} collective-permute-done((bf16[128,2176]{1,0:T(8,128)(2,1)S(1)}, bf16[128,2176]{1,0:T(8,128)(2,1)S(1)}, u32[]{:S(2)}, u32[]{:S(2)}) %collective-permute-start.7) | collective-permute-done | bytes 557088 | tf_op jit(solution)/shard_map/ppermute | solution.py:287
  42.6 1.4 pick.6
  44.0 8.2 %collective-permute-done.10 = bf16[128,2176]{1,0:T(8,128)(2,1)S(1)} collective-permute-done((bf16[128,2176]{1,0:T(8,128)(2,1)S(1)}, bf16[128,2176]{1,0:T(8,128)(2,1)S(1)}, u32[]{:S(2)}, u32[]{:S(2)}) %collective-permute-start.10) | collective-permute-done | bytes 557088 | tf_op jit(solution)/shard_map/ppermute | solution.py:287
  52.4 1.5 collective-permute-done.11.refs_0_
  54.0 1.6 collective-permute-start.13
  56.2 2.0 %collective-permute-start.15 = (bf16[128,2176]{1,0:T(8,128)(2,1)S(1)}, bf16[128,2176]{1,0:T(8,128)(2,1)S(1)}, u32[]{:S(2)}, u32[]{:S(2)}) collective-permute-start(bf16[128,2176]{1,0:T(8,128)(2,1)S(1)} %collective-permute-done.refs_1_), channel_id=1, source_target_pairs={{0,1},{1,0},{2,3},{3,2},{4,5},{5,4},{6,7},{7,6},{8,9},{9,8},{10,11... | collective-permute-start | bytes 1671176 | tf_op jit(solution)/shard_map/ppermute | solution.py:287
  59.7 5.6 %expert_rows.7 = (bf16[256,2048]{1,0:T(8,128)(2,1)S(1)}, bf16[256,2048]{1,0:T(8,128)(2,1)S(1)}) custom-call(s32[2]{0:T(128)S(1)} %pad_add_fusion.who_ref, bf16[256,2176]{1,0:T(8,128)(2,1)S(1)} %get-tuple-element.93.refs_0_, bf16[256,2176]{1,0:T(8,128)(2,1)S(1)} %collective-permute-done.3.refs_1_, bf16[2048,1536]{1,0:T(8,128)(2,1)S(1)} %bitcast.10, ...), custom_call_target="tpu_custom_call" | custom-call | flops 1000 | bytes 1000 | tf_op jit(solution)/shard_map/expert_rows/pallas_call | solution.py:136
  65.8 2.0 %collective-permute-start.18 = (bf16[128,2176]{1,0:T(8,128)(2,1)S(1)}, bf16[128,2176]{1,0:T(8,128)(2,1)S(1)}, u32[]{:S(2)}, u32[]{:S(2)}) collective-permute-start(bf16[128,2176]{1,0:T(8,128)(2,1)S(1)} %collective-permute-done.8.refs_0_), channel_id=1, source_target_pairs={{0,1},{1,0},{2,3},{3,2},{4,5},{5,4},{6,7},{7,6},{8,9},{9,8},{10,11... | collective-permute-start | bytes 1671176 | tf_op jit(solution)/shard_map/ppermute | solution.py:287
  68.0 1.4 collective-permute-start.20
  69.5 1.4 pick.7
  70.9 4.4 %expert_rows.8 = (bf16[192,2048]{1,0:T(8,128)(2,1)S(1)}, bf16[192,2048]{1,0:T(8,128)(2,1)S(1)}) custom-call(s32[2]{0:T(128)S(1)} %pad_add_fusion.who_ref, bf16[192,2176]{1,0:T(8,128)(2,1)S(1)} %get-tuple-element.110.refs_0_, bf16[192,2176]{1,0:T(8,128)(2,1)S(1)} %collective-permute-done.16.refs_1_, bf16[2048,1536]{1,0:T(8,128)(2,1)S(1)} %bitcast.11, ...), custom_call_target="tpu_custom_call" | custom-call | flops 1000 | bytes 1000 | tf_op jit(solution)/shard_map/expert_rows/pallas_call | solution.py:136
  75.3 2.8 %expert_rows.9.mine = bf16[192,2048]{1,0:T(8,128)(2,1)S(1)} custom-call(s32[2]{0:T(128)S(1)} %pad_add_fusion.who_ref, bf16[192,2176]{1,0:T(8,128)(2,1)S(1)} %get-tuple-element.113.refs_0_, bf16[2048,1536]{1,0:T(8,128)(2,1)S(1)} %bitcast.12, bf16[768,2048]{1,0:T(8,128)(2,1)S(1)} %bitcast.19), custom_call_target="tpu_custom_call" | custom-call | flops 1000 | bytes 1000 | tf_op jit(solution)/shard_map/expert_rows/pallas_call | solution.py:136
  78.0 2.4 %collective-permute-done.18.refs_0_ = bf16[128,2176]{1,0:T(8,128)(2,1)S(1)} collective-permute-done((bf16[128,2176]{1,0:T(8,128)(2,1)S(1)}, bf16[128,2176]{1,0:T(8,128)(2,1)S(1)}, u32[]{:S(2)}, u32[]{:S(2)}) %collective-permute-start.18) | collective-permute-done | bytes 557088 | tf_op jit(solution)/shard_map/ppermute | solution.py:287
  82.6 2.6 %expert_rows.10.mine = bf16[192,2048]{1,0:T(8,128)(2,1)S(1)} custom-call(s32[2]{0:T(128)S(1)} %pad_add_fusion.who_ref, bf16[192,2176]{1,0:T(8,128)(2,1)S(1)} %get-tuple-element.122.refs_0_, bf16[2048,1536]{1,0:T(8,128)(2,1)S(1)} %bitcast.13, bf16[768,2048]{1,0:T(8,128)(2,1)S(1)} %bitcast.20), custom_call_target="tpu_custom_call" | custom-call | flops 1000 | bytes 1000 | tf_op jit(solution)/shard_map/expert_rows/pallas_call | solution.py:136
  85.2 2.6 %expert_rows.11 = bf16[192,2048]{1,0:T(8,128)(2,1)S(1)} custom-call(s32[2]{0:T(128)S(1)} %pad_add_fusion.who_ref, bf16[192,2176]{1,0:T(8,128)(2,1)S(1)} %collective-permute-done.21.refs_0_, bf16[2048,1536]{1,0:T(8,128)(2,1)S(1)} %bitcast.14, bf16[768,2048]{1,0:T(8,128)(2,1)S(1)} %bitcast.21), custom_call_target="tpu_custom_call" | custom-call | flops 1000 | bytes 1000 | tf_op jit(solution)/shard_map/expert_rows/pallas_call | solution.py:136
  88.8 2.6 %expert_rows.12 = bf16[192,2048]{1,0:T(8,128)(2,1)S(1)} custom-call(s32[2]{0:T(128)S(1)} %pad_add_fusion.who_ref, bf16[192,2176]{1,0:T(8,128)(2,1)S(1)} %collective-permute-done.17.refs_0_, bf16[2048,1536]{1,0:T(8,128)(2,1)S(1)} %bitcast.15, bf16[768,2048]{1,0:T(8,128)(2,1)S(1)} %bitcast.22), custom_call_target="tpu_custom_call" | custom-call | flops 1000 | bytes 1000 | tf_op jit(solution)/shard_map/expert_rows/pallas_call | solution.py:136
  92.1 1.5 collective-permute-start.24
  93.6 1.7 collective-permute-start.25
  95.3 1.7 collective-permute-start.26
  97.6 4.4 %expert_rows.13 = (bf16[192,2048]{1,0:T(8,128)(2,1)S(1)}, bf16[192,2048]{1,0:T(8,128)(2,1)S(1)}) custom-call(s32[2]{0:T(128)S(1)} %pad_add_fusion.who_ref, bf16[192,2176]{1,0:T(8,128)(2,1)S(1)} %get-tuple-element.140.refs_0_, bf16[192,2176]{1,0:T(8,128)(2,1)S(1)} %collective-permute-done.27.refs_1_, bf16[2048,1536]{1,0:T(8,128)(2,1)S(1)} %bitcast.16, ...), custom_call_target="tpu_custom_call" | custom-call | flops 1000 | bytes 1000 | tf_op jit(solution)/shard_map/expert_rows/pallas_call | solution.py:136
  103.4 3.0 %collective-permute-done.24 = bf16[128,2048]{1,0:T(8,128)(2,1)S(1)} collective-permute-done((bf16[128,2048]{1,0:T(8,128)(2,1)S(1)}, bf16[128,2048]{1,0:T(8,128)(2,1)S(1)}, u32[]{:S(2)}, u32[]{:S(2)}) %collective-permute-start.24) | collective-permute-done | bytes 524320 | tf_op jit(solution)/shard_map/ppermute | solution.py:287
  109.5 1.4 collective-permute-start.32
  111.0 1.7 collective-permute-start.29
  113.4 8.4 %collective-permute-done.31 = bf16[128,2048]{1,0:T(8,128)(2,1)S(1)} collective-permute-done((bf16[128,2048]{1,0:T(8,128)(2,1)S(1)}, bf16[128,2048]{1,0:T(8,128)(2,1)S(1)}, u32[]{:S(2)}, u32[]{:S(2)}) %collective-permute-start.31) | collective-permute-done | bytes 524320 | tf_op jit(solution)/shard_map/ppermute | solution.py:287
  123.5 1.7 collective-permute-start.35
  127.2 8.0 %collective-permute-done.35 = bf16[128,2048]{1,0:T(8,128)(2,1)S(1)} collective-permute-done((bf16[128,2048]{1,0:T(8,128)(2,1)S(1)}, bf16[128,2048]{1,0:T(8,128)(2,1)S(1)}, u32[]{:S(2)}, u32[]{:S(2)}) %collective-permute-start.35) | collective-permute-done | bytes 524320 | tf_op jit(solution)/shard_map/ppermute | solution.py:287
  135.4 1.6 collective-permute-done.33
  137.2 1.8 collective-permute-start.36
  140.6 3.1 %collective-permute-start.40 = (bf16[128,2048]{1,0:T(8,128)(2,1)S(1)}, bf16[128,2048]{1,0:T(8,128)(2,1)S(1)}, u32[]{:S(2)}, u32[]{:S(2)}) collective-permute-start(bf16[128,2048]{1,0:T(8,128)(2,1)S(1)} %add_convert_fusion.2.refs_9_), channel_id=1, source_target_pairs={{0,1},{1,0},{2,3},{3,2},{4,5},{5,4},{6,7},{7,6},{8,9},{9,8},{10,11... | collective-permute-start | bytes 1572872 | tf_op jit(solution)/shard_map/ppermute | solution.py:287
  145.3 3.3 %collective-permute-done.36.refs_3_ = bf16[128,2048]{1,0:T(8,128)(2,1)S(1)} collective-permute-done((bf16[128,2048]{1,0:T(8,128)(2,1)S(1)}, bf16[128,2048]{1,0:T(8,128)(2,1)S(1)}, u32[]{:S(2)}, u32[]{:S(2)}) %collective-permute-start.36) | collective-permute-done | bytes 524320 | tf_op jit(solution)/shard_map/ppermute | solution.py:287
  148.6 3.7 %collective-permute-done.40.refs_10_ = bf16[128,2048]{1,0:T(8,128)(2,1)S(1)} collective-permute-done((bf16[128,2048]{1,0:T(8,128)(2,1)S(1)}, bf16[128,2048]{1,0:T(8,128)(2,1)S(1)}, u32[]{:S(2)}, u32[]{:S(2)}) %collective-permute-start.40) | collective-permute-done | bytes 524320 | tf_op jit(solution)/shard_map/ppermute | solution.py:287
  153.3 2.0 %collective-permute-start.46 = (f32[8,2048]{1,0:T(8,128)S(1)}, f32[8,2048]{1,0:T(8,128)S(1)}, u32[]{:S(2)}, u32[]{:S(2)}) collective-permute-start(f32[8,2048]{1,0:T(8,128)S(1)} %get-tuple-element.177), channel_id=1, source_target_pairs={{0,1},{1,0},{2,3},{3,2},{4,5},{5,4},{6,7},{7,6},{8,9},{9,8},{10,11... | collective-permute-start | bytes 196616 | tf_op jit(solution)/shard_map/ppermute | solution.py:287
  156.7 1.9 %collective-permute-start.41 = (bf16[128,2048]{1,0:T(8,128)(2,1)S(1)}, bf16[128,2048]{1,0:T(8,128)(2,1)S(1)}, u32[]{:S(2)}, u32[]{:S(2)}) collective-permute-start(bf16[128,2048]{1,0:T(8,128)(2,1)S(1)} %get-tuple-element.170), channel_id=1, source_target_pairs={{0,16},{4,20},{8,24},{12,28},{16,0},{20,4},{24,8},{28,12},{1,17},{... | collective-permute-start | bytes 1572872 | tf_op jit(solution)/shard_map/ppermute | solution.py:287
  158.6 2.0 %collective-permute-start.42 = (bf16[128,2048]{1,0:T(8,128)(2,1)S(1)}, bf16[128,2048]{1,0:T(8,128)(2,1)S(1)}, u32[]{:S(2)}, u32[]{:S(2)}) collective-permute-start(bf16[128,2048]{1,0:T(8,128)(2,1)S(1)} %get-tuple-element.171), channel_id=1, source_target_pairs={{0,1},{1,0},{2,3},{3,2},{4,5},{5,4},{6,7},{7,6},{8,9},{9,8},{10,11... | collective-permute-start | bytes 1572872 | tf_op jit(solution)/shard_map/ppermute | solution.py:287
  161.6 9.4 %all_gather.3 = bf16[64,2048]{1,0:T(8,128)(2,1)S(1)} all-gather(bf16[8,2048]{1,0:T(8,128)(2,1)S(1)} %multiply_convert_fusion), channel_id=1, replica_groups=mesh['center'=8,'expert'=4] {'center'}, dimensions={0}, use_global_device_ids=true | all-gather | bytes 294912 | tf_op jit(solution)/shard_map/all_gather | solution.py:462
  171.1 2.8 %fusion.1 = f32[64]{0:T(128)S(1)} fusion(bf16[64,2048]{1,0:T(8,128)(2,1)S(1)} %all_gather.3, bf16[2048,2048]{1,0:T(8,128)(2,1)S(1)} %bitcast.25, f32[2048]{0:T(1024)S(1)} %multiply_reduce_fusion, f32[64]{0:T(128)S(1)} %multiply_reduce_fusion.1), kind=kOutput, calls=%fused_computation.3 | convolution fusion | flops 537395136 | bytes 8659456 | tf_op jit(solution)/shard_map/dot_general | solution.py:465
  177.1 1.5 collective-permute-start.50
  179.7 1.9 %collective-permute-done.50 = f32[64]{0:T(128)S(1)} collective-permute-done((f32[64]{0:T(128)S(1)}, f32[64]{0:T(128)S(1)}, u32[]{:S(2)}, u32[]{:S(2)}) %collective-permute-start.50) | collective-permute-done | bytes 288 | tf_op jit(solution)/shard_map/ppermute | solution.py:287
  (115 shorter events, 37.1 us)
Async XLA Ops:
  2.8 9.8 %collective-permute-start.5 = (bf16[128,2176]{1,0:T(8,128)(2,1)}, bf16[128,2176]{1,0:T(8,128)(2,1)S(1)}, u32[]{:S(2)}, u32[]{:S(2)}) collective-permute-start(bf16[128,2176]{1,0:T(8,128)(2,1)} %enter.1.refs_0_), channel_id=1, source_target_pairs={{1,2},{2,1},{5,6},{6,5},{9,10},{10,9},{13,14},{14,13},{17,18},{18,... | collective-permute-start | bytes 1671176 | tf_op jit(solution)/shard_map/ppermute | solution.py:287
  3.7 18.4 %collective-permute-start.2 = (bf16[128,2176]{1,0:T(8,128)(2,1)}, bf16[128,2176]{1,0:T(8,128)(2,1)S(1)}, u32[]{:S(2)}, u32[]{:S(2)}) collective-permute-start(bf16[128,2176]{1,0:T(8,128)(2,1)} %enter.1.refs_0_), channel_id=1, source_target_pairs={{0,1},{1,0},{2,3},{3,2},{4,5},{5,4},{6,7},{7,6},{8,9},{9,8},{10,11... | collective-permute-start | bytes 1671176 | tf_op jit(solution)/shard_map/ppermute | solution.py:287
  9.5 14.0 %collective-permute-start.1 = (bf16[128,2176]{1,0:T(8,128)(2,1)}, bf16[128,2176]{1,0:T(8,128)(2,1)S(1)}, u32[]{:S(2)}, u32[]{:S(2)}) collective-permute-start(bf16[128,2176]{1,0:T(8,128)(2,1)} %enter.1.refs_0_), channel_id=1, source_target_pairs={{0,16},{4,20},{8,24},{12,28},{16,0},{20,4},{24,8},{28,12},{1,17},{... | collective-permute-start | bytes 1671176 | tf_op jit(solution)/shard_map/ppermute | solution.py:287
  11.1 13.7 %collective-permute-start = (bf16[128,2176]{1,0:T(8,128)(2,1)}, bf16[128,2176]{1,0:T(8,128)(2,1)S(1)}, u32[]{:S(2)}, u32[]{:S(2)}) collective-permute-start(bf16[128,2176]{1,0:T(8,128)(2,1)} %enter.1.refs_0_), channel_id=1, source_target_pairs={{0,8},{4,12},{8,0},{12,4},{16,24},{20,28},{24,16},{28,20},{1,9},{5... | collective-permute-start | bytes 1671176 | tf_op jit(solution)/shard_map/ppermute | solution.py:287
  24.8 13.8 %collective-permute-start.6 = (bf16[128,2176]{1,0:T(8,128)(2,1)S(1)}, bf16[128,2176]{1,0:T(8,128)(2,1)S(1)}, u32[]{:S(2)}, u32[]{:S(2)}) collective-permute-start(bf16[128,2176]{1,0:T(8,128)(2,1)S(1)} %collective-permute-done.2.refs_3_), channel_id=1, source_target_pairs={{1,2},{2,1},{5,6},{6,5},{9,10},{10,9},{13,14},{14,13},{17,18},{18,... | collective-permute-start | bytes 1671176 | tf_op jit(solution)/shard_map/ppermute | solution.py:287
  25.5 12.9 %collective-permute-start.7 = (bf16[128,2176]{1,0:T(8,128)(2,1)S(1)}, bf16[128,2176]{1,0:T(8,128)(2,1)S(1)}, u32[]{:S(2)}, u32[]{:S(2)}) collective-permute-start(bf16[128,2176]{1,0:T(8,128)(2,1)S(1)} %collective-permute-done.5), channel_id=1, source_target_pairs={{0,1},{1,0},{2,3},{3,2},{4,5},{5,4},{6,7},{7,6},{8,9},{9,8},{10,11... | collective-permute-start | bytes 1671176 | tf_op jit(solution)/shard_map/ppermute | solution.py:287
  27.6 12.3 %collective-permute-start.8 = (bf16[128,2176]{1,0:T(8,128)(2,1)S(1)}, bf16[128,2176]{1,0:T(8,128)(2,1)S(1)}, u32[]{:S(2)}, u32[]{:S(2)}) collective-permute-start(bf16[128,2176]{1,0:T(8,128)(2,1)S(1)} %collective-permute-done.1.refs_2_), channel_id=1, source_target_pairs={{0,8},{4,12},{8,0},{12,4},{16,24},{20,28},{24,16},{28,20},{1,9},{5... | collective-permute-start | bytes 1671176 | tf_op jit(solution)/shard_map/ppermute | solution.py:287
  29.1 12.0 %collective-permute-start.9 = (bf16[128,2176]{1,0:T(8,128)(2,1)S(1)}, bf16[128,2176]{1,0:T(8,128)(2,1)S(1)}, u32[]{:S(2)}, u32[]{:S(2)}) collective-permute-start(bf16[128,2176]{1,0:T(8,128)(2,1)S(1)} %collective-permute-done.2.refs_3_), channel_id=1, source_target_pairs={{0,16},{4,20},{8,24},{12,28},{16,0},{20,4},{24,8},{28,12},{1,17},{... | collective-permute-start | bytes 1671176 | tf_op jit(solution)/shard_map/ppermute | solution.py:287
  41.1 11.1 %collective-permute-start.10 = (bf16[128,2176]{1,0:T(8,128)(2,1)S(1)}, bf16[128,2176]{1,0:T(8,128)(2,1)S(1)}, u32[]{:S(2)}, u32[]{:S(2)}) collective-permute-start(bf16[128,2176]{1,0:T(8,128)(2,1)S(1)} %collective-permute-done.6), channel_id=1, source_target_pairs={{0,1},{1,0},{2,3},{3,2},{4,5},{5,4},{6,7},{7,6},{8,9},{9,8},{10,11... | collective-permute-start | bytes 1671176 | tf_op jit(solution)/shard_map/ppermute | solution.py:287
  41.5 12.4 %collective-permute-start.11 = (bf16[128,2176]{1,0:T(8,128)(2,1)S(1)}, bf16[128,2176]{1,0:T(8,128)(2,1)S(1)}, u32[]{:S(2)}, u32[]{:S(2)}) collective-permute-start(bf16[128,2176]{1,0:T(8,128)(2,1)S(1)} %add.86.refs_2_), channel_id=1, source_target_pairs={{0,8},{4,12},{8,0},{12,4},{16,24},{20,28},{24,16},{28,20},{1,9},{5... | collective-permute-start | bytes 1671176 | tf_op jit(solution)/shard_map/ppermute | solution.py:287
  42.0 12.0 %collective-permute-start.12 = (bf16[128,2176]{1,0:T(8,128)(2,1)S(1)}, bf16[128,2176]{1,0:T(8,128)(2,1)S(1)}, u32[]{:S(2)}, u32[]{:S(2)}) collective-permute-start(bf16[128,2176]{1,0:T(8,128)(2,1)S(1)} %add.86.refs_2_), channel_id=1, source_target_pairs={{0,16},{4,20},{8,24},{12,28},{16,0},{20,4},{24,8},{28,12},{1,17},{... | collective-permute-start | bytes 1671176 | tf_op jit(solution)/shard_map/ppermute | solution.py:287
  42.6 17.1 %collective-permute-start.3 = (bf16[256,2176]{1,0:T(8,128)(2,1)S(1)}, bf16[256,2176]{1,0:T(8,128)(2,1)S(1)}, u32[]{:S(2)}, u32[]{:S(2)}) collective-permute-start(bf16[256,2176]{1,0:T(8,128)(2,1)S(1)} %get-tuple-element.94), channel_id=1, source_target_pairs={{0,4},{4,0},{8,12},{12,8},{16,20},{20,16},{24,28},{28,24},{1,5},{5... | collective-permute-start | bytes 3342344 | tf_op jit(solution)/shard_map/ppermute | solution.py:287
  54.0 11.4 %collective-permute-start.13 = (bf16[128,2176]{1,0:T(8,128)(2,1)S(1)}, bf16[128,2176]{1,0:T(8,128)(2,1)S(1)}, u32[]{:S(2)}, u32[]{:S(2)}) collective-permute-start(bf16[128,2176]{1,0:T(8,128)(2,1)S(1)} %add.87.refs_2_), channel_id=1, source_target_pairs={{0,8},{4,12},{8,0},{12,4},{16,24},{20,28},{24,16},{28,20},{1,9},{5... | collective-permute-start | bytes 1671176 | tf_op jit(solution)/shard_map/ppermute | solution.py:287
  55.6 9.8 %collective-permute-start.14 = (bf16[128,2176]{1,0:T(8,128)(2,1)S(1)}, bf16[128,2176]{1,0:T(8,128)(2,1)S(1)}, u32[]{:S(2)}, u32[]{:S(2)}) collective-permute-start(bf16[128,2176]{1,0:T(8,128)(2,1)S(1)} %add.87.refs_2_), channel_id=1, source_target_pairs={{0,16},{4,20},{8,24},{12,28},{16,0},{20,4},{24,8},{28,12},{1,17},{... | collective-permute-start | bytes 1671176 | tf_op jit(solution)/shard_map/ppermute | solution.py:287
  56.2 9.5 %collective-permute-start.15 = (bf16[128,2176]{1,0:T(8,128)(2,1)S(1)}, bf16[128,2176]{1,0:T(8,128)(2,1)S(1)}, u32[]{:S(2)}, u32[]{:S(2)}) collective-permute-start(bf16[128,2176]{1,0:T(8,128)(2,1)S(1)} %collective-permute-done.refs_1_), channel_id=1, source_target_pairs={{0,1},{1,0},{2,3},{3,2},{4,5},{5,4},{6,7},{7,6},{8,9},{9,8},{10,11... | collective-permute-start | bytes 1671176 | tf_op jit(solution)/shard_map/ppermute | solution.py:287
  59.6 11.3 %collective-permute-start.16 = (bf16[192,2176]{1,0:T(8,128)(2,1)S(1)}, bf16[192,2176]{1,0:T(8,128)(2,1)S(1)}, u32[]{:S(2)}, u32[]{:S(2)}) collective-permute-start(bf16[192,2176]{1,0:T(8,128)(2,1)S(1)} %get-tuple-element.111), channel_id=1, source_target_pairs={{0,4},{4,0},{8,12},{12,8},{16,20},{20,16},{24,28},{28,24},{1,5},{5... | collective-permute-start | bytes 2506760 | tf_op jit(solution)/shard_map/ppermute | solution.py:287
  65.8 14.7 %collective-permute-start.18 = (bf16[128,2176]{1,0:T(8,128)(2,1)S(1)}, bf16[128,2176]{1,0:T(8,128)(2,1)S(1)}, u32[]{:S(2)}, u32[]{:S(2)}) collective-permute-start(bf16[128,2176]{1,0:T(8,128)(2,1)S(1)} %collective-permute-done.8.refs_0_), channel_id=1, source_target_pairs={{0,1},{1,0},{2,3},{3,2},{4,5},{5,4},{6,7},{7,6},{8,9},{9,8},{10,11... | collective-permute-start | bytes 1671176 | tf_op jit(solution)/shard_map/ppermute | solution.py:287
  67.8 12.8 %collective-permute-start.19 = (bf16[128,2176]{1,0:T(8,128)(2,1)S(1)}, bf16[128,2176]{1,0:T(8,128)(2,1)S(1)}, u32[]{:S(2)}, u32[]{:S(2)}) collective-permute-start(bf16[128,2176]{1,0:T(8,128)(2,1)S(1)} %collective-permute-done.12.refs_1_), channel_id=1, source_target_pairs={{0,8},{4,12},{8,0},{12,4},{16,24},{20,28},{24,16},{28,20},{1,9},{5... | collective-permute-start | bytes 1671176 | tf_op jit(solution)/shard_map/ppermute | solution.py:287
  68.0 12.6 %collective-permute-start.20 = (bf16[128,2176]{1,0:T(8,128)(2,1)S(1)}, bf16[128,2176]{1,0:T(8,128)(2,1)S(1)}, u32[]{:S(2)}, u32[]{:S(2)}) collective-permute-start(bf16[128,2176]{1,0:T(8,128)(2,1)S(1)} %collective-permute-done.13.refs_0_), channel_id=1, source_target_pairs={{0,16},{4,20},{8,24},{12,28},{16,0},{20,4},{24,8},{28,12},{1,17},{... | collective-permute-start | bytes 1671176 | tf_op jit(solution)/shard_map/ppermute | solution.py:287
  82.1 6.7 %collective-permute-start.17 = (bf16[192,2176]{1,0:T(8,128)(2,1)S(1)}, bf16[192,2176]{1,0:T(8,128)(2,1)S(1)}, u32[]{:S(2)}, u32[]{:S(2)}) collective-permute-start(bf16[192,2176]{1,0:T(8,128)(2,1)S(1)} %get-tuple-element.114), channel_id=1, source_target_pairs={{0,4},{4,0},{8,12},{12,8},{16,20},{20,16},{24,28},{28,24},{1,5},{5... | collective-permute-start | bytes 2506760 | tf_op jit(solution)/shard_map/ppermute | solution.py:287
  87.7 3.8 %collective-permute-start.23 = (bf16[192,2048]{1,0:T(8,128)(2,1)S(1)}, bf16[192,2048]{1,0:T(8,128)(2,1)S(1)}, u32[]{:S(2)}, u32[]{:S(2)}) collective-permute-start(bf16[192,2048]{1,0:T(8,128)(2,1)S(1)} %expert_rows.11), channel_id=1, source_target_pairs={{0,4},{4,0},{8,12},{12,8},{16,20},{20,16},{24,28},{28,24},{1,5},{5... | collective-permute-start | bytes 2359304 | tf_op jit(solution)/shard_map/ppermute | solution.py:287
  87.9 14.8 %collective-permute-start.4 = (bf16[256,2048]{1,0:T(8,128)(2,1)S(1)}, bf16[256,2048]{1,0:T(8,128)(2,1)S(1)}, u32[]{:S(2)}, u32[]{:S(2)}) collective-permute-start(bf16[256,2048]{1,0:T(8,128)(2,1)S(1)} %get-tuple-element.96), channel_id=1, source_target_pairs={{0,4},{4,0},{8,12},{12,8},{16,20},{20,16},{24,28},{28,24},{1,5},{5... | collective-permute-start | bytes 3145736 | tf_op jit(solution)/shard_map/ppermute | solution.py:287
  88.3 5.3 %collective-permute-start.27 = (bf16[192,2176]{1,0:T(8,128)(2,1)S(1)}, bf16[192,2176]{1,0:T(8,128)(2,1)S(1)}, u32[]{:S(2)}, u32[]{:S(2)}) collective-permute-start(bf16[192,2176]{1,0:T(8,128)(2,1)S(1)} %get-tuple-element.141), channel_id=1, source_target_pairs={{0,4},{4,0},{8,12},{12,8},{16,20},{20,16},{24,28},{28,24},{1,5},{5... | collective-permute-start | bytes 2506760 | tf_op jit(solution)/shard_map/ppermute | solution.py:287
  88.4 6.9 %collective-permute-start.28 = (bf16[192,2048]{1,0:T(8,128)(2,1)S(1)}, bf16[192,2048]{1,0:T(8,128)(2,1)S(1)}, u32[]{:S(2)}, u32[]{:S(2)}) collective-permute-start(bf16[192,2048]{1,0:T(8,128)(2,1)S(1)} %get-tuple-element.144), channel_id=1, source_target_pairs={{0,4},{4,0},{8,12},{12,8},{16,20},{20,16},{24,28},{28,24},{1,5},{5... | collective-permute-start | bytes 2359304 | tf_op jit(solution)/shard_map/ppermute | solution.py:287
  91.4 10.6 %collective-permute-start.22 = (bf16[192,2048]{1,0:T(8,128)(2,1)S(1)}, bf16[192,2048]{1,0:T(8,128)(2,1)S(1)}, u32[]{:S(2)}, u32[]{:S(2)}) collective-permute-start(bf16[192,2048]{1,0:T(8,128)(2,1)S(1)} %expert_rows.12), channel_id=1, source_target_pairs={{0,4},{4,0},{8,12},{12,8},{16,20},{20,16},{24,28},{28,24},{1,5},{5... | collective-permute-start | bytes 2359304 | tf_op jit(solution)/shard_map/ppermute | solution.py:287
  92.1 14.3 %collective-permute-start.24 = (bf16[128,2048]{1,0:T(8,128)(2,1)S(1)}, bf16[128,2048]{1,0:T(8,128)(2,1)S(1)}, u32[]{:S(2)}, u32[]{:S(2)}) collective-permute-start(bf16[128,2048]{1,0:T(8,128)(2,1)S(1)} %get-tuple-element.136), channel_id=1, source_target_pairs={{0,16},{4,20},{8,24},{12,28},{16,0},{20,4},{24,8},{28,12},{1,17},{... | collective-permute-start | bytes 1572872 | tf_op jit(solution)/shard_map/ppermute | solution.py:287
  93.6 14.0 %collective-permute-start.25 = (bf16[128,2048]{1,0:T(8,128)(2,1)S(1)}, bf16[128,2048]{1,0:T(8,128)(2,1)S(1)}, u32[]{:S(2)}, u32[]{:S(2)}) collective-permute-start(bf16[128,2048]{1,0:T(8,128)(2,1)S(1)} %get-tuple-element.139), channel_id=1, source_target_pairs={{0,8},{4,12},{8,0},{12,4},{16,24},{20,28},{24,16},{28,20},{1,9},{5... | collective-permute-start | bytes 1572872 | tf_op jit(solution)/shard_map/ppermute | solution.py:287
  95.3 13.7 %collective-permute-start.26 = (bf16[128,2048]{1,0:T(8,128)(2,1)S(1)}, bf16[128,2048]{1,0:T(8,128)(2,1)S(1)}, u32[]{:S(2)}, u32[]{:S(2)}) collective-permute-start(bf16[128,2048]{1,0:T(8,128)(2,1)S(1)} %get-tuple-element.126), channel_id=1, source_target_pairs={{0,1},{1,0},{2,3},{3,2},{4,5},{5,4},{6,7},{7,6},{8,9},{9,8},{10,11... | collective-permute-start | bytes 1572872 | tf_op jit(solution)/shard_map/ppermute | solution.py:287
  102.0 10.8 %collective-permute-start.30 = (bf16[192,2048]{1,0:T(8,128)(2,1)S(1)}, bf16[192,2048]{1,0:T(8,128)(2,1)S(1)}, u32[]{:S(2)}, u32[]{:S(2)}) collective-permute-start(bf16[192,2048]{1,0:T(8,128)(2,1)S(1)} %get-tuple-element.152), channel_id=1, source_target_pairs={{0,4},{4,0},{8,12},{12,8},{16,20},{20,16},{24,28},{28,24},{1,5},{5... | collective-permute-start | bytes 2359304 | tf_op jit(solution)/shard_map/ppermute | solution.py:287
  109.0 12.8 %collective-permute-start.31 = (bf16[128,2048]{1,0:T(8,128)(2,1)S(1)}, bf16[128,2048]{1,0:T(8,128)(2,1)S(1)}, u32[]{:S(2)}, u32[]{:S(2)}) collective-permute-start(bf16[128,2048]{1,0:T(8,128)(2,1)S(1)} %add_convert_fusion.6), channel_id=1, source_target_pairs={{0,8},{4,12},{8,0},{12,4},{16,24},{20,28},{24,16},{28,20},{1,9},{5... | collective-permute-start | bytes 1572872 | tf_op jit(solution)/shard_map/ppermute | solution.py:287
  109.5 12.7 %collective-permute-start.32 = (bf16[128,2048]{1,0:T(8,128)(2,1)S(1)}, bf16[128,2048]{1,0:T(8,128)(2,1)S(1)}, u32[]{:S(2)}, u32[]{:S(2)}) collective-permute-start(bf16[128,2048]{1,0:T(8,128)(2,1)S(1)} %get-tuple-element.159), channel_id=1, source_target_pairs={{0,16},{4,20},{8,24},{12,28},{16,0},{20,4},{24,8},{28,12},{1,17},{... | collective-permute-start | bytes 1572872 | tf_op jit(solution)/shard_map/ppermute | solution.py:287
  111.0 12.6 %collective-permute-start.29 = (bf16[128,2048]{1,0:T(8,128)(2,1)S(1)}, bf16[128,2048]{1,0:T(8,128)(2,1)S(1)}, u32[]{:S(2)}, u32[]{:S(2)}) collective-permute-start(bf16[128,2048]{1,0:T(8,128)(2,1)S(1)} %get-tuple-element.149), channel_id=1, source_target_pairs={{0,1},{1,0},{2,3},{3,2},{4,5},{5,4},{6,7},{7,6},{8,9},{9,8},{10,11... | collective-permute-start | bytes 1572872 | tf_op jit(solution)/shard_map/ppermute | solution.py:287
  123.5 11.7 %collective-permute-start.35 = (bf16[128,2048]{1,0:T(8,128)(2,1)S(1)}, bf16[128,2048]{1,0:T(8,128)(2,1)S(1)}, u32[]{:S(2)}, u32[]{:S(2)}) collective-permute-start(bf16[128,2048]{1,0:T(8,128)(2,1)S(1)} %add_convert_fusion.3), channel_id=1, source_target_pairs={{0,1},{1,0},{2,3},{3,2},{4,5},{5,4},{6,7},{7,6},{8,9},{9,8},{10,11... | collective-permute-start | bytes 1572872 | tf_op jit(solution)/shard_map/ppermute | solution.py:287
  125.2 11.8 %collective-permute-start.33 = (bf16[128,2048]{1,0:T(8,128)(2,1)S(1)}, bf16[128,2048]{1,0:T(8,128)(2,1)S(1)}, u32[]{:S(2)}, u32[]{:S(2)}) collective-permute-start(bf16[128,2048]{1,0:T(8,128)(2,1)S(1)} %get-tuple-element.160), channel_id=1, source_target_pairs={{0,8},{4,12},{8,0},{12,4},{16,24},{20,28},{24,16},{28,20},{1,9},{5... | collective-permute-start | bytes 1572872 | tf_op jit(solution)/shard_map/ppermute | solution.py:287
  125.8 11.2 %collective-permute-start.34 = (bf16[128,2048]{1,0:T(8,128)(2,1)S(1)}, bf16[128,2048]{1,0:T(8,128)(2,1)S(1)}, u32[]{:S(2)}, u32[]{:S(2)}) collective-permute-start(bf16[128,2048]{1,0:T(8,128)(2,1)S(1)} %add_convert_fusion.4), channel_id=1, source_target_pairs={{0,16},{4,20},{8,24},{12,28},{16,0},{20,4},{24,8},{28,12},{1,17},{... | collective-permute-start | bytes 1572872 | tf_op jit(solution)/shard_map/ppermute | solution.py:287
  137.2 11.3 %collective-permute-start.36 = (bf16[128,2048]{1,0:T(8,128)(2,1)S(1)}, bf16[128,2048]{1,0:T(8,128)(2,1)S(1)}, u32[]{:S(2)}, u32[]{:S(2)}) collective-permute-start(bf16[128,2048]{1,0:T(8,128)(2,1)S(1)} %add_convert_fusion.5), channel_id=1, source_target_pairs={{0,8},{4,12},{8,0},{12,4},{16,24},{20,28},{24,16},{28,20},{1,9},{5... | collective-permute-start | bytes 1572872 | tf_op jit(solution)/shard_map/ppermute | solution.py:287
  139.1 9.5 %collective-permute-start.38 = (bf16[128,2048]{1,0:T(8,128)(2,1)S(1)}, bf16[128,2048]{1,0:T(8,128)(2,1)S(1)}, u32[]{:S(2)}, u32[]{:S(2)}) collective-permute-start(bf16[128,2048]{1,0:T(8,128)(2,1)S(1)} %get-tuple-element.167), channel_id=1, source_target_pairs={{0,16},{4,20},{8,24},{12,28},{16,0},{20,4},{24,8},{28,12},{1,17},{... | collective-permute-start | bytes 1572872 | tf_op jit(solution)/shard_map/ppermute | solution.py:287
  139.9 8.7 %collective-permute-start.39 = (bf16[128,2048]{1,0:T(8,128)(2,1)S(1)}, bf16[128,2048]{1,0:T(8,128)(2,1)S(1)}, u32[]{:S(2)}, u32[]{:S(2)}) collective-permute-start(bf16[128,2048]{1,0:T(8,128)(2,1)S(1)} %add_convert_fusion.1), channel_id=1, source_target_pairs={{1,2},{2,1},{5,6},{6,5},{9,10},{10,9},{13,14},{14,13},{17,18},{18,... | collective-permute-start | bytes 1572872 | tf_op jit(solution)/shard_map/ppermute | solution.py:287
  140.6 11.7 %collective-permute-start.40 = (bf16[128,2048]{1,0:T(8,128)(2,1)S(1)}, bf16[128,2048]{1,0:T(8,128)(2,1)S(1)}, u32[]{:S(2)}, u32[]{:S(2)}) collective-permute-start(bf16[128,2048]{1,0:T(8,128)(2,1)S(1)} %add_convert_fusion.2.refs_9_), channel_id=1, source_target_pairs={{0,1},{1,0},{2,3},{3,2},{4,5},{5,4},{6,7},{7,6},{8,9},{9,8},{10,11... | collective-permute-start | bytes 1572872 | tf_op jit(solution)/shard_map/ppermute | solution.py:287
  144.7 12.0 %collective-permute-start.44 = (f32[8,2048]{1,0:T(8,128)S(1)}, f32[8,2048]{1,0:T(8,128)S(1)}, u32[]{:S(2)}, u32[]{:S(2)}) collective-permute-start(f32[8,2048]{1,0:T(8,128)S(1)} %get-tuple-element.175), channel_id=1, source_target_pairs={{0,8},{4,12},{8,0},{12,4},{16,24},{20,28},{24,16},{28,20},{1,9},{5... | collective-permute-start | bytes 196616 | tf_op jit(solution)/shard_map/ppermute | solution.py:287
  153.1 5.5 %collective-permute-start.45 = (f32[8,2048]{1,0:T(8,128)S(1)}, f32[8,2048]{1,0:T(8,128)S(1)}, u32[]{:S(2)}, u32[]{:S(2)}) collective-permute-start(f32[8,2048]{1,0:T(8,128)S(1)} %get-tuple-element.176), channel_id=1, source_target_pairs={{0,16},{4,20},{8,24},{12,28},{16,0},{20,4},{24,8},{28,12},{1,17},{... | collective-permute-start | bytes 196616 | tf_op jit(solution)/shard_map/ppermute | solution.py:287
  153.3 7.4 %collective-permute-start.46 = (f32[8,2048]{1,0:T(8,128)S(1)}, f32[8,2048]{1,0:T(8,128)S(1)}, u32[]{:S(2)}, u32[]{:S(2)}) collective-permute-start(f32[8,2048]{1,0:T(8,128)S(1)} %get-tuple-element.177), channel_id=1, source_target_pairs={{0,1},{1,0},{2,3},{3,2},{4,5},{5,4},{6,7},{7,6},{8,9},{9,8},{10,11... | collective-permute-start | bytes 196616 | tf_op jit(solution)/shard_map/ppermute | solution.py:287
  155.3 6.0 %collective-permute-start.47 = (f32[8,2048]{1,0:T(8,128)S(1)}, f32[8,2048]{1,0:T(8,128)S(1)}, u32[]{:S(2)}, u32[]{:S(2)}) collective-permute-start(f32[8,2048]{1,0:T(8,128)S(1)} %get-tuple-element.178), channel_id=1, source_target_pairs={{1,2},{2,1},{5,6},{6,5},{9,10},{10,9},{13,14},{14,13},{17,18},{18,... | collective-permute-start | bytes 196616 | tf_op jit(solution)/shard_map/ppermute | solution.py:287
  155.9 17.9 %collective-permute-start.37 = (bf16[128,2048]{1,0:T(8,128)(2,1)S(1)}, bf16[128,2048]{1,0:T(8,128)(2,1)S(1)}, u32[]{:S(2)}, u32[]{:S(2)}) collective-permute-start(bf16[128,2048]{1,0:T(8,128)(2,1)S(1)} %get-tuple-element.164), channel_id=1, source_target_pairs={{0,8},{4,12},{8,0},{12,4},{16,24},{20,28},{24,16},{28,20},{1,9},{5... | collective-permute-start | bytes 1572872 | tf_op jit(solution)/shard_map/ppermute | solution.py:287
  156.7 17.2 %collective-permute-start.41 = (bf16[128,2048]{1,0:T(8,128)(2,1)S(1)}, bf16[128,2048]{1,0:T(8,128)(2,1)S(1)}, u32[]{:S(2)}, u32[]{:S(2)}) collective-permute-start(bf16[128,2048]{1,0:T(8,128)(2,1)S(1)} %get-tuple-element.170), channel_id=1, source_target_pairs={{0,16},{4,20},{8,24},{12,28},{16,0},{20,4},{24,8},{28,12},{1,17},{... | collective-permute-start | bytes 1572872 | tf_op jit(solution)/shard_map/ppermute | solution.py:287
  158.6 15.2 %collective-permute-start.42 = (bf16[128,2048]{1,0:T(8,128)(2,1)S(1)}, bf16[128,2048]{1,0:T(8,128)(2,1)S(1)}, u32[]{:S(2)}, u32[]{:S(2)}) collective-permute-start(bf16[128,2048]{1,0:T(8,128)(2,1)S(1)} %get-tuple-element.171), channel_id=1, source_target_pairs={{0,1},{1,0},{2,3},{3,2},{4,5},{5,4},{6,7},{7,6},{8,9},{9,8},{10,11... | collective-permute-start | bytes 1572872 | tf_op jit(solution)/shard_map/ppermute | solution.py:287
  160.6 13.2 %collective-permute-start.43 = (bf16[128,2048]{1,0:T(8,128)(2,1)S(1)}, bf16[128,2048]{1,0:T(8,128)(2,1)S(1)}, u32[]{:S(2)}, u32[]{:S(2)}) collective-permute-start(bf16[128,2048]{1,0:T(8,128)(2,1)S(1)} %get-tuple-element.172), channel_id=1, source_target_pairs={{1,2},{2,1},{5,6},{6,5},{9,10},{10,9},{13,14},{14,13},{17,18},{18,... | collective-permute-start | bytes 1572872 | tf_op jit(solution)/shard_map/ppermute | solution.py:287
  177.1 4.4 %collective-permute-start.50 = (f32[64]{0:T(128)S(1)}, f32[64]{0:T(128)S(1)}, u32[]{:S(2)}, u32[]{:S(2)}) collective-permute-start(f32[64]{0:T(128)S(1)} %fusion.1), channel_id=1, source_target_pairs={{0,24},{4,28},{8,16},{12,20},{16,8},{20,12},{24,0},{28,4},{1,25},{... | collective-permute-start | bytes 776 | tf_op jit(solution)/shard_map/ppermute | solution.py:287
  (10 other events, 254.7 us)

commit v7 on v6

--- a/solution.py
+++ b/solution.py
@@ -323,9 +323,8 @@
     mine, other, choice = picked(bx2, by2, b3)
     third = (mine, crossed(other), choice)
     (first,) = worked(first)
-    d2, d3, d1 = at_once(
-        (SWAP_X, by2), (SWAP_Y, bx3), (SWAP_Z, d0), behind=(bx3, by3, bx1, mine, first[1])
-    )
+    (d1,) = at_once((SWAP_Z, d0), behind=(bx1, mine))
+    d2, d3 = at_once((SWAP_X, by2), (SWAP_Y, bx3), behind=(bx3, by3, bx1, mine, first[1]))
     mine, other, choice = picked(bx3, by3, bx1)
     fourth = (mine, crossed(other), choice)
     (third,) = worked(third)

time: 184 us -> 184 us (level)
  no operation moved by 1% of the time
where the time goes in v7:
time: 184 us; the launch traced here: 183 us
  waiting for transfers between devices  65.6 us (36%)
  starting transfers between devices  56.4 us (31%)
  Pallas kernels  39.1 us (21%)
  blocking collectives  9.35 us (5%)
  other arithmetic  8.33 us (5%)
  matrix products  2.75 us (1%)
    ppermute x52, waiting for transfers between devices, at_once(): lax.ppermute(value, way[0], way[1])  65.6 us
    ppermute x52, starting transfers between devices, at_once(): lax.ppermute(value, way[0], way[1])  56.4 us
    pallas_call x7, Pallas kernels, expert_rows(): pl.pallas_call(functools.partial(expert_kernel, expert_count, len(parts))...  24.8 us
    all_gather x1, blocking collectives, local(): shard_part = lax.all_gather(pooled, 'center', axis=0, tiled=True)  9.35 us
    pallas_call x5, Pallas kernels, pick(): pl.pallas_call(functools.partial(pick_kernel, capacity, expert_count), ou...  7.07 us
    reduce_sum x1, other arithmetic, local(): bank_norms = jnp.sum(bank_values * bank_values, axis=1)  5.08 us
  transfers between devices with their start and end apart: 52, of which 27 were waited for; matrix products, arithmetic and copies ran while one was open for 5% of the time, Pallas kernels for 19%

profile of v7, /device:TPU:0, one launch (start us, length us, event | category | flops | bytes accessed | tf_op | source)
XLA Modules:
  0.0 183.3 jit_solution(9099677904521025263)
XLA Ops:
  0.6 2.2 %enter.1.refs_0_ = bf16[128,2176]{1,0:T(8,128)(2,1)} custom-call(bf16[128,2048]{1,0:T(8,128)(2,1)} %refs_0_.1, s32[8,128]{1,0:T(8,128)} %bitcast.26, f32[8,128]{1,0:T(8,128)} %bitcast.27, s32[1,128]{1,0:T(1,128)} %refs_3_.1), custom_call_target="tpu_custom_call" | custom-call | flops 1000 | bytes 1000 | tf_op jit(solution)/shard_map/enter/pallas_call | solution.py:220
  3.7 5.9 %collective-permute-start.2 = (bf16[128,2176]{1,0:T(8,128)(2,1)}, bf16[128,2176]{1,0:T(8,128)(2,1)S(1)}, u32[]{:S(2)}, u32[]{:S(2)}) collective-permute-start(bf16[128,2176]{1,0:T(8,128)(2,1)} %enter.1.refs_0_), channel_id=1, source_target_pairs={{0,1},{1,0},{2,3},{3,2},{4,5},{5,4},{6,7},{7,6},{8,9},{9,8},{10,11... | collective-permute-start | bytes 1671176 | tf_op jit(solution)/shard_map/ppermute | solution.py:287
  9.5 1.5 collective-permute-start.1
  11.1 1.5 collective-permute-start
  12.6 9.5 %collective-permute-done.2.refs_3_ = bf16[128,2176]{1,0:T(8,128)(2,1)S(1)} collective-permute-done((bf16[128,2176]{1,0:T(8,128)(2,1)}, bf16[128,2176]{1,0:T(8,128)(2,1)S(1)}, u32[]{:S(2)}, u32[]{:S(2)}) %collective-permute-start.2) | collective-permute-done | bytes 557088 | tf_op jit(solution)/shard_map/ppermute | solution.py:287
  22.1 1.5 collective-permute-done.1.refs_2_
  25.5 2.1 %collective-permute-start.7 = (bf16[128,2176]{1,0:T(8,128)(2,1)S(1)}, bf16[128,2176]{1,0:T(8,128)(2,1)S(1)}, u32[]{:S(2)}, u32[]{:S(2)}) collective-permute-start(bf16[128,2176]{1,0:T(8,128)(2,1)S(1)} %collective-permute-done.5), channel_id=1, source_target_pairs={{0,1},{1,0},{2,3},{3,2},{4,5},{5,4},{6,7},{7,6},{8,9},{9,8},{10,11... | collective-permute-start | bytes 1671176 | tf_op jit(solution)/shard_map/ppermute | solution.py:287
  27.6 1.5 collective-permute-start.8
  29.6 5.1 %multiply_reduce_fusion = f32[2048]{0:T(1024)S(1)} fusion(bf16[2048,2048]{1,0:T(8,128)(2,1)} %param.13), kind=kLoop, calls=%fused_computation | loop fusion | flops 12580864 | bytes 8396800 | tf_op jit(solution)/shard_map/reduce_sum | solution.py:438
  34.7 1.5 pick.5
  36.2 2.2 %collective-permute-done.7 = bf16[128,2176]{1,0:T(8,128)(2,1)S(1)} collective-permute-done((bf16[128,2176]{1,0:T(8,128)(2,1)S(1)}, bf16[128,2176]{1,0:T(8,128)(2,1)S(1)}, u32[]{:S(2)}, u32[]{:S(2)}) %collective-permute-start.7) | collective-permute-done | bytes 557088 | tf_op jit(solution)/shard_map/ppermute | solution.py:287
  42.6 1.4 pick.6
  44.0 8.2 %collective-permute-done.10 = bf16[128,2176]{1,0:T(8,128)(2,1)S(1)} collective-permute-done((bf16[128,2176]{1,0:T(8,128)(2,1)S(1)}, bf16[128,2176]{1,0:T(8,128)(2,1)S(1)}, u32[]{:S(2)}, u32[]{:S(2)}) %collective-permute-start.10) | collective-permute-done | bytes 557088 | tf_op jit(solution)/shard_map/ppermute | solution.py:287
  52.4 1.5 collective-permute-done.11.refs_0_
  54.0 1.6 collective-permute-start.13
  56.2 2.0 %collective-permute-start.15 = (bf16[128,2176]{1,0:T(8,128)(2,1)S(1)}, bf16[128,2176]{1,0:T(8,128)(2,1)S(1)}, u32[]{:S(2)}, u32[]{:S(2)}) collective-permute-start(bf16[128,2176]{1,0:T(8,128)(2,1)S(1)} %collective-permute-done.refs_1_), channel_id=1, source_target_pairs={{0,1},{1,0},{2,3},{3,2},{4,5},{5,4},{6,7},{7,6},{8,9},{9,8},{10,11... | collective-permute-start | bytes 1671176 | tf_op jit(solution)/shard_map/ppermute | solution.py:287
  59.7 5.6 %expert_rows.7 = (bf16[256,2048]{1,0:T(8,128)(2,1)S(1)}, bf16[256,2048]{1,0:T(8,128)(2,1)S(1)}) custom-call(s32[2]{0:T(128)S(1)} %pad_add_fusion.who_ref, bf16[256,2176]{1,0:T(8,128)(2,1)S(1)} %get-tuple-element.93.refs_0_, bf16[256,2176]{1,0:T(8,128)(2,1)S(1)} %collective-permute-done.3.refs_1_, bf16[2048,1536]{1,0:T(8,128)(2,1)S(1)} %bitcast.10, ...), custom_call_target="tpu_custom_call" | custom-call | flops 1000 | bytes 1000 | tf_op jit(solution)/shard_map/expert_rows/pallas_call | solution.py:136
  65.8 2.0 %collective-permute-start.18 = (bf16[128,2176]{1,0:T(8,128)(2,1)S(1)}, bf16[128,2176]{1,0:T(8,128)(2,1)S(1)}, u32[]{:S(2)}, u32[]{:S(2)}) collective-permute-start(bf16[128,2176]{1,0:T(8,128)(2,1)S(1)} %collective-permute-done.8.refs_0_), channel_id=1, source_target_pairs={{0,1},{1,0},{2,3},{3,2},{4,5},{5,4},{6,7},{7,6},{8,9},{9,8},{10,11... | collective-permute-start | bytes 1671176 | tf_op jit(solution)/shard_map/ppermute | solution.py:287
  68.0 1.4 collective-permute-start.20
  69.5 1.4 pick.7
  70.9 4.4 %expert_rows.8 = (bf16[192,2048]{1,0:T(8,128)(2,1)S(1)}, bf16[192,2048]{1,0:T(8,128)(2,1)S(1)}) custom-call(s32[2]{0:T(128)S(1)} %pad_add_fusion.who_ref, bf16[192,2176]{1,0:T(8,128)(2,1)S(1)} %get-tuple-element.110.refs_0_, bf16[192,2176]{1,0:T(8,128)(2,1)S(1)} %collective-permute-done.16.refs_1_, bf16[2048,1536]{1,0:T(8,128)(2,1)S(1)} %bitcast.11, ...), custom_call_target="tpu_custom_call" | custom-call | flops 1000 | bytes 1000 | tf_op jit(solution)/shard_map/expert_rows/pallas_call | solution.py:136
  75.3 2.8 %expert_rows.9.mine = bf16[192,2048]{1,0:T(8,128)(2,1)S(1)} custom-call(s32[2]{0:T(128)S(1)} %pad_add_fusion.who_ref, bf16[192,2176]{1,0:T(8,128)(2,1)S(1)} %get-tuple-element.113.refs_0_, bf16[2048,1536]{1,0:T(8,128)(2,1)S(1)} %bitcast.12, bf16[768,2048]{1,0:T(8,128)(2,1)S(1)} %bitcast.19), custom_call_target="tpu_custom_call" | custom-call | flops 1000 | bytes 1000 | tf_op jit(solution)/shard_map/expert_rows/pallas_call | solution.py:136
  78.0 2.4 %collective-permute-done.18.refs_0_ = bf16[128,2176]{1,0:T(8,128)(2,1)S(1)} collective-permute-done((bf16[128,2176]{1,0:T(8,128)(2,1)S(1)}, bf16[128,2176]{1,0:T(8,128)(2,1)S(1)}, u32[]{:S(2)}, u32[]{:S(2)}) %collective-permute-start.18) | collective-permute-done | bytes 557088 | tf_op jit(solution)/shard_map/ppermute | solution.py:287
  82.6 2.6 %expert_rows.10.mine = bf16[192,2048]{1,0:T(8,128)(2,1)S(1)} custom-call(s32[2]{0:T(128)S(1)} %pad_add_fusion.who_ref, bf16[192,2176]{1,0:T(8,128)(2,1)S(1)} %get-tuple-element.122.refs_0_, bf16[2048,1536]{1,0:T(8,128)(2,1)S(1)} %bitcast.13, bf16[768,2048]{1,0:T(8,128)(2,1)S(1)} %bitcast.20), custom_call_target="tpu_custom_call" | custom-call | flops 1000 | bytes 1000 | tf_op jit(solution)/shard_map/expert_rows/pallas_call | solution.py:136
  85.2 2.6 %expert_rows.11 = bf16[192,2048]{1,0:T(8,128)(2,1)S(1)} custom-call(s32[2]{0:T(128)S(1)} %pad_add_fusion.who_ref, bf16[192,2176]{1,0:T(8,128)(2,1)S(1)} %collective-permute-done.21.refs_0_, bf16[2048,1536]{1,0:T(8,128)(2,1)S(1)} %bitcast.14, bf16[768,2048]{1,0:T(8,128)(2,1)S(1)} %bitcast.21), custom_call_target="tpu_custom_call" | custom-call | flops 1000 | bytes 1000 | tf_op jit(solution)/shard_map/expert_rows/pallas_call | solution.py:136
  88.8 2.6 %expert_rows.12 = bf16[192,2048]{1,0:T(8,128)(2,1)S(1)} custom-call(s32[2]{0:T(128)S(1)} %pad_add_fusion.who_ref, bf16[192,2176]{1,0:T(8,128)(2,1)S(1)} %collective-permute-done.17.refs_0_, bf16[2048,1536]{1,0:T(8,128)(2,1)S(1)} %bitcast.15, bf16[768,2048]{1,0:T(8,128)(2,1)S(1)} %bitcast.22), custom_call_target="tpu_custom_call" | custom-call | flops 1000 | bytes 1000 | tf_op jit(solution)/shard_map/expert_rows/pallas_call | solution.py:136
  92.1 1.5 collective-permute-start.24
  93.6 1.7 collective-permute-start.25
  95.3 1.7 collective-permute-start.26
  97.6 4.4 %expert_rows.13 = (bf16[192,2048]{1,0:T(8,128)(2,1)S(1)}, bf16[192,2048]{1,0:T(8,128)(2,1)S(1)}) custom-call(s32[2]{0:T(128)S(1)} %pad_add_fusion.who_ref, bf16[192,2176]{1,0:T(8,128)(2,1)S(1)} %get-tuple-element.140.refs_0_, bf16[192,2176]{1,0:T(8,128)(2,1)S(1)} %collective-permute-done.27.refs_1_, bf16[2048,1536]{1,0:T(8,128)(2,1)S(1)} %bitcast.16, ...), custom_call_target="tpu_custom_call" | custom-call | flops 1000 | bytes 1000 | tf_op jit(solution)/shard_map/expert_rows/pallas_call | solution.py:136
  103.4 3.0 %collective-permute-done.24 = bf16[128,2048]{1,0:T(8,128)(2,1)S(1)} collective-permute-done((bf16[128,2048]{1,0:T(8,128)(2,1)S(1)}, bf16[128,2048]{1,0:T(8,128)(2,1)S(1)}, u32[]{:S(2)}, u32[]{:S(2)}) %collective-permute-start.24) | collective-permute-done | bytes 524320 | tf_op jit(solution)/shard_map/ppermute | solution.py:287
  109.5 1.4 collective-permute-start.32
  111.0 1.7 collective-permute-start.29
  113.4 8.4 %collective-permute-done.31 = bf16[128,2048]{1,0:T(8,128)(2,1)S(1)} collective-permute-done((bf16[128,2048]{1,0:T(8,128)(2,1)S(1)}, bf16[128,2048]{1,0:T(8,128)(2,1)S(1)}, u32[]{:S(2)}, u32[]{:S(2)}) %collective-permute-start.31) | collective-permute-done | bytes 524320 | tf_op jit(solution)/shard_map/ppermute | solution.py:287
  123.5 1.7 collective-permute-start.35
  127.2 8.0 %collective-permute-done.35 = bf16[128,2048]{1,0:T(8,128)(2,1)S(1)} collective-permute-done((bf16[128,2048]{1,0:T(8,128)(2,1)S(1)}, bf16[128,2048]{1,0:T(8,128)(2,1)S(1)}, u32[]{:S(2)}, u32[]{:S(2)}) %collective-permute-start.35) | collective-permute-done | bytes 524320 | tf_op jit(solution)/shard_map/ppermute | solution.py:287
  135.4 1.6 collective-permute-done.33
  137.2 1.8 collective-permute-start.36
  140.6 3.1 %collective-permute-start.40 = (bf16[128,2048]{1,0:T(8,128)(2,1)S(1)}, bf16[128,2048]{1,0:T(8,128)(2,1)S(1)}, u32[]{:S(2)}, u32[]{:S(2)}) collective-permute-start(bf16[128,2048]{1,0:T(8,128)(2,1)S(1)} %add_convert_fusion.2.refs_9_), channel_id=1, source_target_pairs={{0,1},{1,0},{2,3},{3,2},{4,5},{5,4},{6,7},{7,6},{8,9},{9,8},{10,11... | collective-permute-start | bytes 1572872 | tf_op jit(solution)/shard_map/ppermute | solution.py:287
  145.3 3.3 %collective-permute-done.36.refs_3_ = bf16[128,2048]{1,0:T(8,128)(2,1)S(1)} collective-permute-done((bf16[128,2048]{1,0:T(8,128)(2,1)S(1)}, bf16[128,2048]{1,0:T(8,128)(2,1)S(1)}, u32[]{:S(2)}, u32[]{:S(2)}) %collective-permute-start.36) | collective-permute-done | bytes 524320 | tf_op jit(solution)/shard_map/ppermute | solution.py:287
  148.6 3.7 %collective-permute-done.40.refs_10_ = bf16[128,2048]{1,0:T(8,128)(2,1)S(1)} collective-permute-done((bf16[128,2048]{1,0:T(8,128)(2,1)S(1)}, bf16[128,2048]{1,0:T(8,128)(2,1)S(1)}, u32[]{:S(2)}, u32[]{:S(2)}) %collective-permute-start.40) | collective-permute-done | bytes 524320 | tf_op jit(solution)/shard_map/ppermute | solution.py:287
  153.3 2.0 %collective-permute-start.46 = (f32[8,2048]{1,0:T(8,128)S(1)}, f32[8,2048]{1,0:T(8,128)S(1)}, u32[]{:S(2)}, u32[]{:S(2)}) collective-permute-start(f32[8,2048]{1,0:T(8,128)S(1)} %get-tuple-element.177), channel_id=1, source_target_pairs={{0,1},{1,0},{2,3},{3,2},{4,5},{5,4},{6,7},{7,6},{8,9},{9,8},{10,11... | collective-permute-start | bytes 196616 | tf_op jit(solution)/shard_map/ppermute | solution.py:287
  156.7 1.9 %collective-permute-start.41 = (bf16[128,2048]{1,0:T(8,128)(2,1)S(1)}, bf16[128,2048]{1,0:T(8,128)(2,1)S(1)}, u32[]{:S(2)}, u32[]{:S(2)}) collective-permute-start(bf16[128,2048]{1,0:T(8,128)(2,1)S(1)} %get-tuple-element.170), channel_id=1, source_target_pairs={{0,16},{4,20},{8,24},{12,28},{16,0},{20,4},{24,8},{28,12},{1,17},{... | collective-permute-start | bytes 1572872 | tf_op jit(solution)/shard_map/ppermute | solution.py:287
  158.6 2.0 %collective-permute-start.42 = (bf16[128,2048]{1,0:T(8,128)(2,1)S(1)}, bf16[128,2048]{1,0:T(8,128)(2,1)S(1)}, u32[]{:S(2)}, u32[]{:S(2)}) collective-permute-start(bf16[128,2048]{1,0:T(8,128)(2,1)S(1)} %get-tuple-element.171), channel_id=1, source_target_pairs={{0,1},{1,0},{2,3},{3,2},{4,5},{5,4},{6,7},{7,6},{8,9},{9,8},{10,11... | collective-permute-start | bytes 1572872 | tf_op jit(solution)/shard_map/ppermute | solution.py:287
  161.6 9.4 %all_gather.3 = bf16[64,2048]{1,0:T(8,128)(2,1)S(1)} all-gather(bf16[8,2048]{1,0:T(8,128)(2,1)S(1)} %multiply_convert_fusion), channel_id=1, replica_groups=mesh['center'=8,'expert'=4] {'center'}, dimensions={0}, use_global_device_ids=true | all-gather | bytes 294912 | tf_op jit(solution)/shard_map/all_gather | solution.py:461
  171.1 2.8 %fusion.1 = f32[64]{0:T(128)S(1)} fusion(bf16[64,2048]{1,0:T(8,128)(2,1)S(1)} %all_gather.3, bf16[2048,2048]{1,0:T(8,128)(2,1)S(1)} %bitcast.25, f32[2048]{0:T(1024)S(1)} %multiply_reduce_fusion, f32[64]{0:T(128)S(1)} %multiply_reduce_fusion.1), kind=kOutput, calls=%fused_computation.3 | convolution fusion | flops 537395136 | bytes 8659456 | tf_op jit(solution)/shard_map/dot_general | solution.py:464
  177.1 1.5 collective-permute-start.50
  179.7 1.9 %collective-permute-done.50 = f32[64]{0:T(128)S(1)} collective-permute-done((f32[64]{0:T(128)S(1)}, f32[64]{0:T(128)S(1)}, u32[]{:S(2)}, u32[]{:S(2)}) %collective-permute-start.50) | collective-permute-done | bytes 288 | tf_op jit(solution)/shard_map/ppermute | solution.py:287
  (115 shorter events, 37.1 us)
Async XLA Ops:
  2.8 9.8 %collective-permute-start.5 = (bf16[128,2176]{1,0:T(8,128)(2,1)}, bf16[128,2176]{1,0:T(8,128)(2,1)S(1)}, u32[]{:S(2)}, u32[]{:S(2)}) collective-permute-start(bf16[128,2176]{1,0:T(8,128)(2,1)} %enter.1.refs_0_), channel_id=1, source_target_pairs={{1,2},{2,1},{5,6},{6,5},{9,10},{10,9},{13,14},{14,13},{17,18},{18,... | collective-permute-start | bytes 1671176 | tf_op jit(solution)/shard_map/ppermute | solution.py:287
  3.7 18.4 %collective-permute-start.2 = (bf16[128,2176]{1,0:T(8,128)(2,1)}, bf16[128,2176]{1,0:T(8,128)(2,1)S(1)}, u32[]{:S(2)}, u32[]{:S(2)}) collective-permute-start(bf16[128,2176]{1,0:T(8,128)(2,1)} %enter.1.refs_0_), channel_id=1, source_target_pairs={{0,1},{1,0},{2,3},{3,2},{4,5},{5,4},{6,7},{7,6},{8,9},{9,8},{10,11... | collective-permute-start | bytes 1671176 | tf_op jit(solution)/shard_map/ppermute | solution.py:287
  9.5 14.0 %collective-permute-start.1 = (bf16[128,2176]{1,0:T(8,128)(2,1)}, bf16[128,2176]{1,0:T(8,128)(2,1)S(1)}, u32[]{:S(2)}, u32[]{:S(2)}) collective-permute-start(bf16[128,2176]{1,0:T(8,128)(2,1)} %enter.1.refs_0_), channel_id=1, source_target_pairs={{0,16},{4,20},{8,24},{12,28},{16,0},{20,4},{24,8},{28,12},{1,17},{... | collective-permute-start | bytes 1671176 | tf_op jit(solution)/shard_map/ppermute | solution.py:287
  11.1 13.7 %collective-permute-start = (bf16[128,2176]{1,0:T(8,128)(2,1)}, bf16[128,2176]{1,0:T(8,128)(2,1)S(1)}, u32[]{:S(2)}, u32[]{:S(2)}) collective-permute-start(bf16[128,2176]{1,0:T(8,128)(2,1)} %enter.1.refs_0_), channel_id=1, source_target_pairs={{0,8},{4,12},{8,0},{12,4},{16,24},{20,28},{24,16},{28,20},{1,9},{5... | collective-permute-start | bytes 1671176 | tf_op jit(solution)/shard_map/ppermute | solution.py:287
  24.8 13.8 %collective-permute-start.6 = (bf16[128,2176]{1,0:T(8,128)(2,1)S(1)}, bf16[128,2176]{1,0:T(8,128)(2,1)S(1)}, u32[]{:S(2)}, u32[]{:S(2)}) collective-permute-start(bf16[128,2176]{1,0:T(8,128)(2,1)S(1)} %collective-permute-done.2.refs_3_), channel_id=1, source_target_pairs={{1,2},{2,1},{5,6},{6,5},{9,10},{10,9},{13,14},{14,13},{17,18},{18,... | collective-permute-start | bytes 1671176 | tf_op jit(solution)/shard_map/ppermute | solution.py:287
  25.5 12.9 %collective-permute-start.7 = (bf16[128,2176]{1,0:T(8,128)(2,1)S(1)}, bf16[128,2176]{1,0:T(8,128)(2,1)S(1)}, u32[]{:S(2)}, u32[]{:S(2)}) collective-permute-start(bf16[128,2176]{1,0:T(8,128)(2,1)S(1)} %collective-permute-done.5), channel_id=1, source_target_pairs={{0,1},{1,0},{2,3},{3,2},{4,5},{5,4},{6,7},{7,6},{8,9},{9,8},{10,11... | collective-permute-start | bytes 1671176 | tf_op jit(solution)/shard_map/ppermute | solution.py:287
  27.6 12.3 %collective-permute-start.8 = (bf16[128,2176]{1,0:T(8,128)(2,1)S(1)}, bf16[128,2176]{1,0:T(8,128)(2,1)S(1)}, u32[]{:S(2)}, u32[]{:S(2)}) collective-permute-start(bf16[128,2176]{1,0:T(8,128)(2,1)S(1)} %collective-permute-done.1.refs_2_), channel_id=1, source_target_pairs={{0,8},{4,12},{8,0},{12,4},{16,24},{20,28},{24,16},{28,20},{1,9},{5... | collective-permute-start | bytes 1671176 | tf_op jit(solution)/shard_map/ppermute | solution.py:287
  29.1 12.0 %collective-permute-start.9 = (bf16[128,2176]{1,0:T(8,128)(2,1)S(1)}, bf16[128,2176]{1,0:T(8,128)(2,1)S(1)}, u32[]{:S(2)}, u32[]{:S(2)}) collective-permute-start(bf16[128,2176]{1,0:T(8,128)(2,1)S(1)} %collective-permute-done.2.refs_3_), channel_id=1, source_target_pairs={{0,16},{4,20},{8,24},{12,28},{16,0},{20,4},{24,8},{28,12},{1,17},{... | collective-permute-start | bytes 1671176 | tf_op jit(solution)/shard_map/ppermute | solution.py:287
  41.1 11.1 %collective-permute-start.10 = (bf16[128,2176]{1,0:T(8,128)(2,1)S(1)}, bf16[128,2176]{1,0:T(8,128)(2,1)S(1)}, u32[]{:S(2)}, u32[]{:S(2)}) collective-permute-start(bf16[128,2176]{1,0:T(8,128)(2,1)S(1)} %collective-permute-done.6), channel_id=1, source_target_pairs={{0,1},{1,0},{2,3},{3,2},{4,5},{5,4},{6,7},{7,6},{8,9},{9,8},{10,11... | collective-permute-start | bytes 1671176 | tf_op jit(solution)/shard_map/ppermute | solution.py:287
  41.5 12.4 %collective-permute-start.11 = (bf16[128,2176]{1,0:T(8,128)(2,1)S(1)}, bf16[128,2176]{1,0:T(8,128)(2,1)S(1)}, u32[]{:S(2)}, u32[]{:S(2)}) collective-permute-start(bf16[128,2176]{1,0:T(8,128)(2,1)S(1)} %add.86.refs_2_), channel_id=1, source_target_pairs={{0,8},{4,12},{8,0},{12,4},{16,24},{20,28},{24,16},{28,20},{1,9},{5... | collective-permute-start | bytes 1671176 | tf_op jit(solution)/shard_map/ppermute | solution.py:287
  42.0 12.0 %collective-permute-start.12 = (bf16[128,2176]{1,0:T(8,128)(2,1)S(1)}, bf16[128,2176]{1,0:T(8,128)(2,1)S(1)}, u32[]{:S(2)}, u32[]{:S(2)}) collective-permute-start(bf16[128,2176]{1,0:T(8,128)(2,1)S(1)} %add.86.refs_2_), channel_id=1, source_target_pairs={{0,16},{4,20},{8,24},{12,28},{16,0},{20,4},{24,8},{28,12},{1,17},{... | collective-permute-start | bytes 1671176 | tf_op jit(solution)/shard_map/ppermute | solution.py:287
  42.6 17.1 %collective-permute-start.3 = (bf16[256,2176]{1,0:T(8,128)(2,1)S(1)}, bf16[256,2176]{1,0:T(8,128)(2,1)S(1)}, u32[]{:S(2)}, u32[]{:S(2)}) collective-permute-start(bf16[256,2176]{1,0:T(8,128)(2,1)S(1)} %get-tuple-element.94), channel_id=1, source_target_pairs={{0,4},{4,0},{8,12},{12,8},{16,20},{20,16},{24,28},{28,24},{1,5},{5... | collective-permute-start | bytes 3342344 | tf_op jit(solution)/shard_map/ppermute | solution.py:287
  54.0 11.4 %collective-permute-start.13 = (bf16[128,2176]{1,0:T(8,128)(2,1)S(1)}, bf16[128,2176]{1,0:T(8,128)(2,1)S(1)}, u32[]{:S(2)}, u32[]{:S(2)}) collective-permute-start(bf16[128,2176]{1,0:T(8,128)(2,1)S(1)} %add.87.refs_2_), channel_id=1, source_target_pairs={{0,8},{4,12},{8,0},{12,4},{16,24},{20,28},{24,16},{28,20},{1,9},{5... | collective-permute-start | bytes 1671176 | tf_op jit(solution)/shard_map/ppermute | solution.py:287
  55.6 9.8 %collective-permute-start.14 = (bf16[128,2176]{1,0:T(8,128)(2,1)S(1)}, bf16[128,2176]{1,0:T(8,128)(2,1)S(1)}, u32[]{:S(2)}, u32[]{:S(2)}) collective-permute-start(bf16[128,2176]{1,0:T(8,128)(2,1)S(1)} %add.87.refs_2_), channel_id=1, source_target_pairs={{0,16},{4,20},{8,24},{12,28},{16,0},{20,4},{24,8},{28,12},{1,17},{... | collective-permute-start | bytes 1671176 | tf_op jit(solution)/shard_map/ppermute | solution.py:287
  56.2 9.5 %collective-permute-start.15 = (bf16[128,2176]{1,0:T(8,128)(2,1)S(1)}, bf16[128,2176]{1,0:T(8,128)(2,1)S(1)}, u32[]{:S(2)}, u32[]{:S(2)}) collective-permute-start(bf16[128,2176]{1,0:T(8,128)(2,1)S(1)} %collective-permute-done.refs_1_), channel_id=1, source_target_pairs={{0,1},{1,0},{2,3},{3,2},{4,5},{5,4},{6,7},{7,6},{8,9},{9,8},{10,11... | collective-permute-start | bytes 1671176 | tf_op jit(solution)/shard_map/ppermute | solution.py:287
  59.6 11.3 %collective-permute-start.16 = (bf16[192,2176]{1,0:T(8,128)(2,1)S(1)}, bf16[192,2176]{1,0:T(8,128)(2,1)S(1)}, u32[]{:S(2)}, u32[]{:S(2)}) collective-permute-start(bf16[192,2176]{1,0:T(8,128)(2,1)S(1)} %get-tuple-element.111), channel_id=1, source_target_pairs={{0,4},{4,0},{8,12},{12,8},{16,20},{20,16},{24,28},{28,24},{1,5},{5... | collective-permute-start | bytes 2506760 | tf_op jit(solution)/shard_map/ppermute | solution.py:287
  65.8 14.7 %collective-permute-start.18 = (bf16[128,2176]{1,0:T(8,128)(2,1)S(1)}, bf16[128,2176]{1,0:T(8,128)(2,1)S(1)}, u32[]{:S(2)}, u32[]{:S(2)}) collective-permute-start(bf16[128,2176]{1,0:T(8,128)(2,1)S(1)} %collective-permute-done.8.refs_0_), channel_id=1, source_target_pairs={{0,1},{1,0},{2,3},{3,2},{4,5},{5,4},{6,7},{7,6},{8,9},{9,8},{10,11... | collective-permute-start | bytes 1671176 | tf_op jit(solution)/shard_map/ppermute | solution.py:287
  67.8 12.8 %collective-permute-start.19 = (bf16[128,2176]{1,0:T(8,128)(2,1)S(1)}, bf16[128,2176]{1,0:T(8,128)(2,1)S(1)}, u32[]{:S(2)}, u32[]{:S(2)}) collective-permute-start(bf16[128,2176]{1,0:T(8,128)(2,1)S(1)} %collective-permute-done.12.refs_1_), channel_id=1, source_target_pairs={{0,8},{4,12},{8,0},{12,4},{16,24},{20,28},{24,16},{28,20},{1,9},{5... | collective-permute-start | bytes 1671176 | tf_op jit(solution)/shard_map/ppermute | solution.py:287
  68.0 12.6 %collective-permute-start.20 = (bf16[128,2176]{1,0:T(8,128)(2,1)S(1)}, bf16[128,2176]{1,0:T(8,128)(2,1)S(1)}, u32[]{:S(2)}, u32[]{:S(2)}) collective-permute-start(bf16[128,2176]{1,0:T(8,128)(2,1)S(1)} %collective-permute-done.13.refs_0_), channel_id=1, source_target_pairs={{0,16},{4,20},{8,24},{12,28},{16,0},{20,4},{24,8},{28,12},{1,17},{... | collective-permute-start | bytes 1671176 | tf_op jit(solution)/shard_map/ppermute | solution.py:287
  82.1 6.7 %collective-permute-start.17 = (bf16[192,2176]{1,0:T(8,128)(2,1)S(1)}, bf16[192,2176]{1,0:T(8,128)(2,1)S(1)}, u32[]{:S(2)}, u32[]{:S(2)}) collective-permute-start(bf16[192,2176]{1,0:T(8,128)(2,1)S(1)} %get-tuple-element.114), channel_id=1, source_target_pairs={{0,4},{4,0},{8,12},{12,8},{16,20},{20,16},{24,28},{28,24},{1,5},{5... | collective-permute-start | bytes 2506760 | tf_op jit(solution)/shard_map/ppermute | solution.py:287
  87.7 3.8 %collective-permute-start.23 = (bf16[192,2048]{1,0:T(8,128)(2,1)S(1)}, bf16[192,2048]{1,0:T(8,128)(2,1)S(1)}, u32[]{:S(2)}, u32[]{:S(2)}) collective-permute-start(bf16[192,2048]{1,0:T(8,128)(2,1)S(1)} %expert_rows.11), channel_id=1, source_target_pairs={{0,4},{4,0},{8,12},{12,8},{16,20},{20,16},{24,28},{28,24},{1,5},{5... | collective-permute-start | bytes 2359304 | tf_op jit(solution)/shard_map/ppermute | solution.py:287
  87.9 14.8 %collective-permute-start.4 = (bf16[256,2048]{1,0:T(8,128)(2,1)S(1)}, bf16[256,2048]{1,0:T(8,128)(2,1)S(1)}, u32[]{:S(2)}, u32[]{:S(2)}) collective-permute-start(bf16[256,2048]{1,0:T(8,128)(2,1)S(1)} %get-tuple-element.96), channel_id=1, source_target_pairs={{0,4},{4,0},{8,12},{12,8},{16,20},{20,16},{24,28},{28,24},{1,5},{5... | collective-permute-start | bytes 3145736 | tf_op jit(solution)/shard_map/ppermute | solution.py:287
  88.3 5.3 %collective-permute-start.27 = (bf16[192,2176]{1,0:T(8,128)(2,1)S(1)}, bf16[192,2176]{1,0:T(8,128)(2,1)S(1)}, u32[]{:S(2)}, u32[]{:S(2)}) collective-permute-start(bf16[192,2176]{1,0:T(8,128)(2,1)S(1)} %get-tuple-element.141), channel_id=1, source_target_pairs={{0,4},{4,0},{8,12},{12,8},{16,20},{20,16},{24,28},{28,24},{1,5},{5... | collective-permute-start | bytes 2506760 | tf_op jit(solution)/shard_map/ppermute | solution.py:287
  88.4 6.9 %collective-permute-start.28 = (bf16[192,2048]{1,0:T(8,128)(2,1)S(1)}, bf16[192,2048]{1,0:T(8,128)(2,1)S(1)}, u32[]{:S(2)}, u32[]{:S(2)}) collective-permute-start(bf16[192,2048]{1,0:T(8,128)(2,1)S(1)} %get-tuple-element.144), channel_id=1, source_target_pairs={{0,4},{4,0},{8,12},{12,8},{16,20},{20,16},{24,28},{28,24},{1,5},{5... | collective-permute-start | bytes 2359304 | tf_op jit(solution)/shard_map/ppermute | solution.py:287
  91.4 10.6 %collective-permute-start.22 = (bf16[192,2048]{1,0:T(8,128)(2,1)S(1)}, bf16[192,2048]{1,0:T(8,128)(2,1)S(1)}, u32[]{:S(2)}, u32[]{:S(2)}) collective-permute-start(bf16[192,2048]{1,0:T(8,128)(2,1)S(1)} %expert_rows.12), channel_id=1, source_target_pairs={{0,4},{4,0},{8,12},{12,8},{16,20},{20,16},{24,28},{28,24},{1,5},{5... | collective-permute-start | bytes 2359304 | tf_op jit(solution)/shard_map/ppermute | solution.py:287
  92.1 14.3 %collective-permute-start.24 = (bf16[128,2048]{1,0:T(8,128)(2,1)S(1)}, bf16[128,2048]{1,0:T(8,128)(2,1)S(1)}, u32[]{:S(2)}, u32[]{:S(2)}) collective-permute-start(bf16[128,2048]{1,0:T(8,128)(2,1)S(1)} %get-tuple-element.136), channel_id=1, source_target_pairs={{0,16},{4,20},{8,24},{12,28},{16,0},{20,4},{24,8},{28,12},{1,17},{... | collective-permute-start | bytes 1572872 | tf_op jit(solution)/shard_map/ppermute | solution.py:287
  93.6 14.0 %collective-permute-start.25 = (bf16[128,2048]{1,0:T(8,128)(2,1)S(1)}, bf16[128,2048]{1,0:T(8,128)(2,1)S(1)}, u32[]{:S(2)}, u32[]{:S(2)}) collective-permute-start(bf16[128,2048]{1,0:T(8,128)(2,1)S(1)} %get-tuple-element.139), channel_id=1, source_target_pairs={{0,8},{4,12},{8,0},{12,4},{16,24},{20,28},{24,16},{28,20},{1,9},{5... | collective-permute-start | bytes 1572872 | tf_op jit(solution)/shard_map/ppermute | solution.py:287
  95.3 13.7 %collective-permute-start.26 = (bf16[128,2048]{1,0:T(8,128)(2,1)S(1)}, bf16[128,2048]{1,0:T(8,128)(2,1)S(1)}, u32[]{:S(2)}, u32[]{:S(2)}) collective-permute-start(bf16[128,2048]{1,0:T(8,128)(2,1)S(1)} %get-tuple-element.126), channel_id=1, source_target_pairs={{0,1},{1,0},{2,3},{3,2},{4,5},{5,4},{6,7},{7,6},{8,9},{9,8},{10,11... | collective-permute-start | bytes 1572872 | tf_op jit(solution)/shard_map/ppermute | solution.py:287
  102.0 10.8 %collective-permute-start.30 = (bf16[192,2048]{1,0:T(8,128)(2,1)S(1)}, bf16[192,2048]{1,0:T(8,128)(2,1)S(1)}, u32[]{:S(2)}, u32[]{:S(2)}) collective-permute-start(bf16[192,2048]{1,0:T(8,128)(2,1)S(1)} %get-tuple-element.152), channel_id=1, source_target_pairs={{0,4},{4,0},{8,12},{12,8},{16,20},{20,16},{24,28},{28,24},{1,5},{5... | collective-permute-start | bytes 2359304 | tf_op jit(solution)/shard_map/ppermute | solution.py:287
  109.0 12.8 %collective-permute-start.31 = (bf16[128,2048]{1,0:T(8,128)(2,1)S(1)}, bf16[128,2048]{1,0:T(8,128)(2,1)S(1)}, u32[]{:S(2)}, u32[]{:S(2)}) collective-permute-start(bf16[128,2048]{1,0:T(8,128)(2,1)S(1)} %add_convert_fusion.6), channel_id=1, source_target_pairs={{0,8},{4,12},{8,0},{12,4},{16,24},{20,28},{24,16},{28,20},{1,9},{5... | collective-permute-start | bytes 1572872 | tf_op jit(solution)/shard_map/ppermute | solution.py:287
  109.5 12.7 %collective-permute-start.32 = (bf16[128,2048]{1,0:T(8,128)(2,1)S(1)}, bf16[128,2048]{1,0:T(8,128)(2,1)S(1)}, u32[]{:S(2)}, u32[]{:S(2)}) collective-permute-start(bf16[128,2048]{1,0:T(8,128)(2,1)S(1)} %get-tuple-element.159), channel_id=1, source_target_pairs={{0,16},{4,20},{8,24},{12,28},{16,0},{20,4},{24,8},{28,12},{1,17},{... | collective-permute-start | bytes 1572872 | tf_op jit(solution)/shard_map/ppermute | solution.py:287
  111.0 12.6 %collective-permute-start.29 = (bf16[128,2048]{1,0:T(8,128)(2,1)S(1)}, bf16[128,2048]{1,0:T(8,128)(2,1)S(1)}, u32[]{:S(2)}, u32[]{:S(2)}) collective-permute-start(bf16[128,2048]{1,0:T(8,128)(2,1)S(1)} %get-tuple-element.149), channel_id=1, source_target_pairs={{0,1},{1,0},{2,3},{3,2},{4,5},{5,4},{6,7},{7,6},{8,9},{9,8},{10,11... | collective-permute-start | bytes 1572872 | tf_op jit(solution)/shard_map/ppermute | solution.py:287
  123.5 11.7 %collective-permute-start.35 = (bf16[128,2048]{1,0:T(8,128)(2,1)S(1)}, bf16[128,2048]{1,0:T(8,128)(2,1)S(1)}, u32[]{:S(2)}, u32[]{:S(2)}) collective-permute-start(bf16[128,2048]{1,0:T(8,128)(2,1)S(1)} %add_convert_fusion.3), channel_id=1, source_target_pairs={{0,1},{1,0},{2,3},{3,2},{4,5},{5,4},{6,7},{7,6},{8,9},{9,8},{10,11... | collective-permute-start | bytes 1572872 | tf_op jit(solution)/shard_map/ppermute | solution.py:287
  125.2 11.8 %collective-permute-start.33 = (bf16[128,2048]{1,0:T(8,128)(2,1)S(1)}, bf16[128,2048]{1,0:T(8,128)(2,1)S(1)}, u32[]{:S(2)}, u32[]{:S(2)}) collective-permute-start(bf16[128,2048]{1,0:T(8,128)(2,1)S(1)} %get-tuple-element.160), channel_id=1, source_target_pairs={{0,8},{4,12},{8,0},{12,4},{16,24},{20,28},{24,16},{28,20},{1,9},{5... | collective-permute-start | bytes 1572872 | tf_op jit(solution)/shard_map/ppermute | solution.py:287
  125.8 11.2 %collective-permute-start.34 = (bf16[128,2048]{1,0:T(8,128)(2,1)S(1)}, bf16[128,2048]{1,0:T(8,128)(2,1)S(1)}, u32[]{:S(2)}, u32[]{:S(2)}) collective-permute-start(bf16[128,2048]{1,0:T(8,128)(2,1)S(1)} %add_convert_fusion.4), channel_id=1, source_target_pairs={{0,16},{4,20},{8,24},{12,28},{16,0},{20,4},{24,8},{28,12},{1,17},{... | collective-permute-start | bytes 1572872 | tf_op jit(solution)/shard_map/ppermute | solution.py:287
  137.2 11.3 %collective-permute-start.36 = (bf16[128,2048]{1,0:T(8,128)(2,1)S(1)}, bf16[128,2048]{1,0:T(8,128)(2,1)S(1)}, u32[]{:S(2)}, u32[]{:S(2)}) collective-permute-start(bf16[128,2048]{1,0:T(8,128)(2,1)S(1)} %add_convert_fusion.5), channel_id=1, source_target_pairs={{0,8},{4,12},{8,0},{12,4},{16,24},{20,28},{24,16},{28,20},{1,9},{5... | collective-permute-start | bytes 1572872 | tf_op jit(solution)/shard_map/ppermute | solution.py:287
  139.1 9.5 %collective-permute-start.38 = (bf16[128,2048]{1,0:T(8,128)(2,1)S(1)}, bf16[128,2048]{1,0:T(8,128)(2,1)S(1)}, u32[]{:S(2)}, u32[]{:S(2)}) collective-permute-start(bf16[128,2048]{1,0:T(8,128)(2,1)S(1)} %get-tuple-element.167), channel_id=1, source_target_pairs={{0,16},{4,20},{8,24},{12,28},{16,0},{20,4},{24,8},{28,12},{1,17},{... | collective-permute-start | bytes 1572872 | tf_op jit(solution)/shard_map/ppermute | solution.py:287
  139.9 8.7 %collective-permute-start.39 = (bf16[128,2048]{1,0:T(8,128)(2,1)S(1)}, bf16[128,2048]{1,0:T(8,128)(2,1)S(1)}, u32[]{:S(2)}, u32[]{:S(2)}) collective-permute-start(bf16[128,2048]{1,0:T(8,128)(2,1)S(1)} %add_convert_fusion.1), channel_id=1, source_target_pairs={{1,2},{2,1},{5,6},{6,5},{9,10},{10,9},{13,14},{14,13},{17,18},{18,... | collective-permute-start | bytes 1572872 | tf_op jit(solution)/shard_map/ppermute | solution.py:287
  140.6 11.7 %collective-permute-start.40 = (bf16[128,2048]{1,0:T(8,128)(2,1)S(1)}, bf16[128,2048]{1,0:T(8,128)(2,1)S(1)}, u32[]{:S(2)}, u32[]{:S(2)}) collective-permute-start(bf16[128,2048]{1,0:T(8,128)(2,1)S(1)} %add_convert_fusion.2.refs_9_), channel_id=1, source_target_pairs={{0,1},{1,0},{2,3},{3,2},{4,5},{5,4},{6,7},{7,6},{8,9},{9,8},{10,11... | collective-permute-start | bytes 1572872 | tf_op jit(solution)/shard_map/ppermute | solution.py:287
  144.7 12.0 %collective-permute-start.44 = (f32[8,2048]{1,0:T(8,128)S(1)}, f32[8,2048]{1,0:T(8,128)S(1)}, u32[]{:S(2)}, u32[]{:S(2)}) collective-permute-start(f32[8,2048]{1,0:T(8,128)S(1)} %get-tuple-element.175), channel_id=1, source_target_pairs={{0,8},{4,12},{8,0},{12,4},{16,24},{20,28},{24,16},{28,20},{1,9},{5... | collective-permute-start | bytes 196616 | tf_op jit(solution)/shard_map/ppermute | solution.py:287
  153.1 5.5 %collective-permute-start.45 = (f32[8,2048]{1,0:T(8,128)S(1)}, f32[8,2048]{1,0:T(8,128)S(1)}, u32[]{:S(2)}, u32[]{:S(2)}) collective-permute-start(f32[8,2048]{1,0:T(8,128)S(1)} %get-tuple-element.176), channel_id=1, source_target_pairs={{0,16},{4,20},{8,24},{12,28},{16,0},{20,4},{24,8},{28,12},{1,17},{... | collective-permute-start | bytes 196616 | tf_op jit(solution)/shard_map/ppermute | solution.py:287
  153.3 7.4 %collective-permute-start.46 = (f32[8,2048]{1,0:T(8,128)S(1)}, f32[8,2048]{1,0:T(8,128)S(1)}, u32[]{:S(2)}, u32[]{:S(2)}) collective-permute-start(f32[8,2048]{1,0:T(8,128)S(1)} %get-tuple-element.177), channel_id=1, source_target_pairs={{0,1},{1,0},{2,3},{3,2},{4,5},{5,4},{6,7},{7,6},{8,9},{9,8},{10,11... | collective-permute-start | bytes 196616 | tf_op jit(solution)/shard_map/ppermute | solution.py:287
  155.3 6.0 %collective-permute-start.47 = (f32[8,2048]{1,0:T(8,128)S(1)}, f32[8,2048]{1,0:T(8,128)S(1)}, u32[]{:S(2)}, u32[]{:S(2)}) collective-permute-start(f32[8,2048]{1,0:T(8,128)S(1)} %get-tuple-element.178), channel_id=1, source_target_pairs={{1,2},{2,1},{5,6},{6,5},{9,10},{10,9},{13,14},{14,13},{17,18},{18,... | collective-permute-start | bytes 196616 | tf_op jit(solution)/shard_map/ppermute | solution.py:287
  155.9 17.9 %collective-permute-start.37 = (bf16[128,2048]{1,0:T(8,128)(2,1)S(1)}, bf16[128,2048]{1,0:T(8,128)(2,1)S(1)}, u32[]{:S(2)}, u32[]{:S(2)}) collective-permute-start(bf16[128,2048]{1,0:T(8,128)(2,1)S(1)} %get-tuple-element.164), channel_id=1, source_target_pairs={{0,8},{4,12},{8,0},{12,4},{16,24},{20,28},{24,16},{28,20},{1,9},{5... | collective-permute-start | bytes 1572872 | tf_op jit(solution)/shard_map/ppermute | solution.py:287
  156.7 17.2 %collective-permute-start.41 = (bf16[128,2048]{1,0:T(8,128)(2,1)S(1)}, bf16[128,2048]{1,0:T(8,128)(2,1)S(1)}, u32[]{:S(2)}, u32[]{:S(2)}) collective-permute-start(bf16[128,2048]{1,0:T(8,128)(2,1)S(1)} %get-tuple-element.170), channel_id=1, source_target_pairs={{0,16},{4,20},{8,24},{12,28},{16,0},{20,4},{24,8},{28,12},{1,17},{... | collective-permute-start | bytes 1572872 | tf_op jit(solution)/shard_map/ppermute | solution.py:287
  158.6 15.2 %collective-permute-start.42 = (bf16[128,2048]{1,0:T(8,128)(2,1)S(1)}, bf16[128,2048]{1,0:T(8,128)(2,1)S(1)}, u32[]{:S(2)}, u32[]{:S(2)}) collective-permute-start(bf16[128,2048]{1,0:T(8,128)(2,1)S(1)} %get-tuple-element.171), channel_id=1, source_target_pairs={{0,1},{1,0},{2,3},{3,2},{4,5},{5,4},{6,7},{7,6},{8,9},{9,8},{10,11... | collective-permute-start | bytes 1572872 | tf_op jit(solution)/shard_map/ppermute | solution.py:287
  160.6 13.2 %collective-permute-start.43 = (bf16[128,2048]{1,0:T(8,128)(2,1)S(1)}, bf16[128,2048]{1,0:T(8,128)(2,1)S(1)}, u32[]{:S(2)}, u32[]{:S(2)}) collective-permute-start(bf16[128,2048]{1,0:T(8,128)(2,1)S(1)} %get-tuple-element.172), channel_id=1, source_target_pairs={{1,2},{2,1},{5,6},{6,5},{9,10},{10,9},{13,14},{14,13},{17,18},{18,... | collective-permute-start | bytes 1572872 | tf_op jit(solution)/shard_map/ppermute | solution.py:287
  177.1 4.4 %collective-permute-start.50 = (f32[64]{0:T(128)S(1)}, f32[64]{0:T(128)S(1)}, u32[]{:S(2)}, u32[]{:S(2)}) collective-permute-start(f32[64]{0:T(128)S(1)} %fusion.1), channel_id=1, source_target_pairs={{0,24},{4,28},{8,16},{12,20},{16,8},{20,12},{24,0},{28,4},{1,25},{... | collective-permute-start | bytes 776 | tf_op jit(solution)/shard_map/ppermute | solution.py:287
  (10 other events, 254.7 us)
